TPU v7x, 128 devices: a whole 4x4x4 slice. The times are simulated.
128 devices in a mesh: row: 8 (over y, core), col: 16 (over z, x).
Axes of the slice: x: 4, y: 4, z: 4, core: 2. Of those that a mesh axis runs over, the one named last changes fastest.
Arguments:
- theta: bfloat16 [6144, 6144], P('row', 'col'), may hold values from -8 to 8
- start_basis: bfloat16 [6144, 2048], P('row', 'col'), may hold values from -6 to 6
Outputs:
- subspace: bfloat16 [6144, 2048], P('row', 'col')
- gram: float32 [2048, 2048], P('col', 'row')
All inputs are finite; a program needn't handle non-finite values.
Results may differ from a plain program's by a relative error of at most 0.0042.
Values may be sent and summed in bfloat16 or wider, within the bound.
No kernel may reach another device: no remote copies, remote signals or barrier semaphores. Data moves between devices by JAX's collectives and lax.ppermute only.
A program may use at most 128 MiB of HBM per device.

v0:
```python
import jax
import jax.numpy as jnp
from jax import lax
from jax.sharding import PartitionSpec as P

ORDER = 6144


def lead_dot(left, right):
    return lax.dot_general(
        left, right, (((0,), (0,)), ((), ())), preferred_element_type=jnp.float32
    )


def tail_dot(left, right):
    return lax.dot_general(
        left, right, (((1,), (1,)), ((), ())), preferred_element_type=jnp.float32
    )


def per_device(theta, start_basis):
    fro = lax.psum(jnp.sum(theta.astype(jnp.float32) ** 2), ("row", "col"))
    slab = lax.all_gather(theta, "row", axis=0, tiled=True)
    raw_block = lax.psum_scatter(tail_dot(slab, theta), "col", scatter_dimension=0, tiled=True)
    density = (raw_block * (ORDER / (4.0 * fro))).astype(jnp.bfloat16)
    first_part = jnp.dot(
        density,
        lax.all_gather(start_basis, "col", axis=1, tiled=True),
        preferred_element_type=jnp.float32,
    )
    first = lax.psum_scatter(first_part, "row", scatter_dimension=1, tiled=True).astype(
        jnp.bfloat16
    )
    second_part = lead_dot(density, lax.all_gather(first, "row", axis=1, tiled=True))
    subspace = lax.psum_scatter(second_part, "col", scatter_dimension=1, tiled=True).astype(
        jnp.bfloat16
    )
    gram_part = lead_dot(subspace, lax.all_gather(subspace, "col", axis=1, tiled=True))
    gram = lax.psum_scatter(gram_part, "row", scatter_dimension=1, tiled=True) / ORDER
    return (subspace, gram)


def solution(mesh):
    in_specs = (P("row", "col"), P("row", "col"))
    out_specs = (P("row", "col"), P("col", "row"))
    return jax.shard_map(
        per_device, mesh=mesh, in_specs=in_specs, out_specs=out_specs, check_vma=False
    )
```

profile of v0, /device:TPU:1, one launch (start us, length us, event | category | flops | bytes accessed | tf_op | source)
XLA Modules:
  0.0 477.5 jit_solution(4935590142315438624)
XLA Ops:
  7.2 0.0 all-gather.5.cloned.1.call-start
  7.2 0.7 all-gather.5.cloned.1.call-update
  7.9 0.0 all-gather.7.cloned.1.call-start
  7.9 0.7 all-gather.7.cloned.1.call-update
  8.6 0.0 reduce-scatter.5.cloned.1.call-start
  8.7 39.0 %all-gather.5.cloned.1.call-done = bf16[6144,384]{1,0:T(8,128)(2,1)} async-done(((bf16[768,384]{1,0:T(8,128)(2,1)}), bf16[6144,384]{1,0:T(8,128)(2,1)}) %all-gather.5.cloned.1.call-update) | async-done | bytes 4718608 | tf_op jit(solution)/shard_map/all_gather | solution.py:23
  47.7 10.9 %fusion.2 = f32[6144,768]{1,0:T(8,128)} fusion(bf16[6144,384]{1,0:T(8,128)(2,1)} %all-gather.5.cloned.1.call-done, bf16[768,384]{1,0:T(8,128)(2,1)} %param.2), kind=kOutput, calls=%fused_computation.5 | convolution fusion | flops 3623878656 | bytes 24182784 | tf_op jit(solution)/shard_map/dot_general | solution.py:16
  58.6 0.0 copy-start
  58.6 0.0 reduce-scatter.5.cloned.1.call-update
  58.6 0.0 reduce-scatter.7.cloned.1.call-start
  58.7 1.0 copy-done
  59.7 0.9 multiply_reduce_fusion
  60.6 65.6 %psum.7 = f32[]{:T(128)} all-reduce(f32[]{:T(128)} %multiply_reduce_fusion), channel_id=1, replica_groups=mesh['row'=8,'col'=16] {'row','col'}, use_global_device_ids=true, to_apply=%region_2.0 | all-reduce | flops 1 | bytes 8 | tf_op jit(solution)/shard_map/psum | solution.py:22
  126.9 0.0 all-gather.7.cloned.1.call-done
  126.9 100.0 %reduce-scatter.5.cloned.1.call-done = f32[384,768]{1,0:T(8,128)} async-done(((f32[6144,768]{1,0:T(8,128)}), f32[384,768]{1,0:T(8,128)}) %reduce-scatter.5.cloned.1.call-update) | async-done | bytes 1179664 | tf_op jit(solution)/shard_map/reduce_scatter | solution.py:24
  226.9 5.3 %fusion.1 = f32[384,2048]{1,0:T(8,128)} fusion(bf16[768,2048]{1,0:T(8,128)(2,1)} %all-gather.7.cloned.1.call-done, f32[384,768]{1,0:T(8,128)} %reduce-scatter.5.cloned.1.call-done, f32[]{:T(128)S(6)} %div.9), kind=kOutput, calls=%fused_computation.3 | convolution fusion | flops 1208549376 | bytes 7471108 | tf_op jit(solution)/shard_map/dot_general | solution.py:26
  232.2 0.0 copy-start.1
  232.2 0.0 reduce-scatter.7.cloned.1.call-update
  232.2 0.0 all-gather.9.cloned.1.call-start
  232.2 32.5 %reduce-scatter.7.cloned.1.call-done = f32[384,256]{1,0:T(8,128)} async-done(((f32[384,2048]{1,0:T(8,128)}), f32[384,256]{1,0:T(8,128)}) %reduce-scatter.7.cloned.1.call-update) | async-done | bytes 393232 | tf_op jit(solution)/shard_map/reduce_scatter | solution.py:31
  264.8 1.7 convert_element_type.14
  266.5 0.0 all-gather.9.cloned.1.call-update
  266.5 0.0 reduce-scatter.9.cloned.1.call-start
  266.5 27.7 %all-gather.9.cloned.1.call-done = bf16[384,2048]{1,0:T(8,128)(2,1)} async-done(((bf16[384,256]{1,0:T(8,128)(2,1)}), bf16[384,2048]{1,0:T(8,128)(2,1)}) %all-gather.9.cloned.1.call-update) | async-done | bytes 1572880 | tf_op jit(solution)/shard_map/all_gather | solution.py:34
  294.2 0.0 copy-done.1
  294.2 5.9 %fusion = f32[768,2048]{1,0:T(8,128)} fusion(bf16[384,2048]{1,0:T(8,128)(2,1)} %all-gather.9.cloned.1.call-done, f32[384,768]{1,0:T(8,128)S(1)} %copy-done.1, f32[]{:T(128)S(6)} %div.9), kind=kOutput, calls=%fused_computation.2 | convolution fusion | flops 1208549376 | bytes 9043972 | tf_op jit(solution)/shard_map/dot_general | solution.py:10
  300.1 0.0 reduce-scatter.9.cloned.1.call-update
  300.1 0.0 all-gather.11.cloned.1.call-start
  300.2 81.1 %reduce-scatter.9.cloned.1.call-done = f32[768,128]{1,0:T(8,128)} async-done(((f32[768,2048]{1,0:T(8,128)}), f32[768,128]{1,0:T(8,128)}) %reduce-scatter.9.cloned.1.call-update) | async-done | bytes 393232 | tf_op jit(solution)/shard_map/reduce_scatter | solution.py:35
  381.3 1.7 convert_element_type.15
  382.9 0.0 all-gather.11.cloned.1.call-update
  383.0 0.0 reduce-scatter.11.cloned.1.call-start
  383.0 53.1 %all-gather.11.cloned.1.call-done = bf16[768,2048]{1,0:T(8,128)(2,1)} async-done(((bf16[768,128]{1,0:T(8,128)(2,1)}), bf16[768,2048]{1,0:T(8,128)(2,1)}) %all-gather.11.cloned.1.call-update) | async-done | bytes 3145744 | tf_op jit(solution)/shard_map/all_gather | solution.py:38
  436.1 3.6 fusion.3
  439.7 0.0 reduce-scatter.11.cloned.1.call-update
  439.8 29.4 %reduce-scatter.11.cloned.1.call-done = f32[128,256]{1,0:T(8,128)} async-done(((f32[128,2048]{1,0:T(8,128)}), f32[128,256]{1,0:T(8,128)}) %reduce-scatter.11.cloned.1.call-update) | async-done | bytes 131088 | tf_op jit(solution)/shard_map/reduce_scatter | solution.py:39
  469.1 1.6 broadcast_multiply_fusion
Async XLA Ops:
  7.2 40.5 %all-gather.5.cloned.1.call-start = ((), (), s32[]{:S(2)}) async-start(), calls=%async_computation.4 | async-start | bytes 5308416 | tf_op jit(solution)/shard_map/all_gather | solution.py:23
  7.9 119.0 %all-gather.7.cloned.1.call-start = ((), (), s32[]{:S(2)}) async-start(), calls=%async_computation.6 | async-start | bytes 3342336 | tf_op jit(solution)/shard_map/all_gather | solution.py:28
  8.6 218.2 %reduce-scatter.5.cloned.1.call-start = ((), (), s32[]{:S(2)}) async-start(), calls=%async_computation.5 | async-start | bytes 20054016 | tf_op jit(solution)/shard_map/reduce_scatter | solution.py:24
  58.6 1.1 copy-start
  58.6 206.1 %reduce-scatter.7.cloned.1.call-start = ((), (), s32[]{:S(2)}) async-start(), calls=%async_computation.7 | async-start | bytes 3538944 | tf_op jit(solution)/shard_map/reduce_scatter | solution.py:31
  232.2 62.0 %copy-start.1 = (f32[384,768]{1,0:T(8,128)S(1)}, f32[384,768]{1,0:T(8,128)}, u32[]{:S(2)}) copy-start(f32[384,768]{1,0:T(8,128)} %reduce-scatter.5.cloned.1.call-done) | copy-start | bytes 3538948
  232.2 62.0 %all-gather.9.cloned.1.call-start = ((), (), s32[]{:S(2)}) async-start(), calls=%async_computation.8 | async-start | bytes 1769472 | tf_op jit(solution)/shard_map/all_gather | solution.py:34
  266.5 114.8 %reduce-scatter.9.cloned.1.call-start = ((), (), s32[]{:S(2)}) async-start(), calls=%async_computation.9 | async-start | bytes 6684672 | tf_op jit(solution)/shard_map/reduce_scatter | solution.py:35
  300.1 136.0 %all-gather.11.cloned.1.call-start = ((), (), s32[]{:S(2)}) async-start(), calls=%async_computation.10 | async-start | bytes 3342336 | tf_op jit(solution)/shard_map/all_gather | solution.py:38
  383.0 86.2 %reduce-scatter.11.cloned.1.call-start = ((), (), s32[]{:S(2)}) async-start(), calls=%async_computation.11 | async-start | bytes 1179648 | tf_op jit(solution)/shard_map/reduce_scatter | solution.py:39
Sparse Core Ops, SparseCore 0:
  9.7 37.9 all-gather.4
  49.8 51.6 all-gather.6
  105.0 121.8 reduce-scatter.4
  232.3 32.4 reduce-scatter.6
  266.9 27.2 all-gather.8
  300.3 80.9 reduce-scatter.8
  383.9 52.1 all-gather.10
  439.9 29.1 reduce-scatter.10
where the time goes:
time: 480 us; the launch traced here: 478 us
  waiting for transfers between devices  364 us (76%)
  blocking collectives  65.6 us (14%)
  matrix products  25.7 us (5%)
  between operations  14.8 us (3%)
  other arithmetic  5.85 us (1%)
    reduce_scatter x1, waiting for transfers between devices, per_device(): lax.psum_scatter(tail_dot(slab, theta), 'col', scatter_dimension=0, tiled...  100 us
    reduce_scatter x1, waiting for transfers between devices, per_device(): lax.psum_scatter(second_part, 'col', scatter_dimension=1, tiled=True)  81.1 us
    psum x1, blocking collectives, per_device(): fro = lax.psum(jnp.sum(theta.astype(jnp.float32) ** 2), ('row', 'col'))  65.6 us
    all_gather x1, waiting for transfers between devices, per_device(): lax.all_gather(subspace, 'col', axis=1, tiled=True)  53.1 us
    all_gather x1, waiting for transfers between devices, per_device(): slab = lax.all_gather(theta, 'row', axis=0, tiled=True)  39 us
    reduce_scatter x1, waiting for transfers between devices, per_device(): lax.psum_scatter(first_part, 'row', scatter_dimension=1, tiled=True)  32.5 us
    reduce_scatter x1, waiting for transfers between devices, per_device(): lax.psum_scatter(gram_part, 'row', scatter_dimension=1, tiled=True) / ORDER  29.4 us
    all_gather x1, waiting for transfers between devices, per_device(): lax.all_gather(first, 'row', axis=1, tiled=True)  27.7 us
  transfers between devices with their start and end apart: 8, of which 7 were waited for; matrix products, arithmetic and copies ran while one was open for 2% of the time, Pallas kernels for 0%

commit v1 on v0

v1 whole, which is shorter than its diff:
```python
import jax
import jax.numpy as jnp
from jax import lax
from jax.sharding import Mesh, PartitionSpec as P

ORDER = 6144
ALL = ("y", "core", "z", "x")


def other_core(x):
    return lax.ppermute(x, "core", [(0, 1), (1, 0)])


def core_sum_half(parts, core):
    mine = lax.dynamic_index_in_dim(parts, core, 0, keepdims=False)
    theirs = lax.dynamic_index_in_dim(parts, 1 - core, 0, keepdims=False)
    return mine + other_core(theirs)


def three_terms(value, width):
    high = lax.reduce_precision(value, 8, 7)
    mid = lax.reduce_precision(value - high, 8, 7)
    low = value - high - mid
    rows = jnp.stack([high, mid, low] + [jnp.zeros_like(value)] * 13)
    return jnp.broadcast_to(rows[:, None], (16, width)).astype(jnp.bfloat16)


def sum_over_rows(part, core, square=None):
    n, width = part.shape
    half = core_sum_half(part.reshape(2, n // 2, width), core)
    pieces = half.astype(jnp.bfloat16).reshape(4, n // 8, width)
    if square is not None:
        square = square + other_core(jnp.full((8, 128), square))[0, 0]
        extra = jnp.broadcast_to(three_terms(square, width)[None], (4, 16, width))
        pieces = jnp.concatenate([pieces, extra], 1)
    got = lax.all_to_all(pieces, "y", 0, 0).astype(jnp.float32)
    total = jnp.sum(got[:, n // 8 :, 0])
    piece = jnp.sum(got[:, : n // 8], axis=0).astype(jnp.bfloat16)
    mine = lax.all_gather(piece, "y", axis=0).reshape(n // 2, width)
    theirs = other_core(mine)
    first = core == 0
    return jnp.concatenate([jnp.where(first, mine, theirs), jnp.where(first, theirs, mine)], 0), total


def per_device(theta, basis):
    core = lax.axis_index("core")
    slab = lax.all_gather(theta, ("z", "x"), axis=0)
    square = jnp.sum(slab.astype(jnp.float32) ** 2)

    def down(x, square=None):
        out = lax.dot_general(slab, x, (((1,), (0,)), ((), ())), preferred_element_type=jnp.float32)
        return sum_over_rows(out.reshape(-1, x.shape[1]), core, square)

    def up(t, scale):
        t = t.reshape(slab.shape[0], slab.shape[2], -1)
        out = lax.dot_general(slab, t, (((0, 2), (0, 1)), ((), ())), preferred_element_type=jnp.float32)
        return (out * scale).astype(jnp.bfloat16)

    total, fro = down(basis, square)
    scale = ORDER / (4.0 * fro)
    first = up(total, scale)
    subspace = up(down(first)[0], scale)

    along_x = lax.all_gather(subspace, "x", axis=0)
    along_z = lax.all_gather(subspace, "z", axis=0)
    part = jnp.einsum("brn,arm->bamn", along_z, along_x, preferred_element_type=jnp.float32)
    part = part.reshape(4, 4, 2, 64, 128).transpose(2, 0, 1, 3, 4).reshape(2, 16, 64, 128)
    half = core_sum_half(part, core)
    got = lax.all_to_all(half, ("y", "x"), 0, 0).reshape(4, 4, 64, 128)
    rows = jnp.sum(got, axis=0).reshape(2, 2, 64, 128)
    mine = lax.dynamic_index_in_dim(rows, core, 0, keepdims=False)
    theirs = other_core(lax.dynamic_index_in_dim(rows, 1 - core, 0, keepdims=False))
    first_half = core == 0
    both = jnp.stack([jnp.where(first_half, mine, theirs), jnp.where(first_half, theirs, mine)])
    gram = both.transpose(0, 2, 1, 3).reshape(128, 256) / ORDER
    return subspace, gram


def solution(mesh):
    sizes = (mesh.shape["row"] // 2, 2, 4, mesh.shape["col"] // 4)
    fine = Mesh(mesh.devices.reshape(sizes), ALL)
    spec = P(("y", "core"), ("z", "x"))
    return jax.shard_map(
        per_device,
        mesh=fine,
        in_specs=(spec, spec),
        out_specs=(spec, P(("z", "x"), ("y", "core"))),
        check_vma=False,
    )
```

time: 480 us -> 264 us (0.55)
  waiting for transfers between devices: 364 us -> 90.3 us
  blocking collectives: 65.6 us -> 89.6 us
  starting transfers between devices: 0.32 us -> 18.6 us
  local copies, waits for them, and re-layouts: 1.01 us -> 9.28 us
  between operations: 14.8 us -> 19.8 us
    reduce_scatter x4 -> x0, waiting for transfers between devices: 243 us -> none  [the longest x1 100 us: per_device(): lax.psum_scatter(tail_dot(slab, theta), 'col', scatter_dimension=0, tiled...]
    psum x1 -> x0, blocking collectives: 65.6 us -> none  [per_device(): fro = lax.psum(jnp.sum(theta.astype(jnp.float32) ** 2), ('row', 'col'))]
    all_to_all x0 -> x3, blocking collectives: none -> 45 us  [the longest x2 30.2 us: sum_over_rows(): got = lax.all_to_all(pieces, 'y', 0, 0).astype(jnp.float32)]
    all_gather x0 -> x4, blocking collectives: none -> 44.6 us  [the longest x2 22.2 us: sum_over_rows(): mine = lax.all_gather(piece, 'y', axis=0).reshape(n // 2, width)]
    all_gather x4 -> x1, waiting for transfers between devices: 120 us -> 81.3 us  [per_device(): slab = lax.all_gather(theta, ('z', 'x'), axis=0)]
    ppermute x0 -> x7, starting transfers between devices: none -> 18.6 us  [other_core(): return lax.ppermute(x, 'core', [(0, 1), (1, 0)])]
    ppermute x0 -> x7, waiting for transfers between devices: none -> 8.34 us  [other_core(): return lax.ppermute(x, 'core', [(0, 1), (1, 0)])]
    reduce_sum x1 -> x5, other arithmetic: 0.9 us -> 6.33 us  [the longest x1 5.45 us: per_device(): square = jnp.sum(slab.astype(jnp.float32) ** 2)]
  transfers between devices with their start and end apart: 8 -> 8, of which waited for: 7 -> 7; matrix products, arithmetic and copies ran while one was open for 2% -> 3% of each run, Pallas kernels for 0% -> 0%
where the time goes in v1:
time: 264 us
  waiting for transfers between devices  90.3 us (34%)
  blocking collectives  89.6 us (34%)
  matrix products  26.2 us (10%)
  between operations  19.8 us (8%)
  starting transfers between devices  18.6 us (7%)
  other arithmetic  10.1 us (4%)
  local copies, waits for them, and re-layouts  9.28 us (4%)
    all_gather x1, waiting for transfers between devices, per_device(): slab = lax.all_gather(theta, ('z', 'x'), axis=0)  81.3 us
    all_to_all x2, blocking collectives, sum_over_rows(): got = lax.all_to_all(pieces, 'y', 0, 0).astype(jnp.float32)  30.2 us
    all_gather x2, blocking collectives, sum_over_rows(): mine = lax.all_gather(piece, 'y', axis=0).reshape(n // 2, width)  22.2 us
    dot_general x2, matrix products, down(): lax.dot_general(slab, x, (((1,), (0,)), ((), ())), preferred_element_type...  18.8 us
    ppermute x7, starting transfers between devices, other_core(): return lax.ppermute(x, 'core', [(0, 1), (1, 0)])  18.6 us
    all_to_all x1, blocking collectives, per_device(): got = lax.all_to_all(half, ('y', 'x'), 0, 0).reshape(4, 4, 64, 128)  14.8 us
    all_gather x1, blocking collectives, per_device(): along_z = lax.all_gather(subspace, 'z', axis=0)  11.9 us
    all_gather x1, blocking collectives, per_device(): along_x = lax.all_gather(subspace, 'x', axis=0)  10.4 us
  transfers between devices with their start and end apart: 8, of which 7 were waited for; matrix products, arithmetic and copies ran while one was open for 3% of the time, Pallas kernels for 0%

profile of v1, /device:TPU:1, one launch (start us, length us, event | category | flops | bytes accessed | tf_op | source)
XLA Modules:
  0.0 263.9 jit_solution(9624975266780714473)
XLA Ops:
  7.2 0.7 all-gather.7.cloned.1.call-update
  7.9 81.3 %all-gather.7.cloned.1.call-done = bf16[12288,384]{1,0:T(8,128)(2,1)} async-done(((bf16[768,384]{1,0:T(8,128)(2,1)}), bf16[12288,384]{1,0:T(8,128)(2,1)}) %all-gather.7.cloned.1.call-update) | async-done | bytes 9437200 | tf_op jit(solution)/shard_map/all_gather | solution.py:47
  89.3 6.2 %fusion.10 = f32[16,384,128]{2,1,0:T(8,128)S(1)} fusion(bf16[16,768,384]{2,1,0:T(8,128)(2,1)} %bitcast.97, bf16[768,128]{1,0:T(8,128)(2,1)S(1)} %copy-done), kind=kOutput, calls=%fused_computation.28 | convolution fusion | flops 1207959552 | bytes 12779520 | tf_op jit(solution)/shard_map/dot_general | solution.py:51
  95.4 1.3 dynamic-slice_bitcast_fusion.1
  96.7 0.7 collective-permute-start
  97.4 5.5 %multiply_reduce_fusion = f32[]{:T(128)} fusion(bf16[16,768,384]{2,1,0:T(8,128)(2,1)S(1)} %bitcast.102), kind=kLoop, calls=%fused_computation | loop fusion | flops 14155775 | bytes 9437188 | tf_op jit(solution)/shard_map/reduce_sum | solution.py:48
  102.9 0.6 broadcast_in_dim.4
  103.5 0.1 collective-permute-start.1
  103.6 1.1 collective-permute-done.1
  104.8 0.5 slice.9
  110.2 0.1 stack.28
  110.3 1.6 fusion.1
  111.9 0.2 pad_maximum_fusion.2
  112.1 15.9 %all_to_all.15 = bf16[4,784,128]{2,1,0:T(8,128)(2,1)S(1)} all-to-all(bf16[4,784,128]{2,1,0:T(8,128)(2,1)S(1)} %pad_maximum_fusion.2), channel_id=1, replica_groups=mesh['y'=4,'core'=2,'z'=4,'x'=4] {'y'}, dimensions={0} | all-to-all | bytes 1605632 | tf_op jit(solution)/shard_map/all_to_all | solution.py:36
  128.1 0.1 convert_element_type.41
  128.2 11.1 %all-gather.1 = bf16[3072,128]{1,0:T(8,128)(2,1)S(1)} all-gather(bf16[768,128]{1,0:T(8,128)(2,1)S(1)} %slice_reduce_fusion), channel_id=3, replica_groups=mesh['y'=4,'core'=2,'z'=4,'x'=4] {'y'}, dimensions={0}, use_global_device_ids=true | all-gather | bytes 983040 | tf_op jit(solution)/shard_map/all_gather | solution.py:39
  139.3 4.5 %collective-permute-start.2 = (bf16[3072,128]{1,0:T(8,128)(2,1)S(1)}, bf16[3072,128]{1,0:T(8,128)(2,1)S(1)}, u32[]{:S(2)}, u32[]{:S(2)}) collective-permute-start(bf16[3072,128]{1,0:T(8,128)(2,1)S(1)} %all-gather.1), channel_id=1, source_target_pairs={{0,16},{16,0},{1,17},{17,1},{2,18},{18,2},{3,19},{19,3},{4,20},{20... | collective-permute-start | bytes 2359304 | tf_op jit(solution)/shard_map/ppermute | solution.py:11
  143.8 0.6 slice_reduce_fusion.1
  145.1 0.6 collective-permute-done.2
  145.8 0.1 broadcast_select_fusion.3
  145.9 1.3 pad_maximum_fusion
  147.1 12.6 %convolution_bitcast_fusion = f32[16,384,128]{1,2,0:T(8,128)S(1)} fusion(bf16[16,768,384]{2,1,0:T(8,128)(2,1)} %bitcast.98, bf16[16,384,128]{2,1,0:T(8,128)(2,1)} %bitcast.108, f32[]{:T(128)S(6)} %div.13), kind=kOutput, calls=%fused_computation.1 | convolution fusion | flops 2416115712 | bytes 14155780 | tf_op jit(solution)/shard_map/dot_general | solution.py:51
  159.8 2.4 copy.26
  162.1 1.7 dynamic-slice_bitcast_fusion
  163.8 0.6 collective-permute-start.3
  164.4 3.0 %collective-permute-done.3 = f32[3072,128]{1,0:T(8,128)S(1)} collective-permute-done((f32[3072,128]{1,0:T(8,128)S(1)}, f32[3072,128]{1,0:T(8,128)S(1)}, u32[]{:S(2)}, u32[]{:S(2)}) %collective-permute-start.3) | collective-permute-done | bytes 1572896 | tf_op jit(solution)/shard_map/ppermute | solution.py:11
  167.5 0.2 fusion
  167.6 14.3 %all_to_all.16 = bf16[4,768,128]{2,1,0:T(8,128)(2,1)S(1)} all-to-all(bf16[4,768,128]{2,1,0:T(8,128)(2,1)S(1)} %bitcast.114), channel_id=1, replica_groups=mesh['y'=4,'core'=2,'z'=4,'x'=4] {'y'}, dimensions={0} | all-to-all | bytes 1572864 | tf_op jit(solution)/shard_map/all_to_all | solution.py:36
  181.9 0.2 reduce_sum.51
  182.1 11.1 %all-gather.2 = bf16[3072,128]{1,0:T(8,128)(2,1)S(1)} all-gather(bf16[768,128]{1,0:T(8,128)(2,1)S(1)} %reduce_sum.51), channel_id=4, replica_groups=mesh['y'=4,'core'=2,'z'=4,'x'=4] {'y'}, dimensions={0}, use_global_device_ids=true | all-gather | bytes 983040 | tf_op jit(solution)/shard_map/all_gather | solution.py:39
  193.2 4.5 %collective-permute-start.4 = (bf16[3072,128]{1,0:T(8,128)(2,1)S(1)}, bf16[3072,128]{1,0:T(8,128)(2,1)S(1)}, u32[]{:S(2)}, u32[]{:S(2)}) collective-permute-start(bf16[3072,128]{1,0:T(8,128)(2,1)S(1)} %all-gather.2), channel_id=1, source_target_pairs={{0,16},{16,0},{1,17},{17,1},{2,18},{18,2},{3,19},{19,3},{4,20},{20... | collective-permute-start | bytes 2359304 | tf_op jit(solution)/shard_map/ppermute | solution.py:11
  197.8 1.9 collective-permute-done.4
  199.7 0.1 broadcast_select_fusion.1
  199.8 0.1 pad_maximum_fusion.1
  199.9 6.9 %fusion.7 = bf16[768,128]{0,1:T(8,128)(2,1)S(1)} fusion(bf16[16,384,128]{2,1,0:T(8,128)(2,1)S(1)} %bitcast.107, bf16[16,768,384]{2,1,0:T(8,128)(2,1)} %bitcast.99, f32[]{:T(128)S(6)} %div.13), kind=kOutput, calls=%fused_computation.18 | convolution fusion | flops 1208156160 | bytes 11206660 | tf_op jit(solution)/shard_map/dot_general | solution.py:56
  206.8 11.9 %all-gather.4 = bf16[3072,128]{0,1:T(8,128)(2,1)S(1)} all-gather(bf16[768,128]{0,1:T(8,128)(2,1)S(1)} %fusion.7), channel_id=6, replica_groups=mesh['y'=4,'core'=2,'z'=4,'x'=4] {'z'}, dimensions={0}, use_global_device_ids=true | all-gather | bytes 983040 | tf_op jit(solution)/shard_map/all_gather | solution.py:65
  218.7 10.4 %all-gather.3 = bf16[3072,128]{0,1:T(8,128)(2,1)S(1)} all-gather(bf16[768,128]{0,1:T(8,128)(2,1)S(1)} %fusion.7), channel_id=5, replica_groups=mesh['y'=4,'core'=2,'z'=4,'x'=4] {'x'}, dimensions={0}, use_global_device_ids=true | all-gather | bytes 983040 | tf_op jit(solution)/shard_map/all_gather | solution.py:64
  229.1 0.4 copy.39
  229.5 0.6 reshape.59
  230.1 0.6 fusion.8
  230.7 0.1 copy.30
  230.8 6.2 %collective-permute-start.5 = (f32[16,64,128]{2,1,0:T(8,128)S(1)}, f32[16,64,128]{2,1,0:T(8,128)S(1)}, u32[]{:S(2)}, u32[]{:S(2)}) collective-permute-start(f32[16,64,128]{2,1,0:T(8,128)S(1)} %dynamic-slice_bitcast_fusion.2), channel_id=1, source_target_pairs={{0,16},{16,0},{1,17},{17,1},{2,18},{18,2},{3,19},{19,3},{4,20},{20... | collective-permute-start | bytes 1572872 | tf_op jit(solution)/shard_map/ppermute | solution.py:11
  237.1 1.5 collective-permute-done.5
  238.7 14.8 %all_to_all.17 = f32[16,64,128]{2,1,0:T(8,128)S(1)} all-to-all(f32[16,64,128]{2,1,0:T(8,128)S(1)} %bitcast_add_fusion.2), channel_id=1, replica_groups=mesh['y'=4,'core'=2,'z'=4,'x'=4] {'y','x'}, dimensions={0} | all-to-all | bytes 1048576 | tf_op jit(solution)/shard_map/all_to_all | solution.py:69
  253.5 1.9 collective-permute-start.6
  255.3 0.8 copy.32
  256.3 0.1 copy.31
  256.4 0.7 copy.44
  (24 shorter events, 0.4 us)
Async XLA Ops:
  7.2 82.1 %copy-start = (bf16[768,128]{1,0:T(8,128)(2,1)S(1)}, bf16[768,128]{1,0:T(8,128)(2,1)}, u32[]{:S(2)}) copy-start(bf16[768,128]{1,0:T(8,128)(2,1)} %param.3) | copy-start | bytes 589828
  7.2 82.1 %all-gather.7.cloned.1.call-start = ((), (), s32[]{:S(2)}) async-start(), calls=%async_computation.3 | async-start | bytes 10027008 | tf_op jit(solution)/shard_map/all_gather | solution.py:47
  89.2 8.1 %slice-start = ((s8[9437184]{0:T(1024)(128)(4,1)}), s8[4194304]{0:T(1024)(128)(4,1)S(1)}, s32[]{:S(2)}) async-start(s8[9437184]{0:T(1024)(128)(4,1)} %bitcast.100), calls=%async_computation.4 | async-start | bytes 8388608
  89.3 8.1 %slice-start.1 = ((s8[9437184]{0:T(1024)(128)(4,1)}), s8[4194304]{0:T(1024)(128)(4,1)S(1)}, s32[]{:S(2)}) async-start(s8[9437184]{0:T(1024)(128)(4,1)} %bitcast.100), calls=%async_computation.5 | async-start | bytes 8388608
  89.3 8.1 %slice-start.2 = ((s8[9437184]{0:T(1024)(128)(4,1)}), s8[1048576]{0:T(1024)(128)(4,1)S(1)}, s32[]{:S(2)}) async-start(s8[9437184]{0:T(1024)(128)(4,1)} %bitcast.100), calls=%async_computation.6 | async-start | bytes 2097152
  96.7 13.6 %collective-permute-start = (f32[3072,128]{1,0:T(8,128)}, f32[3072,128]{1,0:T(8,128)}, u32[]{:S(2)}, u32[]{:S(2)}) collective-permute-start(f32[3072,128]{1,0:T(8,128)} %dynamic-slice_bitcast_fusion.1), channel_id=1, source_target_pairs={{0,16},{16,0},{1,17},{17,1},{2,18},{18,2},{3,19},{19,3},{4,20},{20... | collective-permute-start | bytes 4718600 | tf_op jit(solution)/shard_map/ppermute | solution.py:11
  103.5 1.2 collective-permute-start.1
  139.3 6.4 %collective-permute-start.2 = (bf16[3072,128]{1,0:T(8,128)(2,1)S(1)}, bf16[3072,128]{1,0:T(8,128)(2,1)S(1)}, u32[]{:S(2)}, u32[]{:S(2)}) collective-permute-start(bf16[3072,128]{1,0:T(8,128)(2,1)S(1)} %all-gather.1), channel_id=1, source_target_pairs={{0,16},{16,0},{1,17},{17,1},{2,18},{18,2},{3,19},{19,3},{4,20},{20... | collective-permute-start | bytes 2359304 | tf_op jit(solution)/shard_map/ppermute | solution.py:11
  162.1 5.3 %copy-start.1 = (f32[16,384,128]{2,1,0:T(8,128)S(1)}, f32[16,384,128]{2,1,0:T(8,128)}, u32[]{:S(2)}) copy-start(f32[16,384,128]{2,1,0:T(8,128)} %copy.26) | copy-start | bytes 9437188
  163.8 3.7 %collective-permute-start.3 = (f32[3072,128]{1,0:T(8,128)S(1)}, f32[3072,128]{1,0:T(8,128)S(1)}, u32[]{:S(2)}, u32[]{:S(2)}) collective-permute-start(f32[3072,128]{1,0:T(8,128)S(1)} %dynamic-slice_bitcast_fusion), channel_id=1, source_target_pairs={{0,16},{16,0},{1,17},{17,1},{2,18},{18,2},{3,19},{19,3},{4,20},{20... | collective-permute-start | bytes 4718600 | tf_op jit(solution)/shard_map/ppermute | solution.py:11
  193.2 6.5 %collective-permute-start.4 = (bf16[3072,128]{1,0:T(8,128)(2,1)S(1)}, bf16[3072,128]{1,0:T(8,128)(2,1)S(1)}, u32[]{:S(2)}, u32[]{:S(2)}) collective-permute-start(bf16[3072,128]{1,0:T(8,128)(2,1)S(1)} %all-gather.2), channel_id=1, source_target_pairs={{0,16},{16,0},{1,17},{17,1},{2,18},{18,2},{3,19},{19,3},{4,20},{20... | collective-permute-start | bytes 2359304 | tf_op jit(solution)/shard_map/ppermute | solution.py:11
  230.8 7.8 %collective-permute-start.5 = (f32[16,64,128]{2,1,0:T(8,128)S(1)}, f32[16,64,128]{2,1,0:T(8,128)S(1)}, u32[]{:S(2)}, u32[]{:S(2)}) collective-permute-start(f32[16,64,128]{2,1,0:T(8,128)S(1)} %dynamic-slice_bitcast_fusion.2), channel_id=1, source_target_pairs={{0,16},{16,0},{1,17},{17,1},{2,18},{18,2},{3,19},{19,3},{4,20},{20... | collective-permute-start | bytes 1572872 | tf_op jit(solution)/shard_map/ppermute | solution.py:11
  253.5 2.8 %collective-permute-start.6 = (f32[2,64,128]{2,1,0:T(8,128)S(1)}, f32[2,64,128]{2,1,0:T(8,128)S(1)}, u32[]{:S(2)}, u32[]{:S(2)}) collective-permute-start(f32[2,64,128]{2,1,0:T(8,128)S(1)} %dynamic-slice_bitcast_fusion.3), channel_id=1, source_target_pairs={{0,16},{16,0},{1,17},{17,1},{2,18},{18,2},{3,19},{19,3},{4,20},{20... | collective-permute-start | bytes 196616 | tf_op jit(solution)/shard_map/ppermute | solution.py:11
Sparse Core Ops, SparseCore 0:
  10.1 79.0 all-gather.6

commit v2 on v1

v2 whole, which is shorter than its diff:
```python
import jax
import jax.numpy as jnp
from jax import lax
from jax.experimental import pallas as pl
from jax.experimental.pallas import tpu as pltpu
from jax.sharding import Mesh, PartitionSpec as P

ORDER = 6144
ALL = ("y", "core", "z", "x")
COLS = 384
BLOCKS = 16


def shift(x, axis, by):
    return lax.ppermute(x, axis, [(i, (i + by) % 4) for i in range(4)])


def other_core(x):
    return lax.ppermute(x, "core", [(0, 1), (1, 0)])


def f32_dot(left, right, dims):
    return lax.dot_general(left, right, (dims, ((), ())), preferred_element_type=jnp.float32)


def gather_plane(own):
    rows = own.shape[0]
    half, quarter = rows // 2, rows // 4
    xp, xm, zp, zm = lax.optimization_barrier(
        (shift(own, "x", 1), shift(own, "x", 3), shift(own, "z", 1), shift(own, "z", 3))
    )
    a, b, c, d = lax.optimization_barrier(
        (
            shift(jnp.concatenate([zp, xp[:half]]), "x", 1),
            shift(jnp.concatenate([zm, xm[half:]]), "x", 3),
            shift(jnp.concatenate([xm, zp[:half]]), "z", 1),
            shift(jnp.concatenate([xp, zm[half:]]), "z", 3),
        )
    )
    far_x = jnp.concatenate([a[rows:], b[rows:]])
    far_z = jnp.concatenate([c[rows:], d[rows:]])
    e, f, g, h = lax.optimization_barrier(
        (shift(far_z, "x", 1), shift(far_z, "x", 3), shift(far_x, "z", 1), shift(far_x, "z", 3))
    )
    last = jnp.concatenate(
        lax.optimization_barrier(
            (
                shift(e[:quarter], "x", 1),
                shift(f[quarter:half], "x", 3),
                shift(g[half : half + quarter], "z", 1),
                shift(h[half + quarter :], "z", 3),
            )
        )
    )
    return [own, xp, xm, zp, zm], [a, b, c, d, far_x, far_z], [e, f, g, h], [last]


def three_terms(value):
    high = lax.reduce_precision(value, 8, 7)
    mid = lax.reduce_precision(value - high, 8, 7)
    low = value - high - mid
    lane = lax.broadcasted_iota(jnp.int32, (16, 128), 1)
    row = lax.broadcasted_iota(jnp.int32, (16, 128), 0)
    terms = jnp.where(lane == 0, high, jnp.where(lane == 1, mid, jnp.where(lane == 2, low, 0.0)))
    return jnp.where(row == 0, terms, 0.0).astype(jnp.bfloat16)


def sum_over_rows(mine, theirs, square=None):
    n = mine.shape[1]
    half = mine + other_core(theirs)
    send = half.astype(jnp.bfloat16)
    if square is not None:
        square = square + other_core(jnp.full((8, 128), square))[0, 0]
        extra = jnp.tile(three_terms(square), (4, 1))
        send = jnp.concatenate([send, extra], 1)
    got = [shift(send[16 * d : 16 * d + 16], "y", d) for d in (1, 3, 2)]
    total = half[:16]
    for piece in got:
        total = total + piece[:, :n].astype(jnp.float32)
    fro = None
    if square is not None:
        fro = square + sum(jnp.sum(piece[:, n:].astype(jnp.float32)) for piece in got)
    piece = total.astype(jnp.bfloat16)
    up1, up3, up2 = (shift(piece, "y", 4 - d) for d in (1, 3, 2))
    whole = jnp.concatenate([piece, up1, up2, up3])
    return jnp.concatenate([whole, other_core(whole)]), fro


def apply_kernel(down, scale_ref, t_ref, *refs):
    theta_refs = refs[:BLOCKS]
    outs = refs[BLOCKS : BLOCKS + (2 if down else 1)]
    theta, sems = refs[-2:]
    rows = theta.shape[1]
    copies = []
    for i, ref in enumerate(theta_refs):
        copy = pltpu.make_async_copy(ref.at[pl.ds(0, rows)], theta.at[i], sems.at[i])
        copy.start()
        copies.append(copy)
    total = jnp.zeros((t_ref.shape[0], rows), jnp.float32)
    for i, copy in enumerate(copies):
        copy.wait()
        total += f32_dot(t_ref[:, i * COLS : (i + 1) * COLS], theta[i], ((1,), (1,)))
    x = (total * scale_ref[0, 0]).astype(jnp.bfloat16)
    if not down:
        outs[0][...] = x
        return
    for i in range(BLOCKS):
        part = f32_dot(x, theta[i], ((1,), (0,)))
        outs[0][:, i * COLS : (i + 1) * COLS] = part[:64]
        outs[1][:, i * COLS : (i + 1) * COLS] = part[64:]


def apply(scale, t, blocks, down):
    width, n = t.shape
    rows = blocks[0].shape[0]
    if down:
        out_shape = [jax.ShapeDtypeStruct((64, n), jnp.float32)] * 2
    else:
        out_shape = [jax.ShapeDtypeStruct((width, rows), jnp.bfloat16)]
    vmem = pl.BlockSpec(memory_space=pltpu.VMEM)
    return pl.pallas_call(
        lambda *refs: apply_kernel(down, *refs),
        out_shape=out_shape,
        in_specs=[pl.BlockSpec(memory_space=pltpu.SMEM), vmem] + [pl.BlockSpec(memory_space=pl.ANY)] * BLOCKS,
        out_specs=[vmem] * len(out_shape),
        scratch_shapes=[
            pltpu.VMEM((BLOCKS, rows, COLS), jnp.bfloat16),
            pltpu.SemaphoreType.DMA((BLOCKS,)),
        ],
        compiler_params=pltpu.CompilerParams(vmem_limit_bytes=32 * 2**20),
        cost_estimate=pl.CostEstimate(
            flops=(4 if down else 2) * width * n * rows, bytes_accessed=2 * n * rows, transcendentals=0
        ),
    )(scale.reshape(1, 1), t, *blocks)


def column_order(y, core):
    place = lax.broadcasted_iota(jnp.int32, (128, 128), 0)
    column = lax.broadcasted_iota(jnp.int32, (128, 128), 1)
    half = (place // 64 + core) % 2
    group = (place // 16 + y) % 4
    return (column == half * 64 + group * 16 + place % 16).astype(jnp.bfloat16)


def per_device(theta, basis):
    core, y = lax.axis_index("core"), lax.axis_index("y")
    order = column_order(y, core)
    x = f32_dot(order, basis, ((1,), (1,))).astype(jnp.bfloat16)

    blocks, parts, square = [], [], 0.0
    rows = theta.shape[0]
    for step in gather_plane(theta):
        for block in step:
            block_rows = block[:rows]
            parts.append(f32_dot(x, block_rows, ((1,), (0,))))
            square = square + jnp.sum(block_rows.astype(jnp.float32) ** 2)
            blocks.append(block)
    mine = jnp.concatenate([p[:64] for p in parts], 1)
    theirs = jnp.concatenate([p[64:] for p in parts], 1)
    t, fro = sum_over_rows(mine, theirs, square)
    scale = ORDER / (4.0 * fro)
    t, _ = sum_over_rows(*apply(scale, t, blocks, True))
    (x,) = apply(scale, t, blocks, False)
    subspace = f32_dot(x, order, ((0,), (0,))).astype(jnp.bfloat16)

    along_x = lax.all_gather(subspace, "x", axis=0)
    along_z = lax.all_to_all(jnp.broadcast_to(subspace[None], (4, *subspace.shape)), "z", 0, 0)
    part = jnp.einsum("brn,arm->bamn", along_z, along_x, preferred_element_type=jnp.float32)
    part = part.reshape(4, 4, 2, 64, 128).transpose(2, 0, 1, 3, 4).reshape(2, 16, 64, 128)
    keep = lax.dynamic_index_in_dim(part, core, 0, keepdims=False)
    half = keep + other_core(lax.dynamic_index_in_dim(part, 1 - core, 0, keepdims=False))
    got = lax.all_to_all(half, ("y", "x"), 0, 0).reshape(4, 4, 64, 128)
    sums = jnp.sum(got, axis=0).reshape(2, 2, 64, 128)
    keep = lax.dynamic_index_in_dim(sums, core, 0, keepdims=False)
    theirs = other_core(lax.dynamic_index_in_dim(sums, 1 - core, 0, keepdims=False))
    first_half = core == 0
    both = jnp.stack([jnp.where(first_half, keep, theirs), jnp.where(first_half, theirs, keep)])
    gram = both.transpose(0, 2, 1, 3).reshape(128, 256) / ORDER
    return subspace, gram


def solution(mesh):
    fine = Mesh(mesh.devices.reshape(4, 2, 4, 4), ALL)
    spec = P(("y", "core"), ("z", "x"))
    return jax.shard_map(
        per_device,
        mesh=fine,
        in_specs=(spec, spec),
        out_specs=(spec, P(("z", "x"), ("y", "core"))),
        check_vma=False,
    )
```

time: 264 us -> 251 us (0.951)
  blocking collectives: 89.6 us -> 24.9 us
  starting transfers between devices: 18.6 us -> 52.6 us
  other arithmetic: 10.1 us -> 30.9 us
  local copies, waits for them, and re-layouts: 9.28 us -> 29.7 us
  waiting for transfers between devices: 90.3 us -> 69.9 us
  matrix products: 26.2 us -> 9.93 us
  Pallas kernels: 0 us -> 15.2 us
  between operations: 19.8 us -> 16.8 us
    all_gather x1 -> x0, waiting for transfers between devices: 81.3 us -> none  [per_device(): slab = lax.all_gather(theta, ('z', 'x'), axis=0)]
    ppermute x0 -> x28, waiting for transfers between devices: none -> 60.7 us  [shift(): return lax.ppermute(x, axis, [(i, (i + by) % 4) for i in range(4)])]
    ppermute x0 -> x28, starting transfers between devices: none -> 35.2 us  [shift(): return lax.ppermute(x, axis, [(i, (i + by) % 4) for i in range(4)])]
    all_gather x3 -> x0, blocking collectives: 34.1 us -> none  [the longest x2 22.2 us: sum_over_rows(): mine = lax.all_gather(piece, 'y', axis=0).reshape(n // 2, width)]
    all_to_all x2 -> x0, blocking collectives: 30.2 us -> none  [sum_over_rows(): got = lax.all_to_all(pieces, 'y', 0, 0).astype(jnp.float32)]
    unnamed x12 -> x91, local copies, waits for them, and re-layouts: 1.5 us -> 24 us
    dot_general x3 -> x18, matrix products: 25.7 us -> 9.34 us  [f32_dot(): lax.dot_general(left, right, (dims, ((), ())), preferred_element_type=jnp...]
    pallas_call x0 -> x2, Pallas kernels: none -> 15.2 us  [apply(): pl.pallas_call(lambda *refs: apply_kernel(down, *refs), out_shape=out_sha...]
  transfers between devices with their start and end apart: 8 -> 36, of which waited for: 7 -> 22; matrix products, arithmetic and copies ran while one was open for 3% -> 17% of each run, Pallas kernels for 0% -> 0%
where the time goes in v2:
time: 251 us; the launch traced here: 250 us
  waiting for transfers between devices  69.9 us (28%)
  starting transfers between devices  52.6 us (21%)
  other arithmetic  30.9 us (12%)
  local copies, waits for them, and re-layouts  29.7 us (12%)
  blocking collectives  24.9 us (10%)
  between operations  16.8 us (7%)
  Pallas kernels  15.2 us (6%)
  matrix products  9.93 us (4%)
    ppermute x28, waiting for transfers between devices, shift(): return lax.ppermute(x, axis, [(i, (i + by) % 4) for i in range(4)])  60.7 us
    ppermute x28, starting transfers between devices, shift(): return lax.ppermute(x, axis, [(i, (i + by) % 4) for i in range(4)])  35.2 us
    unnamed x91, local copies, waits for them, and re-layouts  24 us
    reduce_sum x10, other arithmetic, per_device(): square = square + jnp.sum(block_rows.astype(jnp.float32) ** 2)  17.9 us
    pallas_call x2, Pallas kernels, apply(): pl.pallas_call(lambda *refs: apply_kernel(down, *refs), out_shape=out_sha...  15.2 us
    all_to_all x1, blocking collectives, per_device(): got = lax.all_to_all(half, ('y', 'x'), 0, 0).reshape(4, 4, 64, 128)  13.6 us
    ppermute x7, starting transfers between devices, other_core(): return lax.ppermute(x, 'core', [(0, 1), (1, 0)])  13.3 us
    all_gather x1, blocking collectives, per_device(): along_x = lax.all_gather(subspace, 'x', axis=0)  11.3 us
  transfers between devices with their start and end apart: 36, of which 22 were waited for; matrix products, arithmetic and copies ran while one was open for 17% of the time, Pallas kernels for 0%

profile of v2, /device:TPU:1, one launch (start us, length us, event | category | flops | bytes accessed | tf_op | source)
XLA Modules:
  0.0 250.0 jit_solution(2186435355713658658)
XLA Ops:
  0.7 2.1 collective-permute-start
  4.1 1.8 collective-permute-start.2
  5.9 2.1 collective-permute-start.3
  8.0 2.0 multiply_reduce_fusion.15
  11.4 5.4 %collective-permute-done.refs_3_ = bf16[768,384]{1,0:T(8,128)(2,1)S(1)} collective-permute-done((bf16[768,384]{1,0:T(8,128)(2,1)}, bf16[768,384]{1,0:T(8,128)(2,1)S(1)}, u32[]{:S(2)}, u32[]{:S(2)}) %collective-permute-start) | collective-permute-done | bytes 589856 | tf_op jit(solution)/shard_map/ppermute | solution.py:15
  16.9 3.8 %collective-permute-done.2.refs_5_ = bf16[768,384]{1,0:T(8,128)(2,1)S(1)} collective-permute-done((bf16[768,384]{1,0:T(8,128)(2,1)}, bf16[768,384]{1,0:T(8,128)(2,1)S(1)}, u32[]{:S(2)}, u32[]{:S(2)}) %collective-permute-start.2) | collective-permute-done | bytes 589856 | tf_op jit(solution)/shard_map/ppermute | solution.py:15
  26.9 2.3 collective-permute-start.7
  34.7 1.6 slice_dynamic-update-slice_fusion.14
  36.4 1.7 slice_dynamic-update-slice_fusion.13
  38.1 1.6 slice_dynamic-update-slice_fusion.12
  40.7 5.5 %collective-permute-done.6.refs_9_ = bf16[1152,384]{1,0:T(8,128)(2,1)S(1)} collective-permute-done((bf16[1152,384]{1,0:T(8,128)(2,1)}, bf16[1152,384]{1,0:T(8,128)(2,1)S(1)}, u32[]{:S(2)}, u32[]{:S(2)}) %collective-permute-start.6) | collective-permute-done | bytes 884768 | tf_op jit(solution)/shard_map/ppermute | solution.py:15
  46.3 3.0 %collective-permute-done.5.refs_8_ = bf16[1152,384]{1,0:T(8,128)(2,1)} collective-permute-done((bf16[1152,384]{1,0:T(8,128)(2,1)}, bf16[1152,384]{1,0:T(8,128)(2,1)}, u32[]{:S(2)}, u32[]{:S(2)}) %collective-permute-start.5) | collective-permute-done | bytes 884768 | tf_op jit(solution)/shard_map/ppermute | solution.py:15
  49.3 3.1 %collective-permute-done.4.refs_7_ = bf16[1152,384]{1,0:T(8,128)(2,1)S(1)} collective-permute-done((bf16[1152,384]{1,0:T(8,128)(2,1)}, bf16[1152,384]{1,0:T(8,128)(2,1)S(1)}, u32[]{:S(2)}, u32[]{:S(2)}) %collective-permute-start.4) | collective-permute-done | bytes 884768 | tf_op jit(solution)/shard_map/ppermute | solution.py:15
  58.4 2.7 %collective-permute-start.11 = (bf16[768,384]{1,0:T(8,128)(2,1)S(1)}, bf16[768,384]{1,0:T(8,128)(2,1)S(1)}, u32[]{:S(2)}, u32[]{:S(2)}) collective-permute-start(bf16[768,384]{1,0:T(8,128)(2,1)S(1)} %pad_maximum_fusion.6.refs_11_), channel_id=1, source_target_pairs={{0,12},{4,0},{8,4},{12,8},{1,13},{5,1},{9,5},{13,9},{2,14},{6,2},{... | collective-permute-start | bytes 1769480 | tf_op jit(solution)/shard_map/ppermute | solution.py:15
  61.2 2.7 %collective-permute-start.9 = (bf16[768,384]{1,0:T(8,128)(2,1)S(1)}, bf16[768,384]{1,0:T(8,128)(2,1)S(1)}, u32[]{:S(2)}, u32[]{:S(2)}) collective-permute-start(bf16[768,384]{1,0:T(8,128)(2,1)S(1)} %pad_maximum_fusion.7.refs_12_), channel_id=1, source_target_pairs={{0,3},{1,0},{2,1},{3,2},{4,7},{5,4},{6,5},{7,6},{8,11},{9,8},{10,9... | collective-permute-start | bytes 1769480 | tf_op jit(solution)/shard_map/ppermute | solution.py:15
  68.5 2.3 collective-permute-done.10.refs_15_
  70.8 2.3 collective-permute-done.8.refs_13_
  74.5 2.7 %collective-permute-start.13 = (bf16[192,384]{1,0:T(8,128)(2,1)S(1)}, bf16[192,384]{1,0:T(8,128)(2,1)S(1)}, u32[]{:S(2)}, u32[]{:S(2)}) collective-permute-start(bf16[192,384]{1,0:T(8,128)(2,1)S(1)} %slice.202), channel_id=1, source_target_pairs={{0,3},{1,0},{2,1},{3,2},{4,7},{5,4},{6,5},{7,6},{8,11},{9,8},{10,9... | collective-permute-start | bytes 442376 | tf_op jit(solution)/shard_map/ppermute | solution.py:15
  77.2 2.7 %collective-permute-start.15 = (bf16[192,384]{1,0:T(8,128)(2,1)S(1)}, bf16[192,384]{1,0:T(8,128)(2,1)S(1)}, u32[]{:S(2)}, u32[]{:S(2)}) collective-permute-start(bf16[192,384]{1,0:T(8,128)(2,1)S(1)} %slice.204), channel_id=1, source_target_pairs={{0,12},{4,0},{8,4},{12,8},{1,13},{5,1},{9,5},{13,9},{2,14},{6,2},{... | collective-permute-start | bytes 442376 | tf_op jit(solution)/shard_map/ppermute | solution.py:15
  84.7 6.5 %collective-permute-start.17 = (f32[64,6144]{1,0:T(8,128)}, f32[64,6144]{1,0:T(8,128)}, u32[]{:S(2)}, u32[]{:S(2)}) collective-permute-start(f32[64,6144]{1,0:T(8,128)} %get-tuple-element.54), channel_id=1, source_target_pairs={{0,16},{16,0},{1,17},{17,1},{2,18},{18,2},{3,19},{19,3},{4,20},{20... | collective-permute-start | bytes 4718600 | tf_op jit(solution)/shard_map/ppermute | solution.py:19
  93.4 2.0 multiply_reduce_fusion.9
  96.7 2.0 multiply_reduce_fusion.7
  100.0 2.0 multiply_reduce_fusion.6
  102.6 1.9 multiply_reduce_fusion.5
  105.1 2.2 multiply_reduce_fusion.3
  108.6 2.2 multiply_reduce_fusion.1
  112.0 2.0 multiply_reduce_fusion
  120.8 2.1 fusion.33
  127.4 3.4 %collective-permute-done.18 = bf16[16,6272]{1,0:T(8,128)(2,1)S(1)} collective-permute-done((bf16[16,6272]{1,0:T(8,128)(2,1)S(1)}, bf16[16,6272]{1,0:T(8,128)(2,1)S(1)}, u32[]{:S(2)}, u32[]{:S(2)}) %collective-permute-start.18) | collective-permute-done | bytes 200736 | tf_op jit(solution)/shard_map/ppermute | solution.py:15
  130.8 5.4 %collective-permute-done.20 = bf16[16,6272]{1,0:T(8,128)(2,1)S(1)} collective-permute-done((bf16[16,6272]{1,0:T(8,128)(2,1)S(1)}, bf16[16,6272]{1,0:T(8,128)(2,1)S(1)}, u32[]{:S(2)}, u32[]{:S(2)}) %collective-permute-start.20) | collective-permute-done | bytes 200736 | tf_op jit(solution)/shard_map/ppermute | solution.py:15
  144.5 5.7 %collective-permute-done.23 = bf16[16,6144]{1,0:T(8,128)(2,1)} collective-permute-done((bf16[16,6144]{1,0:T(8,128)(2,1)}, bf16[16,6144]{1,0:T(8,128)(2,1)}, u32[]{:S(2)}, u32[]{:S(2)}) %collective-permute-start.23) | collective-permute-done | bytes 196640 | tf_op jit(solution)/shard_map/ppermute | solution.py:15
  153.5 1.6 constant_dynamic-update-slice_fusion.6
  155.1 1.6 constant_dynamic-update-slice_fusion.5
  162.3 8.5 %shard_map.41 = (f32[64,6144]{1,0:T(8,128)S(1)}, f32[64,6144]{1,0:T(8,128)S(1)}) custom-call(f32[1,1]{1,0:T(1,128)} %bitcast.2.refs_0_, bf16[128,6144]{1,0:T(8,128)(2,1)S(1)} %copy-done.23, bf16[768,384]{1,0:T(8,128)(2,1)S(1)} %copy-done.18, bf16[768,384]{1,0:T(8,128)(2,1)S(1)} %copy-done.2, bf16[768,384]{1,0:T(8,128)(2,1)S(1)} %copy-done.4, ...), custom_call_target="tpu_custom_call" | custom-call | flops 2415919104 | bytes 9437184 | tf_op jit(solution)/shard_map/pallas_call | solution.py:121
  171.0 3.4 %collective-permute-done.25 = f32[64,6144]{1,0:T(8,128)S(1)} collective-permute-done((f32[64,6144]{1,0:T(8,128)S(1)}, f32[64,6144]{1,0:T(8,128)S(1)}, u32[]{:S(2)}, u32[]{:S(2)}) %collective-permute-start.25) | collective-permute-done | bytes 1572896 | tf_op jit(solution)/shard_map/ppermute | solution.py:19
  174.7 2.7 %collective-permute-start.27 = (bf16[16,6144]{1,0:T(8,128)(2,1)S(1)}, bf16[16,6144]{1,0:T(8,128)(2,1)S(1)}, u32[]{:S(2)}, u32[]{:S(2)}) collective-permute-start(bf16[16,6144]{1,0:T(8,128)(2,1)S(1)} %get-tuple-element.51), channel_id=1, source_target_pairs={{0,96},{32,0},{64,32},{96,64},{1,97},{33,1},{65,33},{97,65},{2,98}... | collective-permute-start | bytes 589832 | tf_op jit(solution)/shard_map/ppermute | solution.py:15
  177.5 8.9 %collective-permute-done.26 = bf16[16,6144]{1,0:T(8,128)(2,1)S(1)} collective-permute-done((bf16[16,6144]{1,0:T(8,128)(2,1)S(1)}, bf16[16,6144]{1,0:T(8,128)(2,1)S(1)}, u32[]{:S(2)}, u32[]{:S(2)}) %collective-permute-start.26) | collective-permute-done | bytes 196640 | tf_op jit(solution)/shard_map/ppermute | solution.py:15
  186.5 2.4 collective-permute-start.29
  189.6 2.7 %collective-permute-done.29 = bf16[16,6144]{1,0:T(8,128)(2,1)S(1)} collective-permute-done((bf16[16,6144]{1,0:T(8,128)(2,1)S(1)}, bf16[16,6144]{1,0:T(8,128)(2,1)S(1)}, u32[]{:S(2)}, u32[]{:S(2)}) %collective-permute-start.29) | collective-permute-done | bytes 196640 | tf_op jit(solution)/shard_map/ppermute | solution.py:15
  192.4 3.0 %collective-permute-done.30 = bf16[16,6144]{1,0:T(8,128)(2,1)S(1)} collective-permute-done((bf16[16,6144]{1,0:T(8,128)(2,1)S(1)}, bf16[16,6144]{1,0:T(8,128)(2,1)S(1)}, u32[]{:S(2)}, u32[]{:S(2)}) %collective-permute-start.30) | collective-permute-done | bytes 196640 | tf_op jit(solution)/shard_map/ppermute | solution.py:15
  195.4 5.5 %collective-permute-done.31 = bf16[16,6144]{1,0:T(8,128)(2,1)S(1)} collective-permute-done((bf16[16,6144]{1,0:T(8,128)(2,1)S(1)}, bf16[16,6144]{1,0:T(8,128)(2,1)S(1)}, u32[]{:S(2)}, u32[]{:S(2)}) %collective-permute-start.31) | collective-permute-done | bytes 196640 | tf_op jit(solution)/shard_map/ppermute | solution.py:15
  201.9 1.8 collective-permute-done.32
  203.8 6.7 %shard_map.42 = bf16[128,768]{1,0:T(8,128)(2,1)S(1)} custom-call(f32[1,1]{1,0:T(1,128)} %bitcast.2.refs_0_, bf16[128,6144]{1,0:T(8,128)(2,1)S(1)} %constant_dynamic-update-slice_fusion.9.refs_1_, bf16[768,384]{1,0:T(8,128)(2,1)S(1)} %copy-done.18, bf16[768,384]{1,0:T(8,128)(2,1)S(1)} %copy-done.2, bf16[768,384]{1,0:T(8,128)(2,1)S(1)} %copy-done.4, ...), custom_call_target="tpu_custom_call" | custom-call | flops 1207959552 | bytes 9437184 | tf_op jit(solution)/shard_map/pallas_call | solution.py:121
  212.0 4.2 %all-to-all-start = ((bf16[4,768,128]{2,1,0:T(8,128)(2,1)}), bf16[4,768,128]{2,1,0:T(8,128)(2,1)S(1)}, u32[]{:S(2)}, u32[]{:S(2)}) async-start(bf16[4,768,128]{2,1,0:T(8,128)(2,1)} %broadcast_in_dim.34), calls=%async_computation | async-start | bytes 1572864 | tf_op jit(solution)/shard_map/all_to_all | solution.py:167
  216.2 11.3 %all-gather = bf16[3072,128]{1,0:T(8,128)(2,1)S(1)} all-gather(bf16[768,128]{1,0:T(8,128)(2,1)S(1)} %convolution_convert_fusion), channel_id=2, replica_groups=mesh['y'=4,'core'=2,'z'=4,'x'=4] {'x'}, dimensions={0}, use_global_device_ids=true | all-gather | bytes 983040 | tf_op jit(solution)/shard_map/all_gather | solution.py:166
  228.6 2.5 %collective-permute-start.33 = (f32[16,64,128]{2,1,0:T(8,128)S(1)}, f32[16,64,128]{2,1,0:T(8,128)S(1)}, u32[]{:S(2)}, u32[]{:S(2)}) collective-permute-start(f32[16,64,128]{2,1,0:T(8,128)S(1)} %dynamic-slice_bitcast_fusion), channel_id=1, source_target_pairs={{0,16},{16,0},{1,17},{17,1},{2,18},{18,2},{3,19},{19,3},{4,20},{20... | collective-permute-start | bytes 1572872 | tf_op jit(solution)/shard_map/ppermute | solution.py:19
  232.8 13.6 %all_to_all.10 = f32[16,64,128]{2,1,0:T(8,128)S(1)} all-to-all(f32[16,64,128]{2,1,0:T(8,128)S(1)} %bitcast_add_fusion), channel_id=1, replica_groups=mesh['y'=4,'core'=2,'z'=4,'x'=4] {'y','x'}, dimensions={0} | all-to-all | bytes 1048576 | tf_op jit(solution)/shard_map/all_to_all | solution.py:172
  246.4 1.9 collective-permute-start.34
  (205 shorter events, 62.4 us)
Async XLA Ops:
  0.6 9.4 %copy-start = (bf16[768,128]{1,0:T(8,128)(2,1)S(1)}, bf16[768,128]{1,0:T(8,128)(2,1)}, u32[]{:S(2)}) copy-start(bf16[768,128]{1,0:T(8,128)(2,1)} %param.3) | copy-start | bytes 589828
  0.6 9.8 %copy-start.17 = (bf16[768,384]{1,0:T(8,128)(2,1)S(1)}, bf16[768,384]{1,0:T(8,128)(2,1)}, u32[]{:S(2)}) copy-start(bf16[768,384]{1,0:T(8,128)(2,1)} %refs_2_.3) | copy-start | bytes 1769476
  0.7 16.2 %collective-permute-start = (bf16[768,384]{1,0:T(8,128)(2,1)}, bf16[768,384]{1,0:T(8,128)(2,1)S(1)}, u32[]{:S(2)}, u32[]{:S(2)}) collective-permute-start(bf16[768,384]{1,0:T(8,128)(2,1)} %refs_2_.3), channel_id=1, source_target_pairs={{0,1},{1,2},{2,3},{3,0},{4,5},{5,6},{6,7},{7,4},{8,9},{9,10},{10,1... | collective-permute-start | bytes 1769480 | tf_op jit(solution)/shard_map/ppermute | solution.py:15
  2.8 14.1 %collective-permute-start.1 = (bf16[768,384]{1,0:T(8,128)(2,1)}, bf16[768,384]{1,0:T(8,128)(2,1)S(1)}, u32[]{:S(2)}, u32[]{:S(2)}) collective-permute-start(bf16[768,384]{1,0:T(8,128)(2,1)} %refs_2_.3), channel_id=1, source_target_pairs={{0,3},{1,0},{2,1},{3,2},{4,7},{5,4},{6,5},{7,6},{8,11},{9,8},{10,9... | collective-permute-start | bytes 1769480 | tf_op jit(solution)/shard_map/ppermute | solution.py:15
  4.1 16.5 %collective-permute-start.2 = (bf16[768,384]{1,0:T(8,128)(2,1)}, bf16[768,384]{1,0:T(8,128)(2,1)S(1)}, u32[]{:S(2)}, u32[]{:S(2)}) collective-permute-start(bf16[768,384]{1,0:T(8,128)(2,1)} %refs_2_.3), channel_id=1, source_target_pairs={{0,4},{4,8},{8,12},{12,0},{1,5},{5,9},{9,13},{13,1},{2,6},{6,10},{... | collective-permute-start | bytes 1769480 | tf_op jit(solution)/shard_map/ppermute | solution.py:15
  5.9 14.8 %collective-permute-start.3 = (bf16[768,384]{1,0:T(8,128)(2,1)}, bf16[768,384]{1,0:T(8,128)(2,1)S(1)}, u32[]{:S(2)}, u32[]{:S(2)}) collective-permute-start(bf16[768,384]{1,0:T(8,128)(2,1)} %refs_2_.3), channel_id=1, source_target_pairs={{0,12},{4,0},{8,4},{12,8},{1,13},{5,1},{9,5},{13,9},{2,14},{6,2},{... | collective-permute-start | bytes 1769480 | tf_op jit(solution)/shard_map/ppermute | solution.py:15
  10.4 12.1 %copy-start.24 = (bf16[128,768]{1,0:T(8,128)(2,1)}, bf16[128,768]{1,0:T(8,128)(2,1)S(1)}, u32[]{:S(2)}) copy-start(bf16[128,768]{1,0:T(8,128)(2,1)S(1)} %convolution_convert_fusion.1) | copy-start | bytes 589828
  16.9 9.0 %copy-start.1 = (bf16[768,384]{1,0:T(8,128)(2,1)}, bf16[768,384]{1,0:T(8,128)(2,1)S(1)}, u32[]{:S(2)}) copy-start(bf16[768,384]{1,0:T(8,128)(2,1)S(1)} %collective-permute-done.refs_3_) | copy-start | bytes 1769476
  16.9 7.6 %copy-start.3 = (bf16[768,384]{1,0:T(8,128)(2,1)}, bf16[768,384]{1,0:T(8,128)(2,1)S(1)}, u32[]{:S(2)}) copy-start(bf16[768,384]{1,0:T(8,128)(2,1)S(1)} %collective-permute-done.1.refs_4_) | copy-start | bytes 1769476
  25.5 20.7 %collective-permute-start.6 = (bf16[1152,384]{1,0:T(8,128)(2,1)}, bf16[1152,384]{1,0:T(8,128)(2,1)S(1)}, u32[]{:S(2)}, u32[]{:S(2)}) collective-permute-start(bf16[1152,384]{1,0:T(8,128)(2,1)} %pad_maximum_fusion.2), channel_id=1, source_target_pairs={{0,4},{4,8},{8,12},{12,0},{1,5},{5,9},{9,13},{13,1},{2,6},{6,10},{... | collective-permute-start | bytes 2654216 | tf_op jit(solution)/shard_map/ppermute | solution.py:15
  26.9 19.4 %collective-permute-start.7 = (bf16[1152,384]{1,0:T(8,128)(2,1)}, bf16[1152,384]{1,0:T(8,128)(2,1)}, u32[]{:S(2)}, u32[]{:S(2)}) collective-permute-start(bf16[1152,384]{1,0:T(8,128)(2,1)} %pad_maximum_fusion.3), channel_id=1, source_target_pairs={{0,12},{4,0},{8,4},{12,8},{1,13},{5,1},{9,5},{13,9},{2,14},{6,2},{... | collective-permute-start | bytes 2654216 | tf_op jit(solution)/shard_map/ppermute | solution.py:15
  30.3 9.4 %copy-start.25 = (bf16[128,768]{1,0:T(8,128)(2,1)S(1)}, bf16[128,768]{1,0:T(8,128)(2,1)}, u32[]{:S(2)}) copy-start(bf16[128,768]{1,0:T(8,128)(2,1)} %copy-done.24) | copy-start | bytes 589828
  30.3 19.0 %collective-permute-start.5 = (bf16[1152,384]{1,0:T(8,128)(2,1)}, bf16[1152,384]{1,0:T(8,128)(2,1)}, u32[]{:S(2)}, u32[]{:S(2)}) collective-permute-start(bf16[1152,384]{1,0:T(8,128)(2,1)} %pad_maximum_fusion.1), channel_id=1, source_target_pairs={{0,3},{1,0},{2,1},{3,2},{4,7},{5,4},{6,5},{7,6},{8,11},{9,8},{10,9... | collective-permute-start | bytes 2654216 | tf_op jit(solution)/shard_map/ppermute | solution.py:15
  32.6 19.9 %collective-permute-start.4 = (bf16[1152,384]{1,0:T(8,128)(2,1)}, bf16[1152,384]{1,0:T(8,128)(2,1)S(1)}, u32[]{:S(2)}, u32[]{:S(2)}) collective-permute-start(bf16[1152,384]{1,0:T(8,128)(2,1)} %pad_maximum_fusion), channel_id=1, source_target_pairs={{0,1},{1,2},{2,3},{3,0},{4,5},{5,6},{6,7},{7,4},{8,9},{9,10},{10,1... | collective-permute-start | bytes 2654216 | tf_op jit(solution)/shard_map/ppermute | solution.py:15
  55.5 12.0 %copy-start.26 = (bf16[384,384]{1,0:T(8,128)(2,1)}, bf16[384,384]{1,0:T(8,128)(2,1)S(1)}, u32[]{:S(2)}) copy-start(bf16[384,384]{1,0:T(8,128)(2,1)S(1)} %slice.199) | copy-start | bytes 884740
  58.0 9.6 %copy-start.28 = (bf16[384,384]{1,0:T(8,128)(2,1)}, bf16[384,384]{1,0:T(8,128)(2,1)S(1)}, u32[]{:S(2)}) copy-start(bf16[384,384]{1,0:T(8,128)(2,1)S(1)} %slice.200) | copy-start | bytes 884740
  58.3 9.2 %copy-start.19 = (bf16[768,384]{1,0:T(8,128)(2,1)}, bf16[768,384]{1,0:T(8,128)(2,1)S(1)}, u32[]{:S(2)}) copy-start(bf16[768,384]{1,0:T(8,128)(2,1)S(1)} %pad_maximum_fusion.6.refs_11_) | copy-start | bytes 1769476
  58.3 12.5 %collective-permute-start.10 = (bf16[768,384]{1,0:T(8,128)(2,1)S(1)}, bf16[768,384]{1,0:T(8,128)(2,1)S(1)}, u32[]{:S(2)}, u32[]{:S(2)}) collective-permute-start(bf16[768,384]{1,0:T(8,128)(2,1)S(1)} %pad_maximum_fusion.6.refs_11_), channel_id=1, source_target_pairs={{0,4},{4,8},{8,12},{12,0},{1,5},{5,9},{9,13},{13,1},{2,6},{6,10},{... | collective-permute-start | bytes 1769480 | tf_op jit(solution)/shard_map/ppermute | solution.py:15
  58.4 12.4 %collective-permute-start.11 = (bf16[768,384]{1,0:T(8,128)(2,1)S(1)}, bf16[768,384]{1,0:T(8,128)(2,1)S(1)}, u32[]{:S(2)}, u32[]{:S(2)}) collective-permute-start(bf16[768,384]{1,0:T(8,128)(2,1)S(1)} %pad_maximum_fusion.6.refs_11_), channel_id=1, source_target_pairs={{0,12},{4,0},{8,4},{12,8},{1,13},{5,1},{9,5},{13,9},{2,14},{6,2},{... | collective-permute-start | bytes 1769480 | tf_op jit(solution)/shard_map/ppermute | solution.py:15
  61.2 11.9 %collective-permute-start.8 = (bf16[768,384]{1,0:T(8,128)(2,1)S(1)}, bf16[768,384]{1,0:T(8,128)(2,1)S(1)}, u32[]{:S(2)}, u32[]{:S(2)}) collective-permute-start(bf16[768,384]{1,0:T(8,128)(2,1)S(1)} %pad_maximum_fusion.7.refs_12_), channel_id=1, source_target_pairs={{0,1},{1,2},{2,3},{3,0},{4,5},{5,6},{6,7},{7,4},{8,9},{9,10},{10,1... | collective-permute-start | bytes 1769480 | tf_op jit(solution)/shard_map/ppermute | solution.py:15
  61.2 11.8 %collective-permute-start.9 = (bf16[768,384]{1,0:T(8,128)(2,1)S(1)}, bf16[768,384]{1,0:T(8,128)(2,1)S(1)}, u32[]{:S(2)}, u32[]{:S(2)}) collective-permute-start(bf16[768,384]{1,0:T(8,128)(2,1)S(1)} %pad_maximum_fusion.7.refs_12_), channel_id=1, source_target_pairs={{0,3},{1,0},{2,1},{3,2},{4,7},{5,4},{6,5},{7,6},{8,11},{9,8},{10,9... | collective-permute-start | bytes 1769480 | tf_op jit(solution)/shard_map/ppermute | solution.py:15
  74.4 8.3 %collective-permute-start.12 = (bf16[192,384]{1,0:T(8,128)(2,1)S(1)}, bf16[192,384]{1,0:T(8,128)(2,1)S(1)}, u32[]{:S(2)}, u32[]{:S(2)}) collective-permute-start(bf16[192,384]{1,0:T(8,128)(2,1)S(1)} %slice.201), channel_id=1, source_target_pairs={{0,1},{1,2},{2,3},{3,0},{4,5},{5,6},{6,7},{7,4},{8,9},{9,10},{10,1... | collective-permute-start | bytes 442376 | tf_op jit(solution)/shard_map/ppermute | solution.py:15
  74.5 8.2 %collective-permute-start.13 = (bf16[192,384]{1,0:T(8,128)(2,1)S(1)}, bf16[192,384]{1,0:T(8,128)(2,1)S(1)}, u32[]{:S(2)}, u32[]{:S(2)}) collective-permute-start(bf16[192,384]{1,0:T(8,128)(2,1)S(1)} %slice.202), channel_id=1, source_target_pairs={{0,3},{1,0},{2,1},{3,2},{4,7},{5,4},{6,5},{7,6},{8,11},{9,8},{10,9... | collective-permute-start | bytes 442376 | tf_op jit(solution)/shard_map/ppermute | solution.py:15
  77.2 5.6 %collective-permute-start.14 = (bf16[192,384]{1,0:T(8,128)(2,1)S(1)}, bf16[192,384]{1,0:T(8,128)(2,1)S(1)}, u32[]{:S(2)}, u32[]{:S(2)}) collective-permute-start(bf16[192,384]{1,0:T(8,128)(2,1)S(1)} %slice.203), channel_id=1, source_target_pairs={{0,4},{4,8},{8,12},{12,0},{1,5},{5,9},{9,13},{13,1},{2,6},{6,10},{... | collective-permute-start | bytes 442376 | tf_op jit(solution)/shard_map/ppermute | solution.py:15
  77.2 5.6 %collective-permute-start.15 = (bf16[192,384]{1,0:T(8,128)(2,1)S(1)}, bf16[192,384]{1,0:T(8,128)(2,1)S(1)}, u32[]{:S(2)}, u32[]{:S(2)}) collective-permute-start(bf16[192,384]{1,0:T(8,128)(2,1)S(1)} %slice.204), channel_id=1, source_target_pairs={{0,12},{4,0},{8,4},{12,8},{1,13},{5,1},{9,5},{13,9},{2,14},{6,2},{... | collective-permute-start | bytes 442376 | tf_op jit(solution)/shard_map/ppermute | solution.py:15
  84.7 36.1 %collective-permute-start.17 = (f32[64,6144]{1,0:T(8,128)}, f32[64,6144]{1,0:T(8,128)}, u32[]{:S(2)}, u32[]{:S(2)}) collective-permute-start(f32[64,6144]{1,0:T(8,128)} %get-tuple-element.54), channel_id=1, source_target_pairs={{0,16},{16,0},{1,17},{17,1},{2,18},{18,2},{3,19},{19,3},{4,20},{20... | collective-permute-start | bytes 4718600 | tf_op jit(solution)/shard_map/ppermute | solution.py:19
  92.1 10.5 %copy-start.27 = (bf16[384,384]{1,0:T(8,128)(2,1)S(1)}, bf16[384,384]{1,0:T(8,128)(2,1)}, u32[]{:S(2)}) copy-start(bf16[384,384]{1,0:T(8,128)(2,1)} %copy-done.26) | copy-start | bytes 884740
  114.6 1.2 collective-permute-start.16
  122.9 7.9 %collective-permute-start.18 = (bf16[16,6272]{1,0:T(8,128)(2,1)S(1)}, bf16[16,6272]{1,0:T(8,128)(2,1)S(1)}, u32[]{:S(2)}, u32[]{:S(2)}) collective-permute-start(bf16[16,6272]{1,0:T(8,128)(2,1)S(1)} %get-tuple-element.48), channel_id=1, source_target_pairs={{0,32},{32,64},{64,96},{96,0},{1,33},{33,65},{65,97},{97,1},{2,34}... | collective-permute-start | bytes 602120 | tf_op jit(solution)/shard_map/ppermute | solution.py:15
  124.3 6.5 %collective-permute-start.19 = (bf16[16,6272]{1,0:T(8,128)(2,1)S(1)}, bf16[16,6272]{1,0:T(8,128)(2,1)S(1)}, u32[]{:S(2)}, u32[]{:S(2)}) collective-permute-start(bf16[16,6272]{1,0:T(8,128)(2,1)S(1)} %get-tuple-element.47), channel_id=1, source_target_pairs={{0,96},{32,0},{64,32},{96,64},{1,97},{33,1},{65,33},{97,65},{2,98}... | collective-permute-start | bytes 602120 | tf_op jit(solution)/shard_map/ppermute | solution.py:15
  125.8 10.4 %collective-permute-start.20 = (bf16[16,6272]{1,0:T(8,128)(2,1)S(1)}, bf16[16,6272]{1,0:T(8,128)(2,1)S(1)}, u32[]{:S(2)}, u32[]{:S(2)}) collective-permute-start(bf16[16,6272]{1,0:T(8,128)(2,1)S(1)} %get-tuple-element.46), channel_id=1, source_target_pairs={{0,64},{32,96},{64,0},{96,32},{1,65},{33,97},{65,1},{97,33},{2,66}... | collective-permute-start | bytes 602120 | tf_op jit(solution)/shard_map/ppermute | solution.py:15
  137.0 6.9 %collective-permute-start.21 = (bf16[16,6144]{1,0:T(8,128)(2,1)}, bf16[16,6144]{1,0:T(8,128)(2,1)S(1)}, u32[]{:S(2)}, u32[]{:S(2)}) collective-permute-start(bf16[16,6144]{1,0:T(8,128)(2,1)} %get-tuple-element.43), channel_id=1, source_target_pairs={{0,96},{32,0},{64,32},{96,64},{1,97},{33,1},{65,33},{97,65},{2,98}... | collective-permute-start | bytes 589832 | tf_op jit(solution)/shard_map/ppermute | solution.py:15
  138.0 6.4 %collective-permute-start.22 = (bf16[16,6144]{1,0:T(8,128)(2,1)}, bf16[16,6144]{1,0:T(8,128)(2,1)}, u32[]{:S(2)}, u32[]{:S(2)}) collective-permute-start(bf16[16,6144]{1,0:T(8,128)(2,1)} %get-tuple-element.43), channel_id=1, source_target_pairs={{0,64},{32,96},{64,0},{96,32},{1,65},{33,97},{65,1},{97,33},{2,66}... | collective-permute-start | bytes 589832 | tf_op jit(solution)/shard_map/ppermute | solution.py:15
  139.4 10.8 %collective-permute-start.23 = (bf16[16,6144]{1,0:T(8,128)(2,1)}, bf16[16,6144]{1,0:T(8,128)(2,1)}, u32[]{:S(2)}, u32[]{:S(2)}) collective-permute-start(bf16[16,6144]{1,0:T(8,128)(2,1)} %get-tuple-element.43), channel_id=1, source_target_pairs={{0,32},{32,64},{64,96},{96,0},{1,33},{33,65},{65,97},{97,1},{2,34}... | collective-permute-start | bytes 589832 | tf_op jit(solution)/shard_map/ppermute | solution.py:15
  150.1 7.6 %copy-start.16 = (bf16[768,384]{1,0:T(8,128)(2,1)S(1)}, bf16[768,384]{1,0:T(8,128)(2,1)}, u32[]{:S(2)}) copy-start(bf16[768,384]{1,0:T(8,128)(2,1)} %copy-done.15) | copy-start | bytes 1769476
  151.5 5.2 %collective-permute-start.24 = (bf16[64,6144]{1,0:T(8,128)(2,1)S(1)}, bf16[64,6144]{1,0:T(8,128)(2,1)S(1)}, u32[]{:S(2)}, u32[]{:S(2)}) collective-permute-start(bf16[64,6144]{1,0:T(8,128)(2,1)S(1)} %pad_maximum_fusion.4), channel_id=1, source_target_pairs={{0,16},{16,0},{1,17},{17,1},{2,18},{18,2},{3,19},{19,3},{4,20},{20... | collective-permute-start | bytes 2359304 | tf_op jit(solution)/shard_map/ppermute | solution.py:19
  170.9 3.5 %collective-permute-start.25 = (f32[64,6144]{1,0:T(8,128)S(1)}, f32[64,6144]{1,0:T(8,128)S(1)}, u32[]{:S(2)}, u32[]{:S(2)}) collective-permute-start(f32[64,6144]{1,0:T(8,128)S(1)} %get-tuple-element.37), channel_id=1, source_target_pairs={{0,16},{16,0},{1,17},{17,1},{2,18},{18,2},{3,19},{19,3},{4,20},{20... | collective-permute-start | bytes 4718600 | tf_op jit(solution)/shard_map/ppermute | solution.py:19
  174.6 11.9 %collective-permute-start.26 = (bf16[16,6144]{1,0:T(8,128)(2,1)S(1)}, bf16[16,6144]{1,0:T(8,128)(2,1)S(1)}, u32[]{:S(2)}, u32[]{:S(2)}) collective-permute-start(bf16[16,6144]{1,0:T(8,128)(2,1)S(1)} %get-tuple-element.49), channel_id=1, source_target_pairs={{0,32},{32,64},{64,96},{96,0},{1,33},{33,65},{65,97},{97,1},{2,34}... | collective-permute-start | bytes 589832 | tf_op jit(solution)/shard_map/ppermute | solution.py:15
  174.7 11.8 %collective-permute-start.27 = (bf16[16,6144]{1,0:T(8,128)(2,1)S(1)}, bf16[16,6144]{1,0:T(8,128)(2,1)S(1)}, u32[]{:S(2)}, u32[]{:S(2)}) collective-permute-start(bf16[16,6144]{1,0:T(8,128)(2,1)S(1)} %get-tuple-element.51), channel_id=1, source_target_pairs={{0,96},{32,0},{64,32},{96,64},{1,97},{33,1},{65,33},{97,65},{2,98}... | collective-permute-start | bytes 589832 | tf_op jit(solution)/shard_map/ppermute | solution.py:15
  177.3 9.1 %collective-permute-start.28 = (bf16[16,6144]{1,0:T(8,128)(2,1)S(1)}, bf16[16,6144]{1,0:T(8,128)(2,1)S(1)}, u32[]{:S(2)}, u32[]{:S(2)}) collective-permute-start(bf16[16,6144]{1,0:T(8,128)(2,1)S(1)} %get-tuple-element.50), channel_id=1, source_target_pairs={{0,64},{32,96},{64,0},{96,32},{1,65},{33,97},{65,1},{97,33},{2,66}... | collective-permute-start | bytes 589832 | tf_op jit(solution)/shard_map/ppermute | solution.py:15
  186.5 5.8 %collective-permute-start.29 = (bf16[16,6144]{1,0:T(8,128)(2,1)S(1)}, bf16[16,6144]{1,0:T(8,128)(2,1)S(1)}, u32[]{:S(2)}, u32[]{:S(2)}) collective-permute-start(bf16[16,6144]{1,0:T(8,128)(2,1)S(1)} %get-tuple-element.39), channel_id=1, source_target_pairs={{0,96},{32,0},{64,32},{96,64},{1,97},{33,1},{65,33},{97,65},{2,98}... | collective-permute-start | bytes 589832 | tf_op jit(solution)/shard_map/ppermute | solution.py:15
  189.0 6.4 %collective-permute-start.30 = (bf16[16,6144]{1,0:T(8,128)(2,1)S(1)}, bf16[16,6144]{1,0:T(8,128)(2,1)S(1)}, u32[]{:S(2)}, u32[]{:S(2)}) collective-permute-start(bf16[16,6144]{1,0:T(8,128)(2,1)S(1)} %get-tuple-element.39), channel_id=1, source_target_pairs={{0,64},{32,96},{64,0},{96,32},{1,65},{33,97},{65,1},{97,33},{2,66}... | collective-permute-start | bytes 589832 | tf_op jit(solution)/shard_map/ppermute | solution.py:15
  189.0 11.9 %collective-permute-start.31 = (bf16[16,6144]{1,0:T(8,128)(2,1)S(1)}, bf16[16,6144]{1,0:T(8,128)(2,1)S(1)}, u32[]{:S(2)}, u32[]{:S(2)}) collective-permute-start(bf16[16,6144]{1,0:T(8,128)(2,1)S(1)} %get-tuple-element.39), channel_id=1, source_target_pairs={{0,32},{32,64},{64,96},{96,0},{1,33},{33,65},{65,97},{97,1},{2,34}... | collective-permute-start | bytes 589832 | tf_op jit(solution)/shard_map/ppermute | solution.py:15
  200.9 2.8 %collective-permute-start.32 = (bf16[64,6144]{1,0:T(8,128)(2,1)S(1)}, bf16[64,6144]{1,0:T(8,128)(2,1)S(1)}, u32[]{:S(2)}, u32[]{:S(2)}) collective-permute-start(bf16[64,6144]{1,0:T(8,128)(2,1)S(1)} %pad_maximum_fusion.5), channel_id=1, source_target_pairs={{0,16},{16,0},{1,17},{17,1},{2,18},{18,2},{3,19},{19,3},{4,20},{20... | collective-permute-start | bytes 2359304 | tf_op jit(solution)/shard_map/ppermute | solution.py:19
  211.0 16.5 %copy-start.31 = (bf16[768,128]{1,0:T(8,128)(2,1)}, bf16[768,128]{1,0:T(8,128)(2,1)S(1)}, u32[]{:S(2)}) copy-start(bf16[768,128]{1,0:T(8,128)(2,1)S(1)} %convolution_convert_fusion) | copy-start | bytes 589828
  212.0 15.9 %all-to-all-start = ((bf16[4,768,128]{2,1,0:T(8,128)(2,1)}), bf16[4,768,128]{2,1,0:T(8,128)(2,1)S(1)}, u32[]{:S(2)}, u32[]{:S(2)}) async-start(bf16[4,768,128]{2,1,0:T(8,128)(2,1)} %broadcast_in_dim.34), calls=%async_computation | async-start | bytes 1572864 | tf_op jit(solution)/shard_map/all_to_all | solution.py:167
  228.6 4.1 %collective-permute-start.33 = (f32[16,64,128]{2,1,0:T(8,128)S(1)}, f32[16,64,128]{2,1,0:T(8,128)S(1)}, u32[]{:S(2)}, u32[]{:S(2)}) collective-permute-start(f32[16,64,128]{2,1,0:T(8,128)S(1)} %dynamic-slice_bitcast_fusion), channel_id=1, source_target_pairs={{0,16},{16,0},{1,17},{17,1},{2,18},{18,2},{3,19},{19,3},{4,20},{20... | collective-permute-start | bytes 1572872 | tf_op jit(solution)/shard_map/ppermute | solution.py:19
  246.4 2.8 %collective-permute-start.34 = (f32[2,64,128]{2,1,0:T(8,128)S(1)}, f32[2,64,128]{2,1,0:T(8,128)S(1)}, u32[]{:S(2)}, u32[]{:S(2)}) collective-permute-start(f32[2,64,128]{2,1,0:T(8,128)S(1)} %dynamic-slice_bitcast_fusion.1), channel_id=1, source_target_pairs={{0,16},{16,0},{1,17},{17,1},{2,18},{18,2},{3,19},{19,3},{4,20},{20... | collective-permute-start | bytes 196616 | tf_op jit(solution)/shard_map/ppermute | solution.py:19
  (24 other events, 87.2 us)

commit v3 on v2

v3 whole, which is shorter than its diff:
```python
import jax
import jax.numpy as jnp
from jax import lax
from jax.experimental import pallas as pl
from jax.experimental.pallas import tpu as pltpu
from jax.sharding import Mesh, PartitionSpec as P

ORDER = 6144
ALL = ("y", "core", "z", "x")
COLS = 384
BLOCKS = 16


def shift(x, axis, by):
    return lax.ppermute(x, axis, [(i, (i + by) % 4) for i in range(4)])


def other_core(x):
    return lax.ppermute(x, "core", [(0, 1), (1, 0)])


def f32_dot(left, right, dims):
    return lax.dot_general(left, right, (dims, ((), ())), preferred_element_type=jnp.float32)


def gather_plane(own):
    half = own.shape[0] // 2
    xp, xm, zp, zm = lax.optimization_barrier(
        (shift(own, "x", 1), shift(own, "x", 3), shift(own, "z", 1), shift(own, "z", 3))
    )
    pp, mm, pm, mp = lax.optimization_barrier(
        (shift(zp, "x", 1), shift(zm, "x", 3), shift(xm, "z", 1), shift(xp, "z", 3))
    )
    a, b, c, d = lax.optimization_barrier(
        (shift(mp, "x", 1), shift(pm, "x", 3), shift(pp, "z", 1), shift(mm, "z", 3))
    )
    far_x, far_z, low, high = lax.optimization_barrier(
        (shift(xp, "x", 1), shift(zp, "z", 1), shift(d[:half], "x", 3), shift(a[half:], "z", 3))
    )
    return [own, xp, xm, zp, zm], [pp, mm, pm, mp], [a, b, c, d], [far_x, far_z, (low, high)]


VMEM = pl.BlockSpec(memory_space=pltpu.VMEM)


def down_kernel(counts, x_ref, *refs):
    total = sum(counts)
    mine_ref, theirs_ref, square_ref = refs[total:]
    square = jnp.zeros((8, 128), jnp.float32)
    at, x = 0, x_ref[...]
    for i, count in enumerate(counts):
        step = x.shape[1] // count
        part = 0.0
        for j in range(count):
            block = refs[at][...]
            at += 1
            part += f32_dot(x[:, j * step : (j + 1) * step], block, ((1,), (0,)))
            wide = block.astype(jnp.float32)
            wide = jnp.sum((wide * wide).reshape(step // 8, 8, COLS), axis=0)
            square += wide[:, :128] + wide[:, 128:256] + wide[:, 256:]
        mine_ref[:, i * COLS : (i + 1) * COLS] = part[:64]
        theirs_ref[:, i * COLS : (i + 1) * COLS] = part[64:]
    square_ref[...] = square


def down_first(x, blocks):
    blocks = [b if isinstance(b, tuple) else (b,) for b in blocks]
    counts = [len(b) for b in blocks]
    flat = [piece for b in blocks for piece in b]
    n = len(blocks) * COLS
    return pl.pallas_call(
        lambda *refs: down_kernel(counts, *refs),
        out_shape=[jax.ShapeDtypeStruct((64, n), jnp.float32)] * 2 + [jax.ShapeDtypeStruct((8, 128), jnp.float32)],
        in_specs=[VMEM] * (1 + len(flat)),
        out_specs=[VMEM] * 3,
        compiler_params=pltpu.CompilerParams(vmem_limit_bytes=16 * 2**20),
        cost_estimate=pl.CostEstimate(
            flops=2 * x.size * n, bytes_accessed=2 * x.shape[1] * n, transcendentals=0
        ),
    )(x, *flat)


def core_sum(mine, theirs):
    return mine + other_core(theirs)


def sum_over_y(half, square=None):
    send = jnp.concatenate([h[16:].astype(jnp.bfloat16) for h in half], 1)
    n = send.shape[1]
    if square is not None:
        high = lax.reduce_precision(square, 8, 7)
        extra = jnp.concatenate([high, square - high]).astype(jnp.bfloat16)
        send = jnp.concatenate([send, jnp.tile(extra, (3, 1))], 1)
    got = lax.optimization_barrier(
        tuple(shift(send[16 * (d - 1) : 16 * d], "y", d) for d in (1, 3, 2))
    )
    total = jnp.concatenate([h[:16] for h in half], 1)
    for piece in got:
        total = total + piece[:, :n].astype(jnp.float32)
    if square is not None:
        for piece in got:
            square = square + piece[:8, n:].astype(jnp.float32) + piece[8:, n:].astype(jnp.float32)
    own = total.astype(jnp.bfloat16)
    up1, up3, up2 = (shift(own, "y", 4 - d) for d in (1, 3, 2))
    mine = [own, up1, up2, up3]
    return mine + [other_core(m) for m in mine], square


def apply_kernel(down, square_ref, *refs):
    t_refs, theta_refs, outs = refs[:8], refs[8 : 9 + BLOCKS], refs[9 + BLOCKS :]
    rows = theta_refs[0].shape[0]
    scale = ORDER / (4.0 * jnp.sum(square_ref[...]))

    def theta(i):
        if i < BLOCKS - 1:
            return theta_refs[i][...]
        return jnp.concatenate([theta_refs[i][...], theta_refs[i + 1][...]])

    total = jnp.zeros((128, rows), jnp.float32)
    for i in range(BLOCKS):
        t = jnp.concatenate([ref[:, i * COLS : (i + 1) * COLS] for ref in t_refs])
        total += f32_dot(t, theta(i), ((1,), (1,)))
    x = (total * scale).astype(jnp.bfloat16)
    if not down:
        outs[0][...] = x
        return
    for i in range(BLOCKS):
        part = f32_dot(x, theta(i), ((1,), (0,)))
        outs[0][:, i * COLS : (i + 1) * COLS] = part[:64]
        outs[1][:, i * COLS : (i + 1) * COLS] = part[64:]


def apply(square, t, blocks, down):
    n, rows = t[0].shape[1], blocks[0].shape[0]
    if down:
        out_shape = [jax.ShapeDtypeStruct((64, n), jnp.float32)] * 2
    else:
        out_shape = [jax.ShapeDtypeStruct((128, rows), jnp.bfloat16)]
    return pl.pallas_call(
        lambda *refs: apply_kernel(down, *refs),
        out_shape=out_shape,
        in_specs=[VMEM] * (1 + len(t) + len(blocks)),
        out_specs=[VMEM] * len(out_shape),
        compiler_params=pltpu.CompilerParams(vmem_limit_bytes=16 * 2**20),
        cost_estimate=pl.CostEstimate(
            flops=(4 if down else 2) * 128 * n * rows, bytes_accessed=2 * n * rows, transcendentals=0
        ),
    )(square, *t, *blocks)


def column_order(y, core):
    place = lax.broadcasted_iota(jnp.int32, (128, 128), 0)
    column = lax.broadcasted_iota(jnp.int32, (128, 128), 1)
    half = (place // 64 + core) % 2
    group = (place // 16 + y) % 4
    return (column == half * 64 + group * 16 + place % 16).astype(jnp.bfloat16)


def per_device(theta, basis):
    core, y = lax.axis_index("core"), lax.axis_index("y")
    order = column_order(y, core)
    x = f32_dot(order, basis, ((1,), (1,))).astype(jnp.bfloat16)

    blocks, half, square = [], [], 0.0
    for step in gather_plane(theta):
        mine, theirs, squares = down_first(x, step)
        half.append(core_sum(mine, theirs))
        square = square + squares
        blocks += step
    blocks = blocks[:-1] + list(blocks[-1])
    t, square = sum_over_y(half, square + other_core(square))
    t, _ = sum_over_y([core_sum(*apply(square, t, blocks, True))])
    (x,) = apply(square, t, blocks, False)
    subspace = f32_dot(x, order, ((0,), (0,))).astype(jnp.bfloat16)

    along_x = lax.all_gather(subspace, "x", axis=0)
    along_z = lax.all_to_all(jnp.broadcast_to(subspace[None], (4, *subspace.shape)), "z", 0, 0)
    part = jnp.einsum("brn,arm->bamn", along_z, along_x, preferred_element_type=jnp.float32)
    part = part.reshape(4, 4, 2, 64, 128).transpose(2, 0, 1, 3, 4).reshape(2, 16, 64, 128)
    keep = lax.dynamic_index_in_dim(part, core, 0, keepdims=False)
    half = keep + other_core(lax.dynamic_index_in_dim(part, 1 - core, 0, keepdims=False))
    got = lax.all_to_all(half, ("y", "x"), 0, 0).reshape(4, 4, 64, 128)
    sums = jnp.sum(got, axis=0).reshape(2, 2, 64, 128)
    keep = lax.dynamic_index_in_dim(sums, core, 0, keepdims=False)
    theirs = other_core(lax.dynamic_index_in_dim(sums, 1 - core, 0, keepdims=False))
    first_half = core == 0
    both = jnp.stack([jnp.where(first_half, keep, theirs), jnp.where(first_half, theirs, keep)])
    gram = both.transpose(0, 2, 1, 3).reshape(128, 256) / ORDER
    return subspace, gram


def solution(mesh):
    fine = Mesh(mesh.devices.reshape(4, 2, 4, 4), ALL)
    spec = P(("y", "core"), ("z", "x"))
    return jax.shard_map(
        per_device,
        mesh=fine,
        in_specs=(spec, spec),
        out_specs=(spec, P(("z", "x"), ("y", "core"))),
        check_vma=False,
    )
```

time: 251 us -> 188 us (0.75)
  other arithmetic: 30.9 us -> 0.82 us
  local copies, waits for them, and re-layouts: 29.7 us -> 3.28 us
  starting transfers between devices: 52.6 us -> 71.8 us
  between operations: 16.8 us -> 1 us
  matrix products: 9.93 us -> 1.36 us
  waiting for transfers between devices: 69.9 us -> 66.1 us
  blocking collectives: 24.9 us -> 27.9 us
    unnamed x91 -> x13, local copies, waits for them, and re-layouts: 24 us -> 1.83 us
    reduce_sum x13 -> x0, other arithmetic: 20.5 us -> none  [the longest x10 17.9 us: per_device(): square = square + jnp.sum(block_rows.astype(jnp.float32) ** 2)]
    ppermute x7 -> x16, starting transfers between devices: 13.3 us -> 32.4 us  [other_core(): return lax.ppermute(x, 'core', [(0, 1), (1, 0)])]
    dot_general x18 -> x2, matrix products: 9.34 us -> 0.76 us  [f32_dot(): lax.dot_general(left, right, (dims, ((), ())), preferred_element_type=jnp...]
    concatenate x9 -> x1, other arithmetic: 5.67 us -> 0.01 us  [sum_over_y(): extra = jnp.concatenate([high, square - high]).astype(jnp.bfloat16)]
    ppermute x28, waiting for transfers between devices: 60.7 us -> 55.5 us  [shift(): return lax.ppermute(x, axis, [(i, (i + by) % 4) for i in range(4)])]
    pallas_call x0 -> x4, Pallas kernels: none -> 3.92 us  [down_first(): pl.pallas_call(lambda *refs: down_kernel(counts, *refs), out_shape=[jax.S...]
    convert_element_type x3 -> x2, other arithmetic: 3.63 us -> 0.2 us  [sum_over_y(): own = total.astype(jnp.bfloat16)]
  transfers between devices with their start and end apart: 36 -> 45, of which waited for: 22 -> 22; matrix products, arithmetic and copies ran while one was open for 17% -> 0% of each run, Pallas kernels for 0% -> 2%
where the time goes in v3:
time: 188 us
  starting transfers between devices  71.8 us (38%)
  waiting for transfers between devices  66.1 us (35%)
  blocking collectives  27.9 us (15%)
  Pallas kernels  15.9 us (8%)
  local copies, waits for them, and re-layouts  3.28 us (2%)
    ppermute x28, waiting for transfers between devices, shift(): return lax.ppermute(x, axis, [(i, (i + by) % 4) for i in range(4)])  55.5 us
    ppermute x28, starting transfers between devices, shift(): return lax.ppermute(x, axis, [(i, (i + by) % 4) for i in range(4)])  35.8 us
    ppermute x16, starting transfers between devices, other_core(): return lax.ppermute(x, 'core', [(0, 1), (1, 0)])  32.4 us
    all_to_all x1, blocking collectives, per_device(): got = lax.all_to_all(half, ('y', 'x'), 0, 0).reshape(4, 4, 64, 128)  15.5 us
    all_gather x1, blocking collectives, per_device(): along_x = lax.all_gather(subspace, 'x', axis=0)  12.4 us
    pallas_call x2, Pallas kernels, apply(): pl.pallas_call(lambda *refs: apply_kernel(down, *refs), out_shape=out_sha...  12 us
    ppermute x16, waiting for transfers between devices, other_core(): return lax.ppermute(x, 'core', [(0, 1), (1, 0)])  10.6 us
    pallas_call x4, Pallas kernels, down_first(): pl.pallas_call(lambda *refs: down_kernel(counts, *refs), out_shape=[jax.S...  3.92 us
  transfers between devices with their start and end apart: 45, of which 22 were waited for; matrix products, arithmetic and copies ran while one was open for 0% of the time, Pallas kernels for 2%

profile of v3, /device:TPU:1, one launch (start us, length us, event | category | flops | bytes accessed | tf_op | source)
XLA Modules:
  0.0 188.1 jit_solution(3455923560983515764)
XLA Ops:
  0.6 2.1 %collective-permute-start = (bf16[768,384]{1,0:T(8,128)(2,1)}, bf16[768,384]{1,0:T(8,128)(2,1)S(1)}, u32[]{:S(2)}, u32[]{:S(2)}) collective-permute-start(bf16[768,384]{1,0:T(8,128)(2,1)} %refs_9_.3), channel_id=1, source_target_pairs={{0,1},{1,2},{2,3},{3,0},{4,5},{5,6},{6,7},{7,4},{8,9},{9,10},{10,1... | collective-permute-start | bytes 1769480 | tf_op jit(solution)/shard_map/ppermute | solution.py:15
  2.8 1.4 collective-permute-start.1
  4.1 1.8 collective-permute-start.2
  5.9 2.1 %collective-permute-start.3 = (bf16[768,384]{1,0:T(8,128)(2,1)}, bf16[768,384]{1,0:T(8,128)(2,1)}, u32[]{:S(2)}, u32[]{:S(2)}) collective-permute-start(bf16[768,384]{1,0:T(8,128)(2,1)} %refs_9_.3), channel_id=1, source_target_pairs={{0,12},{4,0},{8,4},{12,8},{1,13},{5,1},{9,5},{13,9},{2,14},{6,2},{... | collective-permute-start | bytes 1769480 | tf_op jit(solution)/shard_map/ppermute | solution.py:15
  8.0 9.0 %collective-permute-done.refs_2_.refs_10_ = bf16[768,384]{1,0:T(8,128)(2,1)S(1)} collective-permute-done((bf16[768,384]{1,0:T(8,128)(2,1)}, bf16[768,384]{1,0:T(8,128)(2,1)S(1)}, u32[]{:S(2)}, u32[]{:S(2)}) %collective-permute-start) | collective-permute-done | bytes 589856 | tf_op jit(solution)/shard_map/ppermute | solution.py:15
  17.0 3.8 %collective-permute-done.2.refs_4_.refs_12_ = bf16[768,384]{1,0:T(8,128)(2,1)} collective-permute-done((bf16[768,384]{1,0:T(8,128)(2,1)}, bf16[768,384]{1,0:T(8,128)(2,1)}, u32[]{:S(2)}, u32[]{:S(2)}) %collective-permute-start.2) | collective-permute-done | bytes 589856 | tf_op jit(solution)/shard_map/ppermute | solution.py:15
  20.7 2.3 %collective-permute-start.7 = (bf16[768,384]{1,0:T(8,128)(2,1)S(1)}, bf16[768,384]{1,0:T(8,128)(2,1)S(1)}, u32[]{:S(2)}, u32[]{:S(2)}) collective-permute-start(bf16[768,384]{1,0:T(8,128)(2,1)S(1)} %collective-permute-done.refs_2_.refs_10_), channel_id=1, source_target_pairs={{0,12},{4,0},{8,4},{12,8},{1,13},{5,1},{9,5},{13,9},{2,14},{6,2},{... | collective-permute-start | bytes 1769480 | tf_op jit(solution)/shard_map/ppermute | solution.py:15
  23.1 2.7 %collective-permute-start.5 = (bf16[768,384]{1,0:T(8,128)(2,1)}, bf16[768,384]{1,0:T(8,128)(2,1)S(1)}, u32[]{:S(2)}, u32[]{:S(2)}) collective-permute-start(bf16[768,384]{1,0:T(8,128)(2,1)} %collective-permute-done.3.refs_5_.refs_13_), channel_id=1, source_target_pairs={{0,3},{1,0},{2,1},{3,2},{4,7},{5,4},{6,5},{7,6},{8,11},{9,8},{10,9... | collective-permute-start | bytes 1769480 | tf_op jit(solution)/shard_map/ppermute | solution.py:15
  25.8 9.3 %collective-permute-done.4.refs_1_.refs_14_ = bf16[768,384]{1,0:T(8,128)(2,1)S(1)} collective-permute-done((bf16[768,384]{1,0:T(8,128)(2,1)}, bf16[768,384]{1,0:T(8,128)(2,1)S(1)}, u32[]{:S(2)}, u32[]{:S(2)}) %collective-permute-start.4) | collective-permute-done | bytes 589856 | tf_op jit(solution)/shard_map/ppermute | solution.py:15
  36.0 3.0 %collective-permute-done.6.refs_3_.refs_16_ = bf16[768,384]{1,0:T(8,128)(2,1)S(1)} collective-permute-done((bf16[768,384]{1,0:T(8,128)(2,1)}, bf16[768,384]{1,0:T(8,128)(2,1)S(1)}, u32[]{:S(2)}, u32[]{:S(2)}) %collective-permute-start.6) | collective-permute-done | bytes 589856 | tf_op jit(solution)/shard_map/ppermute | solution.py:15
  39.4 2.7 %collective-permute-start.11 = (bf16[768,384]{1,0:T(8,128)(2,1)S(1)}, bf16[768,384]{1,0:T(8,128)(2,1)S(1)}, u32[]{:S(2)}, u32[]{:S(2)}) collective-permute-start(bf16[768,384]{1,0:T(8,128)(2,1)S(1)} %collective-permute-done.5.refs_2_.refs_15_), channel_id=1, source_target_pairs={{0,12},{4,0},{8,4},{12,8},{1,13},{5,1},{9,5},{13,9},{2,14},{6,2},{... | collective-permute-start | bytes 1769480 | tf_op jit(solution)/shard_map/ppermute | solution.py:15
  42.1 2.7 %collective-permute-start.9 = (bf16[768,384]{1,0:T(8,128)(2,1)S(1)}, bf16[768,384]{1,0:T(8,128)(2,1)S(1)}, u32[]{:S(2)}, u32[]{:S(2)}) collective-permute-start(bf16[768,384]{1,0:T(8,128)(2,1)S(1)} %collective-permute-done.6.refs_3_.refs_16_), channel_id=1, source_target_pairs={{0,3},{1,0},{2,1},{3,2},{4,7},{5,4},{6,5},{7,6},{8,11},{9,8},{10,9... | collective-permute-start | bytes 1769480 | tf_op jit(solution)/shard_map/ppermute | solution.py:15
  44.8 1.1 copy-done.1
  45.9 2.1 %shard_map.41 = (f32[64,1920]{1,0:T(8,128)S(1)}, f32[64,1920]{1,0:T(8,128)S(1)}, f32[8,128]{1,0:T(8,128)S(1)}) custom-call(bf16[128,768]{1,0:T(8,128)(2,1)S(1)} %convolution_convert_fusion.1.refs_0_, bf16[768,384]{1,0:T(8,128)(2,1)S(1)} %copy-done.1, bf16[768,384]{1,0:T(8,128)(2,1)S(1)} %collective-permute-done.refs_2_.refs_10_, ...), custom_call_target="tpu_custom_call" | custom-call | flops 377487360 | bytes 2949120 | tf_op jit(solution)/shard_map/pallas_call | solution.py:71
  48.0 5.1 %collective-permute-start.17 = (f32[64,1920]{1,0:T(8,128)S(1)}, f32[64,1920]{1,0:T(8,128)S(1)}, u32[]{:S(2)}, u32[]{:S(2)}) collective-permute-start(f32[64,1920]{1,0:T(8,128)S(1)} %get-tuple-element.59), channel_id=1, source_target_pairs={{0,16},{16,0},{1,17},{17,1},{2,18},{18,2},{3,19},{19,3},{4,20},{20... | collective-permute-start | bytes 1474568 | tf_op jit(solution)/shard_map/ppermute | solution.py:19
  53.1 1.5 collective-permute-done.17
  55.3 1.4 collective-permute-start.18
  56.8 2.0 %collective-permute-start.14 = (bf16[384,384]{1,0:T(8,128)(2,1)S(1)}, bf16[384,384]{1,0:T(8,128)(2,1)S(1)}, u32[]{:S(2)}, u32[]{:S(2)}) collective-permute-start(bf16[384,384]{1,0:T(8,128)(2,1)S(1)} %slice.87), channel_id=1, source_target_pairs={{0,3},{1,0},{2,1},{3,2},{4,7},{5,4},{6,5},{7,6},{8,11},{9,8},{10,9... | collective-permute-start | bytes 884744 | tf_op jit(solution)/shard_map/ppermute | solution.py:15
  58.8 3.0 %collective-permute-start.15 = (bf16[384,384]{1,0:T(8,128)(2,1)S(1)}, bf16[384,384]{1,0:T(8,128)(2,1)S(1)}, u32[]{:S(2)}, u32[]{:S(2)}) collective-permute-start(bf16[384,384]{1,0:T(8,128)(2,1)S(1)} %slice.88), channel_id=1, source_target_pairs={{0,12},{4,0},{8,4},{12,8},{1,13},{5,1},{9,5},{13,9},{2,14},{6,2},{... | collective-permute-start | bytes 884744 | tf_op jit(solution)/shard_map/ppermute | solution.py:15
  62.6 8.1 %collective-permute-done.12.refs_1_.refs_22_ = bf16[768,384]{1,0:T(8,128)(2,1)S(1)} collective-permute-done((bf16[768,384]{1,0:T(8,128)(2,1)S(1)}, bf16[768,384]{1,0:T(8,128)(2,1)S(1)}, u32[]{:S(2)}, u32[]{:S(2)}) %collective-permute-start.12) | collective-permute-done | bytes 589856 | tf_op jit(solution)/shard_map/ppermute | solution.py:15
  71.3 1.2 collective-permute-start.16
  74.8 1.4 collective-permute-start.21
  76.2 1.5 collective-permute-start.22
  77.7 1.6 collective-permute-start.23
  79.3 3.4 %collective-permute-done.21 = bf16[16,6272]{1,0:T(8,128)(2,1)S(1)} collective-permute-done((bf16[16,6272]{1,0:T(8,128)(2,1)S(1)}, bf16[16,6272]{1,0:T(8,128)(2,1)S(1)}, u32[]{:S(2)}, u32[]{:S(2)}) %collective-permute-start.21) | collective-permute-done | bytes 200736 | tf_op jit(solution)/shard_map/ppermute | solution.py:15
  82.7 5.4 %collective-permute-done.23 = bf16[16,6272]{1,0:T(8,128)(2,1)S(1)} collective-permute-done((bf16[16,6272]{1,0:T(8,128)(2,1)S(1)}, bf16[16,6272]{1,0:T(8,128)(2,1)S(1)}, u32[]{:S(2)}, u32[]{:S(2)}) %collective-permute-start.23) | collective-permute-done | bytes 200736 | tf_op jit(solution)/shard_map/ppermute | solution.py:15
  88.2 1.2 collective-permute-start.24
  89.4 1.4 collective-permute-start.25
  90.8 1.8 collective-permute-start.27
  92.6 1.3 collective-permute-done.24.refs_2_
  93.9 3.3 %collective-permute-start.28 = (bf16[16,6144]{1,0:T(8,128)(2,1)S(1)}, bf16[16,6144]{1,0:T(8,128)(2,1)S(1)}, u32[]{:S(2)}, u32[]{:S(2)}) collective-permute-start(bf16[16,6144]{1,0:T(8,128)(2,1)S(1)} %collective-permute-done.24.refs_2_), channel_id=1, source_target_pairs={{0,16},{16,0},{1,17},{17,1},{2,18},{18,2},{3,19},{19,3},{4,20},{20... | collective-permute-start | bytes 589832 | tf_op jit(solution)/shard_map/ppermute | solution.py:19
  97.2 3.1 %collective-permute-start.29 = (bf16[16,6144]{1,0:T(8,128)(2,1)S(1)}, bf16[16,6144]{1,0:T(8,128)(2,1)S(1)}, u32[]{:S(2)}, u32[]{:S(2)}) collective-permute-start(bf16[16,6144]{1,0:T(8,128)(2,1)S(1)} %collective-permute-done.25.refs_3_), channel_id=1, source_target_pairs={{0,16},{16,0},{1,17},{17,1},{2,18},{18,2},{3,19},{19,3},{4,20},{20... | collective-permute-start | bytes 589832 | tf_op jit(solution)/shard_map/ppermute | solution.py:19
  101.2 1.2 collective-permute-start.30
  103.5 7.7 %shard_map.45 = (f32[64,6144]{1,0:T(8,128)S(1)}, f32[64,6144]{1,0:T(8,128)S(1)}) custom-call(f32[8,128]{1,0:T(8,128)S(1)} %convert_add_fusion.refs_0_, bf16[16,6144]{1,0:T(8,128)(2,1)S(1)} %fusion.7.refs_1_, bf16[16,6144]{1,0:T(8,128)(2,1)S(1)} %collective-permute-done.24.refs_2_, bf16[16,6144]{1,0:T(8,128)(2,1)S(1)} %collective-permute-done.25.refs_3_, ...), custom_call_target="tpu_custom_call" | custom-call | flops 2415919104 | bytes 9437184 | tf_op jit(solution)/shard_map/pallas_call | solution.py:139
  111.7 3.0 %collective-permute-done.31 = f32[64,6144]{1,0:T(8,128)S(1)} collective-permute-done((f32[64,6144]{1,0:T(8,128)S(1)}, f32[64,6144]{1,0:T(8,128)S(1)}, u32[]{:S(2)}, u32[]{:S(2)}) %collective-permute-start.31) | collective-permute-done | bytes 1572896 | tf_op jit(solution)/shard_map/ppermute | solution.py:19
  115.1 2.7 %collective-permute-start.33 = (bf16[16,6144]{1,0:T(8,128)(2,1)S(1)}, bf16[16,6144]{1,0:T(8,128)(2,1)S(1)}, u32[]{:S(2)}, u32[]{:S(2)}) collective-permute-start(bf16[16,6144]{1,0:T(8,128)(2,1)S(1)} %get-tuple-element.79), channel_id=1, source_target_pairs={{0,96},{32,0},{64,32},{96,64},{1,97},{33,1},{65,33},{97,65},{2,98}... | collective-permute-start | bytes 589832 | tf_op jit(solution)/shard_map/ppermute | solution.py:15
  117.9 8.7 %collective-permute-done.32 = bf16[16,6144]{1,0:T(8,128)(2,1)S(1)} collective-permute-done((bf16[16,6144]{1,0:T(8,128)(2,1)S(1)}, bf16[16,6144]{1,0:T(8,128)(2,1)S(1)}, u32[]{:S(2)}, u32[]{:S(2)}) %collective-permute-start.32) | collective-permute-done | bytes 196640 | tf_op jit(solution)/shard_map/ppermute | solution.py:15
  126.7 2.4 %collective-permute-start.35 = (bf16[16,6144]{1,0:T(8,128)(2,1)S(1)}, bf16[16,6144]{1,0:T(8,128)(2,1)S(1)}, u32[]{:S(2)}, u32[]{:S(2)}) collective-permute-start(bf16[16,6144]{1,0:T(8,128)(2,1)S(1)} %fusion.4.refs_1_), channel_id=1, source_target_pairs={{0,96},{32,0},{64,32},{96,64},{1,97},{33,1},{65,33},{97,65},{2,98}... | collective-permute-start | bytes 589832 | tf_op jit(solution)/shard_map/ppermute | solution.py:15
  129.8 2.1 %collective-permute-start.38 = (bf16[16,6144]{1,0:T(8,128)(2,1)S(1)}, bf16[16,6144]{1,0:T(8,128)(2,1)S(1)}, u32[]{:S(2)}, u32[]{:S(2)}) collective-permute-start(bf16[16,6144]{1,0:T(8,128)(2,1)S(1)} %fusion.4.refs_1_), channel_id=1, source_target_pairs={{0,16},{16,0},{1,17},{17,1},{2,18},{18,2},{3,19},{19,3},{4,20},{20... | collective-permute-start | bytes 589832 | tf_op jit(solution)/shard_map/ppermute | solution.py:19
  132.8 5.7 %collective-permute-start.39 = (bf16[16,6144]{1,0:T(8,128)(2,1)S(1)}, bf16[16,6144]{1,0:T(8,128)(2,1)S(1)}, u32[]{:S(2)}, u32[]{:S(2)}) collective-permute-start(bf16[16,6144]{1,0:T(8,128)(2,1)S(1)} %collective-permute-done.35.refs_2_), channel_id=1, source_target_pairs={{0,16},{16,0},{1,17},{17,1},{2,18},{18,2},{3,19},{19,3},{4,20},{20... | collective-permute-start | bytes 589832 | tf_op jit(solution)/shard_map/ppermute | solution.py:19
  138.5 1.6 collective-permute-start.40
  142.9 4.3 %shard_map.46 = bf16[128,768]{1,0:T(8,128)(2,1)S(1)} custom-call(f32[8,128]{1,0:T(8,128)S(1)} %convert_add_fusion.refs_0_, bf16[16,6144]{1,0:T(8,128)(2,1)S(1)} %fusion.4.refs_1_, bf16[16,6144]{1,0:T(8,128)(2,1)S(1)} %collective-permute-done.35.refs_2_, bf16[16,6144]{1,0:T(8,128)(2,1)S(1)} %collective-permute-done.36.refs_3_, ...), custom_call_target="tpu_custom_call" | custom-call | flops 1207959552 | bytes 9437184 | tf_op jit(solution)/shard_map/pallas_call | solution.py:139
  148.7 3.5 %all-to-all-start = ((bf16[4,768,128]{2,1,0:T(8,128)(2,1)}), bf16[4,768,128]{2,1,0:T(8,128)(2,1)S(1)}, u32[]{:S(2)}, u32[]{:S(2)}) async-start(bf16[4,768,128]{2,1,0:T(8,128)(2,1)} %broadcast_in_dim.2), calls=%async_computation | async-start | bytes 1572864 | tf_op jit(solution)/shard_map/all_to_all | solution.py:177
  152.2 12.4 %all-gather = bf16[3072,128]{1,0:T(8,128)(2,1)S(1)} all-gather(bf16[768,128]{1,0:T(8,128)(2,1)S(1)} %convolution_convert_fusion), channel_id=2, replica_groups=mesh['y'=4,'core'=2,'z'=4,'x'=4] {'x'}, dimensions={0}, use_global_device_ids=true | all-gather | bytes 983040 | tf_op jit(solution)/shard_map/all_gather | solution.py:176
  165.3 2.0 %collective-permute-start.42 = (f32[16,64,128]{2,1,0:T(8,128)S(1)}, f32[16,64,128]{2,1,0:T(8,128)S(1)}, u32[]{:S(2)}, u32[]{:S(2)}) collective-permute-start(f32[16,64,128]{2,1,0:T(8,128)S(1)} %dynamic-slice_bitcast_fusion), channel_id=1, source_target_pairs={{0,16},{16,0},{1,17},{17,1},{2,18},{18,2},{3,19},{19,3},{4,20},{20... | collective-permute-start | bytes 1572872 | tf_op jit(solution)/shard_map/ppermute | solution.py:19
  167.4 1.5 collective-permute-done.42
  169.0 15.5 %all_to_all.10 = f32[16,64,128]{2,1,0:T(8,128)S(1)} all-to-all(f32[16,64,128]{2,1,0:T(8,128)S(1)} %bitcast_add_fusion), channel_id=1, replica_groups=mesh['y'=4,'core'=2,'z'=4,'x'=4] {'y','x'}, dimensions={0} | all-to-all | bytes 1048576 | tf_op jit(solution)/shard_map/all_to_all | solution.py:182
  184.6 1.9 collective-permute-start.43
  (102 shorter events, 17.2 us)
Async XLA Ops:
  0.6 38.4 %copy-start = (bf16[768,128]{1,0:T(8,128)(2,1)S(1)}, bf16[768,128]{1,0:T(8,128)(2,1)}, u32[]{:S(2)}) copy-start(bf16[768,128]{1,0:T(8,128)(2,1)} %param.3) | copy-start | bytes 589828
  0.6 16.3 %collective-permute-start = (bf16[768,384]{1,0:T(8,128)(2,1)}, bf16[768,384]{1,0:T(8,128)(2,1)S(1)}, u32[]{:S(2)}, u32[]{:S(2)}) collective-permute-start(bf16[768,384]{1,0:T(8,128)(2,1)} %refs_9_.3), channel_id=1, source_target_pairs={{0,1},{1,2},{2,3},{3,0},{4,5},{5,6},{6,7},{7,4},{8,9},{9,10},{10,1... | collective-permute-start | bytes 1769480 | tf_op jit(solution)/shard_map/ppermute | solution.py:15
  2.8 14.2 %collective-permute-start.1 = (bf16[768,384]{1,0:T(8,128)(2,1)}, bf16[768,384]{1,0:T(8,128)(2,1)}, u32[]{:S(2)}, u32[]{:S(2)}) collective-permute-start(bf16[768,384]{1,0:T(8,128)(2,1)} %refs_9_.3), channel_id=1, source_target_pairs={{0,3},{1,0},{2,1},{3,2},{4,7},{5,4},{6,5},{7,6},{8,11},{9,8},{10,9... | collective-permute-start | bytes 1769480 | tf_op jit(solution)/shard_map/ppermute | solution.py:15
  4.1 16.6 %collective-permute-start.2 = (bf16[768,384]{1,0:T(8,128)(2,1)}, bf16[768,384]{1,0:T(8,128)(2,1)}, u32[]{:S(2)}, u32[]{:S(2)}) collective-permute-start(bf16[768,384]{1,0:T(8,128)(2,1)} %refs_9_.3), channel_id=1, source_target_pairs={{0,4},{4,8},{8,12},{12,0},{1,5},{5,9},{9,13},{13,1},{2,6},{6,10},{... | collective-permute-start | bytes 1769480 | tf_op jit(solution)/shard_map/ppermute | solution.py:15
  5.9 14.9 %collective-permute-start.3 = (bf16[768,384]{1,0:T(8,128)(2,1)}, bf16[768,384]{1,0:T(8,128)(2,1)}, u32[]{:S(2)}, u32[]{:S(2)}) collective-permute-start(bf16[768,384]{1,0:T(8,128)(2,1)} %refs_9_.3), channel_id=1, source_target_pairs={{0,12},{4,0},{8,4},{12,8},{1,13},{5,1},{9,5},{13,9},{2,14},{6,2},{... | collective-permute-start | bytes 1769480 | tf_op jit(solution)/shard_map/ppermute | solution.py:15
  20.7 14.4 %collective-permute-start.4 = (bf16[768,384]{1,0:T(8,128)(2,1)}, bf16[768,384]{1,0:T(8,128)(2,1)S(1)}, u32[]{:S(2)}, u32[]{:S(2)}) collective-permute-start(bf16[768,384]{1,0:T(8,128)(2,1)} %collective-permute-done.2.refs_4_.refs_12_), channel_id=1, source_target_pairs={{0,1},{1,2},{2,3},{3,0},{4,5},{5,6},{6,7},{7,4},{8,9},{9,10},{10,1... | collective-permute-start | bytes 1769480 | tf_op jit(solution)/shard_map/ppermute | solution.py:15
  20.7 14.4 %collective-permute-start.7 = (bf16[768,384]{1,0:T(8,128)(2,1)S(1)}, bf16[768,384]{1,0:T(8,128)(2,1)S(1)}, u32[]{:S(2)}, u32[]{:S(2)}) collective-permute-start(bf16[768,384]{1,0:T(8,128)(2,1)S(1)} %collective-permute-done.refs_2_.refs_10_), channel_id=1, source_target_pairs={{0,12},{4,0},{8,4},{12,8},{1,13},{5,1},{9,5},{13,9},{2,14},{6,2},{... | collective-permute-start | bytes 1769480 | tf_op jit(solution)/shard_map/ppermute | solution.py:15
  23.1 12.9 %collective-permute-start.5 = (bf16[768,384]{1,0:T(8,128)(2,1)}, bf16[768,384]{1,0:T(8,128)(2,1)S(1)}, u32[]{:S(2)}, u32[]{:S(2)}) collective-permute-start(bf16[768,384]{1,0:T(8,128)(2,1)} %collective-permute-done.3.refs_5_.refs_13_), channel_id=1, source_target_pairs={{0,3},{1,0},{2,1},{3,2},{4,7},{5,4},{6,5},{7,6},{8,11},{9,8},{10,9... | collective-permute-start | bytes 1769480 | tf_op jit(solution)/shard_map/ppermute | solution.py:15
  25.8 13.2 %collective-permute-start.6 = (bf16[768,384]{1,0:T(8,128)(2,1)}, bf16[768,384]{1,0:T(8,128)(2,1)S(1)}, u32[]{:S(2)}, u32[]{:S(2)}) collective-permute-start(bf16[768,384]{1,0:T(8,128)(2,1)} %collective-permute-done.1.refs_3_.refs_11_), channel_id=1, source_target_pairs={{0,4},{4,8},{8,12},{12,0},{1,5},{5,9},{9,13},{13,1},{2,6},{6,10},{... | collective-permute-start | bytes 1769480 | tf_op jit(solution)/shard_map/ppermute | solution.py:15
  39.0 15.6 %collective-permute-start.10 = (bf16[768,384]{1,0:T(8,128)(2,1)S(1)}, bf16[768,384]{1,0:T(8,128)(2,1)S(1)}, u32[]{:S(2)}, u32[]{:S(2)}) collective-permute-start(bf16[768,384]{1,0:T(8,128)(2,1)S(1)} %collective-permute-done.4.refs_1_.refs_14_), channel_id=1, source_target_pairs={{0,4},{4,8},{8,12},{12,0},{1,5},{5,9},{9,13},{13,1},{2,6},{6,10},{... | collective-permute-start | bytes 1769480 | tf_op jit(solution)/shard_map/ppermute | solution.py:15
  39.4 15.9 %collective-permute-start.11 = (bf16[768,384]{1,0:T(8,128)(2,1)S(1)}, bf16[768,384]{1,0:T(8,128)(2,1)S(1)}, u32[]{:S(2)}, u32[]{:S(2)}) collective-permute-start(bf16[768,384]{1,0:T(8,128)(2,1)S(1)} %collective-permute-done.5.refs_2_.refs_15_), channel_id=1, source_target_pairs={{0,12},{4,0},{8,4},{12,8},{1,13},{5,1},{9,5},{13,9},{2,14},{6,2},{... | collective-permute-start | bytes 1769480 | tf_op jit(solution)/shard_map/ppermute | solution.py:15
  42.1 14.6 %collective-permute-start.8 = (bf16[768,384]{1,0:T(8,128)(2,1)S(1)}, bf16[768,384]{1,0:T(8,128)(2,1)S(1)}, u32[]{:S(2)}, u32[]{:S(2)}) collective-permute-start(bf16[768,384]{1,0:T(8,128)(2,1)S(1)} %collective-permute-done.7.refs_4_.refs_17_), channel_id=1, source_target_pairs={{0,1},{1,2},{2,3},{3,0},{4,5},{5,6},{6,7},{7,4},{8,9},{9,10},{10,1... | collective-permute-start | bytes 1769480 | tf_op jit(solution)/shard_map/ppermute | solution.py:15
  42.1 14.6 %collective-permute-start.9 = (bf16[768,384]{1,0:T(8,128)(2,1)S(1)}, bf16[768,384]{1,0:T(8,128)(2,1)S(1)}, u32[]{:S(2)}, u32[]{:S(2)}) collective-permute-start(bf16[768,384]{1,0:T(8,128)(2,1)S(1)} %collective-permute-done.6.refs_3_.refs_16_), channel_id=1, source_target_pairs={{0,3},{1,0},{2,1},{3,2},{4,7},{5,4},{6,5},{7,6},{8,11},{9,8},{10,9... | collective-permute-start | bytes 1769480 | tf_op jit(solution)/shard_map/ppermute | solution.py:15
  48.0 6.6 %collective-permute-start.17 = (f32[64,1920]{1,0:T(8,128)S(1)}, f32[64,1920]{1,0:T(8,128)S(1)}, u32[]{:S(2)}, u32[]{:S(2)}) collective-permute-start(f32[64,1920]{1,0:T(8,128)S(1)} %get-tuple-element.59), channel_id=1, source_target_pairs={{0,16},{16,0},{1,17},{17,1},{2,18},{18,2},{3,19},{19,3},{4,20},{20... | collective-permute-start | bytes 1474568 | tf_op jit(solution)/shard_map/ppermute | solution.py:19
  54.6 16.1 %collective-permute-start.12 = (bf16[768,384]{1,0:T(8,128)(2,1)S(1)}, bf16[768,384]{1,0:T(8,128)(2,1)S(1)}, u32[]{:S(2)}, u32[]{:S(2)}) collective-permute-start(bf16[768,384]{1,0:T(8,128)(2,1)S(1)} %collective-permute-done.refs_2_.refs_10_), channel_id=1, source_target_pairs={{0,1},{1,2},{2,3},{3,0},{4,5},{5,6},{6,7},{7,4},{8,9},{9,10},{10,1... | collective-permute-start | bytes 1769480 | tf_op jit(solution)/shard_map/ppermute | solution.py:15
  54.6 16.1 %collective-permute-start.13 = (bf16[768,384]{1,0:T(8,128)(2,1)}, bf16[768,384]{1,0:T(8,128)(2,1)S(1)}, u32[]{:S(2)}, u32[]{:S(2)}) collective-permute-start(bf16[768,384]{1,0:T(8,128)(2,1)} %collective-permute-done.2.refs_4_.refs_12_), channel_id=1, source_target_pairs={{0,4},{4,8},{8,12},{12,0},{1,5},{5,9},{9,13},{13,1},{2,6},{6,10},{... | collective-permute-start | bytes 1769480 | tf_op jit(solution)/shard_map/ppermute | solution.py:15
  55.3 6.6 %collective-permute-start.18 = (f32[64,1536]{1,0:T(8,128)S(1)}, f32[64,1536]{1,0:T(8,128)S(1)}, u32[]{:S(2)}, u32[]{:S(2)}) collective-permute-start(f32[64,1536]{1,0:T(8,128)S(1)} %get-tuple-element.61), channel_id=1, source_target_pairs={{0,16},{16,0},{1,17},{17,1},{2,18},{18,2},{3,19},{19,3},{4,20},{20... | collective-permute-start | bytes 1179656 | tf_op jit(solution)/shard_map/ppermute | solution.py:19
  56.8 13.9 %collective-permute-start.14 = (bf16[384,384]{1,0:T(8,128)(2,1)S(1)}, bf16[384,384]{1,0:T(8,128)(2,1)S(1)}, u32[]{:S(2)}, u32[]{:S(2)}) collective-permute-start(bf16[384,384]{1,0:T(8,128)(2,1)S(1)} %slice.87), channel_id=1, source_target_pairs={{0,3},{1,0},{2,1},{3,2},{4,7},{5,4},{6,5},{7,6},{8,11},{9,8},{10,9... | collective-permute-start | bytes 884744 | tf_op jit(solution)/shard_map/ppermute | solution.py:15
  58.8 11.8 %collective-permute-start.15 = (bf16[384,384]{1,0:T(8,128)(2,1)S(1)}, bf16[384,384]{1,0:T(8,128)(2,1)S(1)}, u32[]{:S(2)}, u32[]{:S(2)}) collective-permute-start(bf16[384,384]{1,0:T(8,128)(2,1)S(1)} %slice.88), channel_id=1, source_target_pairs={{0,12},{4,0},{8,4},{12,8},{1,13},{5,1},{9,5},{13,9},{2,14},{6,2},{... | collective-permute-start | bytes 884744 | tf_op jit(solution)/shard_map/ppermute | solution.py:15
  71.3 2.0 %collective-permute-start.16 = (f32[8,128]{1,0:T(8,128)S(1)}, f32[8,128]{1,0:T(8,128)S(1)}, u32[]{:S(2)}, u32[]{:S(2)}) collective-permute-start(f32[8,128]{1,0:T(8,128)S(1)} %add_add_fusion), channel_id=1, source_target_pairs={{0,16},{16,0},{1,17},{17,1},{2,18},{18,2},{3,19},{19,3},{4,20},{20... | collective-permute-start | bytes 12296 | tf_op jit(solution)/shard_map/ppermute | solution.py:19
  72.4 1.8 collective-permute-start.19
  72.5 2.1 %collective-permute-start.20 = (f32[64,1152]{1,0:T(8,128)S(1)}, f32[64,1152]{1,0:T(8,128)S(1)}, u32[]{:S(2)}, u32[]{:S(2)}) collective-permute-start(f32[64,1152]{1,0:T(8,128)S(1)} %get-tuple-element.65), channel_id=1, source_target_pairs={{0,16},{16,0},{1,17},{17,1},{2,18},{18,2},{3,19},{19,3},{4,20},{20... | collective-permute-start | bytes 884744 | tf_op jit(solution)/shard_map/ppermute | solution.py:19
  74.8 28.8 %copy-start.2 = (bf16[768,384]{1,0:T(8,128)(2,1)S(1)}, bf16[768,384]{1,0:T(8,128)(2,1)}, u32[]{:S(2)}) copy-start(bf16[768,384]{1,0:T(8,128)(2,1)} %refs_9_.3) | copy-start | bytes 1769476
  74.8 7.9 %collective-permute-start.21 = (bf16[16,6272]{1,0:T(8,128)(2,1)S(1)}, bf16[16,6272]{1,0:T(8,128)(2,1)S(1)}, u32[]{:S(2)}, u32[]{:S(2)}) collective-permute-start(bf16[16,6272]{1,0:T(8,128)(2,1)S(1)} %get-tuple-element.83), channel_id=1, source_target_pairs={{0,32},{32,64},{64,96},{96,0},{1,33},{33,65},{65,97},{97,1},{2,34}... | collective-permute-start | bytes 602120 | tf_op jit(solution)/shard_map/ppermute | solution.py:15
  76.2 6.5 %collective-permute-start.22 = (bf16[16,6272]{1,0:T(8,128)(2,1)S(1)}, bf16[16,6272]{1,0:T(8,128)(2,1)S(1)}, u32[]{:S(2)}, u32[]{:S(2)}) collective-permute-start(bf16[16,6272]{1,0:T(8,128)(2,1)S(1)} %get-tuple-element.82), channel_id=1, source_target_pairs={{0,96},{32,0},{64,32},{96,64},{1,97},{33,1},{65,33},{97,65},{2,98}... | collective-permute-start | bytes 602120 | tf_op jit(solution)/shard_map/ppermute | solution.py:15
  77.7 10.4 %collective-permute-start.23 = (bf16[16,6272]{1,0:T(8,128)(2,1)S(1)}, bf16[16,6272]{1,0:T(8,128)(2,1)S(1)}, u32[]{:S(2)}, u32[]{:S(2)}) collective-permute-start(bf16[16,6272]{1,0:T(8,128)(2,1)S(1)} %get-tuple-element.81), channel_id=1, source_target_pairs={{0,64},{32,96},{64,0},{96,32},{1,65},{33,97},{65,1},{97,33},{2,66}... | collective-permute-start | bytes 602120 | tf_op jit(solution)/shard_map/ppermute | solution.py:15
  88.2 5.7 %collective-permute-start.24 = (bf16[16,6144]{1,0:T(8,128)(2,1)S(1)}, bf16[16,6144]{1,0:T(8,128)(2,1)S(1)}, u32[]{:S(2)}, u32[]{:S(2)}) collective-permute-start(bf16[16,6144]{1,0:T(8,128)(2,1)S(1)} %fusion.7.refs_1_), channel_id=1, source_target_pairs={{0,96},{32,0},{64,32},{96,64},{1,97},{33,1},{65,33},{97,65},{2,98}... | collective-permute-start | bytes 589832 | tf_op jit(solution)/shard_map/ppermute | solution.py:15
  89.4 7.8 %collective-permute-start.25 = (bf16[16,6144]{1,0:T(8,128)(2,1)S(1)}, bf16[16,6144]{1,0:T(8,128)(2,1)S(1)}, u32[]{:S(2)}, u32[]{:S(2)}) collective-permute-start(bf16[16,6144]{1,0:T(8,128)(2,1)S(1)} %fusion.7.refs_1_), channel_id=1, source_target_pairs={{0,64},{32,96},{64,0},{96,32},{1,65},{33,97},{65,1},{97,33},{2,66}... | collective-permute-start | bytes 589832 | tf_op jit(solution)/shard_map/ppermute | solution.py:15
  90.8 10.4 %collective-permute-start.26 = (bf16[16,6144]{1,0:T(8,128)(2,1)S(1)}, bf16[16,6144]{1,0:T(8,128)(2,1)S(1)}, u32[]{:S(2)}, u32[]{:S(2)}) collective-permute-start(bf16[16,6144]{1,0:T(8,128)(2,1)S(1)} %fusion.7.refs_1_), channel_id=1, source_target_pairs={{0,32},{32,64},{64,96},{96,0},{1,33},{33,65},{65,97},{97,1},{2,34}... | collective-permute-start | bytes 589832 | tf_op jit(solution)/shard_map/ppermute | solution.py:15
  90.8 11.7 %collective-permute-start.27 = (bf16[16,6144]{1,0:T(8,128)(2,1)S(1)}, bf16[16,6144]{1,0:T(8,128)(2,1)S(1)}, u32[]{:S(2)}, u32[]{:S(2)}) collective-permute-start(bf16[16,6144]{1,0:T(8,128)(2,1)S(1)} %fusion.7.refs_1_), channel_id=1, source_target_pairs={{0,16},{16,0},{1,17},{17,1},{2,18},{18,2},{3,19},{19,3},{4,20},{20... | collective-permute-start | bytes 589832 | tf_op jit(solution)/shard_map/ppermute | solution.py:19
  93.9 8.6 %collective-permute-start.28 = (bf16[16,6144]{1,0:T(8,128)(2,1)S(1)}, bf16[16,6144]{1,0:T(8,128)(2,1)S(1)}, u32[]{:S(2)}, u32[]{:S(2)}) collective-permute-start(bf16[16,6144]{1,0:T(8,128)(2,1)S(1)} %collective-permute-done.24.refs_2_), channel_id=1, source_target_pairs={{0,16},{16,0},{1,17},{17,1},{2,18},{18,2},{3,19},{19,3},{4,20},{20... | collective-permute-start | bytes 589832 | tf_op jit(solution)/shard_map/ppermute | solution.py:19
  97.2 5.2 %collective-permute-start.29 = (bf16[16,6144]{1,0:T(8,128)(2,1)S(1)}, bf16[16,6144]{1,0:T(8,128)(2,1)S(1)}, u32[]{:S(2)}, u32[]{:S(2)}) collective-permute-start(bf16[16,6144]{1,0:T(8,128)(2,1)S(1)} %collective-permute-done.25.refs_3_), channel_id=1, source_target_pairs={{0,16},{16,0},{1,17},{17,1},{2,18},{18,2},{3,19},{19,3},{4,20},{20... | collective-permute-start | bytes 589832 | tf_op jit(solution)/shard_map/ppermute | solution.py:19
  101.2 2.3 %collective-permute-start.30 = (bf16[16,6144]{1,0:T(8,128)(2,1)S(1)}, bf16[16,6144]{1,0:T(8,128)(2,1)S(1)}, u32[]{:S(2)}, u32[]{:S(2)}) collective-permute-start(bf16[16,6144]{1,0:T(8,128)(2,1)S(1)} %collective-permute-done.26.refs_4_), channel_id=1, source_target_pairs={{0,16},{16,0},{1,17},{17,1},{2,18},{18,2},{3,19},{19,3},{4,20},{20... | collective-permute-start | bytes 589832 | tf_op jit(solution)/shard_map/ppermute | solution.py:19
  111.2 3.5 %collective-permute-start.31 = (f32[64,6144]{1,0:T(8,128)S(1)}, f32[64,6144]{1,0:T(8,128)S(1)}, u32[]{:S(2)}, u32[]{:S(2)}) collective-permute-start(f32[64,6144]{1,0:T(8,128)S(1)} %get-tuple-element.70), channel_id=1, source_target_pairs={{0,16},{16,0},{1,17},{17,1},{2,18},{18,2},{3,19},{19,3},{4,20},{20... | collective-permute-start | bytes 4718600 | tf_op jit(solution)/shard_map/ppermute | solution.py:19
  115.0 11.6 %collective-permute-start.32 = (bf16[16,6144]{1,0:T(8,128)(2,1)S(1)}, bf16[16,6144]{1,0:T(8,128)(2,1)S(1)}, u32[]{:S(2)}, u32[]{:S(2)}) collective-permute-start(bf16[16,6144]{1,0:T(8,128)(2,1)S(1)} %get-tuple-element.80), channel_id=1, source_target_pairs={{0,32},{32,64},{64,96},{96,0},{1,33},{33,65},{65,97},{97,1},{2,34}... | collective-permute-start | bytes 589832 | tf_op jit(solution)/shard_map/ppermute | solution.py:15
  115.1 11.5 %collective-permute-start.33 = (bf16[16,6144]{1,0:T(8,128)(2,1)S(1)}, bf16[16,6144]{1,0:T(8,128)(2,1)S(1)}, u32[]{:S(2)}, u32[]{:S(2)}) collective-permute-start(bf16[16,6144]{1,0:T(8,128)(2,1)S(1)} %get-tuple-element.79), channel_id=1, source_target_pairs={{0,96},{32,0},{64,32},{96,64},{1,97},{33,1},{65,33},{97,65},{2,98}... | collective-permute-start | bytes 589832 | tf_op jit(solution)/shard_map/ppermute | solution.py:15
  117.7 8.9 %collective-permute-start.34 = (bf16[16,6144]{1,0:T(8,128)(2,1)S(1)}, bf16[16,6144]{1,0:T(8,128)(2,1)S(1)}, u32[]{:S(2)}, u32[]{:S(2)}) collective-permute-start(bf16[16,6144]{1,0:T(8,128)(2,1)S(1)} %get-tuple-element.78), channel_id=1, source_target_pairs={{0,64},{32,96},{64,0},{96,32},{1,65},{33,97},{65,1},{97,33},{2,66}... | collective-permute-start | bytes 589832 | tf_op jit(solution)/shard_map/ppermute | solution.py:15
  126.7 6.1 %collective-permute-start.35 = (bf16[16,6144]{1,0:T(8,128)(2,1)S(1)}, bf16[16,6144]{1,0:T(8,128)(2,1)S(1)}, u32[]{:S(2)}, u32[]{:S(2)}) collective-permute-start(bf16[16,6144]{1,0:T(8,128)(2,1)S(1)} %fusion.4.refs_1_), channel_id=1, source_target_pairs={{0,96},{32,0},{64,32},{96,64},{1,97},{33,1},{65,33},{97,65},{2,98}... | collective-permute-start | bytes 589832 | tf_op jit(solution)/shard_map/ppermute | solution.py:15
  129.1 9.4 %collective-permute-start.36 = (bf16[16,6144]{1,0:T(8,128)(2,1)S(1)}, bf16[16,6144]{1,0:T(8,128)(2,1)S(1)}, u32[]{:S(2)}, u32[]{:S(2)}) collective-permute-start(bf16[16,6144]{1,0:T(8,128)(2,1)S(1)} %fusion.4.refs_1_), channel_id=1, source_target_pairs={{0,64},{32,96},{64,0},{96,32},{1,65},{33,97},{65,1},{97,33},{2,66}... | collective-permute-start | bytes 589832 | tf_op jit(solution)/shard_map/ppermute | solution.py:15
  129.1 11.9 %collective-permute-start.37 = (bf16[16,6144]{1,0:T(8,128)(2,1)S(1)}, bf16[16,6144]{1,0:T(8,128)(2,1)S(1)}, u32[]{:S(2)}, u32[]{:S(2)}) collective-permute-start(bf16[16,6144]{1,0:T(8,128)(2,1)S(1)} %fusion.4.refs_1_), channel_id=1, source_target_pairs={{0,32},{32,64},{64,96},{96,0},{1,33},{33,65},{65,97},{97,1},{2,34}... | collective-permute-start | bytes 589832 | tf_op jit(solution)/shard_map/ppermute | solution.py:15
  129.8 12.1 %collective-permute-start.38 = (bf16[16,6144]{1,0:T(8,128)(2,1)S(1)}, bf16[16,6144]{1,0:T(8,128)(2,1)S(1)}, u32[]{:S(2)}, u32[]{:S(2)}) collective-permute-start(bf16[16,6144]{1,0:T(8,128)(2,1)S(1)} %fusion.4.refs_1_), channel_id=1, source_target_pairs={{0,16},{16,0},{1,17},{17,1},{2,18},{18,2},{3,19},{19,3},{4,20},{20... | collective-permute-start | bytes 589832 | tf_op jit(solution)/shard_map/ppermute | solution.py:19
  132.8 9.1 %collective-permute-start.39 = (bf16[16,6144]{1,0:T(8,128)(2,1)S(1)}, bf16[16,6144]{1,0:T(8,128)(2,1)S(1)}, u32[]{:S(2)}, u32[]{:S(2)}) collective-permute-start(bf16[16,6144]{1,0:T(8,128)(2,1)S(1)} %collective-permute-done.35.refs_2_), channel_id=1, source_target_pairs={{0,16},{16,0},{1,17},{17,1},{2,18},{18,2},{3,19},{19,3},{4,20},{20... | collective-permute-start | bytes 589832 | tf_op jit(solution)/shard_map/ppermute | solution.py:19
  138.5 3.4 %collective-permute-start.40 = (bf16[16,6144]{1,0:T(8,128)(2,1)S(1)}, bf16[16,6144]{1,0:T(8,128)(2,1)S(1)}, u32[]{:S(2)}, u32[]{:S(2)}) collective-permute-start(bf16[16,6144]{1,0:T(8,128)(2,1)S(1)} %collective-permute-done.36.refs_3_), channel_id=1, source_target_pairs={{0,16},{16,0},{1,17},{17,1},{2,18},{18,2},{3,19},{19,3},{4,20},{20... | collective-permute-start | bytes 589832 | tf_op jit(solution)/shard_map/ppermute | solution.py:19
  141.0 1.9 %collective-permute-start.41 = (bf16[16,6144]{1,0:T(8,128)(2,1)S(1)}, bf16[16,6144]{1,0:T(8,128)(2,1)S(1)}, u32[]{:S(2)}, u32[]{:S(2)}) collective-permute-start(bf16[16,6144]{1,0:T(8,128)(2,1)S(1)} %collective-permute-done.37.refs_4_), channel_id=1, source_target_pairs={{0,16},{16,0},{1,17},{17,1},{2,18},{18,2},{3,19},{19,3},{4,20},{20... | collective-permute-start | bytes 589832 | tf_op jit(solution)/shard_map/ppermute | solution.py:19
  147.7 16.9 %copy-start.3 = (bf16[768,128]{1,0:T(8,128)(2,1)}, bf16[768,128]{1,0:T(8,128)(2,1)S(1)}, u32[]{:S(2)}) copy-start(bf16[768,128]{1,0:T(8,128)(2,1)S(1)} %convolution_convert_fusion) | copy-start | bytes 589828
  148.7 15.9 %all-to-all-start = ((bf16[4,768,128]{2,1,0:T(8,128)(2,1)}), bf16[4,768,128]{2,1,0:T(8,128)(2,1)S(1)}, u32[]{:S(2)}, u32[]{:S(2)}) async-start(bf16[4,768,128]{2,1,0:T(8,128)(2,1)} %broadcast_in_dim.2), calls=%async_computation | async-start | bytes 1572864 | tf_op jit(solution)/shard_map/all_to_all | solution.py:177
  165.3 3.6 %collective-permute-start.42 = (f32[16,64,128]{2,1,0:T(8,128)S(1)}, f32[16,64,128]{2,1,0:T(8,128)S(1)}, u32[]{:S(2)}, u32[]{:S(2)}) collective-permute-start(f32[16,64,128]{2,1,0:T(8,128)S(1)} %dynamic-slice_bitcast_fusion), channel_id=1, source_target_pairs={{0,16},{16,0},{1,17},{17,1},{2,18},{18,2},{3,19},{19,3},{4,20},{20... | collective-permute-start | bytes 1572872 | tf_op jit(solution)/shard_map/ppermute | solution.py:19
  184.6 2.8 %collective-permute-start.43 = (f32[2,64,128]{2,1,0:T(8,128)S(1)}, f32[2,64,128]{2,1,0:T(8,128)S(1)}, u32[]{:S(2)}, u32[]{:S(2)}) collective-permute-start(f32[2,64,128]{2,1,0:T(8,128)S(1)} %dynamic-slice_bitcast_fusion.1), channel_id=1, source_target_pairs={{0,16},{16,0},{1,17},{17,1},{2,18},{18,2},{3,19},{19,3},{4,20},{20... | collective-permute-start | bytes 196616 | tf_op jit(solution)/shard_map/ppermute | solution.py:19
  (1 other events, 1.1 us)

commit v4 on v3

--- a/solution.py
+++ b/solution.py
@@ -9,6 +9,8 @@
 ALL = ("y", "core", "z", "x")
 COLS = 384
 BLOCKS = 16
+KEPT = 5
+SPLIT = 16
 
 
 def shift(x, axis, by):
@@ -23,29 +25,31 @@
     return lax.dot_general(left, right, (dims, ((), ())), preferred_element_type=jnp.float32)
 
 
-def gather_plane(own):
+def after(x, *others):
+    return lax.optimization_barrier((x, *others))[0]
+
+
+def gather_and_apply(own, x):
     half = own.shape[0] // 2
-    xp, xm, zp, zm = lax.optimization_barrier(
-        (shift(own, "x", 1), shift(own, "x", 3), shift(own, "z", 1), shift(own, "z", 3))
-    )
-    pp, mm, pm, mp = lax.optimization_barrier(
-        (shift(zp, "x", 1), shift(zm, "x", 3), shift(xm, "z", 1), shift(xp, "z", 3))
-    )
-    a, b, c, d = lax.optimization_barrier(
-        (shift(mp, "x", 1), shift(pm, "x", 3), shift(pp, "z", 1), shift(mm, "z", 3))
-    )
-    far_x, far_z, low, high = lax.optimization_barrier(
-        (shift(xp, "x", 1), shift(zp, "z", 1), shift(d[:half], "x", 3), shift(a[half:], "z", 3))
-    )
-    return [own, xp, xm, zp, zm], [pp, mm, pm, mp], [a, b, c, d], [far_x, far_z, (low, high)]
+    xp, xm, zp, zm = (shift(own, "x", 1), shift(own, "x", 3), shift(own, "z", 1), shift(own, "z", 3))
+    first = down_first(x, [own, xp, xm, zp, zm], keep=True)
+    pp, mm, pm, mp = (shift(zp, "x", 1), shift(zm, "x", 3), shift(xm, "z", 1), shift(xp, "z", 3))
+    pp, mm, pm, mp = (after(block, first[2]) for block in (pp, mm, pm, mp))
+    a, b, c, d = (shift(mp, "x", 1), shift(pm, "x", 3), shift(pp, "z", 1), shift(mm, "z", 3))
+    second = down_first(x, [pp, mm, pm, mp])
+    far_x, far_z, low, high = (shift(xp, "x", 1), shift(zp, "z", 1), shift(d[:half], "x", 3), shift(a[half:], "z", 3))
+    third = down_first(x, [a, b, c, d])
+    fourth = down_first(x, [far_x, far_z, (low, high)])
+    blocks = [first[3], pp, mm, pm, mp, a, b, c, d, far_x, far_z, low, high]
+    return blocks, [first[:3], second, third, fourth]
 
 
 VMEM = pl.BlockSpec(memory_space=pltpu.VMEM)
 
 
-def down_kernel(counts, x_ref, *refs):
+def down_kernel(counts, keep, x_ref, *refs):
     total = sum(counts)
-    mine_ref, theirs_ref, square_ref = refs[total:]
+    mine_ref, theirs_ref, square_ref = refs[total : total + 3]
     square = jnp.zeros((8, 128), jnp.float32)
     at, x = 0, x_ref[...]
     for i, count in enumerate(counts):
@@ -53,6 +57,8 @@
         part = 0.0
         for j in range(count):
             block = refs[at][...]
+            if keep:
+                refs[-1][at] = block
             at += 1
             part += f32_dot(x[:, j * step : (j + 1) * step], block, ((1,), (0,)))
             wide = block.astype(jnp.float32)
@@ -63,17 +69,20 @@
     square_ref[...] = square
 
 
-def down_first(x, blocks):
+def down_first(x, blocks, keep=False):
     blocks = [b if isinstance(b, tuple) else (b,) for b in blocks]
     counts = [len(b) for b in blocks]
     flat = [piece for b in blocks for piece in b]
     n = len(blocks) * COLS
+    out_shape = [jax.ShapeDtypeStruct((64, n), jnp.float32)] * 2 + [jax.ShapeDtypeStruct((8, 128), jnp.float32)]
+    if keep:
+        out_shape.append(jax.ShapeDtypeStruct((len(flat), *flat[0].shape), jnp.bfloat16))
     return pl.pallas_call(
-        lambda *refs: down_kernel(counts, *refs),
-        out_shape=[jax.ShapeDtypeStruct((64, n), jnp.float32)] * 2 + [jax.ShapeDtypeStruct((8, 128), jnp.float32)],
+        lambda *refs: down_kernel(counts, keep, *refs),
+        out_shape=out_shape,
         in_specs=[VMEM] * (1 + len(flat)),
-        out_specs=[VMEM] * 3,
-        compiler_params=pltpu.CompilerParams(vmem_limit_bytes=16 * 2**20),
+        out_specs=[VMEM] * len(out_shape),
+        compiler_params=pltpu.CompilerParams(vmem_limit_bytes=12 * 2**20),
         cost_estimate=pl.CostEstimate(
             flops=2 * x.size * n, bytes_accessed=2 * x.shape[1] * n, transcendentals=0
         ),
@@ -106,42 +115,61 @@
     return mine + [other_core(m) for m in mine], square
 
 
-def apply_kernel(down, square_ref, *refs):
-    t_refs, theta_refs, outs = refs[:8], refs[8 : 9 + BLOCKS], refs[9 + BLOCKS :]
+def apply_kernel(down, widths, square_ref, *refs):
+    pieces = 8 * len(widths)
+    t_refs, (kept_ref, *theta_refs) = refs[:pieces], refs[pieces : pieces + BLOCKS - KEPT + 2]
+    outs, t_ref = list(refs[pieces + BLOCKS - KEPT + 2 : -1]), refs[-1]
     rows = theta_refs[0].shape[0]
-    scale = ORDER / (4.0 * jnp.sum(square_ref[...]))
+    at = 0
+    for i, width in enumerate(widths):
+        for j in range(8):
+            t_ref[16 * j : 16 * j + 16, at : at + width] = t_refs[8 * i + j][...]
+        at += width
 
     def theta(i):
+        if i < KEPT:
+            return kept_ref[i]
         if i < BLOCKS - 1:
-            return theta_refs[i][...]
-        return jnp.concatenate([theta_refs[i][...], theta_refs[i + 1][...]])
-
+            return theta_refs[i - KEPT][...]
+        return jnp.concatenate([theta_refs[-2][...], theta_refs[-1][...]])
+
+    if not down:
+        order_ref, *outs = outs
     total = jnp.zeros((128, rows), jnp.float32)
     for i in range(BLOCKS):
-        t = jnp.concatenate([ref[:, i * COLS : (i + 1) * COLS] for ref in t_refs])
-        total += f32_dot(t, theta(i), ((1,), (1,)))
+        total += f32_dot(t_ref[:, i * COLS : (i + 1) * COLS], theta(i), ((1,), (1,)))
+    scale = ORDER / (4.0 * jnp.sum(square_ref[...]))
     x = (total * scale).astype(jnp.bfloat16)
     if not down:
-        outs[0][...] = x
+        subspace = f32_dot(x, order_ref[...], ((0,), (0,))).astype(jnp.bfloat16)
+        outs[0][...] = subspace
+        for i in range(4):
+            outs[1][i] = subspace
+        outs[2][...] = f32_dot(order_ref[...], x, ((0,), (0,))).astype(jnp.bfloat16)
         return
     for i in range(BLOCKS):
         part = f32_dot(x, theta(i), ((1,), (0,)))
-        outs[0][:, i * COLS : (i + 1) * COLS] = part[:64]
-        outs[1][:, i * COLS : (i + 1) * COLS] = part[64:]
-
-
-def apply(square, t, blocks, down):
-    n, rows = t[0].shape[1], blocks[0].shape[0]
+        which, at = (0, i) if i < SPLIT else (1, i - SPLIT)
+        outs[2 * which][:, at * COLS : (at + 1) * COLS] = part[:64]
+        outs[2 * which + 1][:, at * COLS : (at + 1) * COLS] = part[64:]
+
+
+def apply(square, t, blocks, order=None):
+    widths = [piece.shape[1] for piece in t[::8]]
+    n, rows = sum(widths), blocks[1].shape[0]
+    down = order is None
     if down:
-        out_shape = [jax.ShapeDtypeStruct((64, n), jnp.float32)] * 2
+        out_shape = [jax.ShapeDtypeStruct((64, k * COLS), jnp.float32) for k in (SPLIT, BLOCKS - SPLIT) for _ in range(2) if k]
     else:
-        out_shape = [jax.ShapeDtypeStruct((128, rows), jnp.bfloat16)]
+        out_shape = [jax.ShapeDtypeStruct(shape, jnp.bfloat16) for shape in ((rows, 128), (4, rows, 128), (128, rows))]
+        blocks = [*blocks, order]
     return pl.pallas_call(
-        lambda *refs: apply_kernel(down, *refs),
+        lambda *refs: apply_kernel(down, widths, *refs),
         out_shape=out_shape,
         in_specs=[VMEM] * (1 + len(t) + len(blocks)),
         out_specs=[VMEM] * len(out_shape),
-        compiler_params=pltpu.CompilerParams(vmem_limit_bytes=16 * 2**20),
+        scratch_shapes=[pltpu.VMEM((128, n), jnp.bfloat16)],
+        compiler_params=pltpu.CompilerParams(vmem_limit_bytes=12 * 2**20),
         cost_estimate=pl.CostEstimate(
             flops=(4 if down else 2) * 128 * n * rows, bytes_accessed=2 * n * rows, transcendentals=0
         ),
@@ -161,20 +189,15 @@
     order = column_order(y, core)
     x = f32_dot(order, basis, ((1,), (1,))).astype(jnp.bfloat16)
 
-    blocks, half, square = [], [], 0.0
-    for step in gather_plane(theta):
-        mine, theirs, squares = down_first(x, step)
-        half.append(core_sum(mine, theirs))
-        square = square + squares
-        blocks += step
-    blocks = blocks[:-1] + list(blocks[-1])
+    blocks, steps = gather_and_apply(theta, x)
+    half = [core_sum(mine, theirs) for mine, theirs, _ in steps]
+    square = sum(squares for _, _, squares in steps)
     t, square = sum_over_y(half, square + other_core(square))
-    t, _ = sum_over_y([core_sum(*apply(square, t, blocks, True))])
-    (x,) = apply(square, t, blocks, False)
-    subspace = f32_dot(x, order, ((0,), (0,))).astype(jnp.bfloat16)
+    t, _ = sum_over_y([core_sum(*apply(square, t, blocks))])
+    subspace, copies, turned = apply(square, t, blocks, order)
 
     along_x = lax.all_gather(subspace, "x", axis=0)
-    along_z = lax.all_to_all(jnp.broadcast_to(subspace[None], (4, *subspace.shape)), "z", 0, 0)
+    along_z = lax.all_to_all(copies, "z", 0, 0)
     part = jnp.einsum("brn,arm->bamn", along_z, along_x, preferred_element_type=jnp.float32)
     part = part.reshape(4, 4, 2, 64, 128).transpose(2, 0, 1, 3, 4).reshape(2, 16, 64, 128)
     keep = lax.dynamic_index_in_dim(part, core, 0, keepdims=False)

time: 188 us -> 182 us (0.968)
  waiting for transfers between devices: 66.1 us -> 61.5 us
    ppermute x28, waiting for transfers between devices: 55.5 us -> 52.6 us  [shift(): return lax.ppermute(x, axis, [(i, (i + by) % 4) for i in range(4)])]
  transfers between devices with their start and end apart: 45 -> 45, of which waited for: 22 -> 22; matrix products, arithmetic and copies ran while one was open for 0% -> 1% of each run, Pallas kernels for 2% -> 2%
where the time goes in v4:
time: 182 us
  starting transfers between devices  72.4 us (40%)
  waiting for transfers between devices  61.5 us (34%)
  blocking collectives  27.7 us (15%)
  Pallas kernels  14.7 us (8%)
  local copies, waits for them, and re-layouts  2.25 us (1%)
    ppermute x28, waiting for transfers between devices, shift(): return lax.ppermute(x, axis, [(i, (i + by) % 4) for i in range(4)])  52.6 us
    ppermute x28, starting transfers between devices, shift(): return lax.ppermute(x, axis, [(i, (i + by) % 4) for i in range(4)])  35.6 us
    ppermute x16, starting transfers between devices, other_core(): return lax.ppermute(x, 'core', [(0, 1), (1, 0)])  33.2 us
    all_to_all x1, blocking collectives, per_device(): got = lax.all_to_all(half, ('y', 'x'), 0, 0).reshape(4, 4, 64, 128)  15.4 us
    all_gather x1, blocking collectives, per_device(): along_x = lax.all_gather(subspace, 'x', axis=0)  12.3 us
    pallas_call x2, Pallas kernels, apply(): pl.pallas_call(lambda *refs: apply_kernel(down, widths, *refs), out_shape...  10.6 us
    ppermute x16, waiting for transfers between devices, other_core(): return lax.ppermute(x, 'core', [(0, 1), (1, 0)])  8.88 us
    pallas_call x4, Pallas kernels, down_first(): pl.pallas_call(lambda *refs: down_kernel(counts, keep, *refs), out_shape=...  4.15 us
  transfers between devices with their start and end apart: 45, of which 22 were waited for; matrix products, arithmetic and copies ran while one was open for 1% of the time, Pallas kernels for 2%

profile of v4, /device:TPU:1, one launch (start us, length us, event | category | flops | bytes accessed | tf_op | source)
XLA Modules:
  0.0 181.5 jit_solution(16245683698491232282)
XLA Ops:
  0.6 2.1 %collective-permute-start = (bf16[768,384]{1,0:T(8,128)(2,1)}, bf16[768,384]{1,0:T(8,128)(2,1)S(1)}, u32[]{:S(2)}, u32[]{:S(2)}) collective-permute-start(bf16[768,384]{1,0:T(8,128)(2,1)} %refs_1_.1), channel_id=1, source_target_pairs={{0,1},{1,2},{2,3},{3,0},{4,5},{5,6},{6,7},{7,4},{8,9},{9,10},{10,1... | collective-permute-start | bytes 1769480 | tf_op jit(solution)/shard_map/ppermute | solution.py:17
  2.8 3.8 %collective-permute-start.3 = (bf16[768,384]{1,0:T(8,128)(2,1)}, bf16[768,384]{1,0:T(8,128)(2,1)}, u32[]{:S(2)}, u32[]{:S(2)}) collective-permute-start(bf16[768,384]{1,0:T(8,128)(2,1)} %refs_1_.1), channel_id=1, source_target_pairs={{0,12},{4,0},{8,4},{12,8},{1,13},{5,1},{9,5},{13,9},{2,14},{6,2},{... | collective-permute-start | bytes 1769480 | tf_op jit(solution)/shard_map/ppermute | solution.py:17
  6.5 1.5 collective-permute-start.1
  8.0 9.0 %collective-permute-done.refs_2_ = bf16[768,384]{1,0:T(8,128)(2,1)S(1)} collective-permute-done((bf16[768,384]{1,0:T(8,128)(2,1)}, bf16[768,384]{1,0:T(8,128)(2,1)S(1)}, u32[]{:S(2)}, u32[]{:S(2)}) %collective-permute-start) | collective-permute-done | bytes 589856 | tf_op jit(solution)/shard_map/ppermute | solution.py:17
  16.9 4.1 %collective-permute-start.7 = (bf16[768,384]{1,0:T(8,128)(2,1)S(1)}, bf16[768,384]{1,0:T(8,128)(2,1)S(1)}, u32[]{:S(2)}, u32[]{:S(2)}) collective-permute-start(bf16[768,384]{1,0:T(8,128)(2,1)S(1)} %collective-permute-done.refs_2_), channel_id=1, source_target_pairs={{0,12},{4,0},{8,4},{12,8},{1,13},{5,1},{9,5},{13,9},{2,14},{6,2},{... | collective-permute-start | bytes 1769480 | tf_op jit(solution)/shard_map/ppermute | solution.py:17
  21.0 1.3 collective-permute-start.5
  23.3 1.1 copy-done.1
  24.3 2.3 %shard_map.41 = (f32[64,1920]{1,0:T(8,128)S(1)}, f32[64,1920]{1,0:T(8,128)S(1)}, f32[8,128]{1,0:T(8,128)S(1)}, bf16[5,768,384]{2,1,0:T(8,128)(2,1)S(1)}) custom-call(bf16[128,768]{1,0:T(8,128)(2,1)S(1)} %convolution_convert_fusion.refs_0_, bf16[768,384]{1,0:T(8,128)(2,1)S(1)} %copy-done.1, bf16[768,384]{1,0:T(8,128)(2,1)S(1)} %collective-permute-done.refs_2_, ...), custom_call_target="tpu_custom_call" | custom-call | flops 377487360 | bytes 2949120 | tf_op jit(solution)/shard_map/pallas_call | solution.py:80
  26.6 5.6 %collective-permute-done.7.refs_4_.refs_13_ = bf16[768,384]{1,0:T(8,128)(2,1)S(1)} collective-permute-done((bf16[768,384]{1,0:T(8,128)(2,1)S(1)}, bf16[768,384]{1,0:T(8,128)(2,1)S(1)}, u32[]{:S(2)}, u32[]{:S(2)}) %collective-permute-start.7) | collective-permute-done | bytes 589856 | tf_op jit(solution)/shard_map/ppermute | solution.py:17
  32.2 2.1 %collective-permute-done.5.refs_2_.refs_11_ = bf16[768,384]{1,0:T(8,128)(2,1)S(1)} collective-permute-done((bf16[768,384]{1,0:T(8,128)(2,1)}, bf16[768,384]{1,0:T(8,128)(2,1)S(1)}, u32[]{:S(2)}, u32[]{:S(2)}) %collective-permute-start.5) | collective-permute-done | bytes 589856 | tf_op jit(solution)/shard_map/ppermute | solution.py:17
  34.3 1.3 collective-permute-start.11
  35.6 2.9 %collective-permute-start.17 = (f32[64,1920]{1,0:T(8,128)S(1)}, f32[64,1920]{1,0:T(8,128)S(1)}, u32[]{:S(2)}, u32[]{:S(2)}) collective-permute-start(f32[64,1920]{1,0:T(8,128)S(1)} %get-tuple-element.38), channel_id=1, source_target_pairs={{0,16},{16,0},{1,17},{17,1},{2,18},{18,2},{3,19},{19,3},{4,20},{20... | collective-permute-start | bytes 1474568 | tf_op jit(solution)/shard_map/ppermute | solution.py:21
  39.4 3.3 %collective-permute-start.18 = (f32[64,1536]{1,0:T(8,128)S(1)}, f32[64,1536]{1,0:T(8,128)S(1)}, u32[]{:S(2)}, u32[]{:S(2)}) collective-permute-start(f32[64,1536]{1,0:T(8,128)S(1)} %get-tuple-element.40), channel_id=1, source_target_pairs={{0,16},{16,0},{1,17},{17,1},{2,18},{18,2},{3,19},{19,3},{4,20},{20... | collective-permute-start | bytes 1179656 | tf_op jit(solution)/shard_map/ppermute | solution.py:21
  42.9 6.3 %collective-permute-done.8.refs_1_.refs_14_ = bf16[768,384]{1,0:T(8,128)(2,1)S(1)} collective-permute-done((bf16[768,384]{1,0:T(8,128)(2,1)S(1)}, bf16[768,384]{1,0:T(8,128)(2,1)S(1)}, u32[]{:S(2)}, u32[]{:S(2)}) %collective-permute-start.8) | collective-permute-done | bytes 589856 | tf_op jit(solution)/shard_map/ppermute | solution.py:17
  49.3 2.7 %collective-permute-start.15 = (bf16[384,384]{1,0:T(8,128)(2,1)S(1)}, bf16[384,384]{1,0:T(8,128)(2,1)S(1)}, u32[]{:S(2)}, u32[]{:S(2)}) collective-permute-start(bf16[384,384]{1,0:T(8,128)(2,1)S(1)} %slice.114), channel_id=1, source_target_pairs={{0,12},{4,0},{8,4},{12,8},{1,13},{5,1},{9,5},{13,9},{2,14},{6,2},{... | collective-permute-start | bytes 884744 | tf_op jit(solution)/shard_map/ppermute | solution.py:17
  52.1 5.1 %collective-permute-start.14 = (bf16[384,384]{1,0:T(8,128)(2,1)S(1)}, bf16[384,384]{1,0:T(8,128)(2,1)S(1)}, u32[]{:S(2)}, u32[]{:S(2)}) collective-permute-start(bf16[384,384]{1,0:T(8,128)(2,1)S(1)} %slice.113), channel_id=1, source_target_pairs={{0,3},{1,0},{2,1},{3,2},{4,7},{5,4},{6,5},{7,6},{8,11},{9,8},{10,9... | collective-permute-start | bytes 884744 | tf_op jit(solution)/shard_map/ppermute | solution.py:17
  58.3 4.0 %collective-permute-done.12.refs_1_.refs_18_ = bf16[768,384]{1,0:T(8,128)(2,1)S(1)} collective-permute-done((bf16[768,384]{1,0:T(8,128)(2,1)S(1)}, bf16[768,384]{1,0:T(8,128)(2,1)S(1)}, u32[]{:S(2)}, u32[]{:S(2)}) %collective-permute-start.12) | collective-permute-done | bytes 589856 | tf_op jit(solution)/shard_map/ppermute | solution.py:17
  62.3 3.7 %collective-permute-done.13.refs_2_.refs_19_ = bf16[768,384]{1,0:T(8,128)(2,1)S(1)} collective-permute-done((bf16[768,384]{1,0:T(8,128)(2,1)}, bf16[768,384]{1,0:T(8,128)(2,1)S(1)}, u32[]{:S(2)}, u32[]{:S(2)}) %collective-permute-start.13) | collective-permute-done | bytes 589856 | tf_op jit(solution)/shard_map/ppermute | solution.py:17
  66.6 2.2 %collective-permute-start.16 = (f32[8,128]{1,0:T(8,128)S(1)}, f32[8,128]{1,0:T(8,128)S(1)}, u32[]{:S(2)}, u32[]{:S(2)}) collective-permute-start(f32[8,128]{1,0:T(8,128)S(1)} %add_add_fusion), channel_id=1, source_target_pairs={{0,16},{16,0},{1,17},{17,1},{2,18},{18,2},{3,19},{19,3},{4,20},{20... | collective-permute-start | bytes 12296 | tf_op jit(solution)/shard_map/ppermute | solution.py:21
  69.6 1.0 collective-permute-done.19
  71.2 1.4 collective-permute-start.21
  72.6 1.5 collective-permute-start.22
  74.1 1.6 collective-permute-start.23
  75.7 3.4 %collective-permute-done.21 = bf16[16,6272]{1,0:T(8,128)(2,1)S(1)} collective-permute-done((bf16[16,6272]{1,0:T(8,128)(2,1)S(1)}, bf16[16,6272]{1,0:T(8,128)(2,1)S(1)}, u32[]{:S(2)}, u32[]{:S(2)}) %collective-permute-start.21) | collective-permute-done | bytes 200736 | tf_op jit(solution)/shard_map/ppermute | solution.py:17
  79.1 5.4 %collective-permute-done.23 = bf16[16,6272]{1,0:T(8,128)(2,1)S(1)} collective-permute-done((bf16[16,6272]{1,0:T(8,128)(2,1)S(1)}, bf16[16,6272]{1,0:T(8,128)(2,1)S(1)}, u32[]{:S(2)}, u32[]{:S(2)}) %collective-permute-start.23) | collective-permute-done | bytes 200736 | tf_op jit(solution)/shard_map/ppermute | solution.py:17
  84.6 1.2 collective-permute-start.24
  85.8 1.4 collective-permute-start.25
  87.1 1.8 %collective-permute-start.27 = (bf16[16,6144]{1,0:T(8,128)(2,1)S(1)}, bf16[16,6144]{1,0:T(8,128)(2,1)S(1)}, u32[]{:S(2)}, u32[]{:S(2)}) collective-permute-start(bf16[16,6144]{1,0:T(8,128)(2,1)S(1)} %fusion.7.refs_1_), channel_id=1, source_target_pairs={{0,16},{16,0},{1,17},{17,1},{2,18},{18,2},{3,19},{19,3},{4,20},{20... | collective-permute-start | bytes 589832 | tf_op jit(solution)/shard_map/ppermute | solution.py:21
  89.0 1.3 collective-permute-done.24.refs_2_
  90.3 3.3 %collective-permute-start.28 = (bf16[16,6144]{1,0:T(8,128)(2,1)S(1)}, bf16[16,6144]{1,0:T(8,128)(2,1)S(1)}, u32[]{:S(2)}, u32[]{:S(2)}) collective-permute-start(bf16[16,6144]{1,0:T(8,128)(2,1)S(1)} %collective-permute-done.24.refs_2_), channel_id=1, source_target_pairs={{0,16},{16,0},{1,17},{17,1},{2,18},{18,2},{3,19},{19,3},{4,20},{20... | collective-permute-start | bytes 589832 | tf_op jit(solution)/shard_map/ppermute | solution.py:21
  93.6 3.1 %collective-permute-start.29 = (bf16[16,6144]{1,0:T(8,128)(2,1)S(1)}, bf16[16,6144]{1,0:T(8,128)(2,1)S(1)}, u32[]{:S(2)}, u32[]{:S(2)}) collective-permute-start(bf16[16,6144]{1,0:T(8,128)(2,1)S(1)} %collective-permute-done.25.refs_3_), channel_id=1, source_target_pairs={{0,16},{16,0},{1,17},{17,1},{2,18},{18,2},{3,19},{19,3},{4,20},{20... | collective-permute-start | bytes 589832 | tf_op jit(solution)/shard_map/ppermute | solution.py:21
  97.6 1.2 collective-permute-start.30
  98.8 1.0 collective-permute-done.30.refs_8_
  99.9 6.3 %shard_map.45 = (f32[64,6144]{1,0:T(8,128)S(1)}, f32[64,6144]{1,0:T(8,128)S(1)}) custom-call(f32[8,128]{1,0:T(8,128)S(1)} %convert_add_fusion.refs_0_, bf16[16,6144]{1,0:T(8,128)(2,1)S(1)} %fusion.7.refs_1_, bf16[16,6144]{1,0:T(8,128)(2,1)S(1)} %collective-permute-done.24.refs_2_, bf16[16,6144]{1,0:T(8,128)(2,1)S(1)} %collective-permute-done.25.refs_3_, ...), custom_call_target="tpu_custom_call" | custom-call | flops 2415919104 | bytes 9437184 | tf_op jit(solution)/shard_map/pallas_call | solution.py:166
  106.7 3.0 %collective-permute-done.31 = f32[64,6144]{1,0:T(8,128)S(1)} collective-permute-done((f32[64,6144]{1,0:T(8,128)S(1)}, f32[64,6144]{1,0:T(8,128)S(1)}, u32[]{:S(2)}, u32[]{:S(2)}) %collective-permute-start.31) | collective-permute-done | bytes 1572896 | tf_op jit(solution)/shard_map/ppermute | solution.py:21
  110.1 2.7 %collective-permute-start.33 = (bf16[16,6144]{1,0:T(8,128)(2,1)S(1)}, bf16[16,6144]{1,0:T(8,128)(2,1)S(1)}, u32[]{:S(2)}, u32[]{:S(2)}) collective-permute-start(bf16[16,6144]{1,0:T(8,128)(2,1)S(1)} %get-tuple-element.61), channel_id=1, source_target_pairs={{0,96},{32,0},{64,32},{96,64},{1,97},{33,1},{65,33},{97,65},{2,98}... | collective-permute-start | bytes 589832 | tf_op jit(solution)/shard_map/ppermute | solution.py:17
  112.9 8.7 %collective-permute-done.32 = bf16[16,6144]{1,0:T(8,128)(2,1)S(1)} collective-permute-done((bf16[16,6144]{1,0:T(8,128)(2,1)S(1)}, bf16[16,6144]{1,0:T(8,128)(2,1)S(1)}, u32[]{:S(2)}, u32[]{:S(2)}) %collective-permute-start.32) | collective-permute-done | bytes 196640 | tf_op jit(solution)/shard_map/ppermute | solution.py:17
  121.7 2.4 %collective-permute-start.35 = (bf16[16,6144]{1,0:T(8,128)(2,1)S(1)}, bf16[16,6144]{1,0:T(8,128)(2,1)S(1)}, u32[]{:S(2)}, u32[]{:S(2)}) collective-permute-start(bf16[16,6144]{1,0:T(8,128)(2,1)S(1)} %fusion.4.refs_1_), channel_id=1, source_target_pairs={{0,96},{32,0},{64,32},{96,64},{1,97},{33,1},{65,33},{97,65},{2,98}... | collective-permute-start | bytes 589832 | tf_op jit(solution)/shard_map/ppermute | solution.py:17
  124.8 2.1 %collective-permute-start.38 = (bf16[16,6144]{1,0:T(8,128)(2,1)S(1)}, bf16[16,6144]{1,0:T(8,128)(2,1)S(1)}, u32[]{:S(2)}, u32[]{:S(2)}) collective-permute-start(bf16[16,6144]{1,0:T(8,128)(2,1)S(1)} %fusion.4.refs_1_), channel_id=1, source_target_pairs={{0,16},{16,0},{1,17},{17,1},{2,18},{18,2},{3,19},{19,3},{4,20},{20... | collective-permute-start | bytes 589832 | tf_op jit(solution)/shard_map/ppermute | solution.py:21
  127.8 5.7 %collective-permute-start.39 = (bf16[16,6144]{1,0:T(8,128)(2,1)S(1)}, bf16[16,6144]{1,0:T(8,128)(2,1)S(1)}, u32[]{:S(2)}, u32[]{:S(2)}) collective-permute-start(bf16[16,6144]{1,0:T(8,128)(2,1)S(1)} %collective-permute-done.35.refs_2_), channel_id=1, source_target_pairs={{0,16},{16,0},{1,17},{17,1},{2,18},{18,2},{3,19},{19,3},{4,20},{20... | collective-permute-start | bytes 589832 | tf_op jit(solution)/shard_map/ppermute | solution.py:21
  133.5 1.6 collective-permute-start.40
  137.9 4.2 %shard_map.46 = (bf16[768,128]{1,0:T(8,128)(2,1)}, bf16[4,768,128]{2,1,0:T(8,128)(2,1)}, bf16[128,768]{1,0:T(8,128)(2,1)}) custom-call(f32[8,128]{1,0:T(8,128)S(1)} %convert_add_fusion.refs_0_, bf16[16,6144]{1,0:T(8,128)(2,1)S(1)} %fusion.4.refs_1_, bf16[16,6144]{1,0:T(8,128)(2,1)S(1)} %collective-permute-done.35.refs_2_, ...), custom_call_target="tpu_custom_call" | custom-call | flops 1207959552 | bytes 9437184 | tf_op jit(solution)/shard_map/pallas_call | solution.py:166
  142.1 3.6 %all-to-all-start = ((bf16[4,768,128]{2,1,0:T(8,128)(2,1)}), bf16[4,768,128]{2,1,0:T(8,128)(2,1)S(1)}, u32[]{:S(2)}, u32[]{:S(2)}) async-start(bf16[4,768,128]{2,1,0:T(8,128)(2,1)} %get-tuple-element.55), calls=%async_computation | async-start | bytes 1572864 | tf_op jit(solution)/shard_map/all_to_all | solution.py:200
  145.8 12.3 %all-gather = bf16[3072,128]{1,0:T(8,128)(2,1)S(1)} all-gather(bf16[768,128]{1,0:T(8,128)(2,1)S(1)} %copy-done.2), channel_id=2, replica_groups=mesh['y'=4,'core'=2,'z'=4,'x'=4] {'x'}, dimensions={0}, use_global_device_ids=true | all-gather | bytes 983040 | tf_op jit(solution)/shard_map/all_gather | solution.py:199
  158.9 2.1 %collective-permute-start.42 = (f32[16,64,128]{2,1,0:T(8,128)S(1)}, f32[16,64,128]{2,1,0:T(8,128)S(1)}, u32[]{:S(2)}, u32[]{:S(2)}) collective-permute-start(f32[16,64,128]{2,1,0:T(8,128)S(1)} %dynamic-slice_bitcast_fusion), channel_id=1, source_target_pairs={{0,16},{16,0},{1,17},{17,1},{2,18},{18,2},{3,19},{19,3},{4,20},{20... | collective-permute-start | bytes 1572872 | tf_op jit(solution)/shard_map/ppermute | solution.py:21
  160.9 1.5 collective-permute-done.42
  162.5 15.4 %all_to_all.10 = f32[16,64,128]{2,1,0:T(8,128)S(1)} all-to-all(f32[16,64,128]{2,1,0:T(8,128)S(1)} %bitcast_add_fusion), channel_id=1, replica_groups=mesh['y'=4,'core'=2,'z'=4,'x'=4] {'y','x'}, dimensions={0} | all-to-all | bytes 1048576 | tf_op jit(solution)/shard_map/all_to_all | solution.py:205
  178.0 1.9 %collective-permute-start.43 = (f32[2,64,128]{2,1,0:T(8,128)S(1)}, f32[2,64,128]{2,1,0:T(8,128)S(1)}, u32[]{:S(2)}, u32[]{:S(2)}) collective-permute-start(f32[2,64,128]{2,1,0:T(8,128)S(1)} %dynamic-slice_bitcast_fusion.1), channel_id=1, source_target_pairs={{0,16},{16,0},{1,17},{17,1},{2,18},{18,2},{3,19},{19,3},{4,20},{20... | collective-permute-start | bytes 196616 | tf_op jit(solution)/shard_map/ppermute | solution.py:21
  (99 shorter events, 14.1 us)
Async XLA Ops:
  0.6 22.2 %copy-start = (bf16[768,128]{1,0:T(8,128)(2,1)S(1)}, bf16[768,128]{1,0:T(8,128)(2,1)}, u32[]{:S(2)}) copy-start(bf16[768,128]{1,0:T(8,128)(2,1)} %param.3) | copy-start | bytes 589828
  0.6 16.3 %collective-permute-start = (bf16[768,384]{1,0:T(8,128)(2,1)}, bf16[768,384]{1,0:T(8,128)(2,1)S(1)}, u32[]{:S(2)}, u32[]{:S(2)}) collective-permute-start(bf16[768,384]{1,0:T(8,128)(2,1)} %refs_1_.1), channel_id=1, source_target_pairs={{0,1},{1,2},{2,3},{3,0},{4,5},{5,6},{6,7},{7,4},{8,9},{9,10},{10,1... | collective-permute-start | bytes 1769480 | tf_op jit(solution)/shard_map/ppermute | solution.py:17
  2.8 18.3 %collective-permute-start.3 = (bf16[768,384]{1,0:T(8,128)(2,1)}, bf16[768,384]{1,0:T(8,128)(2,1)}, u32[]{:S(2)}, u32[]{:S(2)}) collective-permute-start(bf16[768,384]{1,0:T(8,128)(2,1)} %refs_1_.1), channel_id=1, source_target_pairs={{0,12},{4,0},{8,4},{12,8},{1,13},{5,1},{9,5},{13,9},{2,14},{6,2},{... | collective-permute-start | bytes 1769480 | tf_op jit(solution)/shard_map/ppermute | solution.py:17
  6.5 15.8 %collective-permute-start.2 = (bf16[768,384]{1,0:T(8,128)(2,1)}, bf16[768,384]{1,0:T(8,128)(2,1)}, u32[]{:S(2)}, u32[]{:S(2)}) collective-permute-start(bf16[768,384]{1,0:T(8,128)(2,1)} %refs_1_.1), channel_id=1, source_target_pairs={{0,4},{4,8},{8,12},{12,0},{1,5},{5,9},{9,13},{13,1},{2,6},{6,10},{... | collective-permute-start | bytes 1769480 | tf_op jit(solution)/shard_map/ppermute | solution.py:17
  6.5 16.3 %collective-permute-start.1 = (bf16[768,384]{1,0:T(8,128)(2,1)}, bf16[768,384]{1,0:T(8,128)(2,1)}, u32[]{:S(2)}, u32[]{:S(2)}) collective-permute-start(bf16[768,384]{1,0:T(8,128)(2,1)} %refs_1_.1), channel_id=1, source_target_pairs={{0,3},{1,0},{2,1},{3,2},{4,7},{5,4},{6,5},{7,6},{8,11},{9,8},{10,9... | collective-permute-start | bytes 1769480 | tf_op jit(solution)/shard_map/ppermute | solution.py:17
  16.9 15.3 %collective-permute-start.7 = (bf16[768,384]{1,0:T(8,128)(2,1)S(1)}, bf16[768,384]{1,0:T(8,128)(2,1)S(1)}, u32[]{:S(2)}, u32[]{:S(2)}) collective-permute-start(bf16[768,384]{1,0:T(8,128)(2,1)S(1)} %collective-permute-done.refs_2_), channel_id=1, source_target_pairs={{0,12},{4,0},{8,4},{12,8},{1,13},{5,1},{9,5},{13,9},{2,14},{6,2},{... | collective-permute-start | bytes 1769480 | tf_op jit(solution)/shard_map/ppermute | solution.py:17
  21.0 13.3 %collective-permute-start.5 = (bf16[768,384]{1,0:T(8,128)(2,1)}, bf16[768,384]{1,0:T(8,128)(2,1)S(1)}, u32[]{:S(2)}, u32[]{:S(2)}) collective-permute-start(bf16[768,384]{1,0:T(8,128)(2,1)} %collective-permute-done.3.refs_5_), channel_id=1, source_target_pairs={{0,3},{1,0},{2,1},{3,2},{4,7},{5,4},{6,5},{7,6},{8,11},{9,8},{10,9... | collective-permute-start | bytes 1769480 | tf_op jit(solution)/shard_map/ppermute | solution.py:17
  22.3 16.2 %collective-permute-start.4 = (bf16[768,384]{1,0:T(8,128)(2,1)}, bf16[768,384]{1,0:T(8,128)(2,1)S(1)}, u32[]{:S(2)}, u32[]{:S(2)}) collective-permute-start(bf16[768,384]{1,0:T(8,128)(2,1)} %collective-permute-done.2.refs_4_), channel_id=1, source_target_pairs={{0,1},{1,2},{2,3},{3,0},{4,5},{5,6},{6,7},{7,4},{8,9},{9,10},{10,1... | collective-permute-start | bytes 1769480 | tf_op jit(solution)/shard_map/ppermute | solution.py:17
  22.8 15.9 %collective-permute-start.6 = (bf16[768,384]{1,0:T(8,128)(2,1)}, bf16[768,384]{1,0:T(8,128)(2,1)S(1)}, u32[]{:S(2)}, u32[]{:S(2)}) collective-permute-start(bf16[768,384]{1,0:T(8,128)(2,1)} %collective-permute-done.1.refs_3_), channel_id=1, source_target_pairs={{0,4},{4,8},{8,12},{12,0},{1,5},{5,9},{9,13},{13,1},{2,6},{6,10},{... | collective-permute-start | bytes 1769480 | tf_op jit(solution)/shard_map/ppermute | solution.py:17
  23.2 1.1 copy-start.1
  32.2 17.0 %collective-permute-start.8 = (bf16[768,384]{1,0:T(8,128)(2,1)S(1)}, bf16[768,384]{1,0:T(8,128)(2,1)S(1)}, u32[]{:S(2)}, u32[]{:S(2)}) collective-permute-start(bf16[768,384]{1,0:T(8,128)(2,1)S(1)} %collective-permute-done.7.refs_4_.refs_13_), channel_id=1, source_target_pairs={{0,1},{1,2},{2,3},{3,0},{4,5},{5,6},{6,7},{7,4},{8,9},{9,10},{10,1... | collective-permute-start | bytes 1769480 | tf_op jit(solution)/shard_map/ppermute | solution.py:17
  34.3 14.9 %collective-permute-start.11 = (bf16[768,384]{1,0:T(8,128)(2,1)S(1)}, bf16[768,384]{1,0:T(8,128)(2,1)S(1)}, u32[]{:S(2)}, u32[]{:S(2)}) collective-permute-start(bf16[768,384]{1,0:T(8,128)(2,1)S(1)} %collective-permute-done.5.refs_2_.refs_11_), channel_id=1, source_target_pairs={{0,12},{4,0},{8,4},{12,8},{1,13},{5,1},{9,5},{13,9},{2,14},{6,2},{... | collective-permute-start | bytes 1769480 | tf_op jit(solution)/shard_map/ppermute | solution.py:17
  35.6 7.1 %collective-permute-start.17 = (f32[64,1920]{1,0:T(8,128)S(1)}, f32[64,1920]{1,0:T(8,128)S(1)}, u32[]{:S(2)}, u32[]{:S(2)}) collective-permute-start(f32[64,1920]{1,0:T(8,128)S(1)} %get-tuple-element.38), channel_id=1, source_target_pairs={{0,16},{16,0},{1,17},{17,1},{2,18},{18,2},{3,19},{19,3},{4,20},{20... | collective-permute-start | bytes 1474568 | tf_op jit(solution)/shard_map/ppermute | solution.py:21
  38.5 13.5 %collective-permute-start.10 = (bf16[768,384]{1,0:T(8,128)(2,1)S(1)}, bf16[768,384]{1,0:T(8,128)(2,1)S(1)}, u32[]{:S(2)}, u32[]{:S(2)}) collective-permute-start(bf16[768,384]{1,0:T(8,128)(2,1)S(1)} %collective-permute-done.4.refs_1_.refs_10_), channel_id=1, source_target_pairs={{0,4},{4,8},{8,12},{12,0},{1,5},{5,9},{9,13},{13,1},{2,6},{6,10},{... | collective-permute-start | bytes 1769480 | tf_op jit(solution)/shard_map/ppermute | solution.py:17
  39.4 10.0 %collective-permute-start.18 = (f32[64,1536]{1,0:T(8,128)S(1)}, f32[64,1536]{1,0:T(8,128)S(1)}, u32[]{:S(2)}, u32[]{:S(2)}) collective-permute-start(f32[64,1536]{1,0:T(8,128)S(1)} %get-tuple-element.40), channel_id=1, source_target_pairs={{0,16},{16,0},{1,17},{17,1},{2,18},{18,2},{3,19},{19,3},{4,20},{20... | collective-permute-start | bytes 1179656 | tf_op jit(solution)/shard_map/ppermute | solution.py:21
  42.7 14.9 %collective-permute-start.9 = (bf16[768,384]{1,0:T(8,128)(2,1)S(1)}, bf16[768,384]{1,0:T(8,128)(2,1)S(1)}, u32[]{:S(2)}, u32[]{:S(2)}) collective-permute-start(bf16[768,384]{1,0:T(8,128)(2,1)S(1)} %collective-permute-done.6.refs_3_.refs_12_), channel_id=1, source_target_pairs={{0,3},{1,0},{2,1},{3,2},{4,7},{5,4},{6,5},{7,6},{8,11},{9,8},{10,9... | collective-permute-start | bytes 1769480 | tf_op jit(solution)/shard_map/ppermute | solution.py:17
  49.2 13.1 %collective-permute-start.12 = (bf16[768,384]{1,0:T(8,128)(2,1)S(1)}, bf16[768,384]{1,0:T(8,128)(2,1)S(1)}, u32[]{:S(2)}, u32[]{:S(2)}) collective-permute-start(bf16[768,384]{1,0:T(8,128)(2,1)S(1)} %collective-permute-done.refs_2_), channel_id=1, source_target_pairs={{0,1},{1,2},{2,3},{3,0},{4,5},{5,6},{6,7},{7,4},{8,9},{9,10},{10,1... | collective-permute-start | bytes 1769480 | tf_op jit(solution)/shard_map/ppermute | solution.py:17
  49.2 16.8 %collective-permute-start.13 = (bf16[768,384]{1,0:T(8,128)(2,1)}, bf16[768,384]{1,0:T(8,128)(2,1)S(1)}, u32[]{:S(2)}, u32[]{:S(2)}) collective-permute-start(bf16[768,384]{1,0:T(8,128)(2,1)} %collective-permute-done.2.refs_4_), channel_id=1, source_target_pairs={{0,4},{4,8},{8,12},{12,0},{1,5},{5,9},{9,13},{13,1},{2,6},{6,10},{... | collective-permute-start | bytes 1769480 | tf_op jit(solution)/shard_map/ppermute | solution.py:17
  49.3 16.7 %collective-permute-start.15 = (bf16[384,384]{1,0:T(8,128)(2,1)S(1)}, bf16[384,384]{1,0:T(8,128)(2,1)S(1)}, u32[]{:S(2)}, u32[]{:S(2)}) collective-permute-start(bf16[384,384]{1,0:T(8,128)(2,1)S(1)} %slice.114), channel_id=1, source_target_pairs={{0,12},{4,0},{8,4},{12,8},{1,13},{5,1},{9,5},{13,9},{2,14},{6,2},{... | collective-permute-start | bytes 884744 | tf_op jit(solution)/shard_map/ppermute | solution.py:17
  52.1 13.9 %collective-permute-start.14 = (bf16[384,384]{1,0:T(8,128)(2,1)S(1)}, bf16[384,384]{1,0:T(8,128)(2,1)S(1)}, u32[]{:S(2)}, u32[]{:S(2)}) collective-permute-start(bf16[384,384]{1,0:T(8,128)(2,1)S(1)} %slice.113), channel_id=1, source_target_pairs={{0,3},{1,0},{2,1},{3,2},{4,7},{5,4},{6,5},{7,6},{8,11},{9,8},{10,9... | collective-permute-start | bytes 884744 | tf_op jit(solution)/shard_map/ppermute | solution.py:17
  66.6 3.0 %collective-permute-start.16 = (f32[8,128]{1,0:T(8,128)S(1)}, f32[8,128]{1,0:T(8,128)S(1)}, u32[]{:S(2)}, u32[]{:S(2)}) collective-permute-start(f32[8,128]{1,0:T(8,128)S(1)} %add_add_fusion), channel_id=1, source_target_pairs={{0,16},{16,0},{1,17},{17,1},{2,18},{18,2},{3,19},{19,3},{4,20},{20... | collective-permute-start | bytes 12296 | tf_op jit(solution)/shard_map/ppermute | solution.py:21
  68.8 1.8 collective-permute-start.19
  68.9 2.1 %collective-permute-start.20 = (f32[64,1152]{1,0:T(8,128)S(1)}, f32[64,1152]{1,0:T(8,128)S(1)}, u32[]{:S(2)}, u32[]{:S(2)}) collective-permute-start(f32[64,1152]{1,0:T(8,128)S(1)} %get-tuple-element.44), channel_id=1, source_target_pairs={{0,16},{16,0},{1,17},{17,1},{2,18},{18,2},{3,19},{19,3},{4,20},{20... | collective-permute-start | bytes 884744 | tf_op jit(solution)/shard_map/ppermute | solution.py:21
  71.2 7.9 %collective-permute-start.21 = (bf16[16,6272]{1,0:T(8,128)(2,1)S(1)}, bf16[16,6272]{1,0:T(8,128)(2,1)S(1)}, u32[]{:S(2)}, u32[]{:S(2)}) collective-permute-start(bf16[16,6272]{1,0:T(8,128)(2,1)S(1)} %get-tuple-element.65), channel_id=1, source_target_pairs={{0,32},{32,64},{64,96},{96,0},{1,33},{33,65},{65,97},{97,1},{2,34}... | collective-permute-start | bytes 602120 | tf_op jit(solution)/shard_map/ppermute | solution.py:17
  72.6 6.5 %collective-permute-start.22 = (bf16[16,6272]{1,0:T(8,128)(2,1)S(1)}, bf16[16,6272]{1,0:T(8,128)(2,1)S(1)}, u32[]{:S(2)}, u32[]{:S(2)}) collective-permute-start(bf16[16,6272]{1,0:T(8,128)(2,1)S(1)} %get-tuple-element.64), channel_id=1, source_target_pairs={{0,96},{32,0},{64,32},{96,64},{1,97},{33,1},{65,33},{97,65},{2,98}... | collective-permute-start | bytes 602120 | tf_op jit(solution)/shard_map/ppermute | solution.py:17
  74.1 10.4 %collective-permute-start.23 = (bf16[16,6272]{1,0:T(8,128)(2,1)S(1)}, bf16[16,6272]{1,0:T(8,128)(2,1)S(1)}, u32[]{:S(2)}, u32[]{:S(2)}) collective-permute-start(bf16[16,6272]{1,0:T(8,128)(2,1)S(1)} %get-tuple-element.63), channel_id=1, source_target_pairs={{0,64},{32,96},{64,0},{96,32},{1,65},{33,97},{65,1},{97,33},{2,66}... | collective-permute-start | bytes 602120 | tf_op jit(solution)/shard_map/ppermute | solution.py:17
  84.6 5.7 %collective-permute-start.24 = (bf16[16,6144]{1,0:T(8,128)(2,1)S(1)}, bf16[16,6144]{1,0:T(8,128)(2,1)S(1)}, u32[]{:S(2)}, u32[]{:S(2)}) collective-permute-start(bf16[16,6144]{1,0:T(8,128)(2,1)S(1)} %fusion.7.refs_1_), channel_id=1, source_target_pairs={{0,96},{32,0},{64,32},{96,64},{1,97},{33,1},{65,33},{97,65},{2,98}... | collective-permute-start | bytes 589832 | tf_op jit(solution)/shard_map/ppermute | solution.py:17
  85.8 7.8 %collective-permute-start.25 = (bf16[16,6144]{1,0:T(8,128)(2,1)S(1)}, bf16[16,6144]{1,0:T(8,128)(2,1)S(1)}, u32[]{:S(2)}, u32[]{:S(2)}) collective-permute-start(bf16[16,6144]{1,0:T(8,128)(2,1)S(1)} %fusion.7.refs_1_), channel_id=1, source_target_pairs={{0,64},{32,96},{64,0},{96,32},{1,65},{33,97},{65,1},{97,33},{2,66}... | collective-permute-start | bytes 589832 | tf_op jit(solution)/shard_map/ppermute | solution.py:17
  87.1 10.4 %collective-permute-start.26 = (bf16[16,6144]{1,0:T(8,128)(2,1)S(1)}, bf16[16,6144]{1,0:T(8,128)(2,1)S(1)}, u32[]{:S(2)}, u32[]{:S(2)}) collective-permute-start(bf16[16,6144]{1,0:T(8,128)(2,1)S(1)} %fusion.7.refs_1_), channel_id=1, source_target_pairs={{0,32},{32,64},{64,96},{96,0},{1,33},{33,65},{65,97},{97,1},{2,34}... | collective-permute-start | bytes 589832 | tf_op jit(solution)/shard_map/ppermute | solution.py:17
  87.1 11.7 %collective-permute-start.27 = (bf16[16,6144]{1,0:T(8,128)(2,1)S(1)}, bf16[16,6144]{1,0:T(8,128)(2,1)S(1)}, u32[]{:S(2)}, u32[]{:S(2)}) collective-permute-start(bf16[16,6144]{1,0:T(8,128)(2,1)S(1)} %fusion.7.refs_1_), channel_id=1, source_target_pairs={{0,16},{16,0},{1,17},{17,1},{2,18},{18,2},{3,19},{19,3},{4,20},{20... | collective-permute-start | bytes 589832 | tf_op jit(solution)/shard_map/ppermute | solution.py:21
  90.3 8.6 %collective-permute-start.28 = (bf16[16,6144]{1,0:T(8,128)(2,1)S(1)}, bf16[16,6144]{1,0:T(8,128)(2,1)S(1)}, u32[]{:S(2)}, u32[]{:S(2)}) collective-permute-start(bf16[16,6144]{1,0:T(8,128)(2,1)S(1)} %collective-permute-done.24.refs_2_), channel_id=1, source_target_pairs={{0,16},{16,0},{1,17},{17,1},{2,18},{18,2},{3,19},{19,3},{4,20},{20... | collective-permute-start | bytes 589832 | tf_op jit(solution)/shard_map/ppermute | solution.py:21
  93.6 5.2 %collective-permute-start.29 = (bf16[16,6144]{1,0:T(8,128)(2,1)S(1)}, bf16[16,6144]{1,0:T(8,128)(2,1)S(1)}, u32[]{:S(2)}, u32[]{:S(2)}) collective-permute-start(bf16[16,6144]{1,0:T(8,128)(2,1)S(1)} %collective-permute-done.25.refs_3_), channel_id=1, source_target_pairs={{0,16},{16,0},{1,17},{17,1},{2,18},{18,2},{3,19},{19,3},{4,20},{20... | collective-permute-start | bytes 589832 | tf_op jit(solution)/shard_map/ppermute | solution.py:21
  97.6 2.3 %collective-permute-start.30 = (bf16[16,6144]{1,0:T(8,128)(2,1)S(1)}, bf16[16,6144]{1,0:T(8,128)(2,1)S(1)}, u32[]{:S(2)}, u32[]{:S(2)}) collective-permute-start(bf16[16,6144]{1,0:T(8,128)(2,1)S(1)} %collective-permute-done.26.refs_4_), channel_id=1, source_target_pairs={{0,16},{16,0},{1,17},{17,1},{2,18},{18,2},{3,19},{19,3},{4,20},{20... | collective-permute-start | bytes 589832 | tf_op jit(solution)/shard_map/ppermute | solution.py:21
  106.2 3.5 %collective-permute-start.31 = (f32[64,6144]{1,0:T(8,128)S(1)}, f32[64,6144]{1,0:T(8,128)S(1)}, u32[]{:S(2)}, u32[]{:S(2)}) collective-permute-start(f32[64,6144]{1,0:T(8,128)S(1)} %get-tuple-element.50), channel_id=1, source_target_pairs={{0,16},{16,0},{1,17},{17,1},{2,18},{18,2},{3,19},{19,3},{4,20},{20... | collective-permute-start | bytes 4718600 | tf_op jit(solution)/shard_map/ppermute | solution.py:21
  110.0 11.6 %collective-permute-start.32 = (bf16[16,6144]{1,0:T(8,128)(2,1)S(1)}, bf16[16,6144]{1,0:T(8,128)(2,1)S(1)}, u32[]{:S(2)}, u32[]{:S(2)}) collective-permute-start(bf16[16,6144]{1,0:T(8,128)(2,1)S(1)} %get-tuple-element.62), channel_id=1, source_target_pairs={{0,32},{32,64},{64,96},{96,0},{1,33},{33,65},{65,97},{97,1},{2,34}... | collective-permute-start | bytes 589832 | tf_op jit(solution)/shard_map/ppermute | solution.py:17
  110.1 11.5 %collective-permute-start.33 = (bf16[16,6144]{1,0:T(8,128)(2,1)S(1)}, bf16[16,6144]{1,0:T(8,128)(2,1)S(1)}, u32[]{:S(2)}, u32[]{:S(2)}) collective-permute-start(bf16[16,6144]{1,0:T(8,128)(2,1)S(1)} %get-tuple-element.61), channel_id=1, source_target_pairs={{0,96},{32,0},{64,32},{96,64},{1,97},{33,1},{65,33},{97,65},{2,98}... | collective-permute-start | bytes 589832 | tf_op jit(solution)/shard_map/ppermute | solution.py:17
  112.7 8.9 %collective-permute-start.34 = (bf16[16,6144]{1,0:T(8,128)(2,1)S(1)}, bf16[16,6144]{1,0:T(8,128)(2,1)S(1)}, u32[]{:S(2)}, u32[]{:S(2)}) collective-permute-start(bf16[16,6144]{1,0:T(8,128)(2,1)S(1)} %get-tuple-element.60), channel_id=1, source_target_pairs={{0,64},{32,96},{64,0},{96,32},{1,65},{33,97},{65,1},{97,33},{2,66}... | collective-permute-start | bytes 589832 | tf_op jit(solution)/shard_map/ppermute | solution.py:17
  121.7 6.1 %collective-permute-start.35 = (bf16[16,6144]{1,0:T(8,128)(2,1)S(1)}, bf16[16,6144]{1,0:T(8,128)(2,1)S(1)}, u32[]{:S(2)}, u32[]{:S(2)}) collective-permute-start(bf16[16,6144]{1,0:T(8,128)(2,1)S(1)} %fusion.4.refs_1_), channel_id=1, source_target_pairs={{0,96},{32,0},{64,32},{96,64},{1,97},{33,1},{65,33},{97,65},{2,98}... | collective-permute-start | bytes 589832 | tf_op jit(solution)/shard_map/ppermute | solution.py:17
  124.1 9.4 %collective-permute-start.36 = (bf16[16,6144]{1,0:T(8,128)(2,1)S(1)}, bf16[16,6144]{1,0:T(8,128)(2,1)S(1)}, u32[]{:S(2)}, u32[]{:S(2)}) collective-permute-start(bf16[16,6144]{1,0:T(8,128)(2,1)S(1)} %fusion.4.refs_1_), channel_id=1, source_target_pairs={{0,64},{32,96},{64,0},{96,32},{1,65},{33,97},{65,1},{97,33},{2,66}... | collective-permute-start | bytes 589832 | tf_op jit(solution)/shard_map/ppermute | solution.py:17
  124.1 11.9 %collective-permute-start.37 = (bf16[16,6144]{1,0:T(8,128)(2,1)S(1)}, bf16[16,6144]{1,0:T(8,128)(2,1)S(1)}, u32[]{:S(2)}, u32[]{:S(2)}) collective-permute-start(bf16[16,6144]{1,0:T(8,128)(2,1)S(1)} %fusion.4.refs_1_), channel_id=1, source_target_pairs={{0,32},{32,64},{64,96},{96,0},{1,33},{33,65},{65,97},{97,1},{2,34}... | collective-permute-start | bytes 589832 | tf_op jit(solution)/shard_map/ppermute | solution.py:17
  124.8 12.3 %collective-permute-start.38 = (bf16[16,6144]{1,0:T(8,128)(2,1)S(1)}, bf16[16,6144]{1,0:T(8,128)(2,1)S(1)}, u32[]{:S(2)}, u32[]{:S(2)}) collective-permute-start(bf16[16,6144]{1,0:T(8,128)(2,1)S(1)} %fusion.4.refs_1_), channel_id=1, source_target_pairs={{0,16},{16,0},{1,17},{17,1},{2,18},{18,2},{3,19},{19,3},{4,20},{20... | collective-permute-start | bytes 589832 | tf_op jit(solution)/shard_map/ppermute | solution.py:21
  127.8 9.3 %collective-permute-start.39 = (bf16[16,6144]{1,0:T(8,128)(2,1)S(1)}, bf16[16,6144]{1,0:T(8,128)(2,1)S(1)}, u32[]{:S(2)}, u32[]{:S(2)}) collective-permute-start(bf16[16,6144]{1,0:T(8,128)(2,1)S(1)} %collective-permute-done.35.refs_2_), channel_id=1, source_target_pairs={{0,16},{16,0},{1,17},{17,1},{2,18},{18,2},{3,19},{19,3},{4,20},{20... | collective-permute-start | bytes 589832 | tf_op jit(solution)/shard_map/ppermute | solution.py:21
  133.5 3.6 %collective-permute-start.40 = (bf16[16,6144]{1,0:T(8,128)(2,1)S(1)}, bf16[16,6144]{1,0:T(8,128)(2,1)S(1)}, u32[]{:S(2)}, u32[]{:S(2)}) collective-permute-start(bf16[16,6144]{1,0:T(8,128)(2,1)S(1)} %collective-permute-done.36.refs_3_), channel_id=1, source_target_pairs={{0,16},{16,0},{1,17},{17,1},{2,18},{18,2},{3,19},{19,3},{4,20},{20... | collective-permute-start | bytes 589832 | tf_op jit(solution)/shard_map/ppermute | solution.py:21
  136.0 1.9 %collective-permute-start.41 = (bf16[16,6144]{1,0:T(8,128)(2,1)S(1)}, bf16[16,6144]{1,0:T(8,128)(2,1)S(1)}, u32[]{:S(2)}, u32[]{:S(2)}) collective-permute-start(bf16[16,6144]{1,0:T(8,128)(2,1)S(1)} %collective-permute-done.37.refs_4_), channel_id=1, source_target_pairs={{0,16},{16,0},{1,17},{17,1},{2,18},{18,2},{3,19},{19,3},{4,20},{20... | collective-permute-start | bytes 589832 | tf_op jit(solution)/shard_map/ppermute | solution.py:21
  142.1 3.6 %copy-start.2 = (bf16[768,128]{1,0:T(8,128)(2,1)S(1)}, bf16[768,128]{1,0:T(8,128)(2,1)}, u32[]{:S(2)}) copy-start(bf16[768,128]{1,0:T(8,128)(2,1)} %get-tuple-element.27) | copy-start | bytes 589828
  142.1 16.0 %all-to-all-start = ((bf16[4,768,128]{2,1,0:T(8,128)(2,1)}), bf16[4,768,128]{2,1,0:T(8,128)(2,1)S(1)}, u32[]{:S(2)}, u32[]{:S(2)}) async-start(bf16[4,768,128]{2,1,0:T(8,128)(2,1)} %get-tuple-element.55), calls=%async_computation | async-start | bytes 1572864 | tf_op jit(solution)/shard_map/all_to_all | solution.py:200
  158.9 3.6 %collective-permute-start.42 = (f32[16,64,128]{2,1,0:T(8,128)S(1)}, f32[16,64,128]{2,1,0:T(8,128)S(1)}, u32[]{:S(2)}, u32[]{:S(2)}) collective-permute-start(f32[16,64,128]{2,1,0:T(8,128)S(1)} %dynamic-slice_bitcast_fusion), channel_id=1, source_target_pairs={{0,16},{16,0},{1,17},{17,1},{2,18},{18,2},{3,19},{19,3},{4,20},{20... | collective-permute-start | bytes 1572872 | tf_op jit(solution)/shard_map/ppermute | solution.py:21
  178.0 2.8 %collective-permute-start.43 = (f32[2,64,128]{2,1,0:T(8,128)S(1)}, f32[2,64,128]{2,1,0:T(8,128)S(1)}, u32[]{:S(2)}, u32[]{:S(2)}) collective-permute-start(f32[2,64,128]{2,1,0:T(8,128)S(1)} %dynamic-slice_bitcast_fusion.1), channel_id=1, source_target_pairs={{0,16},{16,0},{1,17},{17,1},{2,18},{18,2},{3,19},{19,3},{4,20},{20... | collective-permute-start | bytes 196616 | tf_op jit(solution)/shard_map/ppermute | solution.py:21

commit v5 on v4

--- a/solution.py
+++ b/solution.py
@@ -135,18 +135,18 @@
 
     if not down:
         order_ref, *outs = outs
-    total = jnp.zeros((128, rows), jnp.float32)
+    total = jnp.zeros((rows, 128), jnp.float32)
     for i in range(BLOCKS):
-        total += f32_dot(t_ref[:, i * COLS : (i + 1) * COLS], theta(i), ((1,), (1,)))
+        total += f32_dot(theta(i), t_ref[:, i * COLS : (i + 1) * COLS], ((1,), (1,)))
     scale = ORDER / (4.0 * jnp.sum(square_ref[...]))
     x = (total * scale).astype(jnp.bfloat16)
     if not down:
-        subspace = f32_dot(x, order_ref[...], ((0,), (0,))).astype(jnp.bfloat16)
+        subspace = f32_dot(x, order_ref[...], ((1,), (0,))).astype(jnp.bfloat16)
         outs[0][...] = subspace
         for i in range(4):
             outs[1][i] = subspace
-        outs[2][...] = f32_dot(order_ref[...], x, ((0,), (0,))).astype(jnp.bfloat16)
         return
+    x = x.T
     for i in range(BLOCKS):
         part = f32_dot(x, theta(i), ((1,), (0,)))
         which, at = (0, i) if i < SPLIT else (1, i - SPLIT)
@@ -161,7 +161,7 @@
     if down:
         out_shape = [jax.ShapeDtypeStruct((64, k * COLS), jnp.float32) for k in (SPLIT, BLOCKS - SPLIT) for _ in range(2) if k]
     else:
-        out_shape = [jax.ShapeDtypeStruct(shape, jnp.bfloat16) for shape in ((rows, 128), (4, rows, 128), (128, rows))]
+        out_shape = [jax.ShapeDtypeStruct(shape, jnp.bfloat16) for shape in ((rows, 128), (4, rows, 128))]
         blocks = [*blocks, order]
     return pl.pallas_call(
         lambda *refs: apply_kernel(down, widths, *refs),
@@ -194,7 +194,7 @@
     square = sum(squares for _, _, squares in steps)
     t, square = sum_over_y(half, square + other_core(square))
     t, _ = sum_over_y([core_sum(*apply(square, t, blocks))])
-    subspace, copies, turned = apply(square, t, blocks, order)
+    subspace, copies = apply(square, t, blocks, order)
 
     along_x = lax.all_gather(subspace, "x", axis=0)
     along_z = lax.all_to_all(copies, "z", 0, 0)
@@ -202,7 +202,7 @@
     part = part.reshape(4, 4, 2, 64, 128).transpose(2, 0, 1, 3, 4).reshape(2, 16, 64, 128)
     keep = lax.dynamic_index_in_dim(part, core, 0, keepdims=False)
     half = keep + other_core(lax.dynamic_index_in_dim(part, 1 - core, 0, keepdims=False))
-    got = lax.all_to_all(half, ("y", "x"), 0, 0).reshape(4, 4, 64, 128)
+    got = lax.all_to_all(half.astype(jnp.bfloat16), ("y", "x"), 0, 0).astype(jnp.float32).reshape(4, 4, 64, 128)
     sums = jnp.sum(got, axis=0).reshape(2, 2, 64, 128)
     keep = lax.dynamic_index_in_dim(sums, core, 0, keepdims=False)
     theirs = other_core(lax.dynamic_index_in_dim(sums, 1 - core, 0, keepdims=False))

time: 182 us -> 177 us (0.973)
  blocking collectives: 27.7 us -> 25.1 us
  Pallas kernels: 14.7 us -> 12.8 us
    all_to_all x1, blocking collectives: 15.4 us -> 12.8 us  [per_device(): lax.all_to_all(half.astype(jnp.bfloat16), ('y', 'x'), 0, 0)]
    pallas_call x2, Pallas kernels: 10.6 us -> 8.66 us  [apply(): pl.pallas_call(lambda *refs: apply_kernel(down, widths, *refs), out_shape...]
where the time goes in v5:
time: 177 us
  starting transfers between devices  72.2 us (41%)
  waiting for transfers between devices  61.5 us (35%)
  blocking collectives  25.1 us (14%)
  Pallas kernels  12.8 us (7%)
  local copies, waits for them, and re-layouts  2.25 us (1%)
    ppermute x28, waiting for transfers between devices, shift(): return lax.ppermute(x, axis, [(i, (i + by) % 4) for i in range(4)])  52.6 us
    ppermute x28, starting transfers between devices, shift(): return lax.ppermute(x, axis, [(i, (i + by) % 4) for i in range(4)])  35.6 us
    ppermute x16, starting transfers between devices, other_core(): return lax.ppermute(x, 'core', [(0, 1), (1, 0)])  32.9 us
    all_to_all x1, blocking collectives, per_device(): lax.all_to_all(half.astype(jnp.bfloat16), ('y', 'x'), 0, 0)  12.8 us
    all_gather x1, blocking collectives, per_device(): along_x = lax.all_gather(subspace, 'x', axis=0)  12.3 us
    ppermute x16, waiting for transfers between devices, other_core(): return lax.ppermute(x, 'core', [(0, 1), (1, 0)])  8.89 us
    pallas_call x2, Pallas kernels, apply(): pl.pallas_call(lambda *refs: apply_kernel(down, widths, *refs), out_shape...  8.66 us
    pallas_call x4, Pallas kernels, down_first(): pl.pallas_call(lambda *refs: down_kernel(counts, keep, *refs), out_shape=...  4.15 us
  transfers between devices with their start and end apart: 45, of which 22 were waited for; matrix products, arithmetic and copies ran while one was open for 1% of the time, Pallas kernels for 2%

profile of v5, /device:TPU:1, one launch (start us, length us, event | category | flops | bytes accessed | tf_op | source)
XLA Modules:
  0.0 176.8 jit_solution(5705642678287973855)
XLA Ops:
  0.6 2.1 %collective-permute-start = (bf16[768,384]{1,0:T(8,128)(2,1)}, bf16[768,384]{1,0:T(8,128)(2,1)S(1)}, u32[]{:S(2)}, u32[]{:S(2)}) collective-permute-start(bf16[768,384]{1,0:T(8,128)(2,1)} %refs_1_.1), channel_id=1, source_target_pairs={{0,1},{1,2},{2,3},{3,0},{4,5},{5,6},{6,7},{7,4},{8,9},{9,10},{10,1... | collective-permute-start | bytes 1769480 | tf_op jit(solution)/shard_map/ppermute | solution.py:17
  2.8 3.8 %collective-permute-start.3 = (bf16[768,384]{1,0:T(8,128)(2,1)}, bf16[768,384]{1,0:T(8,128)(2,1)}, u32[]{:S(2)}, u32[]{:S(2)}) collective-permute-start(bf16[768,384]{1,0:T(8,128)(2,1)} %refs_1_.1), channel_id=1, source_target_pairs={{0,12},{4,0},{8,4},{12,8},{1,13},{5,1},{9,5},{13,9},{2,14},{6,2},{... | collective-permute-start | bytes 1769480 | tf_op jit(solution)/shard_map/ppermute | solution.py:17
  6.5 1.5 collective-permute-start.1
  8.0 9.0 %collective-permute-done.refs_2_ = bf16[768,384]{1,0:T(8,128)(2,1)S(1)} collective-permute-done((bf16[768,384]{1,0:T(8,128)(2,1)}, bf16[768,384]{1,0:T(8,128)(2,1)S(1)}, u32[]{:S(2)}, u32[]{:S(2)}) %collective-permute-start) | collective-permute-done | bytes 589856 | tf_op jit(solution)/shard_map/ppermute | solution.py:17
  16.9 4.1 %collective-permute-start.7 = (bf16[768,384]{1,0:T(8,128)(2,1)S(1)}, bf16[768,384]{1,0:T(8,128)(2,1)S(1)}, u32[]{:S(2)}, u32[]{:S(2)}) collective-permute-start(bf16[768,384]{1,0:T(8,128)(2,1)S(1)} %collective-permute-done.refs_2_), channel_id=1, source_target_pairs={{0,12},{4,0},{8,4},{12,8},{1,13},{5,1},{9,5},{13,9},{2,14},{6,2},{... | collective-permute-start | bytes 1769480 | tf_op jit(solution)/shard_map/ppermute | solution.py:17
  21.0 1.3 collective-permute-start.5
  23.3 1.1 copy-done.1
  24.3 2.3 %shard_map.41 = (f32[64,1920]{1,0:T(8,128)S(1)}, f32[64,1920]{1,0:T(8,128)S(1)}, f32[8,128]{1,0:T(8,128)S(1)}, bf16[5,768,384]{2,1,0:T(8,128)(2,1)S(1)}) custom-call(bf16[128,768]{1,0:T(8,128)(2,1)S(1)} %convolution_convert_fusion.refs_0_, bf16[768,384]{1,0:T(8,128)(2,1)S(1)} %copy-done.1, bf16[768,384]{1,0:T(8,128)(2,1)S(1)} %collective-permute-done.refs_2_, ...), custom_call_target="tpu_custom_call" | custom-call | flops 377487360 | bytes 2949120 | tf_op jit(solution)/shard_map/pallas_call | solution.py:80
  26.6 5.6 %collective-permute-done.7.refs_4_.refs_13_ = bf16[768,384]{1,0:T(8,128)(2,1)S(1)} collective-permute-done((bf16[768,384]{1,0:T(8,128)(2,1)S(1)}, bf16[768,384]{1,0:T(8,128)(2,1)S(1)}, u32[]{:S(2)}, u32[]{:S(2)}) %collective-permute-start.7) | collective-permute-done | bytes 589856 | tf_op jit(solution)/shard_map/ppermute | solution.py:17
  32.2 2.1 %collective-permute-done.5.refs_2_.refs_11_ = bf16[768,384]{1,0:T(8,128)(2,1)S(1)} collective-permute-done((bf16[768,384]{1,0:T(8,128)(2,1)}, bf16[768,384]{1,0:T(8,128)(2,1)S(1)}, u32[]{:S(2)}, u32[]{:S(2)}) %collective-permute-start.5) | collective-permute-done | bytes 589856 | tf_op jit(solution)/shard_map/ppermute | solution.py:17
  34.3 1.3 collective-permute-start.11
  35.6 2.9 %collective-permute-start.17 = (f32[64,1920]{1,0:T(8,128)S(1)}, f32[64,1920]{1,0:T(8,128)S(1)}, u32[]{:S(2)}, u32[]{:S(2)}) collective-permute-start(f32[64,1920]{1,0:T(8,128)S(1)} %get-tuple-element.38), channel_id=1, source_target_pairs={{0,16},{16,0},{1,17},{17,1},{2,18},{18,2},{3,19},{19,3},{4,20},{20... | collective-permute-start | bytes 1474568 | tf_op jit(solution)/shard_map/ppermute | solution.py:21
  39.4 3.3 %collective-permute-start.18 = (f32[64,1536]{1,0:T(8,128)S(1)}, f32[64,1536]{1,0:T(8,128)S(1)}, u32[]{:S(2)}, u32[]{:S(2)}) collective-permute-start(f32[64,1536]{1,0:T(8,128)S(1)} %get-tuple-element.40), channel_id=1, source_target_pairs={{0,16},{16,0},{1,17},{17,1},{2,18},{18,2},{3,19},{19,3},{4,20},{20... | collective-permute-start | bytes 1179656 | tf_op jit(solution)/shard_map/ppermute | solution.py:21
  42.9 6.3 %collective-permute-done.8.refs_1_.refs_14_ = bf16[768,384]{1,0:T(8,128)(2,1)S(1)} collective-permute-done((bf16[768,384]{1,0:T(8,128)(2,1)S(1)}, bf16[768,384]{1,0:T(8,128)(2,1)S(1)}, u32[]{:S(2)}, u32[]{:S(2)}) %collective-permute-start.8) | collective-permute-done | bytes 589856 | tf_op jit(solution)/shard_map/ppermute | solution.py:17
  49.3 2.7 %collective-permute-start.15 = (bf16[384,384]{1,0:T(8,128)(2,1)S(1)}, bf16[384,384]{1,0:T(8,128)(2,1)S(1)}, u32[]{:S(2)}, u32[]{:S(2)}) collective-permute-start(bf16[384,384]{1,0:T(8,128)(2,1)S(1)} %slice.114), channel_id=1, source_target_pairs={{0,12},{4,0},{8,4},{12,8},{1,13},{5,1},{9,5},{13,9},{2,14},{6,2},{... | collective-permute-start | bytes 884744 | tf_op jit(solution)/shard_map/ppermute | solution.py:17
  52.1 5.1 %collective-permute-start.14 = (bf16[384,384]{1,0:T(8,128)(2,1)S(1)}, bf16[384,384]{1,0:T(8,128)(2,1)S(1)}, u32[]{:S(2)}, u32[]{:S(2)}) collective-permute-start(bf16[384,384]{1,0:T(8,128)(2,1)S(1)} %slice.113), channel_id=1, source_target_pairs={{0,3},{1,0},{2,1},{3,2},{4,7},{5,4},{6,5},{7,6},{8,11},{9,8},{10,9... | collective-permute-start | bytes 884744 | tf_op jit(solution)/shard_map/ppermute | solution.py:17
  58.3 4.0 %collective-permute-done.12.refs_1_.refs_18_ = bf16[768,384]{1,0:T(8,128)(2,1)S(1)} collective-permute-done((bf16[768,384]{1,0:T(8,128)(2,1)S(1)}, bf16[768,384]{1,0:T(8,128)(2,1)S(1)}, u32[]{:S(2)}, u32[]{:S(2)}) %collective-permute-start.12) | collective-permute-done | bytes 589856 | tf_op jit(solution)/shard_map/ppermute | solution.py:17
  62.3 3.7 %collective-permute-done.13.refs_2_.refs_19_ = bf16[768,384]{1,0:T(8,128)(2,1)S(1)} collective-permute-done((bf16[768,384]{1,0:T(8,128)(2,1)}, bf16[768,384]{1,0:T(8,128)(2,1)S(1)}, u32[]{:S(2)}, u32[]{:S(2)}) %collective-permute-start.13) | collective-permute-done | bytes 589856 | tf_op jit(solution)/shard_map/ppermute | solution.py:17
  66.6 2.2 %collective-permute-start.16 = (f32[8,128]{1,0:T(8,128)S(1)}, f32[8,128]{1,0:T(8,128)S(1)}, u32[]{:S(2)}, u32[]{:S(2)}) collective-permute-start(f32[8,128]{1,0:T(8,128)S(1)} %add_add_fusion), channel_id=1, source_target_pairs={{0,16},{16,0},{1,17},{17,1},{2,18},{18,2},{3,19},{19,3},{4,20},{20... | collective-permute-start | bytes 12296 | tf_op jit(solution)/shard_map/ppermute | solution.py:21
  69.6 1.0 collective-permute-done.19
  71.2 1.4 collective-permute-start.21
  72.6 1.5 collective-permute-start.22
  74.1 1.6 collective-permute-start.23
  75.7 3.4 %collective-permute-done.21 = bf16[16,6272]{1,0:T(8,128)(2,1)S(1)} collective-permute-done((bf16[16,6272]{1,0:T(8,128)(2,1)S(1)}, bf16[16,6272]{1,0:T(8,128)(2,1)S(1)}, u32[]{:S(2)}, u32[]{:S(2)}) %collective-permute-start.21) | collective-permute-done | bytes 200736 | tf_op jit(solution)/shard_map/ppermute | solution.py:17
  79.1 5.4 %collective-permute-done.23 = bf16[16,6272]{1,0:T(8,128)(2,1)S(1)} collective-permute-done((bf16[16,6272]{1,0:T(8,128)(2,1)S(1)}, bf16[16,6272]{1,0:T(8,128)(2,1)S(1)}, u32[]{:S(2)}, u32[]{:S(2)}) %collective-permute-start.23) | collective-permute-done | bytes 200736 | tf_op jit(solution)/shard_map/ppermute | solution.py:17
  84.6 1.2 collective-permute-start.24
  85.8 1.4 collective-permute-start.25
  87.1 1.8 %collective-permute-start.27 = (bf16[16,6144]{1,0:T(8,128)(2,1)S(1)}, bf16[16,6144]{1,0:T(8,128)(2,1)S(1)}, u32[]{:S(2)}, u32[]{:S(2)}) collective-permute-start(bf16[16,6144]{1,0:T(8,128)(2,1)S(1)} %fusion.8.refs_1_), channel_id=1, source_target_pairs={{0,16},{16,0},{1,17},{17,1},{2,18},{18,2},{3,19},{19,3},{4,20},{20... | collective-permute-start | bytes 589832 | tf_op jit(solution)/shard_map/ppermute | solution.py:21
  89.0 1.3 collective-permute-done.24.refs_2_
  90.3 3.3 %collective-permute-start.28 = (bf16[16,6144]{1,0:T(8,128)(2,1)S(1)}, bf16[16,6144]{1,0:T(8,128)(2,1)S(1)}, u32[]{:S(2)}, u32[]{:S(2)}) collective-permute-start(bf16[16,6144]{1,0:T(8,128)(2,1)S(1)} %collective-permute-done.24.refs_2_), channel_id=1, source_target_pairs={{0,16},{16,0},{1,17},{17,1},{2,18},{18,2},{3,19},{19,3},{4,20},{20... | collective-permute-start | bytes 589832 | tf_op jit(solution)/shard_map/ppermute | solution.py:21
  93.6 3.1 %collective-permute-start.29 = (bf16[16,6144]{1,0:T(8,128)(2,1)S(1)}, bf16[16,6144]{1,0:T(8,128)(2,1)S(1)}, u32[]{:S(2)}, u32[]{:S(2)}) collective-permute-start(bf16[16,6144]{1,0:T(8,128)(2,1)S(1)} %collective-permute-done.25.refs_3_), channel_id=1, source_target_pairs={{0,16},{16,0},{1,17},{17,1},{2,18},{18,2},{3,19},{19,3},{4,20},{20... | collective-permute-start | bytes 589832 | tf_op jit(solution)/shard_map/ppermute | solution.py:21
  97.6 1.2 collective-permute-start.30
  98.8 1.0 collective-permute-done.30.refs_8_
  99.9 4.7 %shard_map.45 = (f32[64,6144]{1,0:T(8,128)S(1)}, f32[64,6144]{1,0:T(8,128)S(1)}) custom-call(f32[8,128]{1,0:T(8,128)S(1)} %convert_add_fusion.refs_0_, bf16[16,6144]{1,0:T(8,128)(2,1)S(1)} %fusion.8.refs_1_, bf16[16,6144]{1,0:T(8,128)(2,1)S(1)} %collective-permute-done.24.refs_2_, bf16[16,6144]{1,0:T(8,128)(2,1)S(1)} %collective-permute-done.25.refs_3_, ...), custom_call_target="tpu_custom_call" | custom-call | flops 2415919104 | bytes 9437184 | tf_op jit(solution)/shard_map/pallas_call | solution.py:166
  105.0 3.0 %collective-permute-done.31 = f32[64,6144]{1,0:T(8,128)S(1)} collective-permute-done((f32[64,6144]{1,0:T(8,128)S(1)}, f32[64,6144]{1,0:T(8,128)S(1)}, u32[]{:S(2)}, u32[]{:S(2)}) %collective-permute-start.31) | collective-permute-done | bytes 1572896 | tf_op jit(solution)/shard_map/ppermute | solution.py:21
  108.4 2.7 %collective-permute-start.33 = (bf16[16,6144]{1,0:T(8,128)(2,1)S(1)}, bf16[16,6144]{1,0:T(8,128)(2,1)S(1)}, u32[]{:S(2)}, u32[]{:S(2)}) collective-permute-start(bf16[16,6144]{1,0:T(8,128)(2,1)S(1)} %get-tuple-element.61), channel_id=1, source_target_pairs={{0,96},{32,0},{64,32},{96,64},{1,97},{33,1},{65,33},{97,65},{2,98}... | collective-permute-start | bytes 589832 | tf_op jit(solution)/shard_map/ppermute | solution.py:17
  111.2 8.7 %collective-permute-done.32 = bf16[16,6144]{1,0:T(8,128)(2,1)S(1)} collective-permute-done((bf16[16,6144]{1,0:T(8,128)(2,1)S(1)}, bf16[16,6144]{1,0:T(8,128)(2,1)S(1)}, u32[]{:S(2)}, u32[]{:S(2)}) %collective-permute-start.32) | collective-permute-done | bytes 196640 | tf_op jit(solution)/shard_map/ppermute | solution.py:17
  120.0 2.4 %collective-permute-start.35 = (bf16[16,6144]{1,0:T(8,128)(2,1)S(1)}, bf16[16,6144]{1,0:T(8,128)(2,1)S(1)}, u32[]{:S(2)}, u32[]{:S(2)}) collective-permute-start(bf16[16,6144]{1,0:T(8,128)(2,1)S(1)} %fusion.5.refs_1_), channel_id=1, source_target_pairs={{0,96},{32,0},{64,32},{96,64},{1,97},{33,1},{65,33},{97,65},{2,98}... | collective-permute-start | bytes 589832 | tf_op jit(solution)/shard_map/ppermute | solution.py:17
  123.1 2.1 %collective-permute-start.38 = (bf16[16,6144]{1,0:T(8,128)(2,1)S(1)}, bf16[16,6144]{1,0:T(8,128)(2,1)S(1)}, u32[]{:S(2)}, u32[]{:S(2)}) collective-permute-start(bf16[16,6144]{1,0:T(8,128)(2,1)S(1)} %fusion.5.refs_1_), channel_id=1, source_target_pairs={{0,16},{16,0},{1,17},{17,1},{2,18},{18,2},{3,19},{19,3},{4,20},{20... | collective-permute-start | bytes 589832 | tf_op jit(solution)/shard_map/ppermute | solution.py:21
  126.1 5.7 %collective-permute-start.39 = (bf16[16,6144]{1,0:T(8,128)(2,1)S(1)}, bf16[16,6144]{1,0:T(8,128)(2,1)S(1)}, u32[]{:S(2)}, u32[]{:S(2)}) collective-permute-start(bf16[16,6144]{1,0:T(8,128)(2,1)S(1)} %collective-permute-done.35.refs_2_), channel_id=1, source_target_pairs={{0,16},{16,0},{1,17},{17,1},{2,18},{18,2},{3,19},{19,3},{4,20},{20... | collective-permute-start | bytes 589832 | tf_op jit(solution)/shard_map/ppermute | solution.py:21
  131.8 1.6 collective-permute-start.40
  136.3 4.0 %shard_map.46 = (bf16[768,128]{1,0:T(8,128)(2,1)}, bf16[4,768,128]{2,1,0:T(8,128)(2,1)}) custom-call(f32[8,128]{1,0:T(8,128)S(1)} %convert_add_fusion.refs_0_, bf16[16,6144]{1,0:T(8,128)(2,1)S(1)} %fusion.5.refs_1_, bf16[16,6144]{1,0:T(8,128)(2,1)S(1)} %collective-permute-done.35.refs_2_, bf16[16,6144]{1,0:T(8,128)(2,1)S(1)} %collective-permute-done.36.refs_3_, ...), custom_call_target="tpu_custom_call" | custom-call | flops 1207959552 | bytes 9437184 | tf_op jit(solution)/shard_map/pallas_call | solution.py:166
  140.3 3.6 %all-to-all-start = ((bf16[4,768,128]{2,1,0:T(8,128)(2,1)}), bf16[4,768,128]{2,1,0:T(8,128)(2,1)S(1)}, u32[]{:S(2)}, u32[]{:S(2)}) async-start(bf16[4,768,128]{2,1,0:T(8,128)(2,1)} %get-tuple-element.55), calls=%async_computation | async-start | bytes 1572864 | tf_op jit(solution)/shard_map/all_to_all | solution.py:200
  143.9 12.3 %all-gather = bf16[3072,128]{1,0:T(8,128)(2,1)S(1)} all-gather(bf16[768,128]{1,0:T(8,128)(2,1)S(1)} %copy-done.2), channel_id=2, replica_groups=mesh['y'=4,'core'=2,'z'=4,'x'=4] {'x'}, dimensions={0}, use_global_device_ids=true | all-gather | bytes 983040 | tf_op jit(solution)/shard_map/all_gather | solution.py:199
  157.0 2.1 %collective-permute-start.42 = (f32[16,64,128]{2,1,0:T(8,128)S(1)}, f32[16,64,128]{2,1,0:T(8,128)S(1)}, u32[]{:S(2)}, u32[]{:S(2)}) collective-permute-start(f32[16,64,128]{2,1,0:T(8,128)S(1)} %dynamic-slice_bitcast_fusion), channel_id=1, source_target_pairs={{0,16},{16,0},{1,17},{17,1},{2,18},{18,2},{3,19},{19,3},{4,20},{20... | collective-permute-start | bytes 1572872 | tf_op jit(solution)/shard_map/ppermute | solution.py:21
  159.0 1.5 collective-permute-done.42
  160.7 12.8 %all_to_all.10 = bf16[16,64,128]{2,1,0:T(8,128)(2,1)S(1)} all-to-all(bf16[16,64,128]{2,1,0:T(8,128)(2,1)S(1)} %fusion.2), channel_id=1, replica_groups=mesh['y'=4,'core'=2,'z'=4,'x'=4] {'y','x'}, dimensions={0} | all-to-all | bytes 524288 | tf_op jit(solution)/shard_map/all_to_all | solution.py:205
  173.5 1.6 collective-permute-start.43
  (99 shorter events, 14.1 us)
Async XLA Ops:
  0.6 22.2 %copy-start = (bf16[768,128]{1,0:T(8,128)(2,1)S(1)}, bf16[768,128]{1,0:T(8,128)(2,1)}, u32[]{:S(2)}) copy-start(bf16[768,128]{1,0:T(8,128)(2,1)} %param.3) | copy-start | bytes 589828
  0.6 16.3 %collective-permute-start = (bf16[768,384]{1,0:T(8,128)(2,1)}, bf16[768,384]{1,0:T(8,128)(2,1)S(1)}, u32[]{:S(2)}, u32[]{:S(2)}) collective-permute-start(bf16[768,384]{1,0:T(8,128)(2,1)} %refs_1_.1), channel_id=1, source_target_pairs={{0,1},{1,2},{2,3},{3,0},{4,5},{5,6},{6,7},{7,4},{8,9},{9,10},{10,1... | collective-permute-start | bytes 1769480 | tf_op jit(solution)/shard_map/ppermute | solution.py:17
  2.8 18.3 %collective-permute-start.3 = (bf16[768,384]{1,0:T(8,128)(2,1)}, bf16[768,384]{1,0:T(8,128)(2,1)}, u32[]{:S(2)}, u32[]{:S(2)}) collective-permute-start(bf16[768,384]{1,0:T(8,128)(2,1)} %refs_1_.1), channel_id=1, source_target_pairs={{0,12},{4,0},{8,4},{12,8},{1,13},{5,1},{9,5},{13,9},{2,14},{6,2},{... | collective-permute-start | bytes 1769480 | tf_op jit(solution)/shard_map/ppermute | solution.py:17
  6.5 15.8 %collective-permute-start.2 = (bf16[768,384]{1,0:T(8,128)(2,1)}, bf16[768,384]{1,0:T(8,128)(2,1)}, u32[]{:S(2)}, u32[]{:S(2)}) collective-permute-start(bf16[768,384]{1,0:T(8,128)(2,1)} %refs_1_.1), channel_id=1, source_target_pairs={{0,4},{4,8},{8,12},{12,0},{1,5},{5,9},{9,13},{13,1},{2,6},{6,10},{... | collective-permute-start | bytes 1769480 | tf_op jit(solution)/shard_map/ppermute | solution.py:17
  6.5 16.3 %collective-permute-start.1 = (bf16[768,384]{1,0:T(8,128)(2,1)}, bf16[768,384]{1,0:T(8,128)(2,1)}, u32[]{:S(2)}, u32[]{:S(2)}) collective-permute-start(bf16[768,384]{1,0:T(8,128)(2,1)} %refs_1_.1), channel_id=1, source_target_pairs={{0,3},{1,0},{2,1},{3,2},{4,7},{5,4},{6,5},{7,6},{8,11},{9,8},{10,9... | collective-permute-start | bytes 1769480 | tf_op jit(solution)/shard_map/ppermute | solution.py:17
  16.9 15.3 %collective-permute-start.7 = (bf16[768,384]{1,0:T(8,128)(2,1)S(1)}, bf16[768,384]{1,0:T(8,128)(2,1)S(1)}, u32[]{:S(2)}, u32[]{:S(2)}) collective-permute-start(bf16[768,384]{1,0:T(8,128)(2,1)S(1)} %collective-permute-done.refs_2_), channel_id=1, source_target_pairs={{0,12},{4,0},{8,4},{12,8},{1,13},{5,1},{9,5},{13,9},{2,14},{6,2},{... | collective-permute-start | bytes 1769480 | tf_op jit(solution)/shard_map/ppermute | solution.py:17
  21.0 13.3 %collective-permute-start.5 = (bf16[768,384]{1,0:T(8,128)(2,1)}, bf16[768,384]{1,0:T(8,128)(2,1)S(1)}, u32[]{:S(2)}, u32[]{:S(2)}) collective-permute-start(bf16[768,384]{1,0:T(8,128)(2,1)} %collective-permute-done.3.refs_5_), channel_id=1, source_target_pairs={{0,3},{1,0},{2,1},{3,2},{4,7},{5,4},{6,5},{7,6},{8,11},{9,8},{10,9... | collective-permute-start | bytes 1769480 | tf_op jit(solution)/shard_map/ppermute | solution.py:17
  22.3 16.2 %collective-permute-start.4 = (bf16[768,384]{1,0:T(8,128)(2,1)}, bf16[768,384]{1,0:T(8,128)(2,1)S(1)}, u32[]{:S(2)}, u32[]{:S(2)}) collective-permute-start(bf16[768,384]{1,0:T(8,128)(2,1)} %collective-permute-done.2.refs_4_), channel_id=1, source_target_pairs={{0,1},{1,2},{2,3},{3,0},{4,5},{5,6},{6,7},{7,4},{8,9},{9,10},{10,1... | collective-permute-start | bytes 1769480 | tf_op jit(solution)/shard_map/ppermute | solution.py:17
  22.8 15.9 %collective-permute-start.6 = (bf16[768,384]{1,0:T(8,128)(2,1)}, bf16[768,384]{1,0:T(8,128)(2,1)S(1)}, u32[]{:S(2)}, u32[]{:S(2)}) collective-permute-start(bf16[768,384]{1,0:T(8,128)(2,1)} %collective-permute-done.1.refs_3_), channel_id=1, source_target_pairs={{0,4},{4,8},{8,12},{12,0},{1,5},{5,9},{9,13},{13,1},{2,6},{6,10},{... | collective-permute-start | bytes 1769480 | tf_op jit(solution)/shard_map/ppermute | solution.py:17
  23.2 1.1 copy-start.1
  32.2 17.0 %collective-permute-start.8 = (bf16[768,384]{1,0:T(8,128)(2,1)S(1)}, bf16[768,384]{1,0:T(8,128)(2,1)S(1)}, u32[]{:S(2)}, u32[]{:S(2)}) collective-permute-start(bf16[768,384]{1,0:T(8,128)(2,1)S(1)} %collective-permute-done.7.refs_4_.refs_13_), channel_id=1, source_target_pairs={{0,1},{1,2},{2,3},{3,0},{4,5},{5,6},{6,7},{7,4},{8,9},{9,10},{10,1... | collective-permute-start | bytes 1769480 | tf_op jit(solution)/shard_map/ppermute | solution.py:17
  34.3 14.9 %collective-permute-start.11 = (bf16[768,384]{1,0:T(8,128)(2,1)S(1)}, bf16[768,384]{1,0:T(8,128)(2,1)S(1)}, u32[]{:S(2)}, u32[]{:S(2)}) collective-permute-start(bf16[768,384]{1,0:T(8,128)(2,1)S(1)} %collective-permute-done.5.refs_2_.refs_11_), channel_id=1, source_target_pairs={{0,12},{4,0},{8,4},{12,8},{1,13},{5,1},{9,5},{13,9},{2,14},{6,2},{... | collective-permute-start | bytes 1769480 | tf_op jit(solution)/shard_map/ppermute | solution.py:17
  35.6 7.1 %collective-permute-start.17 = (f32[64,1920]{1,0:T(8,128)S(1)}, f32[64,1920]{1,0:T(8,128)S(1)}, u32[]{:S(2)}, u32[]{:S(2)}) collective-permute-start(f32[64,1920]{1,0:T(8,128)S(1)} %get-tuple-element.38), channel_id=1, source_target_pairs={{0,16},{16,0},{1,17},{17,1},{2,18},{18,2},{3,19},{19,3},{4,20},{20... | collective-permute-start | bytes 1474568 | tf_op jit(solution)/shard_map/ppermute | solution.py:21
  38.5 13.5 %collective-permute-start.10 = (bf16[768,384]{1,0:T(8,128)(2,1)S(1)}, bf16[768,384]{1,0:T(8,128)(2,1)S(1)}, u32[]{:S(2)}, u32[]{:S(2)}) collective-permute-start(bf16[768,384]{1,0:T(8,128)(2,1)S(1)} %collective-permute-done.4.refs_1_.refs_10_), channel_id=1, source_target_pairs={{0,4},{4,8},{8,12},{12,0},{1,5},{5,9},{9,13},{13,1},{2,6},{6,10},{... | collective-permute-start | bytes 1769480 | tf_op jit(solution)/shard_map/ppermute | solution.py:17
  39.4 10.0 %collective-permute-start.18 = (f32[64,1536]{1,0:T(8,128)S(1)}, f32[64,1536]{1,0:T(8,128)S(1)}, u32[]{:S(2)}, u32[]{:S(2)}) collective-permute-start(f32[64,1536]{1,0:T(8,128)S(1)} %get-tuple-element.40), channel_id=1, source_target_pairs={{0,16},{16,0},{1,17},{17,1},{2,18},{18,2},{3,19},{19,3},{4,20},{20... | collective-permute-start | bytes 1179656 | tf_op jit(solution)/shard_map/ppermute | solution.py:21
  42.7 14.9 %collective-permute-start.9 = (bf16[768,384]{1,0:T(8,128)(2,1)S(1)}, bf16[768,384]{1,0:T(8,128)(2,1)S(1)}, u32[]{:S(2)}, u32[]{:S(2)}) collective-permute-start(bf16[768,384]{1,0:T(8,128)(2,1)S(1)} %collective-permute-done.6.refs_3_.refs_12_), channel_id=1, source_target_pairs={{0,3},{1,0},{2,1},{3,2},{4,7},{5,4},{6,5},{7,6},{8,11},{9,8},{10,9... | collective-permute-start | bytes 1769480 | tf_op jit(solution)/shard_map/ppermute | solution.py:17
  49.2 13.1 %collective-permute-start.12 = (bf16[768,384]{1,0:T(8,128)(2,1)S(1)}, bf16[768,384]{1,0:T(8,128)(2,1)S(1)}, u32[]{:S(2)}, u32[]{:S(2)}) collective-permute-start(bf16[768,384]{1,0:T(8,128)(2,1)S(1)} %collective-permute-done.refs_2_), channel_id=1, source_target_pairs={{0,1},{1,2},{2,3},{3,0},{4,5},{5,6},{6,7},{7,4},{8,9},{9,10},{10,1... | collective-permute-start | bytes 1769480 | tf_op jit(solution)/shard_map/ppermute | solution.py:17
  49.2 16.8 %collective-permute-start.13 = (bf16[768,384]{1,0:T(8,128)(2,1)}, bf16[768,384]{1,0:T(8,128)(2,1)S(1)}, u32[]{:S(2)}, u32[]{:S(2)}) collective-permute-start(bf16[768,384]{1,0:T(8,128)(2,1)} %collective-permute-done.2.refs_4_), channel_id=1, source_target_pairs={{0,4},{4,8},{8,12},{12,0},{1,5},{5,9},{9,13},{13,1},{2,6},{6,10},{... | collective-permute-start | bytes 1769480 | tf_op jit(solution)/shard_map/ppermute | solution.py:17
  49.3 16.7 %collective-permute-start.15 = (bf16[384,384]{1,0:T(8,128)(2,1)S(1)}, bf16[384,384]{1,0:T(8,128)(2,1)S(1)}, u32[]{:S(2)}, u32[]{:S(2)}) collective-permute-start(bf16[384,384]{1,0:T(8,128)(2,1)S(1)} %slice.114), channel_id=1, source_target_pairs={{0,12},{4,0},{8,4},{12,8},{1,13},{5,1},{9,5},{13,9},{2,14},{6,2},{... | collective-permute-start | bytes 884744 | tf_op jit(solution)/shard_map/ppermute | solution.py:17
  52.1 13.9 %collective-permute-start.14 = (bf16[384,384]{1,0:T(8,128)(2,1)S(1)}, bf16[384,384]{1,0:T(8,128)(2,1)S(1)}, u32[]{:S(2)}, u32[]{:S(2)}) collective-permute-start(bf16[384,384]{1,0:T(8,128)(2,1)S(1)} %slice.113), channel_id=1, source_target_pairs={{0,3},{1,0},{2,1},{3,2},{4,7},{5,4},{6,5},{7,6},{8,11},{9,8},{10,9... | collective-permute-start | bytes 884744 | tf_op jit(solution)/shard_map/ppermute | solution.py:17
  66.6 3.0 %collective-permute-start.16 = (f32[8,128]{1,0:T(8,128)S(1)}, f32[8,128]{1,0:T(8,128)S(1)}, u32[]{:S(2)}, u32[]{:S(2)}) collective-permute-start(f32[8,128]{1,0:T(8,128)S(1)} %add_add_fusion), channel_id=1, source_target_pairs={{0,16},{16,0},{1,17},{17,1},{2,18},{18,2},{3,19},{19,3},{4,20},{20... | collective-permute-start | bytes 12296 | tf_op jit(solution)/shard_map/ppermute | solution.py:21
  68.8 1.8 %collective-permute-start.19 = (f32[64,1536]{1,0:T(8,128)S(1)}, f32[64,1536]{1,0:T(8,128)S(1)}, u32[]{:S(2)}, u32[]{:S(2)}) collective-permute-start(f32[64,1536]{1,0:T(8,128)S(1)} %get-tuple-element.42), channel_id=1, source_target_pairs={{0,16},{16,0},{1,17},{17,1},{2,18},{18,2},{3,19},{19,3},{4,20},{20... | collective-permute-start | bytes 1179656 | tf_op jit(solution)/shard_map/ppermute | solution.py:21
  68.9 2.1 %collective-permute-start.20 = (f32[64,1152]{1,0:T(8,128)S(1)}, f32[64,1152]{1,0:T(8,128)S(1)}, u32[]{:S(2)}, u32[]{:S(2)}) collective-permute-start(f32[64,1152]{1,0:T(8,128)S(1)} %get-tuple-element.44), channel_id=1, source_target_pairs={{0,16},{16,0},{1,17},{17,1},{2,18},{18,2},{3,19},{19,3},{4,20},{20... | collective-permute-start | bytes 884744 | tf_op jit(solution)/shard_map/ppermute | solution.py:21
  71.2 7.9 %collective-permute-start.21 = (bf16[16,6272]{1,0:T(8,128)(2,1)S(1)}, bf16[16,6272]{1,0:T(8,128)(2,1)S(1)}, u32[]{:S(2)}, u32[]{:S(2)}) collective-permute-start(bf16[16,6272]{1,0:T(8,128)(2,1)S(1)} %get-tuple-element.65), channel_id=1, source_target_pairs={{0,32},{32,64},{64,96},{96,0},{1,33},{33,65},{65,97},{97,1},{2,34}... | collective-permute-start | bytes 602120 | tf_op jit(solution)/shard_map/ppermute | solution.py:17
  72.6 6.5 %collective-permute-start.22 = (bf16[16,6272]{1,0:T(8,128)(2,1)S(1)}, bf16[16,6272]{1,0:T(8,128)(2,1)S(1)}, u32[]{:S(2)}, u32[]{:S(2)}) collective-permute-start(bf16[16,6272]{1,0:T(8,128)(2,1)S(1)} %get-tuple-element.64), channel_id=1, source_target_pairs={{0,96},{32,0},{64,32},{96,64},{1,97},{33,1},{65,33},{97,65},{2,98}... | collective-permute-start | bytes 602120 | tf_op jit(solution)/shard_map/ppermute | solution.py:17
  74.1 10.4 %collective-permute-start.23 = (bf16[16,6272]{1,0:T(8,128)(2,1)S(1)}, bf16[16,6272]{1,0:T(8,128)(2,1)S(1)}, u32[]{:S(2)}, u32[]{:S(2)}) collective-permute-start(bf16[16,6272]{1,0:T(8,128)(2,1)S(1)} %get-tuple-element.63), channel_id=1, source_target_pairs={{0,64},{32,96},{64,0},{96,32},{1,65},{33,97},{65,1},{97,33},{2,66}... | collective-permute-start | bytes 602120 | tf_op jit(solution)/shard_map/ppermute | solution.py:17
  84.6 5.7 %collective-permute-start.24 = (bf16[16,6144]{1,0:T(8,128)(2,1)S(1)}, bf16[16,6144]{1,0:T(8,128)(2,1)S(1)}, u32[]{:S(2)}, u32[]{:S(2)}) collective-permute-start(bf16[16,6144]{1,0:T(8,128)(2,1)S(1)} %fusion.8.refs_1_), channel_id=1, source_target_pairs={{0,96},{32,0},{64,32},{96,64},{1,97},{33,1},{65,33},{97,65},{2,98}... | collective-permute-start | bytes 589832 | tf_op jit(solution)/shard_map/ppermute | solution.py:17
  85.8 7.8 %collective-permute-start.25 = (bf16[16,6144]{1,0:T(8,128)(2,1)S(1)}, bf16[16,6144]{1,0:T(8,128)(2,1)S(1)}, u32[]{:S(2)}, u32[]{:S(2)}) collective-permute-start(bf16[16,6144]{1,0:T(8,128)(2,1)S(1)} %fusion.8.refs_1_), channel_id=1, source_target_pairs={{0,64},{32,96},{64,0},{96,32},{1,65},{33,97},{65,1},{97,33},{2,66}... | collective-permute-start | bytes 589832 | tf_op jit(solution)/shard_map/ppermute | solution.py:17
  87.1 10.4 %collective-permute-start.26 = (bf16[16,6144]{1,0:T(8,128)(2,1)S(1)}, bf16[16,6144]{1,0:T(8,128)(2,1)S(1)}, u32[]{:S(2)}, u32[]{:S(2)}) collective-permute-start(bf16[16,6144]{1,0:T(8,128)(2,1)S(1)} %fusion.8.refs_1_), channel_id=1, source_target_pairs={{0,32},{32,64},{64,96},{96,0},{1,33},{33,65},{65,97},{97,1},{2,34}... | collective-permute-start | bytes 589832 | tf_op jit(solution)/shard_map/ppermute | solution.py:17
  87.1 11.7 %collective-permute-start.27 = (bf16[16,6144]{1,0:T(8,128)(2,1)S(1)}, bf16[16,6144]{1,0:T(8,128)(2,1)S(1)}, u32[]{:S(2)}, u32[]{:S(2)}) collective-permute-start(bf16[16,6144]{1,0:T(8,128)(2,1)S(1)} %fusion.8.refs_1_), channel_id=1, source_target_pairs={{0,16},{16,0},{1,17},{17,1},{2,18},{18,2},{3,19},{19,3},{4,20},{20... | collective-permute-start | bytes 589832 | tf_op jit(solution)/shard_map/ppermute | solution.py:21
  90.3 8.6 %collective-permute-start.28 = (bf16[16,6144]{1,0:T(8,128)(2,1)S(1)}, bf16[16,6144]{1,0:T(8,128)(2,1)S(1)}, u32[]{:S(2)}, u32[]{:S(2)}) collective-permute-start(bf16[16,6144]{1,0:T(8,128)(2,1)S(1)} %collective-permute-done.24.refs_2_), channel_id=1, source_target_pairs={{0,16},{16,0},{1,17},{17,1},{2,18},{18,2},{3,19},{19,3},{4,20},{20... | collective-permute-start | bytes 589832 | tf_op jit(solution)/shard_map/ppermute | solution.py:21
  93.6 5.2 %collective-permute-start.29 = (bf16[16,6144]{1,0:T(8,128)(2,1)S(1)}, bf16[16,6144]{1,0:T(8,128)(2,1)S(1)}, u32[]{:S(2)}, u32[]{:S(2)}) collective-permute-start(bf16[16,6144]{1,0:T(8,128)(2,1)S(1)} %collective-permute-done.25.refs_3_), channel_id=1, source_target_pairs={{0,16},{16,0},{1,17},{17,1},{2,18},{18,2},{3,19},{19,3},{4,20},{20... | collective-permute-start | bytes 589832 | tf_op jit(solution)/shard_map/ppermute | solution.py:21
  97.6 2.3 %collective-permute-start.30 = (bf16[16,6144]{1,0:T(8,128)(2,1)S(1)}, bf16[16,6144]{1,0:T(8,128)(2,1)S(1)}, u32[]{:S(2)}, u32[]{:S(2)}) collective-permute-start(bf16[16,6144]{1,0:T(8,128)(2,1)S(1)} %collective-permute-done.26.refs_4_), channel_id=1, source_target_pairs={{0,16},{16,0},{1,17},{17,1},{2,18},{18,2},{3,19},{19,3},{4,20},{20... | collective-permute-start | bytes 589832 | tf_op jit(solution)/shard_map/ppermute | solution.py:21
  104.6 3.5 %collective-permute-start.31 = (f32[64,6144]{1,0:T(8,128)S(1)}, f32[64,6144]{1,0:T(8,128)S(1)}, u32[]{:S(2)}, u32[]{:S(2)}) collective-permute-start(f32[64,6144]{1,0:T(8,128)S(1)} %get-tuple-element.50), channel_id=1, source_target_pairs={{0,16},{16,0},{1,17},{17,1},{2,18},{18,2},{3,19},{19,3},{4,20},{20... | collective-permute-start | bytes 4718600 | tf_op jit(solution)/shard_map/ppermute | solution.py:21
  108.3 11.6 %collective-permute-start.32 = (bf16[16,6144]{1,0:T(8,128)(2,1)S(1)}, bf16[16,6144]{1,0:T(8,128)(2,1)S(1)}, u32[]{:S(2)}, u32[]{:S(2)}) collective-permute-start(bf16[16,6144]{1,0:T(8,128)(2,1)S(1)} %get-tuple-element.62), channel_id=1, source_target_pairs={{0,32},{32,64},{64,96},{96,0},{1,33},{33,65},{65,97},{97,1},{2,34}... | collective-permute-start | bytes 589832 | tf_op jit(solution)/shard_map/ppermute | solution.py:17
  108.4 11.5 %collective-permute-start.33 = (bf16[16,6144]{1,0:T(8,128)(2,1)S(1)}, bf16[16,6144]{1,0:T(8,128)(2,1)S(1)}, u32[]{:S(2)}, u32[]{:S(2)}) collective-permute-start(bf16[16,6144]{1,0:T(8,128)(2,1)S(1)} %get-tuple-element.61), channel_id=1, source_target_pairs={{0,96},{32,0},{64,32},{96,64},{1,97},{33,1},{65,33},{97,65},{2,98}... | collective-permute-start | bytes 589832 | tf_op jit(solution)/shard_map/ppermute | solution.py:17
  111.1 8.9 %collective-permute-start.34 = (bf16[16,6144]{1,0:T(8,128)(2,1)S(1)}, bf16[16,6144]{1,0:T(8,128)(2,1)S(1)}, u32[]{:S(2)}, u32[]{:S(2)}) collective-permute-start(bf16[16,6144]{1,0:T(8,128)(2,1)S(1)} %get-tuple-element.60), channel_id=1, source_target_pairs={{0,64},{32,96},{64,0},{96,32},{1,65},{33,97},{65,1},{97,33},{2,66}... | collective-permute-start | bytes 589832 | tf_op jit(solution)/shard_map/ppermute | solution.py:17
  120.0 6.1 %collective-permute-start.35 = (bf16[16,6144]{1,0:T(8,128)(2,1)S(1)}, bf16[16,6144]{1,0:T(8,128)(2,1)S(1)}, u32[]{:S(2)}, u32[]{:S(2)}) collective-permute-start(bf16[16,6144]{1,0:T(8,128)(2,1)S(1)} %fusion.5.refs_1_), channel_id=1, source_target_pairs={{0,96},{32,0},{64,32},{96,64},{1,97},{33,1},{65,33},{97,65},{2,98}... | collective-permute-start | bytes 589832 | tf_op jit(solution)/shard_map/ppermute | solution.py:17
  122.5 9.4 %collective-permute-start.36 = (bf16[16,6144]{1,0:T(8,128)(2,1)S(1)}, bf16[16,6144]{1,0:T(8,128)(2,1)S(1)}, u32[]{:S(2)}, u32[]{:S(2)}) collective-permute-start(bf16[16,6144]{1,0:T(8,128)(2,1)S(1)} %fusion.5.refs_1_), channel_id=1, source_target_pairs={{0,64},{32,96},{64,0},{96,32},{1,65},{33,97},{65,1},{97,33},{2,66}... | collective-permute-start | bytes 589832 | tf_op jit(solution)/shard_map/ppermute | solution.py:17
  122.5 11.9 %collective-permute-start.37 = (bf16[16,6144]{1,0:T(8,128)(2,1)S(1)}, bf16[16,6144]{1,0:T(8,128)(2,1)S(1)}, u32[]{:S(2)}, u32[]{:S(2)}) collective-permute-start(bf16[16,6144]{1,0:T(8,128)(2,1)S(1)} %fusion.5.refs_1_), channel_id=1, source_target_pairs={{0,32},{32,64},{64,96},{96,0},{1,33},{33,65},{65,97},{97,1},{2,34}... | collective-permute-start | bytes 589832 | tf_op jit(solution)/shard_map/ppermute | solution.py:17
  123.1 12.3 %collective-permute-start.38 = (bf16[16,6144]{1,0:T(8,128)(2,1)S(1)}, bf16[16,6144]{1,0:T(8,128)(2,1)S(1)}, u32[]{:S(2)}, u32[]{:S(2)}) collective-permute-start(bf16[16,6144]{1,0:T(8,128)(2,1)S(1)} %fusion.5.refs_1_), channel_id=1, source_target_pairs={{0,16},{16,0},{1,17},{17,1},{2,18},{18,2},{3,19},{19,3},{4,20},{20... | collective-permute-start | bytes 589832 | tf_op jit(solution)/shard_map/ppermute | solution.py:21
  126.1 9.3 %collective-permute-start.39 = (bf16[16,6144]{1,0:T(8,128)(2,1)S(1)}, bf16[16,6144]{1,0:T(8,128)(2,1)S(1)}, u32[]{:S(2)}, u32[]{:S(2)}) collective-permute-start(bf16[16,6144]{1,0:T(8,128)(2,1)S(1)} %collective-permute-done.35.refs_2_), channel_id=1, source_target_pairs={{0,16},{16,0},{1,17},{17,1},{2,18},{18,2},{3,19},{19,3},{4,20},{20... | collective-permute-start | bytes 589832 | tf_op jit(solution)/shard_map/ppermute | solution.py:21
  131.8 3.6 %collective-permute-start.40 = (bf16[16,6144]{1,0:T(8,128)(2,1)S(1)}, bf16[16,6144]{1,0:T(8,128)(2,1)S(1)}, u32[]{:S(2)}, u32[]{:S(2)}) collective-permute-start(bf16[16,6144]{1,0:T(8,128)(2,1)S(1)} %collective-permute-done.36.refs_3_), channel_id=1, source_target_pairs={{0,16},{16,0},{1,17},{17,1},{2,18},{18,2},{3,19},{19,3},{4,20},{20... | collective-permute-start | bytes 589832 | tf_op jit(solution)/shard_map/ppermute | solution.py:21
  134.4 1.9 %collective-permute-start.41 = (bf16[16,6144]{1,0:T(8,128)(2,1)S(1)}, bf16[16,6144]{1,0:T(8,128)(2,1)S(1)}, u32[]{:S(2)}, u32[]{:S(2)}) collective-permute-start(bf16[16,6144]{1,0:T(8,128)(2,1)S(1)} %collective-permute-done.37.refs_4_), channel_id=1, source_target_pairs={{0,16},{16,0},{1,17},{17,1},{2,18},{18,2},{3,19},{19,3},{4,20},{20... | collective-permute-start | bytes 589832 | tf_op jit(solution)/shard_map/ppermute | solution.py:21
  140.3 3.6 %copy-start.2 = (bf16[768,128]{1,0:T(8,128)(2,1)S(1)}, bf16[768,128]{1,0:T(8,128)(2,1)}, u32[]{:S(2)}) copy-start(bf16[768,128]{1,0:T(8,128)(2,1)} %get-tuple-element.27) | copy-start | bytes 589828
  140.3 16.0 %all-to-all-start = ((bf16[4,768,128]{2,1,0:T(8,128)(2,1)}), bf16[4,768,128]{2,1,0:T(8,128)(2,1)S(1)}, u32[]{:S(2)}, u32[]{:S(2)}) async-start(bf16[4,768,128]{2,1,0:T(8,128)(2,1)} %get-tuple-element.55), calls=%async_computation | async-start | bytes 1572864 | tf_op jit(solution)/shard_map/all_to_all | solution.py:200
  157.0 3.6 %collective-permute-start.42 = (f32[16,64,128]{2,1,0:T(8,128)S(1)}, f32[16,64,128]{2,1,0:T(8,128)S(1)}, u32[]{:S(2)}, u32[]{:S(2)}) collective-permute-start(f32[16,64,128]{2,1,0:T(8,128)S(1)} %dynamic-slice_bitcast_fusion), channel_id=1, source_target_pairs={{0,16},{16,0},{1,17},{17,1},{2,18},{18,2},{3,19},{19,3},{4,20},{20... | collective-permute-start | bytes 1572872 | tf_op jit(solution)/shard_map/ppermute | solution.py:21
  173.5 2.5 %collective-permute-start.43 = (f32[2,64,128]{2,1,0:T(8,128)S(1)}, f32[2,64,128]{2,1,0:T(8,128)S(1)}, u32[]{:S(2)}, u32[]{:S(2)}) collective-permute-start(f32[2,64,128]{2,1,0:T(8,128)S(1)} %dynamic-slice_bitcast_fusion.1), channel_id=1, source_target_pairs={{0,16},{16,0},{1,17},{17,1},{2,18},{18,2},{3,19},{19,3},{4,20},{20... | collective-permute-start | bytes 196616 | tf_op jit(solution)/shard_map/ppermute | solution.py:21

commit v6 on v5

--- a/solution.py
+++ b/solution.py
@@ -37,11 +37,13 @@
     pp, mm, pm, mp = (after(block, first[2]) for block in (pp, mm, pm, mp))
     a, b, c, d = (shift(mp, "x", 1), shift(pm, "x", 3), shift(pp, "z", 1), shift(mm, "z", 3))
     second = down_first(x, [pp, mm, pm, mp])
-    far_x, far_z, low, high = (shift(xp, "x", 1), shift(zp, "z", 1), shift(d[:half], "x", 3), shift(a[half:], "z", 3))
+    low, high = shift(d[:half], "x", 3), shift(a[half:], "z", 3)
+    far_x, far_z = shift(after(xp, a), "x", 1), shift(after(zp, a), "z", 1)
     third = down_first(x, [a, b, c, d])
+    early = reduce_y([core_sum(*step[:2]) for step in (first, second, third)])
     fourth = down_first(x, [far_x, far_z, (low, high)])
     blocks = [first[3], pp, mm, pm, mp, a, b, c, d, far_x, far_z, low, high]
-    return blocks, [first[:3], second, third, fourth]
+    return blocks, early, fourth, first[2] + second[2] + third[2] + fourth[2]
 
 
 VMEM = pl.BlockSpec(memory_space=pltpu.VMEM)
@@ -93,38 +95,53 @@
     return mine + other_core(theirs)
 
 
-def sum_over_y(half, square=None):
+def sum_over_y(half):
+    return gather_y(reduce_y(half))
+
+
+def reduce_y(half):
     send = jnp.concatenate([h[16:].astype(jnp.bfloat16) for h in half], 1)
-    n = send.shape[1]
-    if square is not None:
-        high = lax.reduce_precision(square, 8, 7)
-        extra = jnp.concatenate([high, square - high]).astype(jnp.bfloat16)
-        send = jnp.concatenate([send, jnp.tile(extra, (3, 1))], 1)
-    got = lax.optimization_barrier(
-        tuple(shift(send[16 * (d - 1) : 16 * d], "y", d) for d in (1, 3, 2))
-    )
+    sends = {d: send[16 * (d - 1) : 16 * d] for d in (1, 3, 2)}
+    got = lax.optimization_barrier(tuple(shift(piece, "y", d) for d, piece in sends.items()))
     total = jnp.concatenate([h[:16] for h in half], 1)
     for piece in got:
-        total = total + piece[:, :n].astype(jnp.float32)
-    if square is not None:
-        for piece in got:
-            square = square + piece[:8, n:].astype(jnp.float32) + piece[8:, n:].astype(jnp.float32)
-    own = total.astype(jnp.bfloat16)
+        total = total + piece.astype(jnp.float32)
+    return total.astype(jnp.bfloat16)
+
+
+def gather_y(own):
     up1, up3, up2 = (shift(own, "y", 4 - d) for d in (1, 3, 2))
     mine = [own, up1, up2, up3]
-    return mine + [other_core(m) for m in mine], square
-
-
-def apply_kernel(down, widths, square_ref, *refs):
-    pieces = 8 * len(widths)
+    return mine + [other_core(m) for m in mine]
+
+
+def sum_over_y_at_once(half, square):
+    n = half.shape[1]
+    high = lax.reduce_precision(square, 8, 7)
+    extra = jnp.concatenate([high, square - high]).astype(jnp.bfloat16)
+    send = jnp.concatenate([half.astype(jnp.bfloat16), jnp.tile(extra, (4, 1))], 1)
+    got = lax.optimization_barrier(tuple(shift(send, "y", d) for d in (1, 3, 2)))
+    total = half
+    for d, piece in zip((1, 3, 2), got):
+        turned = jnp.concatenate([piece[16 * d :, :n], piece[: 16 * d, :n]])
+        total = total + turned.astype(jnp.float32)
+        square = square + piece[:8, n:].astype(jnp.float32) + piece[8:16, n:].astype(jnp.float32)
+    mine = total.astype(jnp.bfloat16)
+    return [mine, other_core(mine)], square
+
+
+def apply_kernel(down, count, square_ref, *refs):
+    pieces = count
     t_refs, (kept_ref, *theta_refs) = refs[:pieces], refs[pieces : pieces + BLOCKS - KEPT + 2]
     outs, t_ref = list(refs[pieces + BLOCKS - KEPT + 2 : -1]), refs[-1]
     rows = theta_refs[0].shape[0]
-    at = 0
-    for i, width in enumerate(widths):
-        for j in range(8):
-            t_ref[16 * j : 16 * j + 16, at : at + width] = t_refs[8 * i + j][...]
-        at += width
+    at, row = 0, 0
+    for ref in t_refs:
+        height, width = ref.shape
+        t_ref[row : row + height, at : at + width] = ref[...]
+        row += height
+        if row == 128:
+            at, row = at + width, 0
 
     def theta(i):
         if i < KEPT:
@@ -155,8 +172,7 @@
 
 
 def apply(square, t, blocks, order=None):
-    widths = [piece.shape[1] for piece in t[::8]]
-    n, rows = sum(widths), blocks[1].shape[0]
+    n, rows = sum(piece.size for piece in t) // 128, blocks[1].shape[0]
     down = order is None
     if down:
         out_shape = [jax.ShapeDtypeStruct((64, k * COLS), jnp.float32) for k in (SPLIT, BLOCKS - SPLIT) for _ in range(2) if k]
@@ -164,7 +180,7 @@
         out_shape = [jax.ShapeDtypeStruct(shape, jnp.bfloat16) for shape in ((rows, 128), (4, rows, 128))]
         blocks = [*blocks, order]
     return pl.pallas_call(
-        lambda *refs: apply_kernel(down, widths, *refs),
+        lambda *refs: apply_kernel(down, len(t), *refs),
         out_shape=out_shape,
         in_specs=[VMEM] * (1 + len(t) + len(blocks)),
         out_specs=[VMEM] * len(out_shape),
@@ -189,11 +205,10 @@
     order = column_order(y, core)
     x = f32_dot(order, basis, ((1,), (1,))).astype(jnp.bfloat16)
 
-    blocks, steps = gather_and_apply(theta, x)
-    half = [core_sum(mine, theirs) for mine, theirs, _ in steps]
-    square = sum(squares for _, _, squares in steps)
-    t, square = sum_over_y(half, square + other_core(square))
-    t, _ = sum_over_y([core_sum(*apply(square, t, blocks))])
+    blocks, early, fourth, square = gather_and_apply(theta, x)
+    late, square = sum_over_y_at_once(core_sum(*fourth[:2]), square + other_core(square))
+    t = gather_y(early) + late
+    t = sum_over_y([core_sum(*apply(square, t, blocks))])
     subspace, copies = apply(square, t, blocks, order)
 
     along_x = lax.all_gather(subspace, "x", axis=0)

time: 177 us -> 174 us (0.983)
  waiting for transfers between devices: 61.5 us -> 59.6 us
    ppermute x28 -> x31, starting transfers between devices: 35.6 us -> 39.7 us  [shift(): return lax.ppermute(x, axis, [(i, (i + by) % 4) for i in range(4)])]
    ppermute x16 -> x17, starting transfers between devices: 32.9 us -> 29.4 us  [other_core(): return lax.ppermute(x, 'core', [(0, 1), (1, 0)])]
    ppermute x28 -> x31, waiting for transfers between devices: 52.6 us -> 50.1 us  [shift(): return lax.ppermute(x, axis, [(i, (i + by) % 4) for i in range(4)])]
    ppermute x16 -> x17, waiting for transfers between devices: 8.89 us -> 9.53 us  [other_core(): return lax.ppermute(x, 'core', [(0, 1), (1, 0)])]
  transfers between devices with their start and end apart: 45 -> 49, of which waited for: 22 -> 25; matrix products, arithmetic and copies ran while one was open for 1% -> 1% of each run, Pallas kernels for 2% -> 1%
where the time goes in v6:
time: 174 us
  starting transfers between devices  73.3 us (42%)
  waiting for transfers between devices  59.6 us (34%)
  blocking collectives  24.1 us (14%)
  Pallas kernels  11.5 us (7%)
  local copies, waits for them, and re-layouts  2.25 us (1%)
    ppermute x31, waiting for transfers between devices, shift(): return lax.ppermute(x, axis, [(i, (i + by) % 4) for i in range(4)])  50.1 us
    ppermute x31, starting transfers between devices, shift(): return lax.ppermute(x, axis, [(i, (i + by) % 4) for i in range(4)])  39.7 us
    ppermute x17, starting transfers between devices, other_core(): return lax.ppermute(x, 'core', [(0, 1), (1, 0)])  29.4 us
    all_to_all x1, blocking collectives, per_device(): lax.all_to_all(half.astype(jnp.bfloat16), ('y', 'x'), 0, 0)  12.3 us
    all_gather x1, blocking collectives, per_device(): along_x = lax.all_gather(subspace, 'x', axis=0)  11.9 us
    ppermute x17, waiting for transfers between devices, other_core(): return lax.ppermute(x, 'core', [(0, 1), (1, 0)])  9.53 us
    pallas_call x2, Pallas kernels, apply(): pl.pallas_call(lambda *refs: apply_kernel(down, len(t), *refs), out_shape...  8.71 us
    all_to_all x1, starting transfers between devices, per_device(): along_z = lax.all_to_all(copies, 'z', 0, 0)  4.19 us
  transfers between devices with their start and end apart: 49, of which 25 were waited for; matrix products, arithmetic and copies ran while one was open for 1% of the time, Pallas kernels for 1%

profile of v6, /device:TPU:1, one launch (start us, length us, event | category | flops | bytes accessed | tf_op | source)
XLA Modules:
  0.0 174.0 jit_solution(5371034661484355885)
XLA Ops:
  0.6 2.1 %collective-permute-start = (bf16[768,384]{1,0:T(8,128)(2,1)}, bf16[768,384]{1,0:T(8,128)(2,1)S(1)}, u32[]{:S(2)}, u32[]{:S(2)}) collective-permute-start(bf16[768,384]{1,0:T(8,128)(2,1)} %refs_1_.1), channel_id=1, source_target_pairs={{0,1},{1,2},{2,3},{3,0},{4,5},{5,6},{6,7},{7,4},{8,9},{9,10},{10,1... | collective-permute-start | bytes 1769480 | tf_op jit(solution)/shard_map/ppermute | solution.py:17
  2.8 3.8 %collective-permute-start.3 = (bf16[768,384]{1,0:T(8,128)(2,1)}, bf16[768,384]{1,0:T(8,128)(2,1)S(1)}, u32[]{:S(2)}, u32[]{:S(2)}) collective-permute-start(bf16[768,384]{1,0:T(8,128)(2,1)} %refs_1_.1), channel_id=1, source_target_pairs={{0,12},{4,0},{8,4},{12,8},{1,13},{5,1},{9,5},{13,9},{2,14},{6,2},{... | collective-permute-start | bytes 1769480 | tf_op jit(solution)/shard_map/ppermute | solution.py:17
  6.5 1.5 collective-permute-start.1
  8.0 8.9 %collective-permute-done.refs_2_ = bf16[768,384]{1,0:T(8,128)(2,1)S(1)} collective-permute-done((bf16[768,384]{1,0:T(8,128)(2,1)}, bf16[768,384]{1,0:T(8,128)(2,1)S(1)}, u32[]{:S(2)}, u32[]{:S(2)}) %collective-permute-start) | collective-permute-done | bytes 589856 | tf_op jit(solution)/shard_map/ppermute | solution.py:17
  16.8 4.1 %collective-permute-start.7 = (bf16[768,384]{1,0:T(8,128)(2,1)S(1)}, bf16[768,384]{1,0:T(8,128)(2,1)S(1)}, u32[]{:S(2)}, u32[]{:S(2)}) collective-permute-start(bf16[768,384]{1,0:T(8,128)(2,1)S(1)} %collective-permute-done.refs_2_), channel_id=1, source_target_pairs={{0,12},{4,0},{8,4},{12,8},{1,13},{5,1},{9,5},{13,9},{2,14},{6,2},{... | collective-permute-start | bytes 1769480 | tf_op jit(solution)/shard_map/ppermute | solution.py:17
  20.9 1.3 collective-permute-start.5
  23.2 1.1 copy-done.1
  25.1 6.9 %collective-permute-done.7.refs_4_.refs_15_.refs_13_ = bf16[768,384]{1,0:T(8,128)(2,1)S(1)} collective-permute-done((bf16[768,384]{1,0:T(8,128)(2,1)S(1)}, bf16[768,384]{1,0:T(8,128)(2,1)S(1)}, u32[]{:S(2)}, u32[]{:S(2)}) %collective-permute-start.7) | collective-permute-done | bytes 589856 | tf_op jit(solution)/shard_map/ppermute | solution.py:17
  32.0 1.9 %collective-permute-done.5.refs_2_.refs_13_.refs_11_ = bf16[768,384]{1,0:T(8,128)(2,1)S(1)} collective-permute-done((bf16[768,384]{1,0:T(8,128)(2,1)S(1)}, bf16[768,384]{1,0:T(8,128)(2,1)S(1)}, u32[]{:S(2)}, u32[]{:S(2)}) %collective-permute-start.5) | collective-permute-done | bytes 589856 | tf_op jit(solution)/shard_map/ppermute | solution.py:17
  33.9 1.5 collective-permute-start.11
  36.3 2.2 %collective-permute-start.9 = (bf16[768,384]{1,0:T(8,128)(2,1)S(1)}, bf16[768,384]{1,0:T(8,128)(2,1)S(1)}, u32[]{:S(2)}, u32[]{:S(2)}) collective-permute-start(bf16[768,384]{1,0:T(8,128)(2,1)S(1)} %collective-permute-done.6.refs_3_.refs_14_.refs_12_), channel_id=1, source_target_pairs={{0,3},{1,0},{2,1},{3,2},{4,7},{5,4},{6,5},{7,6},{8,11},{9,8},{10,9... | collective-permute-start | bytes 1769480 | tf_op jit(solution)/shard_map/ppermute | solution.py:17
  38.5 3.6 %collective-permute-start.21 = (f32[64,1920]{1,0:T(8,128)S(1)}, f32[64,1920]{1,0:T(8,128)S(1)}, u32[]{:S(2)}, u32[]{:S(2)}) collective-permute-start(f32[64,1920]{1,0:T(8,128)S(1)} %get-tuple-element.50), channel_id=1, source_target_pairs={{0,16},{16,0},{1,17},{17,1},{2,18},{18,2},{3,19},{19,3},{4,20},{20... | collective-permute-start | bytes 1474568 | tf_op jit(solution)/shard_map/ppermute | solution.py:21
  42.8 6.0 %collective-permute-done.8.refs_1_.refs_16_.refs_14_ = bf16[768,384]{1,0:T(8,128)(2,1)S(1)} collective-permute-done((bf16[768,384]{1,0:T(8,128)(2,1)S(1)}, bf16[768,384]{1,0:T(8,128)(2,1)S(1)}, u32[]{:S(2)}, u32[]{:S(2)}) %collective-permute-start.8) | collective-permute-done | bytes 589856 | tf_op jit(solution)/shard_map/ppermute | solution.py:17
  48.8 3.0 %collective-permute-start.22 = (f32[64,1536]{1,0:T(8,128)S(1)}, f32[64,1536]{1,0:T(8,128)S(1)}, u32[]{:S(2)}, u32[]{:S(2)}) collective-permute-start(f32[64,1536]{1,0:T(8,128)S(1)} %get-tuple-element.52), channel_id=1, source_target_pairs={{0,16},{16,0},{1,17},{17,1},{2,18},{18,2},{3,19},{19,3},{4,20},{20... | collective-permute-start | bytes 1179656 | tf_op jit(solution)/shard_map/ppermute | solution.py:21
  52.5 1.4 collective-permute-start.23
  55.4 1.4 collective-permute-start.24
  56.8 1.5 collective-permute-start.25
  58.3 2.2 %collective-permute-start.15 = (bf16[384,384]{1,0:T(8,128)(2,1)S(1)}, bf16[384,384]{1,0:T(8,128)(2,1)S(1)}, u32[]{:S(2)}, u32[]{:S(2)}) collective-permute-start(bf16[384,384]{1,0:T(8,128)(2,1)S(1)} %slice.117), channel_id=1, source_target_pairs={{0,12},{4,0},{8,4},{12,8},{1,13},{5,1},{9,5},{13,9},{2,14},{6,2},{... | collective-permute-start | bytes 884744 | tf_op jit(solution)/shard_map/ppermute | solution.py:17
  60.5 1.6 collective-permute-done.24
  62.1 2.4 %collective-permute-start.14 = (bf16[384,384]{1,0:T(8,128)(2,1)S(1)}, bf16[384,384]{1,0:T(8,128)(2,1)S(1)}, u32[]{:S(2)}, u32[]{:S(2)}) collective-permute-start(bf16[384,384]{1,0:T(8,128)(2,1)S(1)} %slice.116), channel_id=1, source_target_pairs={{0,3},{1,0},{2,1},{3,2},{4,7},{5,4},{6,5},{7,6},{8,11},{9,8},{10,9... | collective-permute-start | bytes 884744 | tf_op jit(solution)/shard_map/ppermute | solution.py:17
  64.5 1.6 collective-permute-start.26
  66.1 4.0 %collective-permute-done.26 = bf16[16,4992]{1,0:T(8,128)(2,1)S(1)} collective-permute-done((bf16[16,4992]{1,0:T(8,128)(2,1)S(1)}, bf16[16,4992]{1,0:T(8,128)(2,1)S(1)}, u32[]{:S(2)}, u32[]{:S(2)}) %collective-permute-start.26) | collective-permute-done | bytes 159776 | tf_op jit(solution)/shard_map/ppermute | solution.py:17
  71.0 2.5 %collective-permute-start.16 = (f32[8,128]{1,0:T(8,128)S(1)}, f32[8,128]{1,0:T(8,128)S(1)}, u32[]{:S(2)}, u32[]{:S(2)}) collective-permute-start(f32[8,128]{1,0:T(8,128)S(1)} %add_add_fusion), channel_id=1, source_target_pairs={{0,16},{16,0},{1,17},{17,1},{2,18},{18,2},{3,19},{19,3},{4,20},{20... | collective-permute-start | bytes 12296 | tf_op jit(solution)/shard_map/ppermute | solution.py:21
  73.5 1.5 collective-permute-start.27
  75.4 1.2 collective-permute-done.17
  76.8 2.7 %collective-permute-start.19 = (bf16[64,1280]{1,0:T(8,128)(2,1)S(1)}, bf16[64,1280]{1,0:T(8,128)(2,1)S(1)}, u32[]{:S(2)}, u32[]{:S(2)}) collective-permute-start(bf16[64,1280]{1,0:T(8,128)(2,1)S(1)} %pad_maximum_fusion.1), channel_id=1, source_target_pairs={{0,96},{32,0},{64,32},{96,64},{1,97},{33,1},{65,33},{97,65},{2,98}... | collective-permute-start | bytes 491528 | tf_op jit(solution)/shard_map/ppermute | solution.py:17
  79.4 3.0 %collective-permute-start.28 = (bf16[16,4992]{1,0:T(8,128)(2,1)S(1)}, bf16[16,4992]{1,0:T(8,128)(2,1)S(1)}, u32[]{:S(2)}, u32[]{:S(2)}) collective-permute-start(bf16[16,4992]{1,0:T(8,128)(2,1)S(1)} %fusion.8.refs_1_), channel_id=1, source_target_pairs={{0,64},{32,96},{64,0},{96,32},{1,65},{33,97},{65,1},{97,33},{2,66}... | collective-permute-start | bytes 479240 | tf_op jit(solution)/shard_map/ppermute | solution.py:17
  82.4 6.9 %collective-permute-done.28.refs_3_ = bf16[16,4992]{1,0:T(8,128)(2,1)S(1)} collective-permute-done((bf16[16,4992]{1,0:T(8,128)(2,1)S(1)}, bf16[16,4992]{1,0:T(8,128)(2,1)S(1)}, u32[]{:S(2)}, u32[]{:S(2)}) %collective-permute-start.28) | collective-permute-done | bytes 159776 | tf_op jit(solution)/shard_map/ppermute | solution.py:17
  89.3 3.1 %collective-permute-start.30 = (bf16[16,4992]{1,0:T(8,128)(2,1)S(1)}, bf16[16,4992]{1,0:T(8,128)(2,1)S(1)}, u32[]{:S(2)}, u32[]{:S(2)}) collective-permute-start(bf16[16,4992]{1,0:T(8,128)(2,1)S(1)} %fusion.8.refs_1_), channel_id=1, source_target_pairs={{0,16},{16,0},{1,17},{17,1},{2,18},{18,2},{3,19},{19,3},{4,20},{20... | collective-permute-start | bytes 479240 | tf_op jit(solution)/shard_map/ppermute | solution.py:21
  92.4 1.8 %collective-permute-done.29.refs_4_ = bf16[16,4992]{1,0:T(8,128)(2,1)S(1)} collective-permute-done((bf16[16,4992]{1,0:T(8,128)(2,1)S(1)}, bf16[16,4992]{1,0:T(8,128)(2,1)S(1)}, u32[]{:S(2)}, u32[]{:S(2)}) %collective-permute-start.29) | collective-permute-done | bytes 159776 | tf_op jit(solution)/shard_map/ppermute | solution.py:17
  97.1 4.7 %shard_map.45 = (f32[64,6144]{1,0:T(8,128)S(1)}, f32[64,6144]{1,0:T(8,128)S(1)}) custom-call(f32[8,128]{1,0:T(8,128)S(1)} %convert_add_fusion.refs_0_, bf16[16,4992]{1,0:T(8,128)(2,1)S(1)} %fusion.8.refs_1_, bf16[16,4992]{1,0:T(8,128)(2,1)S(1)} %collective-permute-done.27.refs_2_, bf16[16,4992]{1,0:T(8,128)(2,1)S(1)} %collective-permute-done.28.refs_3_, ...), custom_call_target="tpu_custom_call" | custom-call | flops 2415919104 | bytes 9437184 | tf_op jit(solution)/shard_map/pallas_call | solution.py:182
  102.0 3.3 %collective-permute-done.35 = f32[64,6144]{1,0:T(8,128)S(1)} collective-permute-done((f32[64,6144]{1,0:T(8,128)S(1)}, f32[64,6144]{1,0:T(8,128)S(1)}, u32[]{:S(2)}, u32[]{:S(2)}) %collective-permute-start.35) | collective-permute-done | bytes 1572896 | tf_op jit(solution)/shard_map/ppermute | solution.py:21
  105.6 2.7 %collective-permute-start.37 = (bf16[16,6144]{1,0:T(8,128)(2,1)S(1)}, bf16[16,6144]{1,0:T(8,128)(2,1)S(1)}, u32[]{:S(2)}, u32[]{:S(2)}) collective-permute-start(bf16[16,6144]{1,0:T(8,128)(2,1)S(1)} %get-tuple-element.73), channel_id=1, source_target_pairs={{0,96},{32,0},{64,32},{96,64},{1,97},{33,1},{65,33},{97,65},{2,98}... | collective-permute-start | bytes 589832 | tf_op jit(solution)/shard_map/ppermute | solution.py:17
  108.3 9.1 %collective-permute-done.36 = bf16[16,6144]{1,0:T(8,128)(2,1)S(1)} collective-permute-done((bf16[16,6144]{1,0:T(8,128)(2,1)S(1)}, bf16[16,6144]{1,0:T(8,128)(2,1)S(1)}, u32[]{:S(2)}, u32[]{:S(2)}) %collective-permute-start.36) | collective-permute-done | bytes 196640 | tf_op jit(solution)/shard_map/ppermute | solution.py:17
  117.5 2.4 %collective-permute-start.39 = (bf16[16,6144]{1,0:T(8,128)(2,1)S(1)}, bf16[16,6144]{1,0:T(8,128)(2,1)S(1)}, u32[]{:S(2)}, u32[]{:S(2)}) collective-permute-start(bf16[16,6144]{1,0:T(8,128)(2,1)S(1)} %fusion.5.refs_1_), channel_id=1, source_target_pairs={{0,96},{32,0},{64,32},{96,64},{1,97},{33,1},{65,33},{97,65},{2,98}... | collective-permute-start | bytes 589832 | tf_op jit(solution)/shard_map/ppermute | solution.py:17
  120.6 1.8 %collective-permute-start.42 = (bf16[16,6144]{1,0:T(8,128)(2,1)S(1)}, bf16[16,6144]{1,0:T(8,128)(2,1)S(1)}, u32[]{:S(2)}, u32[]{:S(2)}) collective-permute-start(bf16[16,6144]{1,0:T(8,128)(2,1)S(1)} %fusion.5.refs_1_), channel_id=1, source_target_pairs={{0,16},{16,0},{1,17},{17,1},{2,18},{18,2},{3,19},{19,3},{4,20},{20... | collective-permute-start | bytes 589832 | tf_op jit(solution)/shard_map/ppermute | solution.py:21
  122.4 0.9 collective-permute-done.39.refs_2_
  123.4 5.9 %collective-permute-start.43 = (bf16[16,6144]{1,0:T(8,128)(2,1)S(1)}, bf16[16,6144]{1,0:T(8,128)(2,1)S(1)}, u32[]{:S(2)}, u32[]{:S(2)}) collective-permute-start(bf16[16,6144]{1,0:T(8,128)(2,1)S(1)} %collective-permute-done.39.refs_2_), channel_id=1, source_target_pairs={{0,16},{16,0},{1,17},{17,1},{2,18},{18,2},{3,19},{19,3},{4,20},{20... | collective-permute-start | bytes 589832 | tf_op jit(solution)/shard_map/ppermute | solution.py:21
  129.3 1.5 collective-permute-start.44
  130.8 1.0 collective-permute-done.41.refs_4_
  133.7 4.0 %shard_map.46 = (bf16[768,128]{1,0:T(8,128)(2,1)}, bf16[4,768,128]{2,1,0:T(8,128)(2,1)}) custom-call(f32[8,128]{1,0:T(8,128)S(1)} %convert_add_fusion.refs_0_, bf16[16,6144]{1,0:T(8,128)(2,1)S(1)} %fusion.5.refs_1_, bf16[16,6144]{1,0:T(8,128)(2,1)S(1)} %collective-permute-done.39.refs_2_, bf16[16,6144]{1,0:T(8,128)(2,1)S(1)} %collective-permute-done.40.refs_3_, ...), custom_call_target="tpu_custom_call" | custom-call | flops 1207959552 | bytes 9437184 | tf_op jit(solution)/shard_map/pallas_call | solution.py:182
  137.7 4.2 %all-to-all-start = ((bf16[4,768,128]{2,1,0:T(8,128)(2,1)}), bf16[4,768,128]{2,1,0:T(8,128)(2,1)S(1)}, u32[]{:S(2)}, u32[]{:S(2)}) async-start(bf16[4,768,128]{2,1,0:T(8,128)(2,1)} %get-tuple-element.65), calls=%async_computation | async-start | bytes 1572864 | tf_op jit(solution)/shard_map/all_to_all | solution.py:215
  141.9 11.9 %all-gather = bf16[3072,128]{1,0:T(8,128)(2,1)S(1)} all-gather(bf16[768,128]{1,0:T(8,128)(2,1)S(1)} %copy-done.5), channel_id=2, replica_groups=mesh['y'=4,'core'=2,'z'=4,'x'=4] {'x'}, dimensions={0}, use_global_device_ids=true | all-gather | bytes 983040 | tf_op jit(solution)/shard_map/all_gather | solution.py:214
  154.5 2.2 %collective-permute-start.46 = (f32[16,64,128]{2,1,0:T(8,128)S(1)}, f32[16,64,128]{2,1,0:T(8,128)S(1)}, u32[]{:S(2)}, u32[]{:S(2)}) collective-permute-start(f32[16,64,128]{2,1,0:T(8,128)S(1)} %dynamic-slice_bitcast_fusion), channel_id=1, source_target_pairs={{0,16},{16,0},{1,17},{17,1},{2,18},{18,2},{3,19},{19,3},{4,20},{20... | collective-permute-start | bytes 1572872 | tf_op jit(solution)/shard_map/ppermute | solution.py:21
  156.7 1.5 collective-permute-done.46
  158.3 12.3 %all_to_all.10 = bf16[16,64,128]{2,1,0:T(8,128)(2,1)S(1)} all-to-all(bf16[16,64,128]{2,1,0:T(8,128)(2,1)S(1)} %fusion.2), channel_id=1, replica_groups=mesh['y'=4,'core'=2,'z'=4,'x'=4] {'y','x'}, dimensions={0} | all-to-all | bytes 524288 | tf_op jit(solution)/shard_map/all_to_all | solution.py:220
  170.7 1.6 collective-permute-start.47
  172.3 0.9 collective-permute-done.47
  (121 shorter events, 14.7 us)
Async XLA Ops:
  0.6 16.2 %collective-permute-start = (bf16[768,384]{1,0:T(8,128)(2,1)}, bf16[768,384]{1,0:T(8,128)(2,1)S(1)}, u32[]{:S(2)}, u32[]{:S(2)}) collective-permute-start(bf16[768,384]{1,0:T(8,128)(2,1)} %refs_1_.1), channel_id=1, source_target_pairs={{0,1},{1,2},{2,3},{3,0},{4,5},{5,6},{6,7},{7,4},{8,9},{9,10},{10,1... | collective-permute-start | bytes 1769480 | tf_op jit(solution)/shard_map/ppermute | solution.py:17
  2.8 18.2 %collective-permute-start.3 = (bf16[768,384]{1,0:T(8,128)(2,1)}, bf16[768,384]{1,0:T(8,128)(2,1)S(1)}, u32[]{:S(2)}, u32[]{:S(2)}) collective-permute-start(bf16[768,384]{1,0:T(8,128)(2,1)} %refs_1_.1), channel_id=1, source_target_pairs={{0,12},{4,0},{8,4},{12,8},{1,13},{5,1},{9,5},{13,9},{2,14},{6,2},{... | collective-permute-start | bytes 1769480 | tf_op jit(solution)/shard_map/ppermute | solution.py:17
  6.5 15.7 %collective-permute-start.2 = (bf16[768,384]{1,0:T(8,128)(2,1)}, bf16[768,384]{1,0:T(8,128)(2,1)S(1)}, u32[]{:S(2)}, u32[]{:S(2)}) collective-permute-start(bf16[768,384]{1,0:T(8,128)(2,1)} %refs_1_.1), channel_id=1, source_target_pairs={{0,4},{4,8},{8,12},{12,0},{1,5},{5,9},{9,13},{13,1},{2,6},{6,10},{... | collective-permute-start | bytes 1769480 | tf_op jit(solution)/shard_map/ppermute | solution.py:17
  6.5 16.2 %collective-permute-start.1 = (bf16[768,384]{1,0:T(8,128)(2,1)}, bf16[768,384]{1,0:T(8,128)(2,1)S(1)}, u32[]{:S(2)}, u32[]{:S(2)}) collective-permute-start(bf16[768,384]{1,0:T(8,128)(2,1)} %refs_1_.1), channel_id=1, source_target_pairs={{0,3},{1,0},{2,1},{3,2},{4,7},{5,4},{6,5},{7,6},{8,11},{9,8},{10,9... | collective-permute-start | bytes 1769480 | tf_op jit(solution)/shard_map/ppermute | solution.py:17
  16.8 15.1 %collective-permute-start.7 = (bf16[768,384]{1,0:T(8,128)(2,1)S(1)}, bf16[768,384]{1,0:T(8,128)(2,1)S(1)}, u32[]{:S(2)}, u32[]{:S(2)}) collective-permute-start(bf16[768,384]{1,0:T(8,128)(2,1)S(1)} %collective-permute-done.refs_2_), channel_id=1, source_target_pairs={{0,12},{4,0},{8,4},{12,8},{1,13},{5,1},{9,5},{13,9},{2,14},{6,2},{... | collective-permute-start | bytes 1769480 | tf_op jit(solution)/shard_map/ppermute | solution.py:17
  20.9 13.0 %collective-permute-start.5 = (bf16[768,384]{1,0:T(8,128)(2,1)S(1)}, bf16[768,384]{1,0:T(8,128)(2,1)S(1)}, u32[]{:S(2)}, u32[]{:S(2)}) collective-permute-start(bf16[768,384]{1,0:T(8,128)(2,1)S(1)} %collective-permute-done.3.refs_5_), channel_id=1, source_target_pairs={{0,3},{1,0},{2,1},{3,2},{4,7},{5,4},{6,5},{7,6},{8,11},{9,8},{10,9... | collective-permute-start | bytes 1769480 | tf_op jit(solution)/shard_map/ppermute | solution.py:17
  22.2 13.9 %collective-permute-start.4 = (bf16[768,384]{1,0:T(8,128)(2,1)S(1)}, bf16[768,384]{1,0:T(8,128)(2,1)S(1)}, u32[]{:S(2)}, u32[]{:S(2)}) collective-permute-start(bf16[768,384]{1,0:T(8,128)(2,1)S(1)} %collective-permute-done.2.refs_4_), channel_id=1, source_target_pairs={{0,1},{1,2},{2,3},{3,0},{4,5},{5,6},{6,7},{7,4},{8,9},{9,10},{10,1... | collective-permute-start | bytes 1769480 | tf_op jit(solution)/shard_map/ppermute | solution.py:17
  22.7 13.6 %collective-permute-start.6 = (bf16[768,384]{1,0:T(8,128)(2,1)S(1)}, bf16[768,384]{1,0:T(8,128)(2,1)S(1)}, u32[]{:S(2)}, u32[]{:S(2)}) collective-permute-start(bf16[768,384]{1,0:T(8,128)(2,1)S(1)} %collective-permute-done.1.refs_3_), channel_id=1, source_target_pairs={{0,4},{4,8},{8,12},{12,0},{1,5},{5,9},{9,13},{13,1},{2,6},{6,10},{... | collective-permute-start | bytes 1769480 | tf_op jit(solution)/shard_map/ppermute | solution.py:17
  32.0 16.8 %collective-permute-start.8 = (bf16[768,384]{1,0:T(8,128)(2,1)S(1)}, bf16[768,384]{1,0:T(8,128)(2,1)S(1)}, u32[]{:S(2)}, u32[]{:S(2)}) collective-permute-start(bf16[768,384]{1,0:T(8,128)(2,1)S(1)} %collective-permute-done.7.refs_4_.refs_15_.refs_13_), channel_id=1, source_target_pairs={{0,1},{1,2},{2,3},{3,0},{4,5},{5,6},{6,7},{7,4},{8,9},{9,10},{10,1... | collective-permute-start | bytes 1769480 | tf_op jit(solution)/shard_map/ppermute | solution.py:17
  33.9 17.9 %collective-permute-start.11 = (bf16[768,384]{1,0:T(8,128)(2,1)S(1)}, bf16[768,384]{1,0:T(8,128)(2,1)S(1)}, u32[]{:S(2)}, u32[]{:S(2)}) collective-permute-start(bf16[768,384]{1,0:T(8,128)(2,1)S(1)} %collective-permute-done.5.refs_2_.refs_13_.refs_11_), channel_id=1, source_target_pairs={{0,12},{4,0},{8,4},{12,8},{1,13},{5,1},{9,5},{13,9},{2,14},{6,2},{... | collective-permute-start | bytes 1769480 | tf_op jit(solution)/shard_map/ppermute | solution.py:17
  36.1 15.7 %collective-permute-start.10 = (bf16[768,384]{1,0:T(8,128)(2,1)S(1)}, bf16[768,384]{1,0:T(8,128)(2,1)S(1)}, u32[]{:S(2)}, u32[]{:S(2)}) collective-permute-start(bf16[768,384]{1,0:T(8,128)(2,1)S(1)} %collective-permute-done.4.refs_1_.refs_12_.refs_10_), channel_id=1, source_target_pairs={{0,4},{4,8},{8,12},{12,0},{1,5},{5,9},{9,13},{13,1},{2,6},{6,10},{... | collective-permute-start | bytes 1769480 | tf_op jit(solution)/shard_map/ppermute | solution.py:17
  36.3 15.5 %collective-permute-start.9 = (bf16[768,384]{1,0:T(8,128)(2,1)S(1)}, bf16[768,384]{1,0:T(8,128)(2,1)S(1)}, u32[]{:S(2)}, u32[]{:S(2)}) collective-permute-start(bf16[768,384]{1,0:T(8,128)(2,1)S(1)} %collective-permute-done.6.refs_3_.refs_14_.refs_12_), channel_id=1, source_target_pairs={{0,3},{1,0},{2,1},{3,2},{4,7},{5,4},{6,5},{7,6},{8,11},{9,8},{10,9... | collective-permute-start | bytes 1769480 | tf_op jit(solution)/shard_map/ppermute | solution.py:17
  38.5 15.3 %collective-permute-start.21 = (f32[64,1920]{1,0:T(8,128)S(1)}, f32[64,1920]{1,0:T(8,128)S(1)}, u32[]{:S(2)}, u32[]{:S(2)}) collective-permute-start(f32[64,1920]{1,0:T(8,128)S(1)} %get-tuple-element.50), channel_id=1, source_target_pairs={{0,16},{16,0},{1,17},{17,1},{2,18},{18,2},{3,19},{19,3},{4,20},{20... | collective-permute-start | bytes 1474568 | tf_op jit(solution)/shard_map/ppermute | solution.py:21
  48.8 5.2 %collective-permute-start.22 = (f32[64,1536]{1,0:T(8,128)S(1)}, f32[64,1536]{1,0:T(8,128)S(1)}, u32[]{:S(2)}, u32[]{:S(2)}) collective-permute-start(f32[64,1536]{1,0:T(8,128)S(1)} %get-tuple-element.52), channel_id=1, source_target_pairs={{0,16},{16,0},{1,17},{17,1},{2,18},{18,2},{3,19},{19,3},{4,20},{20... | collective-permute-start | bytes 1179656 | tf_op jit(solution)/shard_map/ppermute | solution.py:21
  52.5 2.7 %collective-permute-start.23 = (f32[64,1536]{1,0:T(8,128)S(1)}, f32[64,1536]{1,0:T(8,128)S(1)}, u32[]{:S(2)}, u32[]{:S(2)}) collective-permute-start(f32[64,1536]{1,0:T(8,128)S(1)} %get-tuple-element.54), channel_id=1, source_target_pairs={{0,16},{16,0},{1,17},{17,1},{2,18},{18,2},{3,19},{19,3},{4,20},{20... | collective-permute-start | bytes 1179656 | tf_op jit(solution)/shard_map/ppermute | solution.py:21
  54.1 16.2 %collective-permute-start.13 = (bf16[768,384]{1,0:T(8,128)(2,1)S(1)}, bf16[768,384]{1,0:T(8,128)(2,1)S(1)}, u32[]{:S(2)}, u32[]{:S(2)}) collective-permute-start(bf16[768,384]{1,0:T(8,128)(2,1)S(1)} %collective-permute-done.2.refs_4_), channel_id=1, source_target_pairs={{0,4},{4,8},{8,12},{12,0},{1,5},{5,9},{9,13},{13,1},{2,6},{6,10},{... | collective-permute-start | bytes 1769480 | tf_op jit(solution)/shard_map/ppermute | solution.py:17
  54.2 16.2 %collective-permute-start.12 = (bf16[768,384]{1,0:T(8,128)(2,1)S(1)}, bf16[768,384]{1,0:T(8,128)(2,1)S(1)}, u32[]{:S(2)}, u32[]{:S(2)}) collective-permute-start(bf16[768,384]{1,0:T(8,128)(2,1)S(1)} %collective-permute-done.refs_2_), channel_id=1, source_target_pairs={{0,1},{1,2},{2,3},{3,0},{4,5},{5,6},{6,7},{7,4},{8,9},{9,10},{10,1... | collective-permute-start | bytes 1769480 | tf_op jit(solution)/shard_map/ppermute | solution.py:17
  55.4 6.7 %collective-permute-start.24 = (bf16[16,4992]{1,0:T(8,128)(2,1)S(1)}, bf16[16,4992]{1,0:T(8,128)(2,1)S(1)}, u32[]{:S(2)}, u32[]{:S(2)}) collective-permute-start(bf16[16,4992]{1,0:T(8,128)(2,1)S(1)} %get-tuple-element.77), channel_id=1, source_target_pairs={{0,32},{32,64},{64,96},{96,0},{1,33},{33,65},{65,97},{97,1},{2,34}... | collective-permute-start | bytes 479240 | tf_op jit(solution)/shard_map/ppermute | solution.py:17
  56.8 7.8 %collective-permute-start.25 = (bf16[16,4992]{1,0:T(8,128)(2,1)S(1)}, bf16[16,4992]{1,0:T(8,128)(2,1)S(1)}, u32[]{:S(2)}, u32[]{:S(2)}) collective-permute-start(bf16[16,4992]{1,0:T(8,128)(2,1)S(1)} %get-tuple-element.76), channel_id=1, source_target_pairs={{0,96},{32,0},{64,32},{96,64},{1,97},{33,1},{65,33},{97,65},{2,98}... | collective-permute-start | bytes 479240 | tf_op jit(solution)/shard_map/ppermute | solution.py:17
  58.3 11.8 %collective-permute-start.15 = (bf16[384,384]{1,0:T(8,128)(2,1)S(1)}, bf16[384,384]{1,0:T(8,128)(2,1)S(1)}, u32[]{:S(2)}, u32[]{:S(2)}) collective-permute-start(bf16[384,384]{1,0:T(8,128)(2,1)S(1)} %slice.117), channel_id=1, source_target_pairs={{0,12},{4,0},{8,4},{12,8},{1,13},{5,1},{9,5},{13,9},{2,14},{6,2},{... | collective-permute-start | bytes 884744 | tf_op jit(solution)/shard_map/ppermute | solution.py:17
  62.1 8.0 %collective-permute-start.14 = (bf16[384,384]{1,0:T(8,128)(2,1)S(1)}, bf16[384,384]{1,0:T(8,128)(2,1)S(1)}, u32[]{:S(2)}, u32[]{:S(2)}) collective-permute-start(bf16[384,384]{1,0:T(8,128)(2,1)S(1)} %slice.116), channel_id=1, source_target_pairs={{0,3},{1,0},{2,1},{3,2},{4,7},{5,4},{6,5},{7,6},{8,11},{9,8},{10,9... | collective-permute-start | bytes 884744 | tf_op jit(solution)/shard_map/ppermute | solution.py:17
  64.5 5.6 %collective-permute-start.26 = (bf16[16,4992]{1,0:T(8,128)(2,1)S(1)}, bf16[16,4992]{1,0:T(8,128)(2,1)S(1)}, u32[]{:S(2)}, u32[]{:S(2)}) collective-permute-start(bf16[16,4992]{1,0:T(8,128)(2,1)S(1)} %get-tuple-element.75), channel_id=1, source_target_pairs={{0,64},{32,96},{64,0},{96,32},{1,65},{33,97},{65,1},{97,33},{2,66}... | collective-permute-start | bytes 479240 | tf_op jit(solution)/shard_map/ppermute | solution.py:17
  71.0 4.4 %collective-permute-start.16 = (f32[8,128]{1,0:T(8,128)S(1)}, f32[8,128]{1,0:T(8,128)S(1)}, u32[]{:S(2)}, u32[]{:S(2)}) collective-permute-start(f32[8,128]{1,0:T(8,128)S(1)} %add_add_fusion), channel_id=1, source_target_pairs={{0,16},{16,0},{1,17},{17,1},{2,18},{18,2},{3,19},{19,3},{4,20},{20... | collective-permute-start | bytes 12296 | tf_op jit(solution)/shard_map/ppermute | solution.py:21
  73.5 8.9 %collective-permute-start.27 = (bf16[16,4992]{1,0:T(8,128)(2,1)S(1)}, bf16[16,4992]{1,0:T(8,128)(2,1)S(1)}, u32[]{:S(2)}, u32[]{:S(2)}) collective-permute-start(bf16[16,4992]{1,0:T(8,128)(2,1)S(1)} %fusion.8.refs_1_), channel_id=1, source_target_pairs={{0,96},{32,0},{64,32},{96,64},{1,97},{33,1},{65,33},{97,65},{2,98}... | collective-permute-start | bytes 479240 | tf_op jit(solution)/shard_map/ppermute | solution.py:17
  75.0 1.6 collective-permute-start.17
  76.7 18.3 %collective-permute-start.18 = (bf16[64,1280]{1,0:T(8,128)(2,1)S(1)}, bf16[64,1280]{1,0:T(8,128)(2,1)S(1)}, u32[]{:S(2)}, u32[]{:S(2)}) collective-permute-start(bf16[64,1280]{1,0:T(8,128)(2,1)S(1)} %pad_maximum_fusion.1), channel_id=1, source_target_pairs={{0,32},{32,64},{64,96},{96,0},{1,33},{33,65},{65,97},{97,1},{2,34}... | collective-permute-start | bytes 491528 | tf_op jit(solution)/shard_map/ppermute | solution.py:17
  76.8 18.2 %collective-permute-start.19 = (bf16[64,1280]{1,0:T(8,128)(2,1)S(1)}, bf16[64,1280]{1,0:T(8,128)(2,1)S(1)}, u32[]{:S(2)}, u32[]{:S(2)}) collective-permute-start(bf16[64,1280]{1,0:T(8,128)(2,1)S(1)} %pad_maximum_fusion.1), channel_id=1, source_target_pairs={{0,96},{32,0},{64,32},{96,64},{1,97},{33,1},{65,33},{97,65},{2,98}... | collective-permute-start | bytes 491528 | tf_op jit(solution)/shard_map/ppermute | solution.py:17
  79.4 16.0 %collective-permute-start.20 = (bf16[64,1280]{1,0:T(8,128)(2,1)S(1)}, bf16[64,1280]{1,0:T(8,128)(2,1)S(1)}, u32[]{:S(2)}, u32[]{:S(2)}) collective-permute-start(bf16[64,1280]{1,0:T(8,128)(2,1)S(1)} %pad_maximum_fusion.1), channel_id=1, source_target_pairs={{0,64},{32,96},{64,0},{96,32},{1,65},{33,97},{65,1},{97,33},{2,66}... | collective-permute-start | bytes 491528 | tf_op jit(solution)/shard_map/ppermute | solution.py:17
  79.4 9.9 %collective-permute-start.28 = (bf16[16,4992]{1,0:T(8,128)(2,1)S(1)}, bf16[16,4992]{1,0:T(8,128)(2,1)S(1)}, u32[]{:S(2)}, u32[]{:S(2)}) collective-permute-start(bf16[16,4992]{1,0:T(8,128)(2,1)S(1)} %fusion.8.refs_1_), channel_id=1, source_target_pairs={{0,64},{32,96},{64,0},{96,32},{1,65},{33,97},{65,1},{97,33},{2,66}... | collective-permute-start | bytes 479240 | tf_op jit(solution)/shard_map/ppermute | solution.py:17
  82.4 11.8 %collective-permute-start.29 = (bf16[16,4992]{1,0:T(8,128)(2,1)S(1)}, bf16[16,4992]{1,0:T(8,128)(2,1)S(1)}, u32[]{:S(2)}, u32[]{:S(2)}) collective-permute-start(bf16[16,4992]{1,0:T(8,128)(2,1)S(1)} %fusion.8.refs_1_), channel_id=1, source_target_pairs={{0,32},{32,64},{64,96},{96,0},{1,33},{33,65},{65,97},{97,1},{2,34}... | collective-permute-start | bytes 479240 | tf_op jit(solution)/shard_map/ppermute | solution.py:17
  89.3 6.5 %collective-permute-start.30 = (bf16[16,4992]{1,0:T(8,128)(2,1)S(1)}, bf16[16,4992]{1,0:T(8,128)(2,1)S(1)}, u32[]{:S(2)}, u32[]{:S(2)}) collective-permute-start(bf16[16,4992]{1,0:T(8,128)(2,1)S(1)} %fusion.8.refs_1_), channel_id=1, source_target_pairs={{0,16},{16,0},{1,17},{17,1},{2,18},{18,2},{3,19},{19,3},{4,20},{20... | collective-permute-start | bytes 479240 | tf_op jit(solution)/shard_map/ppermute | solution.py:21
  94.2 1.8 %collective-permute-start.31 = (bf16[16,4992]{1,0:T(8,128)(2,1)S(1)}, bf16[16,4992]{1,0:T(8,128)(2,1)S(1)}, u32[]{:S(2)}, u32[]{:S(2)}) collective-permute-start(bf16[16,4992]{1,0:T(8,128)(2,1)S(1)} %collective-permute-done.27.refs_2_), channel_id=1, source_target_pairs={{0,16},{16,0},{1,17},{17,1},{2,18},{18,2},{3,19},{19,3},{4,20},{20... | collective-permute-start | bytes 479240 | tf_op jit(solution)/shard_map/ppermute | solution.py:21
  95.0 1.6 collective-permute-start.33
  95.6 1.5 collective-permute-start.34
  101.8 3.5 %collective-permute-start.35 = (f32[64,6144]{1,0:T(8,128)S(1)}, f32[64,6144]{1,0:T(8,128)S(1)}, u32[]{:S(2)}, u32[]{:S(2)}) collective-permute-start(f32[64,6144]{1,0:T(8,128)S(1)} %get-tuple-element.60), channel_id=1, source_target_pairs={{0,16},{16,0},{1,17},{17,1},{2,18},{18,2},{3,19},{19,3},{4,20},{20... | collective-permute-start | bytes 4718600 | tf_op jit(solution)/shard_map/ppermute | solution.py:21
  105.5 11.8 %collective-permute-start.36 = (bf16[16,6144]{1,0:T(8,128)(2,1)S(1)}, bf16[16,6144]{1,0:T(8,128)(2,1)S(1)}, u32[]{:S(2)}, u32[]{:S(2)}) collective-permute-start(bf16[16,6144]{1,0:T(8,128)(2,1)S(1)} %get-tuple-element.74), channel_id=1, source_target_pairs={{0,32},{32,64},{64,96},{96,0},{1,33},{33,65},{65,97},{97,1},{2,34}... | collective-permute-start | bytes 589832 | tf_op jit(solution)/shard_map/ppermute | solution.py:17
  105.6 11.8 %collective-permute-start.37 = (bf16[16,6144]{1,0:T(8,128)(2,1)S(1)}, bf16[16,6144]{1,0:T(8,128)(2,1)S(1)}, u32[]{:S(2)}, u32[]{:S(2)}) collective-permute-start(bf16[16,6144]{1,0:T(8,128)(2,1)S(1)} %get-tuple-element.73), channel_id=1, source_target_pairs={{0,96},{32,0},{64,32},{96,64},{1,97},{33,1},{65,33},{97,65},{2,98}... | collective-permute-start | bytes 589832 | tf_op jit(solution)/shard_map/ppermute | solution.py:17
  108.3 9.1 %collective-permute-start.38 = (bf16[16,6144]{1,0:T(8,128)(2,1)S(1)}, bf16[16,6144]{1,0:T(8,128)(2,1)S(1)}, u32[]{:S(2)}, u32[]{:S(2)}) collective-permute-start(bf16[16,6144]{1,0:T(8,128)(2,1)S(1)} %get-tuple-element.72), channel_id=1, source_target_pairs={{0,64},{32,96},{64,0},{96,32},{1,65},{33,97},{65,1},{97,33},{2,66}... | collective-permute-start | bytes 589832 | tf_op jit(solution)/shard_map/ppermute | solution.py:17
  117.5 5.9 %collective-permute-start.39 = (bf16[16,6144]{1,0:T(8,128)(2,1)S(1)}, bf16[16,6144]{1,0:T(8,128)(2,1)S(1)}, u32[]{:S(2)}, u32[]{:S(2)}) collective-permute-start(bf16[16,6144]{1,0:T(8,128)(2,1)S(1)} %fusion.5.refs_1_), channel_id=1, source_target_pairs={{0,96},{32,0},{64,32},{96,64},{1,97},{33,1},{65,33},{97,65},{2,98}... | collective-permute-start | bytes 589832 | tf_op jit(solution)/shard_map/ppermute | solution.py:17
  119.9 9.4 %collective-permute-start.40 = (bf16[16,6144]{1,0:T(8,128)(2,1)S(1)}, bf16[16,6144]{1,0:T(8,128)(2,1)S(1)}, u32[]{:S(2)}, u32[]{:S(2)}) collective-permute-start(bf16[16,6144]{1,0:T(8,128)(2,1)S(1)} %fusion.5.refs_1_), channel_id=1, source_target_pairs={{0,64},{32,96},{64,0},{96,32},{1,65},{33,97},{65,1},{97,33},{2,66}... | collective-permute-start | bytes 589832 | tf_op jit(solution)/shard_map/ppermute | solution.py:17
  119.9 11.9 %collective-permute-start.41 = (bf16[16,6144]{1,0:T(8,128)(2,1)S(1)}, bf16[16,6144]{1,0:T(8,128)(2,1)S(1)}, u32[]{:S(2)}, u32[]{:S(2)}) collective-permute-start(bf16[16,6144]{1,0:T(8,128)(2,1)S(1)} %fusion.5.refs_1_), channel_id=1, source_target_pairs={{0,32},{32,64},{64,96},{96,0},{1,33},{33,65},{65,97},{97,1},{2,34}... | collective-permute-start | bytes 589832 | tf_op jit(solution)/shard_map/ppermute | solution.py:17
  120.6 12.3 %collective-permute-start.42 = (bf16[16,6144]{1,0:T(8,128)(2,1)S(1)}, bf16[16,6144]{1,0:T(8,128)(2,1)S(1)}, u32[]{:S(2)}, u32[]{:S(2)}) collective-permute-start(bf16[16,6144]{1,0:T(8,128)(2,1)S(1)} %fusion.5.refs_1_), channel_id=1, source_target_pairs={{0,16},{16,0},{1,17},{17,1},{2,18},{18,2},{3,19},{19,3},{4,20},{20... | collective-permute-start | bytes 589832 | tf_op jit(solution)/shard_map/ppermute | solution.py:21
  123.4 9.5 %collective-permute-start.43 = (bf16[16,6144]{1,0:T(8,128)(2,1)S(1)}, bf16[16,6144]{1,0:T(8,128)(2,1)S(1)}, u32[]{:S(2)}, u32[]{:S(2)}) collective-permute-start(bf16[16,6144]{1,0:T(8,128)(2,1)S(1)} %collective-permute-done.39.refs_2_), channel_id=1, source_target_pairs={{0,16},{16,0},{1,17},{17,1},{2,18},{18,2},{3,19},{19,3},{4,20},{20... | collective-permute-start | bytes 589832 | tf_op jit(solution)/shard_map/ppermute | solution.py:21
  129.3 3.6 %collective-permute-start.44 = (bf16[16,6144]{1,0:T(8,128)(2,1)S(1)}, bf16[16,6144]{1,0:T(8,128)(2,1)S(1)}, u32[]{:S(2)}, u32[]{:S(2)}) collective-permute-start(bf16[16,6144]{1,0:T(8,128)(2,1)S(1)} %collective-permute-done.40.refs_3_), channel_id=1, source_target_pairs={{0,16},{16,0},{1,17},{17,1},{2,18},{18,2},{3,19},{19,3},{4,20},{20... | collective-permute-start | bytes 589832 | tf_op jit(solution)/shard_map/ppermute | solution.py:21
  131.8 1.9 %collective-permute-start.45 = (bf16[16,6144]{1,0:T(8,128)(2,1)S(1)}, bf16[16,6144]{1,0:T(8,128)(2,1)S(1)}, u32[]{:S(2)}, u32[]{:S(2)}) collective-permute-start(bf16[16,6144]{1,0:T(8,128)(2,1)S(1)} %collective-permute-done.41.refs_4_), channel_id=1, source_target_pairs={{0,16},{16,0},{1,17},{17,1},{2,18},{18,2},{3,19},{19,3},{4,20},{20... | collective-permute-start | bytes 589832 | tf_op jit(solution)/shard_map/ppermute | solution.py:21
  137.7 16.1 %all-to-all-start = ((bf16[4,768,128]{2,1,0:T(8,128)(2,1)}), bf16[4,768,128]{2,1,0:T(8,128)(2,1)S(1)}, u32[]{:S(2)}, u32[]{:S(2)}) async-start(bf16[4,768,128]{2,1,0:T(8,128)(2,1)} %get-tuple-element.65), calls=%async_computation | async-start | bytes 1572864 | tf_op jit(solution)/shard_map/all_to_all | solution.py:215
  154.5 3.7 %collective-permute-start.46 = (f32[16,64,128]{2,1,0:T(8,128)S(1)}, f32[16,64,128]{2,1,0:T(8,128)S(1)}, u32[]{:S(2)}, u32[]{:S(2)}) collective-permute-start(f32[16,64,128]{2,1,0:T(8,128)S(1)} %dynamic-slice_bitcast_fusion), channel_id=1, source_target_pairs={{0,16},{16,0},{1,17},{17,1},{2,18},{18,2},{3,19},{19,3},{4,20},{20... | collective-permute-start | bytes 1572872 | tf_op jit(solution)/shard_map/ppermute | solution.py:21
  170.7 2.5 %collective-permute-start.47 = (f32[2,64,128]{2,1,0:T(8,128)S(1)}, f32[2,64,128]{2,1,0:T(8,128)S(1)}, u32[]{:S(2)}, u32[]{:S(2)}) collective-permute-start(f32[2,64,128]{2,1,0:T(8,128)S(1)} %dynamic-slice_bitcast_fusion.1), channel_id=1, source_target_pairs={{0,16},{16,0},{1,17},{17,1},{2,18},{18,2},{3,19},{19,3},{4,20},{20... | collective-permute-start | bytes 196616 | tf_op jit(solution)/shard_map/ppermute | solution.py:21
  (10 other events, 85.8 us)

commit v7 on v6

--- a/solution.py
+++ b/solution.py
@@ -10,7 +10,7 @@
 COLS = 384
 BLOCKS = 16
 KEPT = 5
-SPLIT = 16
+SPLIT = 8
 
 
 def shift(x, axis, by):
@@ -208,7 +208,8 @@
     blocks, early, fourth, square = gather_and_apply(theta, x)
     late, square = sum_over_y_at_once(core_sum(*fourth[:2]), square + other_core(square))
     t = gather_y(early) + late
-    t = sum_over_y([core_sum(*apply(square, t, blocks))])
+    parts = apply(square, t, blocks)
+    t = sum_over_y([core_sum(*parts[:2])]) + sum_over_y([core_sum(*parts[2:])])
     subspace, copies = apply(square, t, blocks, order)
 
     along_x = lax.all_gather(subspace, "x", axis=0)

time: 174 us -> 173 us (level)
  waiting for transfers between devices: 59.6 us -> 50.8 us
  starting transfers between devices: 73.3 us -> 80.2 us
    ppermute x31 -> x37, starting transfers between devices: 39.7 us -> 47.7 us  [shift(): return lax.ppermute(x, axis, [(i, (i + by) % 4) for i in range(4)])]
    ppermute x31 -> x37, waiting for transfers between devices: 50.1 us -> 42.8 us  [shift(): return lax.ppermute(x, axis, [(i, (i + by) % 4) for i in range(4)])]
    ppermute x17 -> x22, waiting for transfers between devices: 9.53 us -> 7.99 us  [other_core(): return lax.ppermute(x, 'core', [(0, 1), (1, 0)])]
    ppermute x17 -> x22, starting transfers between devices: 29.4 us -> 28.5 us  [other_core(): return lax.ppermute(x, 'core', [(0, 1), (1, 0)])]
  transfers between devices with their start and end apart: 49 -> 60, of which waited for: 25 -> 28; matrix products, arithmetic and copies ran while one was open for 1% -> 1% of each run, Pallas kernels for 1% -> 1%
where the time goes in v7:
time: 173 us; the launch traced here: 172 us
  starting transfers between devices  80.2 us (46%)
  waiting for transfers between devices  50.8 us (29%)
  blocking collectives  24.9 us (14%)
  Pallas kernels  11.1 us (6%)
  local copies, waits for them, and re-layouts  2.24 us (1%)
    ppermute x37, starting transfers between devices, shift(): return lax.ppermute(x, axis, [(i, (i + by) % 4) for i in range(4)])  47.7 us
    ppermute x37, waiting for transfers between devices, shift(): return lax.ppermute(x, axis, [(i, (i + by) % 4) for i in range(4)])  42.8 us
    ppermute x22, starting transfers between devices, other_core(): return lax.ppermute(x, 'core', [(0, 1), (1, 0)])  28.5 us
    all_to_all x1, blocking collectives, per_device(): lax.all_to_all(half.astype(jnp.bfloat16), ('y', 'x'), 0, 0)  12.9 us
    all_gather x1, blocking collectives, per_device(): along_x = lax.all_gather(subspace, 'x', axis=0)  12 us
    pallas_call x2, Pallas kernels, apply(): pl.pallas_call(lambda *refs: apply_kernel(down, len(t), *refs), out_shape...  8.58 us
    ppermute x22, waiting for transfers between devices, other_core(): return lax.ppermute(x, 'core', [(0, 1), (1, 0)])  7.99 us
    all_to_all x1, starting transfers between devices, per_device(): along_z = lax.all_to_all(copies, 'z', 0, 0)  4.03 us
  transfers between devices with their start and end apart: 60, of which 28 were waited for; matrix products, arithmetic and copies ran while one was open for 1% of the time, Pallas kernels for 1%

profile of v7, /device:TPU:1, one launch (start us, length us, event | category | flops | bytes accessed | tf_op | source)
XLA Modules:
  0.0 172.4 jit_solution(4916419896027593516)
XLA Ops:
  0.6 2.1 %collective-permute-start = (bf16[768,384]{1,0:T(8,128)(2,1)}, bf16[768,384]{1,0:T(8,128)(2,1)S(1)}, u32[]{:S(2)}, u32[]{:S(2)}) collective-permute-start(bf16[768,384]{1,0:T(8,128)(2,1)} %refs_1_.1), channel_id=1, source_target_pairs={{0,1},{1,2},{2,3},{3,0},{4,5},{5,6},{6,7},{7,4},{8,9},{9,10},{10,1... | collective-permute-start | bytes 1769480 | tf_op jit(solution)/shard_map/ppermute | solution.py:17
  2.8 3.8 %collective-permute-start.3 = (bf16[768,384]{1,0:T(8,128)(2,1)}, bf16[768,384]{1,0:T(8,128)(2,1)S(1)}, u32[]{:S(2)}, u32[]{:S(2)}) collective-permute-start(bf16[768,384]{1,0:T(8,128)(2,1)} %refs_1_.1), channel_id=1, source_target_pairs={{0,12},{4,0},{8,4},{12,8},{1,13},{5,1},{9,5},{13,9},{2,14},{6,2},{... | collective-permute-start | bytes 1769480 | tf_op jit(solution)/shard_map/ppermute | solution.py:17
  6.5 1.5 collective-permute-start.1
  8.0 8.9 %collective-permute-done.refs_2_ = bf16[768,384]{1,0:T(8,128)(2,1)S(1)} collective-permute-done((bf16[768,384]{1,0:T(8,128)(2,1)}, bf16[768,384]{1,0:T(8,128)(2,1)S(1)}, u32[]{:S(2)}, u32[]{:S(2)}) %collective-permute-start) | collective-permute-done | bytes 589856 | tf_op jit(solution)/shard_map/ppermute | solution.py:17
  16.8 4.1 %collective-permute-start.7 = (bf16[768,384]{1,0:T(8,128)(2,1)S(1)}, bf16[768,384]{1,0:T(8,128)(2,1)S(1)}, u32[]{:S(2)}, u32[]{:S(2)}) collective-permute-start(bf16[768,384]{1,0:T(8,128)(2,1)S(1)} %collective-permute-done.refs_2_), channel_id=1, source_target_pairs={{0,12},{4,0},{8,4},{12,8},{1,13},{5,1},{9,5},{13,9},{2,14},{6,2},{... | collective-permute-start | bytes 1769480 | tf_op jit(solution)/shard_map/ppermute | solution.py:17
  20.9 1.3 collective-permute-start.5
  25.0 7.0 %collective-permute-done.7.refs_4_.refs_15_.refs_21_ = bf16[768,384]{1,0:T(8,128)(2,1)S(1)} collective-permute-done((bf16[768,384]{1,0:T(8,128)(2,1)S(1)}, bf16[768,384]{1,0:T(8,128)(2,1)S(1)}, u32[]{:S(2)}, u32[]{:S(2)}) %collective-permute-start.7) | collective-permute-done | bytes 589856 | tf_op jit(solution)/shard_map/ppermute | solution.py:17
  32.0 1.9 %collective-permute-done.5.refs_2_.refs_13_.refs_19_ = bf16[768,384]{1,0:T(8,128)(2,1)S(1)} collective-permute-done((bf16[768,384]{1,0:T(8,128)(2,1)S(1)}, bf16[768,384]{1,0:T(8,128)(2,1)S(1)}, u32[]{:S(2)}, u32[]{:S(2)}) %collective-permute-start.5) | collective-permute-done | bytes 589856 | tf_op jit(solution)/shard_map/ppermute | solution.py:17
  33.9 1.5 collective-permute-start.11
  36.3 2.2 %collective-permute-start.9 = (bf16[768,384]{1,0:T(8,128)(2,1)S(1)}, bf16[768,384]{1,0:T(8,128)(2,1)S(1)}, u32[]{:S(2)}, u32[]{:S(2)}) collective-permute-start(bf16[768,384]{1,0:T(8,128)(2,1)S(1)} %collective-permute-done.6.refs_3_.refs_14_.refs_20_), channel_id=1, source_target_pairs={{0,3},{1,0},{2,1},{3,2},{4,7},{5,4},{6,5},{7,6},{8,11},{9,8},{10,9... | collective-permute-start | bytes 1769480 | tf_op jit(solution)/shard_map/ppermute | solution.py:17
  38.5 3.6 %collective-permute-start.21 = (f32[64,1920]{1,0:T(8,128)S(1)}, f32[64,1920]{1,0:T(8,128)S(1)}, u32[]{:S(2)}, u32[]{:S(2)}) collective-permute-start(f32[64,1920]{1,0:T(8,128)S(1)} %get-tuple-element.55), channel_id=1, source_target_pairs={{0,16},{16,0},{1,17},{17,1},{2,18},{18,2},{3,19},{19,3},{4,20},{20... | collective-permute-start | bytes 1474568 | tf_op jit(solution)/shard_map/ppermute | solution.py:21
  42.7 6.1 %collective-permute-done.8.refs_1_.refs_16_.refs_22_ = bf16[768,384]{1,0:T(8,128)(2,1)S(1)} collective-permute-done((bf16[768,384]{1,0:T(8,128)(2,1)S(1)}, bf16[768,384]{1,0:T(8,128)(2,1)S(1)}, u32[]{:S(2)}, u32[]{:S(2)}) %collective-permute-start.8) | collective-permute-done | bytes 589856 | tf_op jit(solution)/shard_map/ppermute | solution.py:17
  48.8 3.0 %collective-permute-start.22 = (f32[64,1536]{1,0:T(8,128)S(1)}, f32[64,1536]{1,0:T(8,128)S(1)}, u32[]{:S(2)}, u32[]{:S(2)}) collective-permute-start(f32[64,1536]{1,0:T(8,128)S(1)} %get-tuple-element.57), channel_id=1, source_target_pairs={{0,16},{16,0},{1,17},{17,1},{2,18},{18,2},{3,19},{19,3},{4,20},{20... | collective-permute-start | bytes 1179656 | tf_op jit(solution)/shard_map/ppermute | solution.py:21
  52.4 1.4 collective-permute-start.23
  55.3 1.4 collective-permute-start.24
  56.6 1.5 collective-permute-start.25
  58.2 2.2 %collective-permute-start.15 = (bf16[384,384]{1,0:T(8,128)(2,1)S(1)}, bf16[384,384]{1,0:T(8,128)(2,1)S(1)}, u32[]{:S(2)}, u32[]{:S(2)}) collective-permute-start(bf16[384,384]{1,0:T(8,128)(2,1)S(1)} %slice.138), channel_id=1, source_target_pairs={{0,12},{4,0},{8,4},{12,8},{1,13},{5,1},{9,5},{13,9},{2,14},{6,2},{... | collective-permute-start | bytes 884744 | tf_op jit(solution)/shard_map/ppermute | solution.py:17
  60.4 1.6 collective-permute-done.24
  62.0 2.4 %collective-permute-start.14 = (bf16[384,384]{1,0:T(8,128)(2,1)S(1)}, bf16[384,384]{1,0:T(8,128)(2,1)S(1)}, u32[]{:S(2)}, u32[]{:S(2)}) collective-permute-start(bf16[384,384]{1,0:T(8,128)(2,1)S(1)} %slice.137), channel_id=1, source_target_pairs={{0,3},{1,0},{2,1},{3,2},{4,7},{5,4},{6,5},{7,6},{8,11},{9,8},{10,9... | collective-permute-start | bytes 884744 | tf_op jit(solution)/shard_map/ppermute | solution.py:17
  64.4 1.6 collective-permute-start.26
  66.0 4.0 %collective-permute-done.26 = bf16[16,4992]{1,0:T(8,128)(2,1)S(1)} collective-permute-done((bf16[16,4992]{1,0:T(8,128)(2,1)S(1)}, bf16[16,4992]{1,0:T(8,128)(2,1)S(1)}, u32[]{:S(2)}, u32[]{:S(2)}) %collective-permute-start.26) | collective-permute-done | bytes 159776 | tf_op jit(solution)/shard_map/ppermute | solution.py:17
  70.8 2.5 %collective-permute-start.16 = (f32[8,128]{1,0:T(8,128)S(1)}, f32[8,128]{1,0:T(8,128)S(1)}, u32[]{:S(2)}, u32[]{:S(2)}) collective-permute-start(f32[8,128]{1,0:T(8,128)S(1)} %add_add_fusion), channel_id=1, source_target_pairs={{0,16},{16,0},{1,17},{17,1},{2,18},{18,2},{3,19},{19,3},{4,20},{20... | collective-permute-start | bytes 12296 | tf_op jit(solution)/shard_map/ppermute | solution.py:21
  73.3 1.5 collective-permute-start.27
  75.2 1.3 collective-permute-done.17
  76.6 2.7 %collective-permute-start.19 = (bf16[64,1280]{1,0:T(8,128)(2,1)S(1)}, bf16[64,1280]{1,0:T(8,128)(2,1)S(1)}, u32[]{:S(2)}, u32[]{:S(2)}) collective-permute-start(bf16[64,1280]{1,0:T(8,128)(2,1)S(1)} %pad_maximum_fusion.1), channel_id=1, source_target_pairs={{0,96},{32,0},{64,32},{96,64},{1,97},{33,1},{65,33},{97,65},{2,98}... | collective-permute-start | bytes 491528 | tf_op jit(solution)/shard_map/ppermute | solution.py:17
  79.3 3.0 %collective-permute-start.28 = (bf16[16,4992]{1,0:T(8,128)(2,1)S(1)}, bf16[16,4992]{1,0:T(8,128)(2,1)S(1)}, u32[]{:S(2)}, u32[]{:S(2)}) collective-permute-start(bf16[16,4992]{1,0:T(8,128)(2,1)S(1)} %fusion.5.refs_1_), channel_id=1, source_target_pairs={{0,64},{32,96},{64,0},{96,32},{1,65},{33,97},{65,1},{97,33},{2,66}... | collective-permute-start | bytes 479240 | tf_op jit(solution)/shard_map/ppermute | solution.py:17
  82.3 6.9 %collective-permute-done.28.refs_3_ = bf16[16,4992]{1,0:T(8,128)(2,1)S(1)} collective-permute-done((bf16[16,4992]{1,0:T(8,128)(2,1)S(1)}, bf16[16,4992]{1,0:T(8,128)(2,1)S(1)}, u32[]{:S(2)}, u32[]{:S(2)}) %collective-permute-start.28) | collective-permute-done | bytes 159776 | tf_op jit(solution)/shard_map/ppermute | solution.py:17
  89.2 3.0 %collective-permute-start.30 = (bf16[16,4992]{1,0:T(8,128)(2,1)S(1)}, bf16[16,4992]{1,0:T(8,128)(2,1)S(1)}, u32[]{:S(2)}, u32[]{:S(2)}) collective-permute-start(bf16[16,4992]{1,0:T(8,128)(2,1)S(1)} %fusion.5.refs_1_), channel_id=1, source_target_pairs={{0,16},{16,0},{1,17},{17,1},{2,18},{18,2},{3,19},{19,3},{4,20},{20... | collective-permute-start | bytes 479240 | tf_op jit(solution)/shard_map/ppermute | solution.py:21
  92.2 1.8 %collective-permute-done.29.refs_4_ = bf16[16,4992]{1,0:T(8,128)(2,1)S(1)} collective-permute-done((bf16[16,4992]{1,0:T(8,128)(2,1)S(1)}, bf16[16,4992]{1,0:T(8,128)(2,1)S(1)}, u32[]{:S(2)}, u32[]{:S(2)}) %collective-permute-start.29) | collective-permute-done | bytes 159776 | tf_op jit(solution)/shard_map/ppermute | solution.py:17
  96.9 4.6 %shard_map.45 = (f32[64,3072]{1,0:T(8,128)S(1)}, f32[64,3072]{1,0:T(8,128)S(1)}, f32[64,3072]{1,0:T(8,128)S(1)}, f32[64,3072]{1,0:T(8,128)S(1)}) custom-call(f32[8,128]{1,0:T(8,128)S(1)} %convert_add_fusion.refs_0_, bf16[16,4992]{1,0:T(8,128)(2,1)S(1)} %fusion.5.refs_1_, bf16[16,4992]{1,0:T(8,128)(2,1)S(1)} %collective-permute-done.27.refs_2_, ...), custom_call_target="tpu_custom_call" | custom-call | flops 2415919104 | bytes 9437184 | tf_op jit(solution)/shard_map/pallas_call | solution.py:182
  102.2 1.8 %collective-permute-done.46 = f32[64,3072]{1,0:T(8,128)S(1)} collective-permute-done((f32[64,3072]{1,0:T(8,128)S(1)}, f32[64,3072]{1,0:T(8,128)S(1)}, u32[]{:S(2)}, u32[]{:S(2)}) %collective-permute-start.46) | collective-permute-done | bytes 786464 | tf_op jit(solution)/shard_map/ppermute | solution.py:21
  104.1 2.7 %collective-permute-start.48 = (bf16[16,3072]{1,0:T(8,128)(2,1)S(1)}, bf16[16,3072]{1,0:T(8,128)(2,1)S(1)}, u32[]{:S(2)}, u32[]{:S(2)}) collective-permute-start(bf16[16,3072]{1,0:T(8,128)(2,1)S(1)} %get-tuple-element.88), channel_id=1, source_target_pairs={{0,96},{32,0},{64,32},{96,64},{1,97},{33,1},{65,33},{97,65},{2,98}... | collective-permute-start | bytes 294920 | tf_op jit(solution)/shard_map/ppermute | solution.py:17
  107.6 2.1 %collective-permute-start.37 = (bf16[16,3072]{1,0:T(8,128)(2,1)S(1)}, bf16[16,3072]{1,0:T(8,128)(2,1)S(1)}, u32[]{:S(2)}, u32[]{:S(2)}) collective-permute-start(bf16[16,3072]{1,0:T(8,128)(2,1)S(1)} %get-tuple-element.91), channel_id=1, source_target_pairs={{0,96},{32,0},{64,32},{96,64},{1,97},{33,1},{65,33},{97,65},{2,98}... | collective-permute-start | bytes 294920 | tf_op jit(solution)/shard_map/ppermute | solution.py:17
  109.7 1.8 %collective-permute-start.38 = (bf16[16,3072]{1,0:T(8,128)(2,1)S(1)}, bf16[16,3072]{1,0:T(8,128)(2,1)S(1)}, u32[]{:S(2)}, u32[]{:S(2)}) collective-permute-start(bf16[16,3072]{1,0:T(8,128)(2,1)S(1)} %get-tuple-element.90), channel_id=1, source_target_pairs={{0,64},{32,96},{64,0},{96,32},{1,65},{33,97},{65,1},{97,33},{2,66}... | collective-permute-start | bytes 294920 | tf_op jit(solution)/shard_map/ppermute | solution.py:17
  111.9 2.5 %collective-permute-start.50 = (bf16[16,3072]{1,0:T(8,128)(2,1)S(1)}, bf16[16,3072]{1,0:T(8,128)(2,1)S(1)}, u32[]{:S(2)}, u32[]{:S(2)}) collective-permute-start(bf16[16,3072]{1,0:T(8,128)(2,1)S(1)} %fusion.8.refs_9_), channel_id=1, source_target_pairs={{0,96},{32,0},{64,32},{96,64},{1,97},{33,1},{65,33},{97,65},{2,98}... | collective-permute-start | bytes 294920 | tf_op jit(solution)/shard_map/ppermute | solution.py:17
  114.5 1.4 collective-permute-done.36
  115.9 2.5 %collective-permute-start.53 = (bf16[16,3072]{1,0:T(8,128)(2,1)S(1)}, bf16[16,3072]{1,0:T(8,128)(2,1)S(1)}, u32[]{:S(2)}, u32[]{:S(2)}) collective-permute-start(bf16[16,3072]{1,0:T(8,128)(2,1)S(1)} %fusion.8.refs_9_), channel_id=1, source_target_pairs={{0,16},{16,0},{1,17},{17,1},{2,18},{18,2},{3,19},{19,3},{4,20},{20... | collective-permute-start | bytes 294920 | tf_op jit(solution)/shard_map/ppermute | solution.py:21
  118.4 2.9 %collective-permute-start.39 = (bf16[16,3072]{1,0:T(8,128)(2,1)S(1)}, bf16[16,3072]{1,0:T(8,128)(2,1)S(1)}, u32[]{:S(2)}, u32[]{:S(2)}) collective-permute-start(bf16[16,3072]{1,0:T(8,128)(2,1)S(1)} %fusion.11.refs_1_), channel_id=1, source_target_pairs={{0,96},{32,0},{64,32},{96,64},{1,97},{33,1},{65,33},{97,65},{2,98}... | collective-permute-start | bytes 294920 | tf_op jit(solution)/shard_map/ppermute | solution.py:17
  122.5 2.6 %collective-permute-start.42 = (bf16[16,3072]{1,0:T(8,128)(2,1)S(1)}, bf16[16,3072]{1,0:T(8,128)(2,1)S(1)}, u32[]{:S(2)}, u32[]{:S(2)}) collective-permute-start(bf16[16,3072]{1,0:T(8,128)(2,1)S(1)} %fusion.11.refs_1_), channel_id=1, source_target_pairs={{0,16},{16,0},{1,17},{17,1},{2,18},{18,2},{3,19},{19,3},{4,20},{20... | collective-permute-start | bytes 294920 | tf_op jit(solution)/shard_map/ppermute | solution.py:21
  125.6 1.3 collective-permute-done.40.refs_3_
  126.9 1.8 %collective-permute-start.56 = (bf16[16,3072]{1,0:T(8,128)(2,1)S(1)}, bf16[16,3072]{1,0:T(8,128)(2,1)S(1)}, u32[]{:S(2)}, u32[]{:S(2)}) collective-permute-start(bf16[16,3072]{1,0:T(8,128)(2,1)S(1)} %collective-permute-done.52.refs_12_), channel_id=1, source_target_pairs={{0,16},{16,0},{1,17},{17,1},{2,18},{18,2},{3,19},{19,3},{4,20},{20... | collective-permute-start | bytes 294920 | tf_op jit(solution)/shard_map/ppermute | solution.py:21
  131.6 3.9 %shard_map.46 = (bf16[768,128]{1,0:T(8,128)(2,1)}, bf16[4,768,128]{2,1,0:T(8,128)(2,1)}) custom-call(f32[8,128]{1,0:T(8,128)S(1)} %convert_add_fusion.refs_0_, bf16[16,3072]{1,0:T(8,128)(2,1)S(1)} %fusion.11.refs_1_, bf16[16,3072]{1,0:T(8,128)(2,1)S(1)} %collective-permute-done.39.refs_2_, bf16[16,3072]{1,0:T(8,128)(2,1)S(1)} %collective-permute-done.40.refs_3_, ...), custom_call_target="tpu_custom_call" | custom-call | flops 1207959552 | bytes 9437184 | tf_op jit(solution)/shard_map/pallas_call | solution.py:182
  135.5 4.0 %all-to-all-start = ((bf16[4,768,128]{2,1,0:T(8,128)(2,1)}), bf16[4,768,128]{2,1,0:T(8,128)(2,1)S(1)}, u32[]{:S(2)}, u32[]{:S(2)}) async-start(bf16[4,768,128]{2,1,0:T(8,128)(2,1)} %get-tuple-element.75), calls=%async_computation | async-start | bytes 1572864 | tf_op jit(solution)/shard_map/all_to_all | solution.py:216
  139.6 12.0 %all-gather = bf16[3072,128]{1,0:T(8,128)(2,1)S(1)} all-gather(bf16[768,128]{1,0:T(8,128)(2,1)} %get-tuple-element.37), channel_id=2, replica_groups=mesh['y'=4,'core'=2,'z'=4,'x'=4] {'x'}, dimensions={0}, use_global_device_ids=true | all-gather | bytes 983040 | tf_op jit(solution)/shard_map/all_gather | solution.py:215
  152.4 2.2 %collective-permute-start.57 = (f32[16,64,128]{2,1,0:T(8,128)S(1)}, f32[16,64,128]{2,1,0:T(8,128)S(1)}, u32[]{:S(2)}, u32[]{:S(2)}) collective-permute-start(f32[16,64,128]{2,1,0:T(8,128)S(1)} %dynamic-slice_bitcast_fusion), channel_id=1, source_target_pairs={{0,16},{16,0},{1,17},{17,1},{2,18},{18,2},{3,19},{19,3},{4,20},{20... | collective-permute-start | bytes 1572872 | tf_op jit(solution)/shard_map/ppermute | solution.py:21
  154.5 1.5 collective-permute-done.57
  156.2 12.9 %all_to_all.10 = bf16[16,64,128]{2,1,0:T(8,128)(2,1)S(1)} all-to-all(bf16[16,64,128]{2,1,0:T(8,128)(2,1)S(1)} %fusion.2), channel_id=1, replica_groups=mesh['y'=4,'core'=2,'z'=4,'x'=4] {'y','x'}, dimensions={0} | all-to-all | bytes 524288 | tf_op jit(solution)/shard_map/all_to_all | solution.py:221
  169.1 1.6 collective-permute-start.58
  (135 shorter events, 19.8 us)
Async XLA Ops:
  0.6 16.2 %collective-permute-start = (bf16[768,384]{1,0:T(8,128)(2,1)}, bf16[768,384]{1,0:T(8,128)(2,1)S(1)}, u32[]{:S(2)}, u32[]{:S(2)}) collective-permute-start(bf16[768,384]{1,0:T(8,128)(2,1)} %refs_1_.1), channel_id=1, source_target_pairs={{0,1},{1,2},{2,3},{3,0},{4,5},{5,6},{6,7},{7,4},{8,9},{9,10},{10,1... | collective-permute-start | bytes 1769480 | tf_op jit(solution)/shard_map/ppermute | solution.py:17
  2.8 18.2 %collective-permute-start.3 = (bf16[768,384]{1,0:T(8,128)(2,1)}, bf16[768,384]{1,0:T(8,128)(2,1)S(1)}, u32[]{:S(2)}, u32[]{:S(2)}) collective-permute-start(bf16[768,384]{1,0:T(8,128)(2,1)} %refs_1_.1), channel_id=1, source_target_pairs={{0,12},{4,0},{8,4},{12,8},{1,13},{5,1},{9,5},{13,9},{2,14},{6,2},{... | collective-permute-start | bytes 1769480 | tf_op jit(solution)/shard_map/ppermute | solution.py:17
  6.5 15.7 %collective-permute-start.2 = (bf16[768,384]{1,0:T(8,128)(2,1)}, bf16[768,384]{1,0:T(8,128)(2,1)S(1)}, u32[]{:S(2)}, u32[]{:S(2)}) collective-permute-start(bf16[768,384]{1,0:T(8,128)(2,1)} %refs_1_.1), channel_id=1, source_target_pairs={{0,4},{4,8},{8,12},{12,0},{1,5},{5,9},{9,13},{13,1},{2,6},{6,10},{... | collective-permute-start | bytes 1769480 | tf_op jit(solution)/shard_map/ppermute | solution.py:17
  6.5 16.2 %collective-permute-start.1 = (bf16[768,384]{1,0:T(8,128)(2,1)}, bf16[768,384]{1,0:T(8,128)(2,1)S(1)}, u32[]{:S(2)}, u32[]{:S(2)}) collective-permute-start(bf16[768,384]{1,0:T(8,128)(2,1)} %refs_1_.1), channel_id=1, source_target_pairs={{0,3},{1,0},{2,1},{3,2},{4,7},{5,4},{6,5},{7,6},{8,11},{9,8},{10,9... | collective-permute-start | bytes 1769480 | tf_op jit(solution)/shard_map/ppermute | solution.py:17
  16.8 15.1 %collective-permute-start.7 = (bf16[768,384]{1,0:T(8,128)(2,1)S(1)}, bf16[768,384]{1,0:T(8,128)(2,1)S(1)}, u32[]{:S(2)}, u32[]{:S(2)}) collective-permute-start(bf16[768,384]{1,0:T(8,128)(2,1)S(1)} %collective-permute-done.refs_2_), channel_id=1, source_target_pairs={{0,12},{4,0},{8,4},{12,8},{1,13},{5,1},{9,5},{13,9},{2,14},{6,2},{... | collective-permute-start | bytes 1769480 | tf_op jit(solution)/shard_map/ppermute | solution.py:17
  20.9 13.0 %collective-permute-start.5 = (bf16[768,384]{1,0:T(8,128)(2,1)S(1)}, bf16[768,384]{1,0:T(8,128)(2,1)S(1)}, u32[]{:S(2)}, u32[]{:S(2)}) collective-permute-start(bf16[768,384]{1,0:T(8,128)(2,1)S(1)} %collective-permute-done.3.refs_5_), channel_id=1, source_target_pairs={{0,3},{1,0},{2,1},{3,2},{4,7},{5,4},{6,5},{7,6},{8,11},{9,8},{10,9... | collective-permute-start | bytes 1769480 | tf_op jit(solution)/shard_map/ppermute | solution.py:17
  22.2 13.9 %collective-permute-start.4 = (bf16[768,384]{1,0:T(8,128)(2,1)S(1)}, bf16[768,384]{1,0:T(8,128)(2,1)S(1)}, u32[]{:S(2)}, u32[]{:S(2)}) collective-permute-start(bf16[768,384]{1,0:T(8,128)(2,1)S(1)} %collective-permute-done.2.refs_4_), channel_id=1, source_target_pairs={{0,1},{1,2},{2,3},{3,0},{4,5},{5,6},{6,7},{7,4},{8,9},{9,10},{10,1... | collective-permute-start | bytes 1769480 | tf_op jit(solution)/shard_map/ppermute | solution.py:17
  22.7 13.6 %collective-permute-start.6 = (bf16[768,384]{1,0:T(8,128)(2,1)S(1)}, bf16[768,384]{1,0:T(8,128)(2,1)S(1)}, u32[]{:S(2)}, u32[]{:S(2)}) collective-permute-start(bf16[768,384]{1,0:T(8,128)(2,1)S(1)} %collective-permute-done.1.refs_3_), channel_id=1, source_target_pairs={{0,4},{4,8},{8,12},{12,0},{1,5},{5,9},{9,13},{13,1},{2,6},{6,10},{... | collective-permute-start | bytes 1769480 | tf_op jit(solution)/shard_map/ppermute | solution.py:17
  32.0 16.8 %collective-permute-start.8 = (bf16[768,384]{1,0:T(8,128)(2,1)S(1)}, bf16[768,384]{1,0:T(8,128)(2,1)S(1)}, u32[]{:S(2)}, u32[]{:S(2)}) collective-permute-start(bf16[768,384]{1,0:T(8,128)(2,1)S(1)} %collective-permute-done.7.refs_4_.refs_15_.refs_21_), channel_id=1, source_target_pairs={{0,1},{1,2},{2,3},{3,0},{4,5},{5,6},{6,7},{7,4},{8,9},{9,10},{10,1... | collective-permute-start | bytes 1769480 | tf_op jit(solution)/shard_map/ppermute | solution.py:17
  33.9 17.9 %collective-permute-start.11 = (bf16[768,384]{1,0:T(8,128)(2,1)S(1)}, bf16[768,384]{1,0:T(8,128)(2,1)S(1)}, u32[]{:S(2)}, u32[]{:S(2)}) collective-permute-start(bf16[768,384]{1,0:T(8,128)(2,1)S(1)} %collective-permute-done.5.refs_2_.refs_13_.refs_19_), channel_id=1, source_target_pairs={{0,12},{4,0},{8,4},{12,8},{1,13},{5,1},{9,5},{13,9},{2,14},{6,2},{... | collective-permute-start | bytes 1769480 | tf_op jit(solution)/shard_map/ppermute | solution.py:17
  36.1 15.7 %collective-permute-start.10 = (bf16[768,384]{1,0:T(8,128)(2,1)S(1)}, bf16[768,384]{1,0:T(8,128)(2,1)S(1)}, u32[]{:S(2)}, u32[]{:S(2)}) collective-permute-start(bf16[768,384]{1,0:T(8,128)(2,1)S(1)} %collective-permute-done.4.refs_1_.refs_12_.refs_18_), channel_id=1, source_target_pairs={{0,4},{4,8},{8,12},{12,0},{1,5},{5,9},{9,13},{13,1},{2,6},{6,10},{... | collective-permute-start | bytes 1769480 | tf_op jit(solution)/shard_map/ppermute | solution.py:17
  36.3 15.5 %collective-permute-start.9 = (bf16[768,384]{1,0:T(8,128)(2,1)S(1)}, bf16[768,384]{1,0:T(8,128)(2,1)S(1)}, u32[]{:S(2)}, u32[]{:S(2)}) collective-permute-start(bf16[768,384]{1,0:T(8,128)(2,1)S(1)} %collective-permute-done.6.refs_3_.refs_14_.refs_20_), channel_id=1, source_target_pairs={{0,3},{1,0},{2,1},{3,2},{4,7},{5,4},{6,5},{7,6},{8,11},{9,8},{10,9... | collective-permute-start | bytes 1769480 | tf_op jit(solution)/shard_map/ppermute | solution.py:17
  38.5 15.2 %collective-permute-start.21 = (f32[64,1920]{1,0:T(8,128)S(1)}, f32[64,1920]{1,0:T(8,128)S(1)}, u32[]{:S(2)}, u32[]{:S(2)}) collective-permute-start(f32[64,1920]{1,0:T(8,128)S(1)} %get-tuple-element.55), channel_id=1, source_target_pairs={{0,16},{16,0},{1,17},{17,1},{2,18},{18,2},{3,19},{19,3},{4,20},{20... | collective-permute-start | bytes 1474568 | tf_op jit(solution)/shard_map/ppermute | solution.py:21
  48.8 5.1 %collective-permute-start.22 = (f32[64,1536]{1,0:T(8,128)S(1)}, f32[64,1536]{1,0:T(8,128)S(1)}, u32[]{:S(2)}, u32[]{:S(2)}) collective-permute-start(f32[64,1536]{1,0:T(8,128)S(1)} %get-tuple-element.57), channel_id=1, source_target_pairs={{0,16},{16,0},{1,17},{17,1},{2,18},{18,2},{3,19},{19,3},{4,20},{20... | collective-permute-start | bytes 1179656 | tf_op jit(solution)/shard_map/ppermute | solution.py:21
  53.9 16.2 %collective-permute-start.13 = (bf16[768,384]{1,0:T(8,128)(2,1)S(1)}, bf16[768,384]{1,0:T(8,128)(2,1)S(1)}, u32[]{:S(2)}, u32[]{:S(2)}) collective-permute-start(bf16[768,384]{1,0:T(8,128)(2,1)S(1)} %collective-permute-done.2.refs_4_), channel_id=1, source_target_pairs={{0,4},{4,8},{8,12},{12,0},{1,5},{5,9},{9,13},{13,1},{2,6},{6,10},{... | collective-permute-start | bytes 1769480 | tf_op jit(solution)/shard_map/ppermute | solution.py:17
  54.0 16.2 %collective-permute-start.12 = (bf16[768,384]{1,0:T(8,128)(2,1)S(1)}, bf16[768,384]{1,0:T(8,128)(2,1)S(1)}, u32[]{:S(2)}, u32[]{:S(2)}) collective-permute-start(bf16[768,384]{1,0:T(8,128)(2,1)S(1)} %collective-permute-done.refs_2_), channel_id=1, source_target_pairs={{0,1},{1,2},{2,3},{3,0},{4,5},{5,6},{6,7},{7,4},{8,9},{9,10},{10,1... | collective-permute-start | bytes 1769480 | tf_op jit(solution)/shard_map/ppermute | solution.py:17
  55.3 6.7 %collective-permute-start.24 = (bf16[16,4992]{1,0:T(8,128)(2,1)S(1)}, bf16[16,4992]{1,0:T(8,128)(2,1)S(1)}, u32[]{:S(2)}, u32[]{:S(2)}) collective-permute-start(bf16[16,4992]{1,0:T(8,128)(2,1)S(1)} %get-tuple-element.86), channel_id=1, source_target_pairs={{0,32},{32,64},{64,96},{96,0},{1,33},{33,65},{65,97},{97,1},{2,34}... | collective-permute-start | bytes 479240 | tf_op jit(solution)/shard_map/ppermute | solution.py:17
  56.6 7.8 %collective-permute-start.25 = (bf16[16,4992]{1,0:T(8,128)(2,1)S(1)}, bf16[16,4992]{1,0:T(8,128)(2,1)S(1)}, u32[]{:S(2)}, u32[]{:S(2)}) collective-permute-start(bf16[16,4992]{1,0:T(8,128)(2,1)S(1)} %get-tuple-element.85), channel_id=1, source_target_pairs={{0,96},{32,0},{64,32},{96,64},{1,97},{33,1},{65,33},{97,65},{2,98}... | collective-permute-start | bytes 479240 | tf_op jit(solution)/shard_map/ppermute | solution.py:17
  58.2 11.9 %collective-permute-start.15 = (bf16[384,384]{1,0:T(8,128)(2,1)S(1)}, bf16[384,384]{1,0:T(8,128)(2,1)S(1)}, u32[]{:S(2)}, u32[]{:S(2)}) collective-permute-start(bf16[384,384]{1,0:T(8,128)(2,1)S(1)} %slice.138), channel_id=1, source_target_pairs={{0,12},{4,0},{8,4},{12,8},{1,13},{5,1},{9,5},{13,9},{2,14},{6,2},{... | collective-permute-start | bytes 884744 | tf_op jit(solution)/shard_map/ppermute | solution.py:17
  62.0 8.0 %collective-permute-start.14 = (bf16[384,384]{1,0:T(8,128)(2,1)S(1)}, bf16[384,384]{1,0:T(8,128)(2,1)S(1)}, u32[]{:S(2)}, u32[]{:S(2)}) collective-permute-start(bf16[384,384]{1,0:T(8,128)(2,1)S(1)} %slice.137), channel_id=1, source_target_pairs={{0,3},{1,0},{2,1},{3,2},{4,7},{5,4},{6,5},{7,6},{8,11},{9,8},{10,9... | collective-permute-start | bytes 884744 | tf_op jit(solution)/shard_map/ppermute | solution.py:17
  64.4 5.6 %collective-permute-start.26 = (bf16[16,4992]{1,0:T(8,128)(2,1)S(1)}, bf16[16,4992]{1,0:T(8,128)(2,1)S(1)}, u32[]{:S(2)}, u32[]{:S(2)}) collective-permute-start(bf16[16,4992]{1,0:T(8,128)(2,1)S(1)} %get-tuple-element.84), channel_id=1, source_target_pairs={{0,64},{32,96},{64,0},{96,32},{1,65},{33,97},{65,1},{97,33},{2,66}... | collective-permute-start | bytes 479240 | tf_op jit(solution)/shard_map/ppermute | solution.py:17
  70.8 4.4 %collective-permute-start.16 = (f32[8,128]{1,0:T(8,128)S(1)}, f32[8,128]{1,0:T(8,128)S(1)}, u32[]{:S(2)}, u32[]{:S(2)}) collective-permute-start(f32[8,128]{1,0:T(8,128)S(1)} %add_add_fusion), channel_id=1, source_target_pairs={{0,16},{16,0},{1,17},{17,1},{2,18},{18,2},{3,19},{19,3},{4,20},{20... | collective-permute-start | bytes 12296 | tf_op jit(solution)/shard_map/ppermute | solution.py:21
  73.3 8.9 %collective-permute-start.27 = (bf16[16,4992]{1,0:T(8,128)(2,1)S(1)}, bf16[16,4992]{1,0:T(8,128)(2,1)S(1)}, u32[]{:S(2)}, u32[]{:S(2)}) collective-permute-start(bf16[16,4992]{1,0:T(8,128)(2,1)S(1)} %fusion.5.refs_1_), channel_id=1, source_target_pairs={{0,96},{32,0},{64,32},{96,64},{1,97},{33,1},{65,33},{97,65},{2,98}... | collective-permute-start | bytes 479240 | tf_op jit(solution)/shard_map/ppermute | solution.py:17
  76.5 18.3 %collective-permute-start.18 = (bf16[64,1280]{1,0:T(8,128)(2,1)S(1)}, bf16[64,1280]{1,0:T(8,128)(2,1)S(1)}, u32[]{:S(2)}, u32[]{:S(2)}) collective-permute-start(bf16[64,1280]{1,0:T(8,128)(2,1)S(1)} %pad_maximum_fusion.1), channel_id=1, source_target_pairs={{0,32},{32,64},{64,96},{96,0},{1,33},{33,65},{65,97},{97,1},{2,34}... | collective-permute-start | bytes 491528 | tf_op jit(solution)/shard_map/ppermute | solution.py:17
  76.6 18.2 %collective-permute-start.19 = (bf16[64,1280]{1,0:T(8,128)(2,1)S(1)}, bf16[64,1280]{1,0:T(8,128)(2,1)S(1)}, u32[]{:S(2)}, u32[]{:S(2)}) collective-permute-start(bf16[64,1280]{1,0:T(8,128)(2,1)S(1)} %pad_maximum_fusion.1), channel_id=1, source_target_pairs={{0,96},{32,0},{64,32},{96,64},{1,97},{33,1},{65,33},{97,65},{2,98}... | collective-permute-start | bytes 491528 | tf_op jit(solution)/shard_map/ppermute | solution.py:17
  79.3 16.0 %collective-permute-start.20 = (bf16[64,1280]{1,0:T(8,128)(2,1)S(1)}, bf16[64,1280]{1,0:T(8,128)(2,1)S(1)}, u32[]{:S(2)}, u32[]{:S(2)}) collective-permute-start(bf16[64,1280]{1,0:T(8,128)(2,1)S(1)} %pad_maximum_fusion.1), channel_id=1, source_target_pairs={{0,64},{32,96},{64,0},{96,32},{1,65},{33,97},{65,1},{97,33},{2,66}... | collective-permute-start | bytes 491528 | tf_op jit(solution)/shard_map/ppermute | solution.py:17
  79.3 9.9 %collective-permute-start.28 = (bf16[16,4992]{1,0:T(8,128)(2,1)S(1)}, bf16[16,4992]{1,0:T(8,128)(2,1)S(1)}, u32[]{:S(2)}, u32[]{:S(2)}) collective-permute-start(bf16[16,4992]{1,0:T(8,128)(2,1)S(1)} %fusion.5.refs_1_), channel_id=1, source_target_pairs={{0,64},{32,96},{64,0},{96,32},{1,65},{33,97},{65,1},{97,33},{2,66}... | collective-permute-start | bytes 479240 | tf_op jit(solution)/shard_map/ppermute | solution.py:17
  82.3 11.8 %collective-permute-start.29 = (bf16[16,4992]{1,0:T(8,128)(2,1)S(1)}, bf16[16,4992]{1,0:T(8,128)(2,1)S(1)}, u32[]{:S(2)}, u32[]{:S(2)}) collective-permute-start(bf16[16,4992]{1,0:T(8,128)(2,1)S(1)} %fusion.5.refs_1_), channel_id=1, source_target_pairs={{0,32},{32,64},{64,96},{96,0},{1,33},{33,65},{65,97},{97,1},{2,34}... | collective-permute-start | bytes 479240 | tf_op jit(solution)/shard_map/ppermute | solution.py:17
  89.2 6.5 %collective-permute-start.30 = (bf16[16,4992]{1,0:T(8,128)(2,1)S(1)}, bf16[16,4992]{1,0:T(8,128)(2,1)S(1)}, u32[]{:S(2)}, u32[]{:S(2)}) collective-permute-start(bf16[16,4992]{1,0:T(8,128)(2,1)S(1)} %fusion.5.refs_1_), channel_id=1, source_target_pairs={{0,16},{16,0},{1,17},{17,1},{2,18},{18,2},{3,19},{19,3},{4,20},{20... | collective-permute-start | bytes 479240 | tf_op jit(solution)/shard_map/ppermute | solution.py:21
  101.8 5.0 %collective-permute-start.35 = (f32[64,3072]{1,0:T(8,128)S(1)}, f32[64,3072]{1,0:T(8,128)S(1)}, u32[]{:S(2)}, u32[]{:S(2)}) collective-permute-start(f32[64,3072]{1,0:T(8,128)S(1)} %get-tuple-element.65), channel_id=1, source_target_pairs={{0,16},{16,0},{1,17},{17,1},{2,18},{18,2},{3,19},{19,3},{4,20},{20... | collective-permute-start | bytes 2359304 | tf_op jit(solution)/shard_map/ppermute | solution.py:21
  104.1 5.6 %collective-permute-start.47 = (bf16[16,3072]{1,0:T(8,128)(2,1)S(1)}, bf16[16,3072]{1,0:T(8,128)(2,1)S(1)}, u32[]{:S(2)}, u32[]{:S(2)}) collective-permute-start(bf16[16,3072]{1,0:T(8,128)(2,1)S(1)} %get-tuple-element.89), channel_id=1, source_target_pairs={{0,32},{32,64},{64,96},{96,0},{1,33},{33,65},{65,97},{97,1},{2,34}... | collective-permute-start | bytes 294920 | tf_op jit(solution)/shard_map/ppermute | solution.py:17
  104.1 7.3 %collective-permute-start.48 = (bf16[16,3072]{1,0:T(8,128)(2,1)S(1)}, bf16[16,3072]{1,0:T(8,128)(2,1)S(1)}, u32[]{:S(2)}, u32[]{:S(2)}) collective-permute-start(bf16[16,3072]{1,0:T(8,128)(2,1)S(1)} %get-tuple-element.88), channel_id=1, source_target_pairs={{0,96},{32,0},{64,32},{96,64},{1,97},{33,1},{65,33},{97,65},{2,98}... | collective-permute-start | bytes 294920 | tf_op jit(solution)/shard_map/ppermute | solution.py:17
  106.8 5.1 %collective-permute-start.49 = (bf16[16,3072]{1,0:T(8,128)(2,1)S(1)}, bf16[16,3072]{1,0:T(8,128)(2,1)S(1)}, u32[]{:S(2)}, u32[]{:S(2)}) collective-permute-start(bf16[16,3072]{1,0:T(8,128)(2,1)S(1)} %get-tuple-element.87), channel_id=1, source_target_pairs={{0,64},{32,96},{64,0},{96,32},{1,65},{33,97},{65,1},{97,33},{2,66}... | collective-permute-start | bytes 294920 | tf_op jit(solution)/shard_map/ppermute | solution.py:17
  107.0 8.9 %collective-permute-start.36 = (bf16[16,3072]{1,0:T(8,128)(2,1)S(1)}, bf16[16,3072]{1,0:T(8,128)(2,1)S(1)}, u32[]{:S(2)}, u32[]{:S(2)}) collective-permute-start(bf16[16,3072]{1,0:T(8,128)(2,1)S(1)} %get-tuple-element.92), channel_id=1, source_target_pairs={{0,32},{32,64},{64,96},{96,0},{1,33},{33,65},{65,97},{97,1},{2,34}... | collective-permute-start | bytes 294920 | tf_op jit(solution)/shard_map/ppermute | solution.py:17
  107.6 8.2 %collective-permute-start.37 = (bf16[16,3072]{1,0:T(8,128)(2,1)S(1)}, bf16[16,3072]{1,0:T(8,128)(2,1)S(1)}, u32[]{:S(2)}, u32[]{:S(2)}) collective-permute-start(bf16[16,3072]{1,0:T(8,128)(2,1)S(1)} %get-tuple-element.91), channel_id=1, source_target_pairs={{0,96},{32,0},{64,32},{96,64},{1,97},{33,1},{65,33},{97,65},{2,98}... | collective-permute-start | bytes 294920 | tf_op jit(solution)/shard_map/ppermute | solution.py:17
  109.7 8.6 %collective-permute-start.38 = (bf16[16,3072]{1,0:T(8,128)(2,1)S(1)}, bf16[16,3072]{1,0:T(8,128)(2,1)S(1)}, u32[]{:S(2)}, u32[]{:S(2)}) collective-permute-start(bf16[16,3072]{1,0:T(8,128)(2,1)S(1)} %get-tuple-element.90), channel_id=1, source_target_pairs={{0,64},{32,96},{64,0},{96,32},{1,65},{33,97},{65,1},{97,33},{2,66}... | collective-permute-start | bytes 294920 | tf_op jit(solution)/shard_map/ppermute | solution.py:17
  111.9 9.4 %collective-permute-start.50 = (bf16[16,3072]{1,0:T(8,128)(2,1)S(1)}, bf16[16,3072]{1,0:T(8,128)(2,1)S(1)}, u32[]{:S(2)}, u32[]{:S(2)}) collective-permute-start(bf16[16,3072]{1,0:T(8,128)(2,1)S(1)} %fusion.8.refs_9_), channel_id=1, source_target_pairs={{0,96},{32,0},{64,32},{96,64},{1,97},{33,1},{65,33},{97,65},{2,98}... | collective-permute-start | bytes 294920 | tf_op jit(solution)/shard_map/ppermute | solution.py:17
  114.5 8.0 %collective-permute-start.51 = (bf16[16,3072]{1,0:T(8,128)(2,1)S(1)}, bf16[16,3072]{1,0:T(8,128)(2,1)S(1)}, u32[]{:S(2)}, u32[]{:S(2)}) collective-permute-start(bf16[16,3072]{1,0:T(8,128)(2,1)S(1)} %fusion.8.refs_9_), channel_id=1, source_target_pairs={{0,64},{32,96},{64,0},{96,32},{1,65},{33,97},{65,1},{97,33},{2,66}... | collective-permute-start | bytes 294920 | tf_op jit(solution)/shard_map/ppermute | solution.py:17
  115.8 6.7 %collective-permute-start.52 = (bf16[16,3072]{1,0:T(8,128)(2,1)S(1)}, bf16[16,3072]{1,0:T(8,128)(2,1)S(1)}, u32[]{:S(2)}, u32[]{:S(2)}) collective-permute-start(bf16[16,3072]{1,0:T(8,128)(2,1)S(1)} %fusion.8.refs_9_), channel_id=1, source_target_pairs={{0,32},{32,64},{64,96},{96,0},{1,33},{33,65},{65,97},{97,1},{2,34}... | collective-permute-start | bytes 294920 | tf_op jit(solution)/shard_map/ppermute | solution.py:17
  115.9 9.3 %collective-permute-start.53 = (bf16[16,3072]{1,0:T(8,128)(2,1)S(1)}, bf16[16,3072]{1,0:T(8,128)(2,1)S(1)}, u32[]{:S(2)}, u32[]{:S(2)}) collective-permute-start(bf16[16,3072]{1,0:T(8,128)(2,1)S(1)} %fusion.8.refs_9_), channel_id=1, source_target_pairs={{0,16},{16,0},{1,17},{17,1},{2,18},{18,2},{3,19},{19,3},{4,20},{20... | collective-permute-start | bytes 294920 | tf_op jit(solution)/shard_map/ppermute | solution.py:21
  118.4 6.8 %collective-permute-start.39 = (bf16[16,3072]{1,0:T(8,128)(2,1)S(1)}, bf16[16,3072]{1,0:T(8,128)(2,1)S(1)}, u32[]{:S(2)}, u32[]{:S(2)}) collective-permute-start(bf16[16,3072]{1,0:T(8,128)(2,1)S(1)} %fusion.11.refs_1_), channel_id=1, source_target_pairs={{0,96},{32,0},{64,32},{96,64},{1,97},{33,1},{65,33},{97,65},{2,98}... | collective-permute-start | bytes 294920 | tf_op jit(solution)/shard_map/ppermute | solution.py:17
  121.3 5.6 %collective-permute-start.40 = (bf16[16,3072]{1,0:T(8,128)(2,1)S(1)}, bf16[16,3072]{1,0:T(8,128)(2,1)S(1)}, u32[]{:S(2)}, u32[]{:S(2)}) collective-permute-start(bf16[16,3072]{1,0:T(8,128)(2,1)S(1)} %fusion.11.refs_1_), channel_id=1, source_target_pairs={{0,64},{32,96},{64,0},{96,32},{1,65},{33,97},{65,1},{97,33},{2,66}... | collective-permute-start | bytes 294920 | tf_op jit(solution)/shard_map/ppermute | solution.py:17
  122.5 6.6 %collective-permute-start.41 = (bf16[16,3072]{1,0:T(8,128)(2,1)S(1)}, bf16[16,3072]{1,0:T(8,128)(2,1)S(1)}, u32[]{:S(2)}, u32[]{:S(2)}) collective-permute-start(bf16[16,3072]{1,0:T(8,128)(2,1)S(1)} %fusion.11.refs_1_), channel_id=1, source_target_pairs={{0,32},{32,64},{64,96},{96,0},{1,33},{33,65},{65,97},{97,1},{2,34}... | collective-permute-start | bytes 294920 | tf_op jit(solution)/shard_map/ppermute | solution.py:17
  122.5 7.6 %collective-permute-start.42 = (bf16[16,3072]{1,0:T(8,128)(2,1)S(1)}, bf16[16,3072]{1,0:T(8,128)(2,1)S(1)}, u32[]{:S(2)}, u32[]{:S(2)}) collective-permute-start(bf16[16,3072]{1,0:T(8,128)(2,1)S(1)} %fusion.11.refs_1_), channel_id=1, source_target_pairs={{0,16},{16,0},{1,17},{17,1},{2,18},{18,2},{3,19},{19,3},{4,20},{20... | collective-permute-start | bytes 294920 | tf_op jit(solution)/shard_map/ppermute | solution.py:21
  125.1 5.0 %collective-permute-start.54 = (bf16[16,3072]{1,0:T(8,128)(2,1)S(1)}, bf16[16,3072]{1,0:T(8,128)(2,1)S(1)}, u32[]{:S(2)}, u32[]{:S(2)}) collective-permute-start(bf16[16,3072]{1,0:T(8,128)(2,1)S(1)} %collective-permute-done.50.refs_10_), channel_id=1, source_target_pairs={{0,16},{16,0},{1,17},{17,1},{2,18},{18,2},{3,19},{19,3},{4,20},{20... | collective-permute-start | bytes 294920 | tf_op jit(solution)/shard_map/ppermute | solution.py:21
  125.2 5.7 %collective-permute-start.55 = (bf16[16,3072]{1,0:T(8,128)(2,1)S(1)}, bf16[16,3072]{1,0:T(8,128)(2,1)S(1)}, u32[]{:S(2)}, u32[]{:S(2)}) collective-permute-start(bf16[16,3072]{1,0:T(8,128)(2,1)S(1)} %collective-permute-done.51.refs_11_), channel_id=1, source_target_pairs={{0,16},{16,0},{1,17},{17,1},{2,18},{18,2},{3,19},{19,3},{4,20},{20... | collective-permute-start | bytes 294920 | tf_op jit(solution)/shard_map/ppermute | solution.py:21
  126.9 4.0 %collective-permute-start.56 = (bf16[16,3072]{1,0:T(8,128)(2,1)S(1)}, bf16[16,3072]{1,0:T(8,128)(2,1)S(1)}, u32[]{:S(2)}, u32[]{:S(2)}) collective-permute-start(bf16[16,3072]{1,0:T(8,128)(2,1)S(1)} %collective-permute-done.52.refs_12_), channel_id=1, source_target_pairs={{0,16},{16,0},{1,17},{17,1},{2,18},{18,2},{3,19},{19,3},{4,20},{20... | collective-permute-start | bytes 294920 | tf_op jit(solution)/shard_map/ppermute | solution.py:21
  135.5 16.1 %all-to-all-start = ((bf16[4,768,128]{2,1,0:T(8,128)(2,1)}), bf16[4,768,128]{2,1,0:T(8,128)(2,1)S(1)}, u32[]{:S(2)}, u32[]{:S(2)}) async-start(bf16[4,768,128]{2,1,0:T(8,128)(2,1)} %get-tuple-element.75), calls=%async_computation | async-start | bytes 1572864 | tf_op jit(solution)/shard_map/all_to_all | solution.py:216
  (14 other events, 47.0 us)

commit v8 on v7

--- a/solution.py
+++ b/solution.py
@@ -38,7 +38,7 @@
     a, b, c, d = (shift(mp, "x", 1), shift(pm, "x", 3), shift(pp, "z", 1), shift(mm, "z", 3))
     second = down_first(x, [pp, mm, pm, mp])
     low, high = shift(d[:half], "x", 3), shift(a[half:], "z", 3)
-    far_x, far_z = shift(after(xp, a), "x", 1), shift(after(zp, a), "z", 1)
+    far_x, far_z = shift(after(xp, mp), "x", 1), shift(after(zp, a), "z", 1)
     third = down_first(x, [a, b, c, d])
     early = reduce_y([core_sum(*step[:2]) for step in (first, second, third)])
     fourth = down_first(x, [far_x, far_z, (low, high)])
@@ -102,7 +102,7 @@
 def reduce_y(half):
     send = jnp.concatenate([h[16:].astype(jnp.bfloat16) for h in half], 1)
     sends = {d: send[16 * (d - 1) : 16 * d] for d in (1, 3, 2)}
-    got = lax.optimization_barrier(tuple(shift(piece, "y", d) for d, piece in sends.items()))
+    got = lax.optimization_barrier(tuple(shift(piece, "y", d) for d, piece in sorted(sends.items())))
     total = jnp.concatenate([h[:16] for h in half], 1)
     for piece in got:
         total = total + piece.astype(jnp.float32)
@@ -110,7 +110,7 @@
 
 
 def gather_y(own):
-    up1, up3, up2 = (shift(own, "y", 4 - d) for d in (1, 3, 2))
+    up2, up1, up3 = (shift(own, "y", 4 - d) for d in (2, 1, 3))
     mine = [own, up1, up2, up3]
     return mine + [other_core(m) for m in mine]
 
@@ -217,7 +217,8 @@
     part = jnp.einsum("brn,arm->bamn", along_z, along_x, preferred_element_type=jnp.float32)
     part = part.reshape(4, 4, 2, 64, 128).transpose(2, 0, 1, 3, 4).reshape(2, 16, 64, 128)
     keep = lax.dynamic_index_in_dim(part, core, 0, keepdims=False)
-    half = keep + other_core(lax.dynamic_index_in_dim(part, 1 - core, 0, keepdims=False))
+    give = lax.dynamic_index_in_dim(part, 1 - core, 0, keepdims=False).astype(jnp.bfloat16)
+    half = keep + other_core(give).astype(jnp.float32)
     got = lax.all_to_all(half.astype(jnp.bfloat16), ("y", "x"), 0, 0).astype(jnp.float32).reshape(4, 4, 64, 128)
     sums = jnp.sum(got, axis=0).reshape(2, 2, 64, 128)
     keep = lax.dynamic_index_in_dim(sums, core, 0, keepdims=False)

time: 173 us -> 172 us (level)
  starting transfers between devices: 80.2 us -> 76 us
  waiting for transfers between devices: 50.8 us -> 54.9 us
    ppermute x37, waiting for transfers between devices: 42.8 us -> 47.3 us  [shift(): return lax.ppermute(x, axis, [(i, (i + by) % 4) for i in range(4)])]
    ppermute x37, starting transfers between devices: 47.7 us -> 45.3 us  [shift(): return lax.ppermute(x, axis, [(i, (i + by) % 4) for i in range(4)])]
where the time goes in v8:
time: 172 us
  starting transfers between devices  76 us (44%)
  waiting for transfers between devices  54.9 us (32%)
  blocking collectives  24.2 us (14%)
  Pallas kernels  11.1 us (6%)
  local copies, waits for them, and re-layouts  2.24 us (1%)
    ppermute x37, waiting for transfers between devices, shift(): return lax.ppermute(x, axis, [(i, (i + by) % 4) for i in range(4)])  47.3 us
    ppermute x37, starting transfers between devices, shift(): return lax.ppermute(x, axis, [(i, (i + by) % 4) for i in range(4)])  45.3 us
    ppermute x22, starting transfers between devices, other_core(): return lax.ppermute(x, 'core', [(0, 1), (1, 0)])  27 us
    all_gather x1, blocking collectives, per_device(): along_x = lax.all_gather(subspace, 'x', axis=0)  12.3 us
    all_to_all x1, blocking collectives, per_device(): lax.all_to_all(half.astype(jnp.bfloat16), ('y', 'x'), 0, 0)  11.9 us
    pallas_call x2, Pallas kernels, apply(): pl.pallas_call(lambda *refs: apply_kernel(down, len(t), *refs), out_shape...  8.59 us
    ppermute x22, waiting for transfers between devices, other_core(): return lax.ppermute(x, 'core', [(0, 1), (1, 0)])  7.63 us
    all_to_all x1, starting transfers between devices, per_device(): along_z = lax.all_to_all(copies, 'z', 0, 0)  3.7 us
  transfers between devices with their start and end apart: 60, of which 28 were waited for; matrix products, arithmetic and copies ran while one was open for 1% of the time, Pallas kernels for 1%

profile of v8, /device:TPU:1, one launch (start us, length us, event | category | flops | bytes accessed | tf_op | source)
XLA Modules:
  0.0 171.7 jit_solution(2852417297865733374)
XLA Ops:
  0.6 2.1 %collective-permute-start = (bf16[768,384]{1,0:T(8,128)(2,1)}, bf16[768,384]{1,0:T(8,128)(2,1)S(1)}, u32[]{:S(2)}, u32[]{:S(2)}) collective-permute-start(bf16[768,384]{1,0:T(8,128)(2,1)} %refs_1_.1), channel_id=1, source_target_pairs={{0,1},{1,2},{2,3},{3,0},{4,5},{5,6},{6,7},{7,4},{8,9},{9,10},{10,1... | collective-permute-start | bytes 1769480 | tf_op jit(solution)/shard_map/ppermute | solution.py:17
  2.8 3.8 %collective-permute-start.3 = (bf16[768,384]{1,0:T(8,128)(2,1)}, bf16[768,384]{1,0:T(8,128)(2,1)S(1)}, u32[]{:S(2)}, u32[]{:S(2)}) collective-permute-start(bf16[768,384]{1,0:T(8,128)(2,1)} %refs_1_.1), channel_id=1, source_target_pairs={{0,12},{4,0},{8,4},{12,8},{1,13},{5,1},{9,5},{13,9},{2,14},{6,2},{... | collective-permute-start | bytes 1769480 | tf_op jit(solution)/shard_map/ppermute | solution.py:17
  6.5 1.5 collective-permute-start.1
  8.0 8.9 %collective-permute-done.refs_2_ = bf16[768,384]{1,0:T(8,128)(2,1)S(1)} collective-permute-done((bf16[768,384]{1,0:T(8,128)(2,1)}, bf16[768,384]{1,0:T(8,128)(2,1)S(1)}, u32[]{:S(2)}, u32[]{:S(2)}) %collective-permute-start) | collective-permute-done | bytes 589856 | tf_op jit(solution)/shard_map/ppermute | solution.py:17
  16.8 4.1 %collective-permute-start.7 = (bf16[768,384]{1,0:T(8,128)(2,1)S(1)}, bf16[768,384]{1,0:T(8,128)(2,1)S(1)}, u32[]{:S(2)}, u32[]{:S(2)}) collective-permute-start(bf16[768,384]{1,0:T(8,128)(2,1)S(1)} %collective-permute-done.refs_2_), channel_id=1, source_target_pairs={{0,12},{4,0},{8,4},{12,8},{1,13},{5,1},{9,5},{13,9},{2,14},{6,2},{... | collective-permute-start | bytes 1769480 | tf_op jit(solution)/shard_map/ppermute | solution.py:17
  20.9 1.3 collective-permute-start.5
  25.0 7.0 %collective-permute-done.7.refs_4_.refs_15_.refs_21_ = bf16[768,384]{1,0:T(8,128)(2,1)S(1)} collective-permute-done((bf16[768,384]{1,0:T(8,128)(2,1)S(1)}, bf16[768,384]{1,0:T(8,128)(2,1)S(1)}, u32[]{:S(2)}, u32[]{:S(2)}) %collective-permute-start.7) | collective-permute-done | bytes 589856 | tf_op jit(solution)/shard_map/ppermute | solution.py:17
  32.0 1.9 %collective-permute-done.5.refs_2_.refs_13_.refs_19_ = bf16[768,384]{1,0:T(8,128)(2,1)S(1)} collective-permute-done((bf16[768,384]{1,0:T(8,128)(2,1)S(1)}, bf16[768,384]{1,0:T(8,128)(2,1)S(1)}, u32[]{:S(2)}, u32[]{:S(2)}) %collective-permute-start.5) | collective-permute-done | bytes 589856 | tf_op jit(solution)/shard_map/ppermute | solution.py:17
  33.9 1.5 collective-permute-start.11
  36.3 2.2 %collective-permute-start.9 = (bf16[768,384]{1,0:T(8,128)(2,1)S(1)}, bf16[768,384]{1,0:T(8,128)(2,1)S(1)}, u32[]{:S(2)}, u32[]{:S(2)}) collective-permute-start(bf16[768,384]{1,0:T(8,128)(2,1)S(1)} %collective-permute-done.6.refs_3_.refs_14_.refs_20_), channel_id=1, source_target_pairs={{0,3},{1,0},{2,1},{3,2},{4,7},{5,4},{6,5},{7,6},{8,11},{9,8},{10,9... | collective-permute-start | bytes 1769480 | tf_op jit(solution)/shard_map/ppermute | solution.py:17
  38.5 3.6 %collective-permute-start.21 = (f32[64,1920]{1,0:T(8,128)S(1)}, f32[64,1920]{1,0:T(8,128)S(1)}, u32[]{:S(2)}, u32[]{:S(2)}) collective-permute-start(f32[64,1920]{1,0:T(8,128)S(1)} %get-tuple-element.55), channel_id=1, source_target_pairs={{0,16},{16,0},{1,17},{17,1},{2,18},{18,2},{3,19},{19,3},{4,20},{20... | collective-permute-start | bytes 1474568 | tf_op jit(solution)/shard_map/ppermute | solution.py:21
  42.7 6.1 %collective-permute-done.8.refs_1_.refs_16_.refs_22_ = bf16[768,384]{1,0:T(8,128)(2,1)S(1)} collective-permute-done((bf16[768,384]{1,0:T(8,128)(2,1)S(1)}, bf16[768,384]{1,0:T(8,128)(2,1)S(1)}, u32[]{:S(2)}, u32[]{:S(2)}) %collective-permute-start.8) | collective-permute-done | bytes 589856 | tf_op jit(solution)/shard_map/ppermute | solution.py:17
  48.8 3.0 %collective-permute-start.22 = (f32[64,1536]{1,0:T(8,128)S(1)}, f32[64,1536]{1,0:T(8,128)S(1)}, u32[]{:S(2)}, u32[]{:S(2)}) collective-permute-start(f32[64,1536]{1,0:T(8,128)S(1)} %get-tuple-element.57), channel_id=1, source_target_pairs={{0,16},{16,0},{1,17},{17,1},{2,18},{18,2},{3,19},{19,3},{4,20},{20... | collective-permute-start | bytes 1179656 | tf_op jit(solution)/shard_map/ppermute | solution.py:21
  52.4 1.4 collective-permute-start.23
  55.3 1.4 collective-permute-start.24
  56.6 2.6 %collective-permute-start.25 = (bf16[16,4992]{1,0:T(8,128)(2,1)S(1)}, bf16[16,4992]{1,0:T(8,128)(2,1)S(1)}, u32[]{:S(2)}, u32[]{:S(2)}) collective-permute-start(bf16[16,4992]{1,0:T(8,128)(2,1)S(1)} %get-tuple-element.85), channel_id=1, source_target_pairs={{0,64},{32,96},{64,0},{96,32},{1,65},{33,97},{65,1},{97,33},{2,66}... | collective-permute-start | bytes 479240 | tf_op jit(solution)/shard_map/ppermute | solution.py:17
  59.3 2.2 %collective-permute-start.15 = (bf16[384,384]{1,0:T(8,128)(2,1)S(1)}, bf16[384,384]{1,0:T(8,128)(2,1)S(1)}, u32[]{:S(2)}, u32[]{:S(2)}) collective-permute-start(bf16[384,384]{1,0:T(8,128)(2,1)S(1)} %slice.138), channel_id=1, source_target_pairs={{0,12},{4,0},{8,4},{12,8},{1,13},{5,1},{9,5},{13,9},{2,14},{6,2},{... | collective-permute-start | bytes 884744 | tf_op jit(solution)/shard_map/ppermute | solution.py:17
  62.0 2.4 %collective-permute-start.14 = (bf16[384,384]{1,0:T(8,128)(2,1)S(1)}, bf16[384,384]{1,0:T(8,128)(2,1)S(1)}, u32[]{:S(2)}, u32[]{:S(2)}) collective-permute-start(bf16[384,384]{1,0:T(8,128)(2,1)S(1)} %slice.137), channel_id=1, source_target_pairs={{0,3},{1,0},{2,1},{3,2},{4,7},{5,4},{6,5},{7,6},{8,11},{9,8},{10,9... | collective-permute-start | bytes 884744 | tf_op jit(solution)/shard_map/ppermute | solution.py:17
  64.4 2.1 %collective-permute-done.25 = bf16[16,4992]{1,0:T(8,128)(2,1)S(1)} collective-permute-done((bf16[16,4992]{1,0:T(8,128)(2,1)S(1)}, bf16[16,4992]{1,0:T(8,128)(2,1)S(1)}, u32[]{:S(2)}, u32[]{:S(2)}) %collective-permute-start.25) | collective-permute-done | bytes 159776 | tf_op jit(solution)/shard_map/ppermute | solution.py:17
  66.6 4.4 %collective-permute-done.26 = bf16[16,4992]{1,0:T(8,128)(2,1)S(1)} collective-permute-done((bf16[16,4992]{1,0:T(8,128)(2,1)S(1)}, bf16[16,4992]{1,0:T(8,128)(2,1)S(1)}, u32[]{:S(2)}, u32[]{:S(2)}) %collective-permute-start.26) | collective-permute-done | bytes 159776 | tf_op jit(solution)/shard_map/ppermute | solution.py:17
  71.5 2.2 %collective-permute-start.16 = (f32[8,128]{1,0:T(8,128)S(1)}, f32[8,128]{1,0:T(8,128)S(1)}, u32[]{:S(2)}, u32[]{:S(2)}) collective-permute-start(f32[8,128]{1,0:T(8,128)S(1)} %add_add_fusion), channel_id=1, source_target_pairs={{0,16},{16,0},{1,17},{17,1},{2,18},{18,2},{3,19},{19,3},{4,20},{20... | collective-permute-start | bytes 12296 | tf_op jit(solution)/shard_map/ppermute | solution.py:21
  73.8 1.6 collective-permute-start.27
  75.7 1.3 collective-permute-done.17
  77.1 2.7 %collective-permute-start.19 = (bf16[64,1280]{1,0:T(8,128)(2,1)S(1)}, bf16[64,1280]{1,0:T(8,128)(2,1)S(1)}, u32[]{:S(2)}, u32[]{:S(2)}) collective-permute-start(bf16[64,1280]{1,0:T(8,128)(2,1)S(1)} %pad_maximum_fusion.1), channel_id=1, source_target_pairs={{0,96},{32,0},{64,32},{96,64},{1,97},{33,1},{65,33},{97,65},{2,98}... | collective-permute-start | bytes 491528 | tf_op jit(solution)/shard_map/ppermute | solution.py:17
  80.4 2.3 %collective-permute-start.28 = (bf16[16,4992]{1,0:T(8,128)(2,1)S(1)}, bf16[16,4992]{1,0:T(8,128)(2,1)S(1)}, u32[]{:S(2)}, u32[]{:S(2)}) collective-permute-start(bf16[16,4992]{1,0:T(8,128)(2,1)S(1)} %fusion.5.refs_1_), channel_id=1, source_target_pairs={{0,64},{32,96},{64,0},{96,32},{1,65},{33,97},{65,1},{97,33},{2,66}... | collective-permute-start | bytes 479240 | tf_op jit(solution)/shard_map/ppermute | solution.py:17
  82.8 8.4 %collective-permute-done.28.refs_3_ = bf16[16,4992]{1,0:T(8,128)(2,1)S(1)} collective-permute-done((bf16[16,4992]{1,0:T(8,128)(2,1)S(1)}, bf16[16,4992]{1,0:T(8,128)(2,1)S(1)}, u32[]{:S(2)}, u32[]{:S(2)}) %collective-permute-start.28) | collective-permute-done | bytes 159776 | tf_op jit(solution)/shard_map/ppermute | solution.py:17
  91.2 1.8 %collective-permute-start.30 = (bf16[16,4992]{1,0:T(8,128)(2,1)S(1)}, bf16[16,4992]{1,0:T(8,128)(2,1)S(1)}, u32[]{:S(2)}, u32[]{:S(2)}) collective-permute-start(bf16[16,4992]{1,0:T(8,128)(2,1)S(1)} %fusion.5.refs_1_), channel_id=1, source_target_pairs={{0,16},{16,0},{1,17},{17,1},{2,18},{18,2},{3,19},{19,3},{4,20},{20... | collective-permute-start | bytes 479240 | tf_op jit(solution)/shard_map/ppermute | solution.py:21
  93.0 2.2 %collective-permute-done.29.refs_4_ = bf16[16,4992]{1,0:T(8,128)(2,1)S(1)} collective-permute-done((bf16[16,4992]{1,0:T(8,128)(2,1)S(1)}, bf16[16,4992]{1,0:T(8,128)(2,1)S(1)}, u32[]{:S(2)}, u32[]{:S(2)}) %collective-permute-start.29) | collective-permute-done | bytes 159776 | tf_op jit(solution)/shard_map/ppermute | solution.py:17
  97.8 4.6 %shard_map.45 = (f32[64,3072]{1,0:T(8,128)S(1)}, f32[64,3072]{1,0:T(8,128)S(1)}, f32[64,3072]{1,0:T(8,128)S(1)}, f32[64,3072]{1,0:T(8,128)S(1)}) custom-call(f32[8,128]{1,0:T(8,128)S(1)} %convert_add_fusion.refs_0_, bf16[16,4992]{1,0:T(8,128)(2,1)S(1)} %fusion.5.refs_1_, bf16[16,4992]{1,0:T(8,128)(2,1)S(1)} %collective-permute-done.27.refs_2_, ...), custom_call_target="tpu_custom_call" | custom-call | flops 2415919104 | bytes 9437184 | tf_op jit(solution)/shard_map/pallas_call | solution.py:182
  103.0 1.8 %collective-permute-done.46 = f32[64,3072]{1,0:T(8,128)S(1)} collective-permute-done((f32[64,3072]{1,0:T(8,128)S(1)}, f32[64,3072]{1,0:T(8,128)S(1)}, u32[]{:S(2)}, u32[]{:S(2)}) %collective-permute-start.46) | collective-permute-done | bytes 786464 | tf_op jit(solution)/shard_map/ppermute | solution.py:21
  105.0 1.5 collective-permute-start.48
  106.5 1.2 collective-permute-start.49
  108.5 1.9 %collective-permute-start.37 = (bf16[16,3072]{1,0:T(8,128)(2,1)S(1)}, bf16[16,3072]{1,0:T(8,128)(2,1)S(1)}, u32[]{:S(2)}, u32[]{:S(2)}) collective-permute-start(bf16[16,3072]{1,0:T(8,128)(2,1)S(1)} %get-tuple-element.91), channel_id=1, source_target_pairs={{0,64},{32,96},{64,0},{96,32},{1,65},{33,97},{65,1},{97,33},{2,66}... | collective-permute-start | bytes 294920 | tf_op jit(solution)/shard_map/ppermute | solution.py:17
  110.4 2.3 %collective-permute-done.47 = bf16[16,3072]{1,0:T(8,128)(2,1)S(1)} collective-permute-done((bf16[16,3072]{1,0:T(8,128)(2,1)S(1)}, bf16[16,3072]{1,0:T(8,128)(2,1)S(1)}, u32[]{:S(2)}, u32[]{:S(2)}) %collective-permute-start.47) | collective-permute-done | bytes 98336 | tf_op jit(solution)/shard_map/ppermute | solution.py:17
  112.9 2.8 %collective-permute-start.50 = (bf16[16,3072]{1,0:T(8,128)(2,1)S(1)}, bf16[16,3072]{1,0:T(8,128)(2,1)S(1)}, u32[]{:S(2)}, u32[]{:S(2)}) collective-permute-start(bf16[16,3072]{1,0:T(8,128)(2,1)S(1)} %fusion.9.refs_9_), channel_id=1, source_target_pairs={{0,96},{32,0},{64,32},{96,64},{1,97},{33,1},{65,33},{97,65},{2,98}... | collective-permute-start | bytes 294920 | tf_op jit(solution)/shard_map/ppermute | solution.py:17
  116.9 1.8 %collective-permute-start.53 = (bf16[16,3072]{1,0:T(8,128)(2,1)S(1)}, bf16[16,3072]{1,0:T(8,128)(2,1)S(1)}, u32[]{:S(2)}, u32[]{:S(2)}) collective-permute-start(bf16[16,3072]{1,0:T(8,128)(2,1)S(1)} %fusion.9.refs_9_), channel_id=1, source_target_pairs={{0,16},{16,0},{1,17},{17,1},{2,18},{18,2},{3,19},{19,3},{4,20},{20... | collective-permute-start | bytes 294920 | tf_op jit(solution)/shard_map/ppermute | solution.py:21
  118.8 2.7 %collective-permute-start.39 = (bf16[16,3072]{1,0:T(8,128)(2,1)S(1)}, bf16[16,3072]{1,0:T(8,128)(2,1)S(1)}, u32[]{:S(2)}, u32[]{:S(2)}) collective-permute-start(bf16[16,3072]{1,0:T(8,128)(2,1)S(1)} %fusion.12.refs_1_), channel_id=1, source_target_pairs={{0,96},{32,0},{64,32},{96,64},{1,97},{33,1},{65,33},{97,65},{2,98}... | collective-permute-start | bytes 294920 | tf_op jit(solution)/shard_map/ppermute | solution.py:17
  122.3 2.6 %collective-permute-start.42 = (bf16[16,3072]{1,0:T(8,128)(2,1)S(1)}, bf16[16,3072]{1,0:T(8,128)(2,1)S(1)}, u32[]{:S(2)}, u32[]{:S(2)}) collective-permute-start(bf16[16,3072]{1,0:T(8,128)(2,1)S(1)} %fusion.12.refs_1_), channel_id=1, source_target_pairs={{0,16},{16,0},{1,17},{17,1},{2,18},{18,2},{3,19},{19,3},{4,20},{20... | collective-permute-start | bytes 294920 | tf_op jit(solution)/shard_map/ppermute | solution.py:21
  125.0 1.1 collective-permute-start.55
  126.0 1.1 collective-permute-done.40.refs_3_
  127.2 1.8 %collective-permute-start.56 = (bf16[16,3072]{1,0:T(8,128)(2,1)S(1)}, bf16[16,3072]{1,0:T(8,128)(2,1)S(1)}, u32[]{:S(2)}, u32[]{:S(2)}) collective-permute-start(bf16[16,3072]{1,0:T(8,128)(2,1)S(1)} %collective-permute-done.52.refs_12_), channel_id=1, source_target_pairs={{0,16},{16,0},{1,17},{17,1},{2,18},{18,2},{3,19},{19,3},{4,20},{20... | collective-permute-start | bytes 294920 | tf_op jit(solution)/shard_map/ppermute | solution.py:21
  131.8 3.9 %shard_map.46 = (bf16[768,128]{1,0:T(8,128)(2,1)}, bf16[4,768,128]{2,1,0:T(8,128)(2,1)}) custom-call(f32[8,128]{1,0:T(8,128)S(1)} %convert_add_fusion.refs_0_, bf16[16,3072]{1,0:T(8,128)(2,1)S(1)} %fusion.12.refs_1_, bf16[16,3072]{1,0:T(8,128)(2,1)S(1)} %collective-permute-done.39.refs_2_, bf16[16,3072]{1,0:T(8,128)(2,1)S(1)} %collective-permute-done.40.refs_3_, ...), custom_call_target="tpu_custom_call" | custom-call | flops 1207959552 | bytes 9437184 | tf_op jit(solution)/shard_map/pallas_call | solution.py:182
  135.8 3.7 %all-to-all-start = ((bf16[4,768,128]{2,1,0:T(8,128)(2,1)}), bf16[4,768,128]{2,1,0:T(8,128)(2,1)S(1)}, u32[]{:S(2)}, u32[]{:S(2)}) async-start(bf16[4,768,128]{2,1,0:T(8,128)(2,1)} %get-tuple-element.75), calls=%async_computation | async-start | bytes 1572864 | tf_op jit(solution)/shard_map/all_to_all | solution.py:216
  139.5 12.3 %all-gather = bf16[3072,128]{1,0:T(8,128)(2,1)S(1)} all-gather(bf16[768,128]{1,0:T(8,128)(2,1)} %get-tuple-element.37), channel_id=2, replica_groups=mesh['y'=4,'core'=2,'z'=4,'x'=4] {'x'}, dimensions={0}, use_global_device_ids=true | all-gather | bytes 983040 | tf_op jit(solution)/shard_map/all_gather | solution.py:215
  152.5 2.6 %collective-permute-start.57 = (bf16[16,64,128]{2,1,0:T(8,128)(2,1)S(1)}, bf16[16,64,128]{2,1,0:T(8,128)(2,1)S(1)}, u32[]{:S(2)}, u32[]{:S(2)}) collective-permute-start(bf16[16,64,128]{2,1,0:T(8,128)(2,1)S(1)} %fusion.6), channel_id=1, source_target_pairs={{0,16},{16,0},{1,17},{17,1},{2,18},{18,2},{3,19},{19,3},{4,20},{20... | collective-permute-start | bytes 786440 | tf_op jit(solution)/shard_map/ppermute | solution.py:21
  155.1 1.2 collective-permute-done.57
  156.4 11.9 %all_to_all.10 = bf16[16,64,128]{2,1,0:T(8,128)(2,1)S(1)} all-to-all(bf16[16,64,128]{2,1,0:T(8,128)(2,1)S(1)} %fusion.2), channel_id=1, replica_groups=mesh['y'=4,'core'=2,'z'=4,'x'=4] {'y','x'}, dimensions={0} | all-to-all | bytes 524288 | tf_op jit(solution)/shard_map/all_to_all | solution.py:222
  168.4 1.6 collective-permute-start.58
  (135 shorter events, 20.5 us)
Async XLA Ops:
  0.6 16.2 %collective-permute-start = (bf16[768,384]{1,0:T(8,128)(2,1)}, bf16[768,384]{1,0:T(8,128)(2,1)S(1)}, u32[]{:S(2)}, u32[]{:S(2)}) collective-permute-start(bf16[768,384]{1,0:T(8,128)(2,1)} %refs_1_.1), channel_id=1, source_target_pairs={{0,1},{1,2},{2,3},{3,0},{4,5},{5,6},{6,7},{7,4},{8,9},{9,10},{10,1... | collective-permute-start | bytes 1769480 | tf_op jit(solution)/shard_map/ppermute | solution.py:17
  2.8 18.2 %collective-permute-start.3 = (bf16[768,384]{1,0:T(8,128)(2,1)}, bf16[768,384]{1,0:T(8,128)(2,1)S(1)}, u32[]{:S(2)}, u32[]{:S(2)}) collective-permute-start(bf16[768,384]{1,0:T(8,128)(2,1)} %refs_1_.1), channel_id=1, source_target_pairs={{0,12},{4,0},{8,4},{12,8},{1,13},{5,1},{9,5},{13,9},{2,14},{6,2},{... | collective-permute-start | bytes 1769480 | tf_op jit(solution)/shard_map/ppermute | solution.py:17
  6.5 15.7 %collective-permute-start.2 = (bf16[768,384]{1,0:T(8,128)(2,1)}, bf16[768,384]{1,0:T(8,128)(2,1)S(1)}, u32[]{:S(2)}, u32[]{:S(2)}) collective-permute-start(bf16[768,384]{1,0:T(8,128)(2,1)} %refs_1_.1), channel_id=1, source_target_pairs={{0,4},{4,8},{8,12},{12,0},{1,5},{5,9},{9,13},{13,1},{2,6},{6,10},{... | collective-permute-start | bytes 1769480 | tf_op jit(solution)/shard_map/ppermute | solution.py:17
  6.5 16.2 %collective-permute-start.1 = (bf16[768,384]{1,0:T(8,128)(2,1)}, bf16[768,384]{1,0:T(8,128)(2,1)S(1)}, u32[]{:S(2)}, u32[]{:S(2)}) collective-permute-start(bf16[768,384]{1,0:T(8,128)(2,1)} %refs_1_.1), channel_id=1, source_target_pairs={{0,3},{1,0},{2,1},{3,2},{4,7},{5,4},{6,5},{7,6},{8,11},{9,8},{10,9... | collective-permute-start | bytes 1769480 | tf_op jit(solution)/shard_map/ppermute | solution.py:17
  16.8 15.1 %collective-permute-start.7 = (bf16[768,384]{1,0:T(8,128)(2,1)S(1)}, bf16[768,384]{1,0:T(8,128)(2,1)S(1)}, u32[]{:S(2)}, u32[]{:S(2)}) collective-permute-start(bf16[768,384]{1,0:T(8,128)(2,1)S(1)} %collective-permute-done.refs_2_), channel_id=1, source_target_pairs={{0,12},{4,0},{8,4},{12,8},{1,13},{5,1},{9,5},{13,9},{2,14},{6,2},{... | collective-permute-start | bytes 1769480 | tf_op jit(solution)/shard_map/ppermute | solution.py:17
  20.9 13.0 %collective-permute-start.5 = (bf16[768,384]{1,0:T(8,128)(2,1)S(1)}, bf16[768,384]{1,0:T(8,128)(2,1)S(1)}, u32[]{:S(2)}, u32[]{:S(2)}) collective-permute-start(bf16[768,384]{1,0:T(8,128)(2,1)S(1)} %collective-permute-done.3.refs_5_), channel_id=1, source_target_pairs={{0,3},{1,0},{2,1},{3,2},{4,7},{5,4},{6,5},{7,6},{8,11},{9,8},{10,9... | collective-permute-start | bytes 1769480 | tf_op jit(solution)/shard_map/ppermute | solution.py:17
  22.2 13.9 %collective-permute-start.4 = (bf16[768,384]{1,0:T(8,128)(2,1)S(1)}, bf16[768,384]{1,0:T(8,128)(2,1)S(1)}, u32[]{:S(2)}, u32[]{:S(2)}) collective-permute-start(bf16[768,384]{1,0:T(8,128)(2,1)S(1)} %collective-permute-done.2.refs_4_), channel_id=1, source_target_pairs={{0,1},{1,2},{2,3},{3,0},{4,5},{5,6},{6,7},{7,4},{8,9},{9,10},{10,1... | collective-permute-start | bytes 1769480 | tf_op jit(solution)/shard_map/ppermute | solution.py:17
  22.7 13.6 %collective-permute-start.6 = (bf16[768,384]{1,0:T(8,128)(2,1)S(1)}, bf16[768,384]{1,0:T(8,128)(2,1)S(1)}, u32[]{:S(2)}, u32[]{:S(2)}) collective-permute-start(bf16[768,384]{1,0:T(8,128)(2,1)S(1)} %collective-permute-done.1.refs_3_), channel_id=1, source_target_pairs={{0,4},{4,8},{8,12},{12,0},{1,5},{5,9},{9,13},{13,1},{2,6},{6,10},{... | collective-permute-start | bytes 1769480 | tf_op jit(solution)/shard_map/ppermute | solution.py:17
  32.0 16.8 %collective-permute-start.8 = (bf16[768,384]{1,0:T(8,128)(2,1)S(1)}, bf16[768,384]{1,0:T(8,128)(2,1)S(1)}, u32[]{:S(2)}, u32[]{:S(2)}) collective-permute-start(bf16[768,384]{1,0:T(8,128)(2,1)S(1)} %collective-permute-done.7.refs_4_.refs_15_.refs_21_), channel_id=1, source_target_pairs={{0,1},{1,2},{2,3},{3,0},{4,5},{5,6},{6,7},{7,4},{8,9},{9,10},{10,1... | collective-permute-start | bytes 1769480 | tf_op jit(solution)/shard_map/ppermute | solution.py:17
  33.9 17.9 %collective-permute-start.11 = (bf16[768,384]{1,0:T(8,128)(2,1)S(1)}, bf16[768,384]{1,0:T(8,128)(2,1)S(1)}, u32[]{:S(2)}, u32[]{:S(2)}) collective-permute-start(bf16[768,384]{1,0:T(8,128)(2,1)S(1)} %collective-permute-done.5.refs_2_.refs_13_.refs_19_), channel_id=1, source_target_pairs={{0,12},{4,0},{8,4},{12,8},{1,13},{5,1},{9,5},{13,9},{2,14},{6,2},{... | collective-permute-start | bytes 1769480 | tf_op jit(solution)/shard_map/ppermute | solution.py:17
  36.1 15.7 %collective-permute-start.10 = (bf16[768,384]{1,0:T(8,128)(2,1)S(1)}, bf16[768,384]{1,0:T(8,128)(2,1)S(1)}, u32[]{:S(2)}, u32[]{:S(2)}) collective-permute-start(bf16[768,384]{1,0:T(8,128)(2,1)S(1)} %collective-permute-done.4.refs_1_.refs_12_.refs_18_), channel_id=1, source_target_pairs={{0,4},{4,8},{8,12},{12,0},{1,5},{5,9},{9,13},{13,1},{2,6},{6,10},{... | collective-permute-start | bytes 1769480 | tf_op jit(solution)/shard_map/ppermute | solution.py:17
  36.3 15.5 %collective-permute-start.9 = (bf16[768,384]{1,0:T(8,128)(2,1)S(1)}, bf16[768,384]{1,0:T(8,128)(2,1)S(1)}, u32[]{:S(2)}, u32[]{:S(2)}) collective-permute-start(bf16[768,384]{1,0:T(8,128)(2,1)S(1)} %collective-permute-done.6.refs_3_.refs_14_.refs_20_), channel_id=1, source_target_pairs={{0,3},{1,0},{2,1},{3,2},{4,7},{5,4},{6,5},{7,6},{8,11},{9,8},{10,9... | collective-permute-start | bytes 1769480 | tf_op jit(solution)/shard_map/ppermute | solution.py:17
  38.5 15.2 %collective-permute-start.21 = (f32[64,1920]{1,0:T(8,128)S(1)}, f32[64,1920]{1,0:T(8,128)S(1)}, u32[]{:S(2)}, u32[]{:S(2)}) collective-permute-start(f32[64,1920]{1,0:T(8,128)S(1)} %get-tuple-element.55), channel_id=1, source_target_pairs={{0,16},{16,0},{1,17},{17,1},{2,18},{18,2},{3,19},{19,3},{4,20},{20... | collective-permute-start | bytes 1474568 | tf_op jit(solution)/shard_map/ppermute | solution.py:21
  48.8 5.7 %collective-permute-start.22 = (f32[64,1536]{1,0:T(8,128)S(1)}, f32[64,1536]{1,0:T(8,128)S(1)}, u32[]{:S(2)}, u32[]{:S(2)}) collective-permute-start(f32[64,1536]{1,0:T(8,128)S(1)} %get-tuple-element.57), channel_id=1, source_target_pairs={{0,16},{16,0},{1,17},{17,1},{2,18},{18,2},{3,19},{19,3},{4,20},{20... | collective-permute-start | bytes 1179656 | tf_op jit(solution)/shard_map/ppermute | solution.py:21
  53.8 17.1 %collective-permute-start.12 = (bf16[768,384]{1,0:T(8,128)(2,1)S(1)}, bf16[768,384]{1,0:T(8,128)(2,1)S(1)}, u32[]{:S(2)}, u32[]{:S(2)}) collective-permute-start(bf16[768,384]{1,0:T(8,128)(2,1)S(1)} %collective-permute-done.refs_2_), channel_id=1, source_target_pairs={{0,1},{1,2},{2,3},{3,0},{4,5},{5,6},{6,7},{7,4},{8,9},{9,10},{10,1... | collective-permute-start | bytes 1769480 | tf_op jit(solution)/shard_map/ppermute | solution.py:17
  54.5 16.5 %collective-permute-start.13 = (bf16[768,384]{1,0:T(8,128)(2,1)S(1)}, bf16[768,384]{1,0:T(8,128)(2,1)S(1)}, u32[]{:S(2)}, u32[]{:S(2)}) collective-permute-start(bf16[768,384]{1,0:T(8,128)(2,1)S(1)} %collective-permute-done.2.refs_4_), channel_id=1, source_target_pairs={{0,4},{4,8},{8,12},{12,0},{1,5},{5,9},{9,13},{13,1},{2,6},{6,10},{... | collective-permute-start | bytes 1769480 | tf_op jit(solution)/shard_map/ppermute | solution.py:17
  55.3 6.7 %collective-permute-start.24 = (bf16[16,4992]{1,0:T(8,128)(2,1)S(1)}, bf16[16,4992]{1,0:T(8,128)(2,1)S(1)}, u32[]{:S(2)}, u32[]{:S(2)}) collective-permute-start(bf16[16,4992]{1,0:T(8,128)(2,1)S(1)} %get-tuple-element.86), channel_id=1, source_target_pairs={{0,32},{32,64},{64,96},{96,0},{1,33},{33,65},{65,97},{97,1},{2,34}... | collective-permute-start | bytes 479240 | tf_op jit(solution)/shard_map/ppermute | solution.py:17
  56.6 9.9 %collective-permute-start.25 = (bf16[16,4992]{1,0:T(8,128)(2,1)S(1)}, bf16[16,4992]{1,0:T(8,128)(2,1)S(1)}, u32[]{:S(2)}, u32[]{:S(2)}) collective-permute-start(bf16[16,4992]{1,0:T(8,128)(2,1)S(1)} %get-tuple-element.85), channel_id=1, source_target_pairs={{0,64},{32,96},{64,0},{96,32},{1,65},{33,97},{65,1},{97,33},{2,66}... | collective-permute-start | bytes 479240 | tf_op jit(solution)/shard_map/ppermute | solution.py:17
  59.3 11.7 %collective-permute-start.15 = (bf16[384,384]{1,0:T(8,128)(2,1)S(1)}, bf16[384,384]{1,0:T(8,128)(2,1)S(1)}, u32[]{:S(2)}, u32[]{:S(2)}) collective-permute-start(bf16[384,384]{1,0:T(8,128)(2,1)S(1)} %slice.138), channel_id=1, source_target_pairs={{0,12},{4,0},{8,4},{12,8},{1,13},{5,1},{9,5},{13,9},{2,14},{6,2},{... | collective-permute-start | bytes 884744 | tf_op jit(solution)/shard_map/ppermute | solution.py:17
  62.0 9.0 %collective-permute-start.14 = (bf16[384,384]{1,0:T(8,128)(2,1)S(1)}, bf16[384,384]{1,0:T(8,128)(2,1)S(1)}, u32[]{:S(2)}, u32[]{:S(2)}) collective-permute-start(bf16[384,384]{1,0:T(8,128)(2,1)S(1)} %slice.137), channel_id=1, source_target_pairs={{0,3},{1,0},{2,1},{3,2},{4,7},{5,4},{6,5},{7,6},{8,11},{9,8},{10,9... | collective-permute-start | bytes 884744 | tf_op jit(solution)/shard_map/ppermute | solution.py:17
  66.5 4.4 %collective-permute-start.26 = (bf16[16,4992]{1,0:T(8,128)(2,1)S(1)}, bf16[16,4992]{1,0:T(8,128)(2,1)S(1)}, u32[]{:S(2)}, u32[]{:S(2)}) collective-permute-start(bf16[16,4992]{1,0:T(8,128)(2,1)S(1)} %get-tuple-element.84), channel_id=1, source_target_pairs={{0,96},{32,0},{64,32},{96,64},{1,97},{33,1},{65,33},{97,65},{2,98}... | collective-permute-start | bytes 479240 | tf_op jit(solution)/shard_map/ppermute | solution.py:17
  71.5 4.1 %collective-permute-start.16 = (f32[8,128]{1,0:T(8,128)S(1)}, f32[8,128]{1,0:T(8,128)S(1)}, u32[]{:S(2)}, u32[]{:S(2)}) collective-permute-start(f32[8,128]{1,0:T(8,128)S(1)} %add_add_fusion), channel_id=1, source_target_pairs={{0,16},{16,0},{1,17},{17,1},{2,18},{18,2},{3,19},{19,3},{4,20},{20... | collective-permute-start | bytes 12296 | tf_op jit(solution)/shard_map/ppermute | solution.py:21
  73.8 9.0 %collective-permute-start.27 = (bf16[16,4992]{1,0:T(8,128)(2,1)S(1)}, bf16[16,4992]{1,0:T(8,128)(2,1)S(1)}, u32[]{:S(2)}, u32[]{:S(2)}) collective-permute-start(bf16[16,4992]{1,0:T(8,128)(2,1)S(1)} %fusion.5.refs_1_), channel_id=1, source_target_pairs={{0,96},{32,0},{64,32},{96,64},{1,97},{33,1},{65,33},{97,65},{2,98}... | collective-permute-start | bytes 479240 | tf_op jit(solution)/shard_map/ppermute | solution.py:17
  77.0 18.6 %collective-permute-start.18 = (bf16[64,1280]{1,0:T(8,128)(2,1)S(1)}, bf16[64,1280]{1,0:T(8,128)(2,1)S(1)}, u32[]{:S(2)}, u32[]{:S(2)}) collective-permute-start(bf16[64,1280]{1,0:T(8,128)(2,1)S(1)} %pad_maximum_fusion.1), channel_id=1, source_target_pairs={{0,32},{32,64},{64,96},{96,0},{1,33},{33,65},{65,97},{97,1},{2,34}... | collective-permute-start | bytes 491528 | tf_op jit(solution)/shard_map/ppermute | solution.py:17
  77.1 18.6 %collective-permute-start.19 = (bf16[64,1280]{1,0:T(8,128)(2,1)S(1)}, bf16[64,1280]{1,0:T(8,128)(2,1)S(1)}, u32[]{:S(2)}, u32[]{:S(2)}) collective-permute-start(bf16[64,1280]{1,0:T(8,128)(2,1)S(1)} %pad_maximum_fusion.1), channel_id=1, source_target_pairs={{0,96},{32,0},{64,32},{96,64},{1,97},{33,1},{65,33},{97,65},{2,98}... | collective-permute-start | bytes 491528 | tf_op jit(solution)/shard_map/ppermute | solution.py:17
  79.8 16.4 %collective-permute-start.20 = (bf16[64,1280]{1,0:T(8,128)(2,1)S(1)}, bf16[64,1280]{1,0:T(8,128)(2,1)S(1)}, u32[]{:S(2)}, u32[]{:S(2)}) collective-permute-start(bf16[64,1280]{1,0:T(8,128)(2,1)S(1)} %pad_maximum_fusion.1), channel_id=1, source_target_pairs={{0,64},{32,96},{64,0},{96,32},{1,65},{33,97},{65,1},{97,33},{2,66}... | collective-permute-start | bytes 491528 | tf_op jit(solution)/shard_map/ppermute | solution.py:17
  80.4 10.7 %collective-permute-start.28 = (bf16[16,4992]{1,0:T(8,128)(2,1)S(1)}, bf16[16,4992]{1,0:T(8,128)(2,1)S(1)}, u32[]{:S(2)}, u32[]{:S(2)}) collective-permute-start(bf16[16,4992]{1,0:T(8,128)(2,1)S(1)} %fusion.5.refs_1_), channel_id=1, source_target_pairs={{0,64},{32,96},{64,0},{96,32},{1,65},{33,97},{65,1},{97,33},{2,66}... | collective-permute-start | bytes 479240 | tf_op jit(solution)/shard_map/ppermute | solution.py:17
  82.8 12.4 %collective-permute-start.29 = (bf16[16,4992]{1,0:T(8,128)(2,1)S(1)}, bf16[16,4992]{1,0:T(8,128)(2,1)S(1)}, u32[]{:S(2)}, u32[]{:S(2)}) collective-permute-start(bf16[16,4992]{1,0:T(8,128)(2,1)S(1)} %fusion.5.refs_1_), channel_id=1, source_target_pairs={{0,32},{32,64},{64,96},{96,0},{1,33},{33,65},{65,97},{97,1},{2,34}... | collective-permute-start | bytes 479240 | tf_op jit(solution)/shard_map/ppermute | solution.py:17
  91.2 5.4 %collective-permute-start.30 = (bf16[16,4992]{1,0:T(8,128)(2,1)S(1)}, bf16[16,4992]{1,0:T(8,128)(2,1)S(1)}, u32[]{:S(2)}, u32[]{:S(2)}) collective-permute-start(bf16[16,4992]{1,0:T(8,128)(2,1)S(1)} %fusion.5.refs_1_), channel_id=1, source_target_pairs={{0,16},{16,0},{1,17},{17,1},{2,18},{18,2},{3,19},{19,3},{4,20},{20... | collective-permute-start | bytes 479240 | tf_op jit(solution)/shard_map/ppermute | solution.py:21
  102.7 5.0 %collective-permute-start.35 = (f32[64,3072]{1,0:T(8,128)S(1)}, f32[64,3072]{1,0:T(8,128)S(1)}, u32[]{:S(2)}, u32[]{:S(2)}) collective-permute-start(f32[64,3072]{1,0:T(8,128)S(1)} %get-tuple-element.65), channel_id=1, source_target_pairs={{0,16},{16,0},{1,17},{17,1},{2,18},{18,2},{3,19},{19,3},{4,20},{20... | collective-permute-start | bytes 2359304 | tf_op jit(solution)/shard_map/ppermute | solution.py:21
  105.0 7.8 %collective-permute-start.47 = (bf16[16,3072]{1,0:T(8,128)(2,1)S(1)}, bf16[16,3072]{1,0:T(8,128)(2,1)S(1)}, u32[]{:S(2)}, u32[]{:S(2)}) collective-permute-start(bf16[16,3072]{1,0:T(8,128)(2,1)S(1)} %get-tuple-element.89), channel_id=1, source_target_pairs={{0,32},{32,64},{64,96},{96,0},{1,33},{33,65},{65,97},{97,1},{2,34}... | collective-permute-start | bytes 294920 | tf_op jit(solution)/shard_map/ppermute | solution.py:17
  105.0 7.7 %collective-permute-start.48 = (bf16[16,3072]{1,0:T(8,128)(2,1)S(1)}, bf16[16,3072]{1,0:T(8,128)(2,1)S(1)}, u32[]{:S(2)}, u32[]{:S(2)}) collective-permute-start(bf16[16,3072]{1,0:T(8,128)(2,1)S(1)} %get-tuple-element.88), channel_id=1, source_target_pairs={{0,64},{32,96},{64,0},{96,32},{1,65},{33,97},{65,1},{97,33},{2,66}... | collective-permute-start | bytes 294920 | tf_op jit(solution)/shard_map/ppermute | solution.py:17
  106.5 6.4 %collective-permute-start.49 = (bf16[16,3072]{1,0:T(8,128)(2,1)S(1)}, bf16[16,3072]{1,0:T(8,128)(2,1)S(1)}, u32[]{:S(2)}, u32[]{:S(2)}) collective-permute-start(bf16[16,3072]{1,0:T(8,128)(2,1)S(1)} %get-tuple-element.87), channel_id=1, source_target_pairs={{0,96},{32,0},{64,32},{96,64},{1,97},{33,1},{65,33},{97,65},{2,98}... | collective-permute-start | bytes 294920 | tf_op jit(solution)/shard_map/ppermute | solution.py:17
  107.8 9.1 %collective-permute-start.36 = (bf16[16,3072]{1,0:T(8,128)(2,1)S(1)}, bf16[16,3072]{1,0:T(8,128)(2,1)S(1)}, u32[]{:S(2)}, u32[]{:S(2)}) collective-permute-start(bf16[16,3072]{1,0:T(8,128)(2,1)S(1)} %get-tuple-element.92), channel_id=1, source_target_pairs={{0,32},{32,64},{64,96},{96,0},{1,33},{33,65},{65,97},{97,1},{2,34}... | collective-permute-start | bytes 294920 | tf_op jit(solution)/shard_map/ppermute | solution.py:17
  108.5 8.4 %collective-permute-start.37 = (bf16[16,3072]{1,0:T(8,128)(2,1)S(1)}, bf16[16,3072]{1,0:T(8,128)(2,1)S(1)}, u32[]{:S(2)}, u32[]{:S(2)}) collective-permute-start(bf16[16,3072]{1,0:T(8,128)(2,1)S(1)} %get-tuple-element.91), channel_id=1, source_target_pairs={{0,64},{32,96},{64,0},{96,32},{1,65},{33,97},{65,1},{97,33},{2,66}... | collective-permute-start | bytes 294920 | tf_op jit(solution)/shard_map/ppermute | solution.py:17
  112.7 6.1 %collective-permute-start.38 = (bf16[16,3072]{1,0:T(8,128)(2,1)S(1)}, bf16[16,3072]{1,0:T(8,128)(2,1)S(1)}, u32[]{:S(2)}, u32[]{:S(2)}) collective-permute-start(bf16[16,3072]{1,0:T(8,128)(2,1)S(1)} %get-tuple-element.90), channel_id=1, source_target_pairs={{0,96},{32,0},{64,32},{96,64},{1,97},{33,1},{65,33},{97,65},{2,98}... | collective-permute-start | bytes 294920 | tf_op jit(solution)/shard_map/ppermute | solution.py:17
  112.9 8.6 %collective-permute-start.50 = (bf16[16,3072]{1,0:T(8,128)(2,1)S(1)}, bf16[16,3072]{1,0:T(8,128)(2,1)S(1)}, u32[]{:S(2)}, u32[]{:S(2)}) collective-permute-start(bf16[16,3072]{1,0:T(8,128)(2,1)S(1)} %fusion.9.refs_9_), channel_id=1, source_target_pairs={{0,96},{32,0},{64,32},{96,64},{1,97},{33,1},{65,33},{97,65},{2,98}... | collective-permute-start | bytes 294920 | tf_op jit(solution)/shard_map/ppermute | solution.py:17
  115.8 6.6 %collective-permute-start.51 = (bf16[16,3072]{1,0:T(8,128)(2,1)S(1)}, bf16[16,3072]{1,0:T(8,128)(2,1)S(1)}, u32[]{:S(2)}, u32[]{:S(2)}) collective-permute-start(bf16[16,3072]{1,0:T(8,128)(2,1)S(1)} %fusion.9.refs_9_), channel_id=1, source_target_pairs={{0,64},{32,96},{64,0},{96,32},{1,65},{33,97},{65,1},{97,33},{2,66}... | collective-permute-start | bytes 294920 | tf_op jit(solution)/shard_map/ppermute | solution.py:17
  116.9 5.4 %collective-permute-start.52 = (bf16[16,3072]{1,0:T(8,128)(2,1)S(1)}, bf16[16,3072]{1,0:T(8,128)(2,1)S(1)}, u32[]{:S(2)}, u32[]{:S(2)}) collective-permute-start(bf16[16,3072]{1,0:T(8,128)(2,1)S(1)} %fusion.9.refs_9_), channel_id=1, source_target_pairs={{0,32},{32,64},{64,96},{96,0},{1,33},{33,65},{65,97},{97,1},{2,34}... | collective-permute-start | bytes 294920 | tf_op jit(solution)/shard_map/ppermute | solution.py:17
  116.9 8.0 %collective-permute-start.53 = (bf16[16,3072]{1,0:T(8,128)(2,1)S(1)}, bf16[16,3072]{1,0:T(8,128)(2,1)S(1)}, u32[]{:S(2)}, u32[]{:S(2)}) collective-permute-start(bf16[16,3072]{1,0:T(8,128)(2,1)S(1)} %fusion.9.refs_9_), channel_id=1, source_target_pairs={{0,16},{16,0},{1,17},{17,1},{2,18},{18,2},{3,19},{19,3},{4,20},{20... | collective-permute-start | bytes 294920 | tf_op jit(solution)/shard_map/ppermute | solution.py:21
  118.8 6.1 %collective-permute-start.39 = (bf16[16,3072]{1,0:T(8,128)(2,1)S(1)}, bf16[16,3072]{1,0:T(8,128)(2,1)S(1)}, u32[]{:S(2)}, u32[]{:S(2)}) collective-permute-start(bf16[16,3072]{1,0:T(8,128)(2,1)S(1)} %fusion.12.refs_1_), channel_id=1, source_target_pairs={{0,96},{32,0},{64,32},{96,64},{1,97},{33,1},{65,33},{97,65},{2,98}... | collective-permute-start | bytes 294920 | tf_op jit(solution)/shard_map/ppermute | solution.py:17
  121.5 5.6 %collective-permute-start.40 = (bf16[16,3072]{1,0:T(8,128)(2,1)S(1)}, bf16[16,3072]{1,0:T(8,128)(2,1)S(1)}, u32[]{:S(2)}, u32[]{:S(2)}) collective-permute-start(bf16[16,3072]{1,0:T(8,128)(2,1)S(1)} %fusion.12.refs_1_), channel_id=1, source_target_pairs={{0,64},{32,96},{64,0},{96,32},{1,65},{33,97},{65,1},{97,33},{2,66}... | collective-permute-start | bytes 294920 | tf_op jit(solution)/shard_map/ppermute | solution.py:17
  122.3 7.2 %collective-permute-start.41 = (bf16[16,3072]{1,0:T(8,128)(2,1)S(1)}, bf16[16,3072]{1,0:T(8,128)(2,1)S(1)}, u32[]{:S(2)}, u32[]{:S(2)}) collective-permute-start(bf16[16,3072]{1,0:T(8,128)(2,1)S(1)} %fusion.12.refs_1_), channel_id=1, source_target_pairs={{0,32},{32,64},{64,96},{96,0},{1,33},{33,65},{65,97},{97,1},{2,34}... | collective-permute-start | bytes 294920 | tf_op jit(solution)/shard_map/ppermute | solution.py:17
  122.3 8.1 %collective-permute-start.42 = (bf16[16,3072]{1,0:T(8,128)(2,1)S(1)}, bf16[16,3072]{1,0:T(8,128)(2,1)S(1)}, u32[]{:S(2)}, u32[]{:S(2)}) collective-permute-start(bf16[16,3072]{1,0:T(8,128)(2,1)S(1)} %fusion.12.refs_1_), channel_id=1, source_target_pairs={{0,16},{16,0},{1,17},{17,1},{2,18},{18,2},{3,19},{19,3},{4,20},{20... | collective-permute-start | bytes 294920 | tf_op jit(solution)/shard_map/ppermute | solution.py:21
  124.9 5.5 %collective-permute-start.54 = (bf16[16,3072]{1,0:T(8,128)(2,1)S(1)}, bf16[16,3072]{1,0:T(8,128)(2,1)S(1)}, u32[]{:S(2)}, u32[]{:S(2)}) collective-permute-start(bf16[16,3072]{1,0:T(8,128)(2,1)S(1)} %collective-permute-done.50.refs_10_), channel_id=1, source_target_pairs={{0,16},{16,0},{1,17},{17,1},{2,18},{18,2},{3,19},{19,3},{4,20},{20... | collective-permute-start | bytes 294920 | tf_op jit(solution)/shard_map/ppermute | solution.py:21
  125.0 6.2 %collective-permute-start.55 = (bf16[16,3072]{1,0:T(8,128)(2,1)S(1)}, bf16[16,3072]{1,0:T(8,128)(2,1)S(1)}, u32[]{:S(2)}, u32[]{:S(2)}) collective-permute-start(bf16[16,3072]{1,0:T(8,128)(2,1)S(1)} %collective-permute-done.51.refs_11_), channel_id=1, source_target_pairs={{0,16},{16,0},{1,17},{17,1},{2,18},{18,2},{3,19},{19,3},{4,20},{20... | collective-permute-start | bytes 294920 | tf_op jit(solution)/shard_map/ppermute | solution.py:21
  127.2 4.0 %collective-permute-start.56 = (bf16[16,3072]{1,0:T(8,128)(2,1)S(1)}, bf16[16,3072]{1,0:T(8,128)(2,1)S(1)}, u32[]{:S(2)}, u32[]{:S(2)}) collective-permute-start(bf16[16,3072]{1,0:T(8,128)(2,1)S(1)} %collective-permute-done.52.refs_12_), channel_id=1, source_target_pairs={{0,16},{16,0},{1,17},{17,1},{2,18},{18,2},{3,19},{19,3},{4,20},{20... | collective-permute-start | bytes 294920 | tf_op jit(solution)/shard_map/ppermute | solution.py:21
  135.8 16.0 %all-to-all-start = ((bf16[4,768,128]{2,1,0:T(8,128)(2,1)}), bf16[4,768,128]{2,1,0:T(8,128)(2,1)S(1)}, u32[]{:S(2)}, u32[]{:S(2)}) async-start(bf16[4,768,128]{2,1,0:T(8,128)(2,1)} %get-tuple-element.75), calls=%async_computation | async-start | bytes 1572864 | tf_op jit(solution)/shard_map/all_to_all | solution.py:216
  (14 other events, 46.7 us)
